TPU v7x, 32 devices: a whole 2x2x4 slice. The times are simulated.
32 devices in a mesh: seq: 16 (over z, y, x), head: 2 (over core).
Axes of the slice: x: 2, y: 2, z: 4, core: 2. Of those that a mesh axis runs over, the one named last changes fastest.
Arguments:
- input_rows: bfloat16 [4096, 4096], P(('seq', 'head')), may hold values from -40 to 40
- doc_lengths: int32 [8], replicated, may hold values from 1 to 1024, 4096 in all
- w_query: bfloat16 [4096, 4096], P(None, 'head'), may hold values from -0.09375 to 0.09375
- key_weight: bfloat16 [4096, 1024], P(None, 'head'), may hold values from -0.09375 to 0.09375
- value_weight: bfloat16 [4096, 1024], P(None, 'head'), may hold values from -0.09375 to 0.09375
- w_out: bfloat16 [4096, 4096], P('head'), may hold values from -0.5 to 0.5
Outputs:
- mixed: bfloat16 [4096, 4096], P(('seq', 'head'))
All inputs are finite; a program needn't handle non-finite values.
Results may differ from a plain program's by a relative error of at most 0.013.
Values may be sent and summed in bfloat16 or wider, within the bound.
No kernel may reach another device: no remote copies, remote signals or barrier semaphores. Data moves between devices by JAX's collectives and lax.ppermute only.
A program may use at most 192 MiB of HBM per device.

v0:
```python
import math

import jax
import jax.numpy as jnp
from jax import lax
from jax.sharding import PartitionSpec as P

HEAD_SIZE = 128
REACH = 4


NEG_FILL = -1e30


def passed_along(value, axis, steps):
    count = lax.axis_size(axis)
    first, last = (max(0, -steps), min(count, count - steps))
    return lax.ppermute(value, axis, [(source, source + steps) for source in range(first, last)])


def inverse_frequency():
    table = []
    for number in range(HEAD_SIZE // 2):
        base_freq = 500000.0 ** (-(2.0 * number) / HEAD_SIZE)
        wavelength = 2.0 * math.pi / base_freq
        smooth = (8192.0 / wavelength - 1.0) / 3.0
        if wavelength < 2048.0:
            table.append(base_freq)
        elif wavelength > 8192.0:
            table.append(base_freq / 8.0)
        else:
            table.append((1.0 - smooth) * base_freq / 8.0 + smooth * base_freq)
    return jnp.asarray(table, dtype=jnp.float32)


def rotate(value_matrix, cosine, sine_table):
    half_size = value_matrix.shape[-1] // 2
    first = value_matrix[..., :half_size]
    second = value_matrix[..., half_size:]
    return jnp.concatenate(
        [first * cosine - second * sine_table, second * cosine + first * sine_table], axis=-1
    )


def doc_of(positions, doc_ends):
    return jnp.sum((positions[:, None] >= doc_ends[None, :]).astype(jnp.int32), axis=1)


def body(input_rows, doc_lengths, w_query, key_weight, value_weight, w_out):
    width_q = w_query.shape[1]
    width_k = key_weight.shape[1]
    heads_here = width_q // HEAD_SIZE
    kv_here = width_k // HEAD_SIZE
    query_group = heads_here // kv_here
    piece = lax.all_gather(input_rows, "head", axis=0, tiled=True)
    projected = jnp.concatenate(
        [
            jnp.dot(piece, w_query, preferred_element_type=jnp.float32),
            jnp.dot(piece, key_weight, preferred_element_type=jnp.float32),
            jnp.dot(piece, value_weight, preferred_element_type=jnp.float32),
        ],
        axis=1,
    )
    tok_seq = projected.shape[0]
    seq_index = lax.axis_index("seq")
    positions = seq_index * tok_seq + jnp.arange(tok_seq, dtype=jnp.int32)
    doc_ends = jnp.cumsum(doc_lengths)
    query_docs = doc_of(positions, doc_ends)
    angles = positions.astype(jnp.float32)[:, None] * inverse_frequency()[None, :]
    cosine = jnp.cos(angles)[:, None, :]
    sine_table = jnp.sin(angles)[:, None, :]
    query_matrix = rotate(
        projected[:, :width_q].reshape(tok_seq, heads_here, HEAD_SIZE), cosine, sine_table
    )
    query_matrix = query_matrix.astype(jnp.bfloat16).reshape(
        tok_seq, kv_here, query_group, HEAD_SIZE
    )
    key_matrix = rotate(
        projected[:, width_q : width_q + width_k].reshape(tok_seq, kv_here, HEAD_SIZE),
        cosine,
        sine_table,
    )
    key_matrix = key_matrix.astype(jnp.bfloat16).reshape(tok_seq, width_k)
    value_matrix = projected[:, width_q + width_k :].astype(jnp.bfloat16)
    scale = HEAD_SIZE ** (-0.5)

    def attend(state, key_rows, value_rows, key_pos):
        running_max, running_sum, weighted = state
        count = key_rows.shape[0]
        key_block = key_rows.reshape(count, kv_here, HEAD_SIZE)
        value_block = value_rows.reshape(count, kv_here, HEAD_SIZE)
        key_docs = doc_of(key_pos, doc_ends)
        scores = (
            jnp.einsum(
                "tkgd,skd->kgts", query_matrix, key_block, preferred_element_type=jnp.float32
            )
            * scale
        )
        allowed = (
            (query_docs[:, None] == key_docs[None, :])
            & (key_pos[None, :] <= positions[:, None])
            & (key_pos[None, :] >= 0)
        )
        scores = jnp.where(allowed, scores, NEG_FILL)
        new_max = jnp.maximum(running_max, jnp.max(scores, axis=-1))
        factor = jnp.exp(running_max - new_max)
        weights = jnp.where(allowed, jnp.exp(scores - new_max[..., None]), 0.0)
        running_sum = running_sum * factor + jnp.sum(weights, axis=-1)
        weighted = weighted * factor[..., None] + jnp.einsum(
            "kgts,skd->kgtd",
            weights.astype(jnp.bfloat16),
            value_block,
            preferred_element_type=jnp.float32,
        )
        return (new_max, running_sum, weighted)

    initial = (
        jnp.full((kv_here, query_group, tok_seq), NEG_FILL, jnp.float32),
        jnp.zeros((kv_here, query_group, tok_seq), jnp.float32),
        jnp.zeros((kv_here, query_group, tok_seq, HEAD_SIZE), jnp.float32),
    )
    state = attend(initial, key_matrix, value_matrix, positions)
    for distance in range(1, REACH + 1):
        earlier = passed_along((key_matrix, value_matrix), "seq", distance)
        state = attend(state, earlier[0], earlier[1], positions - distance * tok_seq)
    final_max, final_sum, final_weighted = state
    attended = (final_weighted / final_sum[..., None]).transpose(2, 0, 1, 3)
    attended = attended.reshape(tok_seq, heads_here * HEAD_SIZE).astype(jnp.bfloat16)
    return lax.psum_scatter(
        jnp.dot(attended, w_out, preferred_element_type=jnp.float32).astype(jnp.bfloat16),
        "head",
        scatter_dimension=0,
        tiled=True,
    )


def solution(mesh):
    in_specs = (
        P(("seq", "head"), None),
        P(),
        P(None, "head"),
        P(None, "head"),
        P(None, "head"),
        P("head", None),
    )
    out_specs = P(("seq", "head"), None)
    return jax.shard_map(body, mesh=mesh, in_specs=in_specs, out_specs=out_specs, check_vma=False)
```

profile of v0, /device:TPU:25, one launch (start us, length us, event | category | flops | bytes accessed | tf_op | source)
XLA Modules:
  0.0 132.8 jit_solution(9975176218019796431)
XLA Ops:
  7.3 0.8 reduce-window.8
  8.3 1.2 multiply_cosine_fusion
  10.2 11.0 %all-gather.2.cloned.1.call-done = bf16[256,4096]{1,0:T(8,128)(2,1)} async-done(((bf16[128,4096]{1,0:T(8,128)(2,1)}), bf16[256,4096]{1,0:T(8,128)(2,1)}) %all-gather.2.cloned.1.call-update) | async-done | bytes 2097168 | tf_op jit(solution)/shard_map/all_gather | solution.py:55
  21.2 4.1 %fusion.94 = f32[256,512]{1,0:T(8,128)S(1)} fusion(bf16[256,4096]{1,0:T(8,128)(2,1)} %all-gather.2.cloned.1.call-done, bf16[4096,512]{1,0:T(8,128)(2,1)} %param.10), kind=kOutput, calls=%fused_computation.140 | convolution fusion | flops 1073741824 | bytes 6815744 | tf_op jit(solution)/shard_map/dot_general | solution.py:59
  26.3 3.1 %collective-permute-start.2 = (bf16[256,512]{0,1:T(8,128)(2,1)S(1)}, bf16[256,512]{0,1:T(8,128)(2,1)S(1)}, u32[]{:S(2)}, u32[]{:S(2)}) collective-permute-start(bf16[256,512]{0,1:T(8,128)(2,1)S(1)} %bitcast.275), channel_id=1, source_target_pairs={{0,4},{2,6},{4,8},{6,10},{8,12},{10,14},{12,16},{14,18},{16,20},{1... | collective-permute-start | bytes 786440 | tf_op jit(solution)/shard_map/ppermute | solution.py:18
  29.4 3.1 %collective-permute-start = (bf16[256,512]{0,1:T(8,128)(2,1)S(1)}, bf16[256,512]{0,1:T(8,128)(2,1)S(1)}, u32[]{:S(2)}, u32[]{:S(2)}) collective-permute-start(bf16[256,512]{0,1:T(8,128)(2,1)S(1)} %bitcast.276), channel_id=1, source_target_pairs={{0,2},{2,4},{4,6},{6,8},{8,10},{10,12},{12,14},{14,16},{16,18},{18... | collective-permute-start | bytes 786440 | tf_op jit(solution)/shard_map/ppermute | solution.py:18
  32.5 1.3 collective-permute-start.6
  33.8 1.9 %collective-permute-start.4 = (bf16[256,512]{0,1:T(8,128)(2,1)S(1)}, bf16[256,512]{0,1:T(8,128)(2,1)S(1)}, u32[]{:S(2)}, u32[]{:S(2)}) collective-permute-start(bf16[256,512]{0,1:T(8,128)(2,1)S(1)} %bitcast.278), channel_id=1, source_target_pairs={{0,6},{2,8},{4,10},{6,12},{8,14},{10,16},{12,18},{14,20},{16,22},{... | collective-permute-start | bytes 786440 | tf_op jit(solution)/shard_map/ppermute | solution.py:18
  35.7 4.1 %convolution_convert_fusion.1 = bf16[256,512]{1,0:T(8,128)(2,1)S(1)} fusion(bf16[256,4096]{1,0:T(8,128)(2,1)} %all-gather.2.cloned.1.call-done, bf16[4096,512]{1,0:T(8,128)(2,1)} %param.11), kind=kOutput, calls=%fused_computation.70 | convolution fusion | flops 1073872896 | bytes 6553600 | tf_op jit(solution)/shard_map/dot_general | solution.py:60
  39.9 1.9 %collective-permute-start.1 = (bf16[256,512]{1,0:T(8,128)(2,1)S(1)}, bf16[256,512]{1,0:T(8,128)(2,1)S(1)}, u32[]{:S(2)}, u32[]{:S(2)}) collective-permute-start(bf16[256,512]{1,0:T(8,128)(2,1)S(1)} %convolution_convert_fusion.1), channel_id=1, source_target_pairs={{0,2},{2,4},{4,6},{6,8},{8,10},{10,12},{12,14},{14,16},{16,18},{18... | collective-permute-start | bytes 786440 | tf_op jit(solution)/shard_map/ppermute | solution.py:18
  41.8 8.7 %convolution_bitcast_fusion = f32[32,8,16,128]{3,1,2,0:T(8,128)S(1)} fusion(bf16[256,4096]{1,0:T(8,128)(2,1)} %all-gather.2.cloned.1.call-done, bf16[4096,2048]{1,0:T(8,128)(2,1)} %param.9), kind=kOutput, calls=%fused_computation.69 | convolution fusion | flops 4294967296 | bytes 20971520 | tf_op jit(solution)/shard_map/dot_general | solution.py:58
  51.0 0.8 subtract_convert_fusion
  52.9 0.8 fusion
  53.7 1.9 %collective-permute-start.3 = (bf16[256,512]{1,0:T(8,128)(2,1)S(1)}, bf16[256,512]{1,0:T(8,128)(2,1)S(1)}, u32[]{:S(2)}, u32[]{:S(2)}) collective-permute-start(bf16[256,512]{1,0:T(8,128)(2,1)S(1)} %convolution_convert_fusion.1), channel_id=1, source_target_pairs={{0,4},{2,6},{4,8},{6,10},{8,12},{10,14},{12,16},{14,18},{16,20},{1... | collective-permute-start | bytes 786440 | tf_op jit(solution)/shard_map/ppermute | solution.py:18
  55.6 2.9 %fusion.2 = (f32[4,4,256]{2,1,0:T(4,128)S(1)}, f32[4,256,256,4]{2,1,3,0:T(8,128)}) fusion(pred[256,256]{0,1:T(8,128)(4,1)S(1)} %get-tuple-element.28, bf16[256,4,128,1]{0,2,3,1:T(8,128)(2,1)S(1)} %bitcast.273, bf16[256,4,4,128]{3,0,2,1:T(8,128)(2,1)S(1)} %pad_maximum_fusion), kind=kOutput, calls=%fused_computation.13 | convolution fusion | flops 271577088 | bytes 5586944 | tf_op jit(solution)/shard_map/tkgd,skd->kgts/dot_general | solution.py:94
  58.5 1.9 %collective-permute-start.5 = (bf16[256,512]{1,0:T(8,128)(2,1)S(1)}, bf16[256,512]{1,0:T(8,128)(2,1)S(1)}, u32[]{:S(2)}, u32[]{:S(2)}) collective-permute-start(bf16[256,512]{1,0:T(8,128)(2,1)S(1)} %convolution_convert_fusion.1), channel_id=1, source_target_pairs={{0,6},{2,8},{4,10},{6,12},{8,14},{10,16},{12,18},{14,20},{16,22},{... | collective-permute-start | bytes 786440 | tf_op jit(solution)/shard_map/ppermute | solution.py:18
  60.4 0.9 fusion.1
  61.3 1.5 %collective-permute-start.7 = (bf16[256,512]{1,0:T(8,128)(2,1)S(1)}, bf16[256,512]{1,0:T(8,128)(2,1)S(1)}, u32[]{:S(2)}, u32[]{:S(2)}) collective-permute-start(bf16[256,512]{1,0:T(8,128)(2,1)S(1)} %convolution_convert_fusion.1), channel_id=1, source_target_pairs={{0,8},{2,10},{4,12},{6,14},{8,16},{10,18},{12,20},{14,22},{16,24},... | collective-permute-start | bytes 786440 | tf_op jit(solution)/shard_map/ppermute | solution.py:18
  62.8 2.8 %fusion.4 = (f32[4,4,256]{2,1,0:T(4,128)S(1)}, f32[4,256,256,4]{2,1,3,0:T(8,128)}) fusion(pred[256,256]{0,1:T(8,128)(4,1)S(1)} %get-tuple-element.30, bf16[256,4,128,1]{0,2,3,1:T(8,128)(2,1)S(1)} %bitcast.271, bf16[256,4,4,128]{3,0,2,1:T(8,128)(2,1)S(1)} %pad_maximum_fusion), kind=kOutput, calls=%fused_computation.15 | convolution fusion | flops 271577088 | bytes 5586944 | tf_op jit(solution)/shard_map/tkgd,skd->kgts/dot_general | solution.py:94
  65.6 2.9 %fusion.3 = (f32[4,4,256]{2,1,0:T(4,128)S(1)}, f32[4,256,256,4]{2,1,3,0:T(8,128)}) fusion(pred[256,256]{0,1:T(8,128)(4,1)S(1)} %get-tuple-element.29, bf16[256,4,128,1]{0,2,3,1:T(8,128)(2,1)S(1)} %bitcast.270, bf16[256,4,4,128]{3,0,2,1:T(8,128)(2,1)S(1)} %pad_maximum_fusion), kind=kOutput, calls=%fused_computation.14 | convolution fusion | flops 271577088 | bytes 5586944 | tf_op jit(solution)/shard_map/tkgd,skd->kgts/dot_general | solution.py:94
  68.5 1.0 fusion.5
  69.5 2.5 %fusion.23 = f32[4,4,256,128]{2,3,1,0:T(8,128)} fusion(bf16[256,4,128,1]{0,2,3,1:T(8,128)(2,1)S(1)} %bitcast.274, f32[4,256,256,4]{2,1,3,0:T(8,128)S(1)} %get-tuple-element.43, f32[4,4,256]{2,1,0:T(4,128)S(1)} %get-tuple-element.26, pred[256,256]{0,1:T(8,128)(4,1)S(1)} %get-tuple-element.27), kind=kOutput, calls=%fused_computation.30 | convolution fusion | flops 273678336 | bytes 6635520 | tf_op jit(solution)/shard_map/kgts,skd->kgtd/dot_general | solution.py:109
  72.1 1.0 fusion.7
  73.3 4.9 %fusion.21 = f32[4,4,256,128]{2,3,1,0:T(8,128)} fusion(bf16[256,4,128,1]{0,2,3,1:T(8,128)(2,1)S(1)} %bitcast.280, f32[4,256,256,4]{2,1,3,0:T(8,128)} %copy-done.3, f32[4,4,256]{2,1,0:T(4,128)S(1)} %get-tuple-element.17, pred[256,256]{0,1:T(8,128)(4,1)S(1)} %get-tuple-element.31), kind=kOutput, calls=%fused_computation.29 | convolution fusion | flops 273678336 | bytes 6635520 | tf_op jit(solution)/shard_map/kgts,skd->kgtd/dot_general | solution.py:109
  78.2 1.0 fusion.9
  79.4 4.9 %fusion.19 = f32[4,4,256,128]{2,3,1,0:T(8,128)} fusion(bf16[256,4,128,1]{0,2,3,1:T(8,128)(2,1)S(1)} %bitcast.281, f32[4,256,256,4]{2,1,3,0:T(8,128)} %get-tuple-element.39, f32[4,4,256]{2,1,0:T(4,128)S(1)} %get-tuple-element.16, pred[256,256]{0,1:T(8,128)(4,1)S(1)} %get-tuple-element.28), kind=kOutput, calls=%fused_computation.28 | convolution fusion | flops 273678336 | bytes 6635520 | tf_op jit(solution)/shard_map/kgts,skd->kgtd/dot_general | solution.py:109
  84.3 1.0 fusion.11
  85.5 4.9 %fusion.17 = f32[4,4,256,128]{2,3,1,0:T(8,128)} fusion(bf16[256,4,128,1]{0,2,3,1:T(8,128)(2,1)S(1)} %bitcast.282, f32[4,256,256,4]{2,1,3,0:T(8,128)} %get-tuple-element.37, f32[4,4,256]{2,1,0:T(4,128)S(1)} %get-tuple-element.15, pred[256,256]{0,1:T(8,128)(4,1)S(1)} %get-tuple-element.29), kind=kOutput, calls=%fused_computation.27 | convolution fusion | flops 273678336 | bytes 6635520 | tf_op jit(solution)/shard_map/kgts,skd->kgtd/dot_general | solution.py:109
  90.3 1.0 fusion.13
  91.6 6.6 %fusion.26 = bf16[256,4,4,128]{0,3,2,1:T(8,128)(2,1)S(1)} fusion(f32[4,4,256,128]{2,3,1,0:T(8,128)} %fusion.17, f32[4,4,256,128]{2,3,1,0:T(8,128)} %fusion.19, f32[4,4,256,128]{2,3,1,0:T(8,128)} %fusion.21, f32[4,4,256,128]{2,3,1,0:T(8,128)} %fusion.23, f32[256,4,4]{0,2,1:T(4,128)S(1)} %get-tuple-element.10, f32[256,4,4]{0,2,1:T(4,128)S(1)} %get-tuple-element.13, ...), kind=kOutput, calls=%fused_computation.33 | convolution fusion | flops 279445504 | bytes 14073856 | tf_op jit(solution)/shard_map/kgts,skd->kgtd/dot_general | solution.py:109
  98.2 11.6 %convolution_convert_fusion = bf16[256,4096]{1,0:T(8,128)(2,1)} fusion(bf16[256,2048]{0,1:T(8,128)(2,1)S(1)} %bitcast.269, bf16[2048,4096]{1,0:T(8,128)(2,1)} %param.12), kind=kOutput, calls=%fused_computation | convolution fusion | flops 4296015872 | bytes 19922944 | tf_op jit(solution)/shard_map/dot_general | solution.py:130
  109.8 16.1 %reduce-scatter.2.cloned.1.call-done = bf16[128,4096]{1,0:T(8,128)(2,1)} async-done(((bf16[256,4096]{1,0:T(8,128)(2,1)}), bf16[128,4096]{1,0:T(8,128)(2,1)}) %reduce-scatter.2.cloned.1.call-update) | async-done | bytes 1048592 | tf_op jit(solution)/shard_map/reduce_scatter | solution.py:129
  (44 shorter events, 4.9 us)
Async XLA Ops:
  6.5 14.7 %all-gather.2.cloned.1.call-start = ((), (), s32[]{:S(2)}) async-start(), calls=%async_computation.1 | async-start | bytes 3145728 | tf_op jit(solution)/shard_map/all_gather | solution.py:55
  7.3 118.7 %reduce-scatter.2.cloned.1.call-start = ((), (), s32[]{:S(2)}) async-start(), calls=%async_computation.2 | async-start | bytes 3145728 | tf_op jit(solution)/shard_map/reduce_scatter | solution.py:129
  26.3 27.4 %collective-permute-start.2 = (bf16[256,512]{0,1:T(8,128)(2,1)S(1)}, bf16[256,512]{0,1:T(8,128)(2,1)S(1)}, u32[]{:S(2)}, u32[]{:S(2)}) collective-permute-start(bf16[256,512]{0,1:T(8,128)(2,1)S(1)} %bitcast.275), channel_id=1, source_target_pairs={{0,4},{2,6},{4,8},{6,10},{8,12},{10,14},{12,16},{14,18},{16,20},{1... | collective-permute-start | bytes 786440 | tf_op jit(solution)/shard_map/ppermute | solution.py:18
  29.4 29.1 %collective-permute-start = (bf16[256,512]{0,1:T(8,128)(2,1)S(1)}, bf16[256,512]{0,1:T(8,128)(2,1)S(1)}, u32[]{:S(2)}, u32[]{:S(2)}) collective-permute-start(bf16[256,512]{0,1:T(8,128)(2,1)S(1)} %bitcast.276), channel_id=1, source_target_pairs={{0,2},{2,4},{4,6},{6,8},{8,10},{10,12},{12,14},{14,16},{16,18},{18... | collective-permute-start | bytes 786440 | tf_op jit(solution)/shard_map/ppermute | solution.py:18
  32.5 28.8 %collective-permute-start.6 = (bf16[256,512]{0,1:T(8,128)(2,1)S(1)}, bf16[256,512]{0,1:T(8,128)(2,1)S(1)}, u32[]{:S(2)}, u32[]{:S(2)}) collective-permute-start(bf16[256,512]{0,1:T(8,128)(2,1)S(1)} %bitcast.277), channel_id=1, source_target_pairs={{0,8},{2,10},{4,12},{6,14},{8,16},{10,18},{12,20},{14,22},{16,24},... | collective-permute-start | bytes 786440 | tf_op jit(solution)/shard_map/ppermute | solution.py:18
  33.8 31.8 %collective-permute-start.4 = (bf16[256,512]{0,1:T(8,128)(2,1)S(1)}, bf16[256,512]{0,1:T(8,128)(2,1)S(1)}, u32[]{:S(2)}, u32[]{:S(2)}) collective-permute-start(bf16[256,512]{0,1:T(8,128)(2,1)S(1)} %bitcast.278), channel_id=1, source_target_pairs={{0,6},{2,8},{4,10},{6,12},{8,14},{10,16},{12,18},{14,20},{16,22},{... | collective-permute-start | bytes 786440 | tf_op jit(solution)/shard_map/ppermute | solution.py:18
  39.9 33.2 %collective-permute-start.1 = (bf16[256,512]{1,0:T(8,128)(2,1)S(1)}, bf16[256,512]{1,0:T(8,128)(2,1)S(1)}, u32[]{:S(2)}, u32[]{:S(2)}) collective-permute-start(bf16[256,512]{1,0:T(8,128)(2,1)S(1)} %convolution_convert_fusion.1), channel_id=1, source_target_pairs={{0,2},{2,4},{4,6},{6,8},{8,10},{10,12},{12,14},{14,16},{16,18},{18... | collective-permute-start | bytes 786440 | tf_op jit(solution)/shard_map/ppermute | solution.py:18
  53.7 25.5 %collective-permute-start.3 = (bf16[256,512]{1,0:T(8,128)(2,1)S(1)}, bf16[256,512]{1,0:T(8,128)(2,1)S(1)}, u32[]{:S(2)}, u32[]{:S(2)}) collective-permute-start(bf16[256,512]{1,0:T(8,128)(2,1)S(1)} %convolution_convert_fusion.1), channel_id=1, source_target_pairs={{0,4},{2,6},{4,8},{6,10},{8,12},{10,14},{12,16},{14,18},{16,20},{1... | collective-permute-start | bytes 786440 | tf_op jit(solution)/shard_map/ppermute | solution.py:18
  58.5 26.8 %collective-permute-start.5 = (bf16[256,512]{1,0:T(8,128)(2,1)S(1)}, bf16[256,512]{1,0:T(8,128)(2,1)S(1)}, u32[]{:S(2)}, u32[]{:S(2)}) collective-permute-start(bf16[256,512]{1,0:T(8,128)(2,1)S(1)} %convolution_convert_fusion.1), channel_id=1, source_target_pairs={{0,6},{2,8},{4,10},{6,12},{8,14},{10,16},{12,18},{14,20},{16,22},{... | collective-permute-start | bytes 786440 | tf_op jit(solution)/shard_map/ppermute | solution.py:18
  61.3 10.8 %copy-start.3 = (f32[4,256,256,4]{2,1,3,0:T(8,128)}, f32[4,256,256,4]{2,1,3,0:T(8,128)S(1)}, u32[]{:S(2)}) copy-start(f32[4,256,256,4]{2,1,3,0:T(8,128)S(1)} %get-tuple-element.41) | copy-start | bytes 12582916
  61.3 30.1 %collective-permute-start.7 = (bf16[256,512]{1,0:T(8,128)(2,1)S(1)}, bf16[256,512]{1,0:T(8,128)(2,1)S(1)}, u32[]{:S(2)}, u32[]{:S(2)}) collective-permute-start(bf16[256,512]{1,0:T(8,128)(2,1)S(1)} %convolution_convert_fusion.1), channel_id=1, source_target_pairs={{0,8},{2,10},{4,12},{6,14},{8,16},{10,18},{12,20},{14,22},{16,24},... | collective-permute-start | bytes 786440 | tf_op jit(solution)/shard_map/ppermute | solution.py:18
  73.3 4.9 %copy-start.1 = (f32[4,256,256,4]{2,1,3,0:T(8,128)S(1)}, f32[4,256,256,4]{2,1,3,0:T(8,128)}, u32[]{:S(2)}) copy-start(f32[4,256,256,4]{2,1,3,0:T(8,128)} %get-tuple-element.39) | copy-start | bytes 12582916
  79.4 4.9 %copy-start.2 = (f32[4,256,256,4]{2,1,3,0:T(8,128)S(1)}, f32[4,256,256,4]{2,1,3,0:T(8,128)}, u32[]{:S(2)}) copy-start(f32[4,256,256,4]{2,1,3,0:T(8,128)} %get-tuple-element.37) | copy-start | bytes 12582916
  85.5 4.9 %copy-start = (f32[4,256,256,4]{2,1,3,0:T(8,128)S(1)}, f32[4,256,256,4]{2,1,3,0:T(8,128)}, u32[]{:S(2)}) copy-start(f32[4,256,256,4]{2,1,3,0:T(8,128)} %get-tuple-element.35) | copy-start | bytes 12582916
Sparse Core Ops, SparseCore 0:
  8.9 12.2 all-gather.1
  109.9 15.9 reduce-scatter.1
where the time goes:
time: 134 us; the launch traced here: 133 us
  matrix products  62.4 us (47%)
  waiting for transfers between devices  27.9 us (21%)
  starting transfers between devices  16.7 us (12%)
  between operations  13.7 us (10%)
  other arithmetic  9.82 us (7%)
  local copies, waits for them, and re-layouts  2.27 us (2%)
    dot_general x5, matrix products, attend(): jnp.einsum('kgts,skd->kgtd', weights.astype(jnp.bfloat16), value_block, p...  23.8 us
    ppermute x8, starting transfers between devices, passed_along(): lax.ppermute(value, axis, [(source, source + steps) for source in range(f...  16.6 us
    reduce_scatter x1, waiting for transfers between devices, body(): lax.psum_scatter(jnp.dot(attended, w_out, preferred_element_type=jnp.floa...  16.1 us
    dot_general x1, matrix products, body(): jnp.dot(attended, w_out, preferred_element_type=jnp.float32)  11.6 us
    all_gather x1, waiting for transfers between devices, body(): piece = lax.all_gather(input_rows, 'head', axis=0, tiled=True)  11 us
    dot_general x5, matrix products, attend(): jnp.einsum('tkgd,skd->kgts', query_matrix, key_block, preferred_element_t...  10.2 us
    dot_general x1, matrix products, body(): jnp.dot(piece, w_query, preferred_element_type=jnp.float32)  8.73 us
    reduce_sum x5, other arithmetic, attend(): running_sum = running_sum * factor + jnp.sum(weights, axis=-1)  5.24 us
  transfers between devices with their start and end apart: 10, of which 2 were waited for; matrix products, arithmetic and copies ran while one was open for 39% of the time, Pallas kernels for 0%

commit v1 on v0

v1 whole, which is shorter than its diff:
```python
import functools
import math

import jax
import jax.numpy as jnp
from jax import lax
from jax.experimental import pallas as pl
from jax.experimental.pallas import tpu as pltpu
from jax.sharding import PartitionSpec as P

HEAD_SIZE = 128
LAYER = 4
MASKED = -1e30
SCORE_SCALE = math.log2(math.e) * HEAD_SIZE ** (-0.5)
SWAP = [(0, 1), (1, 0)]
VMEM = pl.BlockSpec(memory_space=pltpu.VMEM)
SMEM = pl.BlockSpec(memory_space=pltpu.SMEM)
ANY = pl.BlockSpec(memory_space=pl.ANY)


def inverse_frequency():
    table = []
    for number in range(HEAD_SIZE // 2):
        base_freq = 500000.0 ** (-(2.0 * number) / HEAD_SIZE)
        wavelength = 2.0 * math.pi / base_freq
        smooth = (8192.0 / wavelength - 1.0) / 3.0
        if wavelength < 2048.0:
            table.append(base_freq)
        elif wavelength > 8192.0:
            table.append(base_freq / 8.0)
        else:
            table.append((1.0 - smooth) * base_freq / 8.0 + smooth * base_freq)
    return table


def dot(a, b):
    return jnp.dot(a, b, preferred_element_type=jnp.float32)


def rotated(block, cosine, sine):
    return block * cosine + pltpu.roll(block, HEAD_SIZE // 2, 1) * sine


def first_half_kernel(chunks, place, lengths, own_hbm, key_hbm, value_hbm, key_sum, value_sum, own, w_key, w_value, cosine, sine, starts, sems):
    depth = w_key.shape[0] // chunks
    row_copy = pltpu.make_async_copy(own_hbm, own, sems.at[2 * chunks])
    row_copy.start()
    copies = []
    for number in range(chunks):
        at = pl.ds(number * depth, depth)
        pair = (
            pltpu.make_async_copy(key_hbm.at[at], w_key.at[at], sems.at[2 * number]),
            pltpu.make_async_copy(value_hbm.at[at], w_value.at[at], sems.at[2 * number + 1]),
        )
        for copy in pair:
            copy.start()
        copies.append(pair)
    tokens = cosine.shape[0]
    lane = lax.broadcasted_iota(jnp.int32, (1, HEAD_SIZE), 1)
    pair_of_lane = lane % (HEAD_SIZE // 2)
    freq = jnp.zeros((1, HEAD_SIZE), jnp.float32)
    for number, value in enumerate(inverse_frequency()):
        freq = jnp.where(pair_of_lane == number, jnp.float32(value), freq)
    positions = place[1] * tokens + lax.broadcasted_iota(jnp.int32, (tokens, HEAD_SIZE), 0)
    angles = positions.astype(jnp.float32) * freq
    cosine[...] = jnp.cos(angles)
    turned = jnp.sin(angles)
    sine[...] = jnp.where(lane < HEAD_SIZE // 2, -turned, turned)
    start = jnp.zeros((tokens, HEAD_SIZE), jnp.int32)
    end = jnp.int32(0)
    for number in range(lengths.shape[0]):
        end = end + lengths[number]
        start = jnp.where(positions >= end, end, start)
    starts[...] = start
    row_copy.wait()
    for number, pair in enumerate(copies):
        at = slice(number * depth, (number + 1) * depth)
        rows = own[:, at]
        for copy, weight, total in zip(pair, (w_key, w_value), (key_sum, value_sum)):
            copy.wait()
            product = dot(rows, weight[at, :])
            total[...] = product if number == 0 else total[...] + product


def second_half_kernel(place, other, w_key, w_value, key_own, value_own, cosine, sine, kv):
    half, width = key_own.shape
    mine = pl.multiple_of(place[0] * half, half)
    theirs = pl.multiple_of((1 - place[0]) * half, half)
    for weight, own, turn, offset in ((w_key, key_own, True, 0), (w_value, value_own, False, width)):
        result = dot(other[...], weight[...])
        for rows, block in ((mine, own[...]), (theirs, result)):
            here = pl.ds(rows, half)
            for head in range(width // HEAD_SIZE):
                at = slice(head * HEAD_SIZE, (head + 1) * HEAD_SIZE)
                out = slice(offset + head * HEAD_SIZE, offset + (head + 1) * HEAD_SIZE)
                piece = block[:, at]
                if turn:
                    piece = rotated(piece, cosine[here, :], sine[here, :])
                kv[here, out] = piece.astype(kv.dtype)


def query_kernel(place, own, other, weight, cosine, sine, query, rows):
    half = own.shape[0]
    rows[pl.ds(pl.multiple_of(place[0] * half, half), half), :] = own[...]
    rows[pl.ds(pl.multiple_of((1 - place[0]) * half, half), half), :] = other[...]
    wide = 4 * HEAD_SIZE
    for number in range(weight.shape[1] // wide):
        result = dot(rows[...], weight[:, number * wide : (number + 1) * wide])
        for head in range(wide // HEAD_SIZE):
            at = slice(head * HEAD_SIZE, (head + 1) * HEAD_SIZE)
            out = slice(number * wide + head * HEAD_SIZE, number * wide + (head + 1) * HEAD_SIZE)
            query[:, out] = rotated(result[:, at], cosine[...], sine[...]).astype(query.dtype)


def relay_kernel(place, kv, from_z, after, to_x, to_y):
    own, earlier = kv[...], from_z[...]
    to_x[...] = jnp.where(place[1] % 2 > 0, earlier, own)
    to_y[...] = jnp.where(place[1] % LAYER >= 2, earlier, own)


def attend_kernel(counts, distances, first, last, place, starts, query, *refs):
    refs = list(refs)
    blocks = [[refs.pop(0) for _ in range(copies)] for copies in counts]
    count = len(counts)

    def part(block, at):
        return block[0][:, at] if len(block) == 1 else block[0][:, at] + block[1][:, at]

    if not first:
        old_max, old_sum, old_acc = (refs.pop(0) for _ in range(3))
    if last:
        attended = refs.pop(0)
    else:
        new_max, new_sum, new_acc = (refs.pop(0) for _ in range(3))
    if first:
        done = refs.pop(0)
        done[...] = jnp.zeros_like(done)
    bias = refs.pop(0)
    tokens = query.shape[0]
    kv_heads = blocks[0][0].shape[1] // (2 * HEAD_SIZE)
    group = query.shape[1] // HEAD_SIZE // kv_heads
    base = place[1] * tokens
    query_pos = base + lax.broadcasted_iota(jnp.int32, (tokens, tokens), 0)
    start = jnp.concatenate([starts[...]] * (tokens // starts.shape[1]), axis=1)
    for number in range(count):
        even, odd = distances[number]
        key_pos = base - tokens * jnp.where(place[1] % 2 > 0, odd, even) + lax.broadcasted_iota(jnp.int32, (tokens, tokens), 1)
        allowed = (key_pos >= start) & (key_pos <= query_pos)
        bias[:, number * tokens : (number + 1) * tokens] = jnp.where(allowed, 0.0, MASKED)

    ones = jnp.ones((count * tokens, HEAD_SIZE), query.dtype)
    for kv_head in range(kv_heads):
        at = slice(kv_head * HEAD_SIZE, (kv_head + 1) * HEAD_SIZE)
        at_value = slice((kv_heads + kv_head) * HEAD_SIZE, (kv_heads + kv_head + 1) * HEAD_SIZE)
        keys = jnp.concatenate([part(block, at) for block in blocks], axis=0)
        values = jnp.concatenate([part(block, at_value) for block in blocks], axis=0)
        values = jnp.concatenate([values, ones], axis=1)
        for member in range(group):
            head = kv_head * group + member
            here = slice(head * HEAD_SIZE, (head + 1) * HEAD_SIZE)
            scores = lax.dot_general(
                query[:, here], keys, (((1,), (1,)), ((), ())), preferred_element_type=jnp.float32
            )
            scores = scores * SCORE_SCALE + bias[...]
            top = jnp.max(scores, axis=1, keepdims=True)
            if not first:
                before = old_max[head][:, :1]
                top = jnp.maximum(top, before)
                factor = jnp.exp2(before - top)
            weights = jnp.exp2(scores - top).astype(query.dtype)
            product = dot(weights, values)
            acc, total = product[:, :HEAD_SIZE], product[:, HEAD_SIZE:]
            if not first:
                acc = acc + old_acc[head] * factor
                total = total + old_sum[head] * factor
            if last:
                attended[:, here] = (acc / total).astype(attended.dtype)
            else:
                new_max[head] = jnp.broadcast_to(top, (tokens, HEAD_SIZE))
                new_sum[head] = total
                new_acc[head] = acc


def out_kernel(low, high, place, attended, weight, own, send):
    half = own.shape[0]
    on_high = place[0] > 0
    wide = 4 * HEAD_SIZE
    for number in range((high - low) // wide):
        at = slice(number * wide, (number + 1) * wide)
        result = dot(attended[...], weight[:, low + number * wide : low + (number + 1) * wide])
        own[:, at] = jnp.where(on_high, result[half:], result[:half])
        send[:, at] = jnp.where(on_high, result[:half], result[half:]).astype(send.dtype)


def add_kernel(own_low, own_high, got_low, got_high, mixed):
    cut = own_low.shape[1]
    for at, own, got in ((slice(0, cut), own_low, got_low), (slice(cut, mixed.shape[1]), own_high, got_high)):
        mixed[:, at] = (own[...] + got[...].astype(jnp.float32)).astype(mixed.dtype)


def call(kernel, name, outs, in_specs, flops, nbytes, limit, scratch=()):
    return pl.pallas_call(
        kernel,
        out_shape=outs,
        in_specs=in_specs,
        out_specs=[VMEM] * len(outs),
        scratch_shapes=list(scratch),
        name=name,
        cost_estimate=pl.CostEstimate(flops=flops, bytes_accessed=nbytes, transcendentals=0),
        compiler_params=pltpu.CompilerParams(vmem_limit_bytes=limit << 20),
    )


def in_hbm(array):
    return pltpu.with_memory_space_constraint(array, pltpu.HBM)


def body(input_rows, doc_lengths, w_query, key_weight, value_weight, w_out):
    half, model = input_rows.shape
    tokens = 2 * half
    width_q, width_k = w_query.shape[1], key_weight.shape[1]
    heads = width_q // HEAD_SIZE
    shards = lax.axis_size("seq")
    place = jnp.stack([lax.axis_index("head"), lax.axis_index("seq")]).astype(jnp.int32)
    bf16, f32 = jnp.bfloat16, jnp.float32
    shape = pltpu.VMEM

    other = lax.ppermute(input_rows, "head", SWAP)

    chunks = 8
    key_own, value_own, own, w_key, w_value, cosine, sine, starts = call(
        functools.partial(first_half_kernel, chunks), "keys_values_own",
        [
            shape((half, width_k), f32), shape((half, width_k), f32), shape((half, model), bf16),
            shape(key_weight.shape, bf16), shape(value_weight.shape, bf16),
            shape((tokens, HEAD_SIZE), f32), shape((tokens, HEAD_SIZE), f32), shape((tokens, HEAD_SIZE), jnp.int32),
        ],
        [SMEM, SMEM, ANY, ANY, ANY], 4 * half * model * width_k, 4 * model * width_k, 16,
        [pltpu.SemaphoreType.DMA((2 * chunks + 1,))],
    )(place, doc_lengths, in_hbm(input_rows), in_hbm(key_weight), in_hbm(value_weight))
    (kv,) = call(
        second_half_kernel, "keys_values_other", [shape((tokens, 2 * width_k), bf16)],
        [SMEM] + [VMEM] * 7, 16 * half * model * width_k, 4 * model * width_k, 16,
    )(place, other, w_key, w_value, key_own, value_own, cosine, sine)

    every = range(shards)

    def sent(value, pairs):
        return lax.ppermute(value, "seq", [(a, b) for a, b in pairs if 0 <= a < shards and 0 <= b < shards])

    from_z = sent(kv, [(i, i + LAYER) for i in every])
    from_d = sent(kv, [(i, i + (3 if i % 2 == 0 else 1)) for i in every])

    (query,) = call(
        query_kernel, "queries", [shape((tokens, width_q), bf16)], [SMEM] + [VMEM] * 5,
        2 * tokens * model * width_q, 2 * model * width_q, 16, [pltpu.VMEM((tokens, model), bf16)],
    )(place, own, other, w_query, cosine, sine)

    state_shape = [shape((heads, tokens, HEAD_SIZE), f32)] * 3
    pair_flops = 6 * heads * tokens * tokens * HEAD_SIZE

    def attend(name, distances, blocks, state, last):
        counts = tuple(len(block) for block in blocks)
        outs = [shape((tokens, width_q), bf16)] if last else state_shape
        return call(
            functools.partial(attend_kernel, counts, distances, state is None, last), name,
            outs + ([shape((8, HEAD_SIZE), f32)] if state is None else []),
            [SMEM] + [VMEM] * (2 + sum(counts) + (0 if state is None else 3)),
            len(counts) * pair_flops, 8 << 20, 16, [pltpu.VMEM((tokens, len(counts) * tokens), f32)],
        )(place, starts, query, *[array for block in blocks for array in block], *(state or ()))

    *state, done = attend("attend_own", ((0, 0),), [(kv,)], None, False)
    to_x, to_y = call(
        relay_kernel, "relay", [shape(kv.shape, bf16)] * 2, [SMEM] + [VMEM] * 3, 0, 2 << 20, 16,
    )(place, kv, from_z, done)
    from_x = sent(to_x, [(i, i ^ 1) for i in every])
    from_y = sent(to_y, [(i, i ^ 2) for i in every])
    state = attend("attend_z_diagonal", ((LAYER, LAYER), (1, 3)), [(from_z,), (from_d,)], state, False)
    (attended,) = attend("attend_x_y", ((3, 1), (2, 2)), [(from_x,), (from_y,)], state, True)

    columns = w_out.shape[1]
    cut = columns // 2
    parts = []
    for low, high in ((0, cut), (cut, columns)):
        own_part, send = call(
            functools.partial(out_kernel, low, high), "out_projection",
            [shape((half, high - low), f32), shape((half, high - low), bf16)],
            [SMEM] + [VMEM] * 2, 2 * tokens * width_q * (high - low), 2 * width_q * (high - low), 16,
        )(place, attended, w_out)
        parts.append((own_part, lax.ppermute(send, "head", SWAP)))
    (mixed,) = call(
        add_kernel, "add", [jax.ShapeDtypeStruct((half, columns), bf16)], [VMEM] * 4, half * columns, 4 << 20, 16,
    )(parts[0][0], parts[1][0], parts[0][1], parts[1][1])
    return mixed


def solution(mesh):
    in_specs = (
        P(("seq", "head"), None),
        P(),
        P(None, "head"),
        P(None, "head"),
        P(None, "head"),
        P("head", None),
    )
    out_specs = P(("seq", "head"), None)
    return jax.shard_map(body, mesh=mesh, in_specs=in_specs, out_specs=out_specs, check_vma=False)
```

time: 134 us -> 63.7 us (0.48)
  matrix products: 62.4 us -> 0 us
  Pallas kernels: 0 us -> 32.4 us
  between operations: 13.7 us -> 0.16 us
  waiting for transfers between devices: 27.9 us -> 17.3 us
  other arithmetic: 9.82 us -> 0.08 us
  starting transfers between devices: 16.7 us -> 7.19 us
  local copies, waits for them, and re-layouts: 2.27 us -> 6.44 us
    dot_general x14 -> x0, matrix products: 62.4 us -> none  [the longest x5 23.8 us: attend(): jnp.einsum('kgts,skd->kgtd', weights.astype(jnp.bfloat16), value_block, p...]
    pallas_call x0 -> x10, Pallas kernels: none -> 32.4 us  [the longest x3 12.7 us: attend(): call(functools.partial(attend_kernel, counts, distances, state is None, l...]
    ppermute x8 -> x7, waiting for transfers between devices: 0.02 us -> 17.3 us  [the longest x4 15.1 us: sent(): lax.ppermute(value, 'seq', [(a, b) for a, b in pairs if 0 <= a < shards a...]
    reduce_scatter x1 -> x0, waiting for transfers between devices: 16.1 us -> none  [body(): lax.psum_scatter(jnp.dot(attended, w_out, preferred_element_type=jnp.floa...]
    all_gather x1 -> x0, waiting for transfers between devices: 11 us -> none  [body(): piece = lax.all_gather(input_rows, 'head', axis=0, tiled=True)]
    ppermute x8 -> x7, starting transfers between devices: 16.6 us -> 7.19 us  [the longest x4 5.87 us: sent(): lax.ppermute(value, 'seq', [(a, b) for a, b in pairs if 0 <= a < shards a...]
    unnamed x9 -> x12, local copies, waits for them, and re-layouts: 0.4 us -> 6.44 us
    reduce_sum x6 -> x0, other arithmetic: 5.33 us -> none  [the longest x5 5.24 us: attend(): running_sum = running_sum * factor + jnp.sum(weights, axis=-1)]
  transfers between devices with their start and end apart: 10 -> 7, of which waited for: 2 -> 4; matrix products, arithmetic and copies ran while one was open for 39% -> 0% of each run, Pallas kernels for 0% -> 28%
where the time goes in v1:
time: 63.7 us; the launch traced here: 63.5 us
  Pallas kernels  32.4 us (51%)
  waiting for transfers between devices  17.3 us (27%)
  starting transfers between devices  7.19 us (11%)
  local copies, waits for them, and re-layouts  6.44 us (10%)
    ppermute x4, waiting for transfers between devices, sent(): lax.ppermute(value, 'seq', [(a, b) for a, b in pairs if 0 <= a < shards a...  15.1 us
    pallas_call x3, Pallas kernels, attend(): call(functools.partial(attend_kernel, counts, distances, state is None, l...  12.7 us
    unnamed x12, local copies, waits for them, and re-layouts  6.44 us
    ppermute x4, starting transfers between devices, sent(): lax.ppermute(value, 'seq', [(a, b) for a, b in pairs if 0 <= a < shards a...  5.87 us
    pallas_call x2, Pallas kernels, body(): call(functools.partial(out_kernel, low, high), 'out_projection', [shape((...  5.78 us
    pallas_call x1, Pallas kernels, body(): call(query_kernel, 'queries', [shape((tokens, width_q), bf16)], [SMEM] +...  5.46 us
    pallas_call x1, Pallas kernels, body(): call(functools.partial(first_half_kernel, chunks), 'keys_values_own', [sh...  4.74 us
    ppermute x2, waiting for transfers between devices, body(): parts.append((own_part, lax.ppermute(send, 'head', SWAP)))  2.21 us
  transfers between devices with their start and end apart: 7, of which 4 were waited for; matrix products, arithmetic and copies ran while one was open for 0% of the time, Pallas kernels for 28%

profile of v1, /device:TPU:25, one launch (start us, length us, event | category | flops | bytes accessed | tf_op | source)
XLA Modules:
  0.0 63.5 jit_solution(17938618036549090605)
XLA Ops:
  0.0 0.7 %collective-permute-start = (bf16[128,4096]{1,0:T(8,128)(2,1)}, bf16[128,4096]{1,0:T(8,128)(2,1)S(1)}, u32[]{:S(2)}, u32[]{:S(2)}) collective-permute-start(bf16[128,4096]{1,0:T(8,128)(2,1)} %own_hbm.1), channel_id=1, source_target_pairs={{0,1},{1,0},{2,3},{3,2},{4,5},{5,4},{6,7},{7,6},{8,9},{9,8},{10,11... | collective-permute-start | bytes 3145736 | tf_op jit(solution)/shard_map/ppermute | solution.py:228
  0.7 0.1 pad_add_fusion.place
  0.8 0.7 %copy-done.1 = s32[8]{0:T(128)S(1)} copy-done((s32[8]{0:T(128)S(1)}, s32[8]{0:T(128)}, u32[]{:S(2)}) %copy-start.1) | copy-done | bytes 56
  1.4 4.7 %keys_values_own.1 = (f32[128,512]{1,0:T(8,128)S(1)}, f32[128,512]{1,0:T(8,128)S(1)}, bf16[128,4096]{1,0:T(8,128)(2,1)S(1)}, bf16[4096,512]{1,0:T(8,128)(2,1)S(1...) custom-call(s32[2]{0:T(128)S(1)} %pad_add_fusion.place, ...), custom_call_target="tpu_custom_call" | custom-call | flops 1073741824 | bytes 8388608 | tf_op jit(solution)/shard_map/keys_values_own/pallas_call | solution.py:231
  6.2 0.0 collective-permute-done.other
  6.2 1.9 %keys_values_other.1.refs_0_.kv = bf16[256,1024]{1,0:T(8,128)(2,1)S(1)} custom-call(s32[2]{0:T(128)S(1)} %pad_add_fusion.place, bf16[128,4096]{1,0:T(8,128)(2,1)S(1)} %collective-permute-done.other, bf16[4096,512]{1,0:T(8,128)(2,1)S(1)} %get-tuple-element.30.w_key, bf16[4096,512]{1,0:T(8,128)(2,1)S(1)} %get-tuple-element.31.w_value, ...), custom_call_target="tpu_custom_call" | custom-call | flops 4294967296 | bytes 8388608 | tf_op jit(solution)/shard_map/keys_values_other/pallas_call | solution.py:241
  8.1 1.3 %collective-permute-start.1 = (bf16[256,1024]{1,0:T(8,128)(2,1)S(1)}, bf16[256,1024]{1,0:T(8,128)(2,1)S(1)}, u32[]{:S(2)}, u32[]{:S(2)}) collective-permute-start(bf16[256,1024]{1,0:T(8,128)(2,1)S(1)} %keys_values_other.1.refs_0_.kv), channel_id=1, source_target_pairs={{0,8},{2,10},{4,12},{6,14},{8,16},{10,18},{12,20},{14,22},{16,24},... | collective-permute-start | bytes 1572872 | tf_op jit(solution)/shard_map/ppermute | solution.py:249
  9.4 4.3 %collective-permute-start.4 = (bf16[256,1024]{1,0:T(8,128)(2,1)S(1)}, bf16[256,1024]{1,0:T(8,128)(2,1)S(1)}, u32[]{:S(2)}, u32[]{:S(2)}) collective-permute-start(bf16[256,1024]{1,0:T(8,128)(2,1)S(1)} %keys_values_other.1.refs_0_.kv), channel_id=1, source_target_pairs={{0,6},{2,4},{4,10},{6,8},{8,14},{10,12},{12,18},{14,16},{16,22},{1... | collective-permute-start | bytes 1572872 | tf_op jit(solution)/shard_map/ppermute | solution.py:249
  13.7 0.0 copy-start
  13.7 5.8 %copy-done = bf16[4096,2048]{1,0:T(8,128)(2,1)S(1)} copy-done((bf16[4096,2048]{1,0:T(8,128)(2,1)S(1)}, bf16[4096,2048]{1,0:T(8,128)(2,1)}, u32[]{:S(2)}) %copy-start) | copy-done | bytes 16777240
  19.4 5.5 %queries.1.query = bf16[256,2048]{1,0:T(8,128)(2,1)S(1)} custom-call(s32[2]{0:T(128)S(1)} %pad_add_fusion.place, bf16[128,4096]{1,0:T(8,128)(2,1)S(1)} %get-tuple-element.27.own, bf16[128,4096]{1,0:T(8,128)(2,1)S(1)} %collective-permute-done.other, bf16[4096,2048]{1,0:T(8,128)(2,1)S(1)} %copy-done, f32[256,128]{1,0:T(8,128)S(1)} %get-tuple-element.28.cosine, ...), custom_call_target="tpu_custom_call" | custom-call | flops 4294967296 | bytes 16777216 | tf_op jit(solution)/shard_map/queries/pallas_call | solution.py:254
  24.9 0.0 slice-start.2
  24.9 2.0 %attend_own.1 = (f32[16,256,128]{2,1,0:T(8,128)S(1)}, f32[16,256,128]{2,1,0:T(8,128)S(1)}, f32[16,256,128]{2,1,0:T(8,128)S(1)}, f32[8,128]{1,0:T(8,128)S(1)}) custom-call(s32[2]{0:T(128)S(1)} %pad_add_fusion.place, s32[256,128]{1,0:T(8,128)S(1)} %get-tuple-element.26.starts, bf16[256,2048]{1,0:T(8,128)(2,1)S(1)} %queries.1.query, ...), custom_call_target="tpu_custom_call" | custom-call | flops 805306368 | bytes 8388608 | tf_op jit(solution)/shard_map/attend_own/pallas_call | solution.py:265
  27.0 0.0 collective-permute-done.1.from_z.refs_0_
  27.0 0.6 %relay.1 = (bf16[256,1024]{1,0:T(8,128)(2,1)S(1)}, bf16[256,1024]{1,0:T(8,128)(2,1)S(1)}) custom-call(s32[2]{0:T(128)S(1)} %pad_add_fusion.place, bf16[256,1024]{1,0:T(8,128)(2,1)S(1)} %keys_values_other.1.refs_0_.kv, bf16[256,1024]{1,0:T(8,128)(2,1)S(1)} %collective-permute-done.1.from_z.refs_0_, f32[8,128]{1,0:T(8,128)S(1)} %get-tuple-element.34.after), custom_call_target="tpu_custom_call" | custom-call | bytes 2097152 | tf_op jit(solution)/shard_map/relay/pallas_call | solution.py:273
  27.6 0.3 collective-permute-start.2
  27.9 0.0 collective-permute-start.3
  27.9 8.8 %collective-permute-done.4.refs_1_ = bf16[256,1024]{1,0:T(8,128)(2,1)S(1)} collective-permute-done((bf16[256,1024]{1,0:T(8,128)(2,1)S(1)}, bf16[256,1024]{1,0:T(8,128)(2,1)S(1)}, u32[]{:S(2)}, u32[]{:S(2)}) %collective-permute-start.4) | collective-permute-done | bytes 524320 | tf_op jit(solution)/shard_map/ppermute | solution.py:249
  36.8 5.2 %attend_z_diagonal.1 = (f32[16,256,128]{2,1,0:T(8,128)S(1)}, f32[16,256,128]{2,1,0:T(8,128)S(1)}, f32[16,256,128]{2,1,0:T(8,128)S(1)}) custom-call(s32[2]{0:T(128)S(1)} %pad_add_fusion.place, s32[256,128]{1,0:T(8,128)S(1)} %get-tuple-element.26.starts, bf16[256,2048]{1,0:T(8,128)(2,1)S(1)} %queries.1.query, ...), custom_call_target="tpu_custom_call" | custom-call | flops 1610612736 | bytes 8388608 | tf_op jit(solution)/shard_map/attend_z_diagonal/pallas_call | solution.py:265
  42.0 0.0 collective-permute-done.2.refs_0_
  42.0 6.3 %collective-permute-done.3.refs_1_ = bf16[256,1024]{1,0:T(8,128)(2,1)S(1)} collective-permute-done((bf16[256,1024]{1,0:T(8,128)(2,1)S(1)}, bf16[256,1024]{1,0:T(8,128)(2,1)S(1)}, u32[]{:S(2)}, u32[]{:S(2)}) %collective-permute-start.3) | collective-permute-done | bytes 524320 | tf_op jit(solution)/shard_map/ppermute | solution.py:249
  48.3 5.4 %attend_x_y.1.attended = bf16[256,2048]{1,0:T(8,128)(2,1)S(1)} custom-call(s32[2]{0:T(128)S(1)} %pad_add_fusion.place, s32[256,128]{1,0:T(8,128)S(1)} %get-tuple-element.26.starts, bf16[256,2048]{1,0:T(8,128)(2,1)S(1)} %queries.1.query, bf16[256,1024]{1,0:T(8,128)(2,1)S(1)} %collective-permute-done.2.refs_0_, ...), custom_call_target="tpu_custom_call" | custom-call | flops 1610612736 | bytes 8388608 | tf_op jit(solution)/shard_map/attend_x_y/pallas_call | solution.py:265
  53.7 0.0 slice-done
  53.7 0.0 slice-done.1
  53.7 0.0 slice-done.2
  53.8 2.9 %out_projection.3 = (f32[128,2048]{1,0:T(8,128)S(1)}, bf16[128,2048]{1,0:T(8,128)(2,1)S(1)}) custom-call(s32[2]{0:T(128)S(1)} %pad_add_fusion.place, bf16[256,2048]{1,0:T(8,128)(2,1)S(1)} %attend_x_y.1.attended, bf16[2048,4096]{1,0:T(8,128)(2,1)S(1)} %bitcast.3), custom_call_target="tpu_custom_call" | custom-call | flops 2147483648 | bytes 8388608 | tf_op jit(solution)/shard_map/out_projection/pallas_call | solution.py:285
  56.7 2.9 %out_projection.2 = (f32[128,2048]{1,0:T(8,128)S(1)}, bf16[128,2048]{1,0:T(8,128)(2,1)S(1)}) custom-call(s32[2]{0:T(128)S(1)} %pad_add_fusion.place, bf16[256,2048]{1,0:T(8,128)(2,1)S(1)} %attend_x_y.1.attended, bf16[2048,4096]{1,0:T(8,128)(2,1)S(1)} %bitcast.3), custom_call_target="tpu_custom_call" | custom-call | flops 2147483648 | bytes 8388608 | tf_op jit(solution)/shard_map/out_projection/pallas_call | solution.py:285
  59.6 0.6 collective-permute-start.6
  60.1 0.1 collective-permute-start.5
  60.2 1.5 %collective-permute-done.6.got_high = bf16[128,2048]{1,0:T(8,128)(2,1)S(1)} collective-permute-done((bf16[128,2048]{1,0:T(8,128)(2,1)S(1)}, bf16[128,2048]{1,0:T(8,128)(2,1)S(1)}, u32[]{:S(2)}, u32[]{:S(2)}) %collective-permute-start.6) | collective-permute-done | bytes 524320 | tf_op jit(solution)/shard_map/ppermute | solution.py:290
  61.7 0.7 %collective-permute-done.5.got_low = bf16[128,2048]{1,0:T(8,128)(2,1)S(1)} collective-permute-done((bf16[128,2048]{1,0:T(8,128)(2,1)S(1)}, bf16[128,2048]{1,0:T(8,128)(2,1)S(1)}, u32[]{:S(2)}, u32[]{:S(2)}) %collective-permute-start.5) | collective-permute-done | bytes 524320 | tf_op jit(solution)/shard_map/ppermute | solution.py:290
  62.4 1.1 %add.3 = bf16[128,4096]{1,0:T(8,128)(2,1)} custom-call(f32[128,2048]{1,0:T(8,128)S(1)} %get-tuple-element.43.own_low, f32[128,2048]{1,0:T(8,128)S(1)} %get-tuple-element.44.own_high, bf16[128,2048]{1,0:T(8,128)(2,1)S(1)} %collective-permute-done.5.got_low, bf16[128,2048]{1,0:T(8,128)(2,1)S(1)} %collective-permute-done.6.got_high), custom_call_target="tpu_custom_call" | custom-call | flops 524288 | bytes 4194304 | tf_op jit(solution)/shard_map/add/pallas_call | solution.py:291
  (6 shorter events, 0.0 us)
Async XLA Ops:
  0.0 6.2 %collective-permute-start = (bf16[128,4096]{1,0:T(8,128)(2,1)}, bf16[128,4096]{1,0:T(8,128)(2,1)S(1)}, u32[]{:S(2)}, u32[]{:S(2)}) collective-permute-start(bf16[128,4096]{1,0:T(8,128)(2,1)} %own_hbm.1), channel_id=1, source_target_pairs={{0,1},{1,0},{2,3},{3,2},{4,5},{5,4},{6,7},{7,6},{8,9},{9,8},{10,11... | collective-permute-start | bytes 3145736 | tf_op jit(solution)/shard_map/ppermute | solution.py:228
  0.8 0.7 %copy-start.1 = (s32[8]{0:T(128)S(1)}, s32[8]{0:T(128)}, u32[]{:S(2)}) copy-start(s32[8]{0:T(128)} %lengths.1) | copy-start | bytes 100
  8.1 18.9 %collective-permute-start.1 = (bf16[256,1024]{1,0:T(8,128)(2,1)S(1)}, bf16[256,1024]{1,0:T(8,128)(2,1)S(1)}, u32[]{:S(2)}, u32[]{:S(2)}) collective-permute-start(bf16[256,1024]{1,0:T(8,128)(2,1)S(1)} %keys_values_other.1.refs_0_.kv), channel_id=1, source_target_pairs={{0,8},{2,10},{4,12},{6,14},{8,16},{10,18},{12,20},{14,22},{16,24},... | collective-permute-start | bytes 1572872 | tf_op jit(solution)/shard_map/ppermute | solution.py:249
  9.4 27.4 %collective-permute-start.4 = (bf16[256,1024]{1,0:T(8,128)(2,1)S(1)}, bf16[256,1024]{1,0:T(8,128)(2,1)S(1)}, u32[]{:S(2)}, u32[]{:S(2)}) collective-permute-start(bf16[256,1024]{1,0:T(8,128)(2,1)S(1)} %keys_values_other.1.refs_0_.kv), channel_id=1, source_target_pairs={{0,6},{2,4},{4,10},{6,8},{8,14},{10,12},{12,18},{14,16},{16,22},{1... | collective-permute-start | bytes 1572872 | tf_op jit(solution)/shard_map/ppermute | solution.py:249
  13.7 5.8 %copy-start = (bf16[4096,2048]{1,0:T(8,128)(2,1)S(1)}, bf16[4096,2048]{1,0:T(8,128)(2,1)}, u32[]{:S(2)}) copy-start(bf16[4096,2048]{1,0:T(8,128)(2,1)} %weight.3) | copy-start | bytes 50331652
  19.4 34.3 %slice-start = ((s8[16777216]{0:T(1024)(128)(4,1)}), s8[4194304]{0:T(1024)(128)(4,1)S(1)}, s32[]{:S(2)}) async-start(s8[16777216]{0:T(1024)(128)(4,1)} %bitcast.2), calls=%async_computation | async-start | bytes 8388608
  19.4 34.3 %slice-start.1 = ((s8[16777216]{0:T(1024)(128)(4,1)}), s8[4194304]{0:T(1024)(128)(4,1)S(1)}, s32[]{:S(2)}) async-start(s8[16777216]{0:T(1024)(128)(4,1)} %bitcast.2), calls=%async_computation.1 | async-start | bytes 8388608
  24.9 28.8 %slice-start.2 = ((s8[16777216]{0:T(1024)(128)(4,1)}), s8[4194304]{0:T(1024)(128)(4,1)S(1)}, s32[]{:S(2)}) async-start(s8[16777216]{0:T(1024)(128)(4,1)} %bitcast.2), calls=%async_computation.2 | async-start | bytes 8388608
  27.6 14.4 %collective-permute-start.2 = (bf16[256,1024]{1,0:T(8,128)(2,1)S(1)}, bf16[256,1024]{1,0:T(8,128)(2,1)S(1)}, u32[]{:S(2)}, u32[]{:S(2)}) collective-permute-start(bf16[256,1024]{1,0:T(8,128)(2,1)S(1)} %get-tuple-element.35), channel_id=1, source_target_pairs={{0,2},{2,0},{4,6},{6,4},{8,10},{10,8},{12,14},{14,12},{16,18},{18,... | collective-permute-start | bytes 1572872 | tf_op jit(solution)/shard_map/ppermute | solution.py:249
  27.9 20.4 %collective-permute-start.3 = (bf16[256,1024]{1,0:T(8,128)(2,1)S(1)}, bf16[256,1024]{1,0:T(8,128)(2,1)S(1)}, u32[]{:S(2)}, u32[]{:S(2)}) collective-permute-start(bf16[256,1024]{1,0:T(8,128)(2,1)S(1)} %get-tuple-element.36), channel_id=1, source_target_pairs={{0,4},{2,6},{4,0},{6,2},{8,12},{10,14},{12,8},{14,10},{16,20},{18,... | collective-permute-start | bytes 1572872 | tf_op jit(solution)/shard_map/ppermute | solution.py:249
  36.8 17.0 %slice-start.3 = ((s8[16777216]{0:T(1024)(128)(4,1)}), s8[4194304]{0:T(1024)(128)(4,1)S(1)}, s32[]{:S(2)}) async-start(s8[16777216]{0:T(1024)(128)(4,1)} %bitcast.2), calls=%async_computation.3 | async-start | bytes 8388608
  59.6 2.1 %collective-permute-start.6 = (bf16[128,2048]{1,0:T(8,128)(2,1)S(1)}, bf16[128,2048]{1,0:T(8,128)(2,1)S(1)}, u32[]{:S(2)}, u32[]{:S(2)}) collective-permute-start(bf16[128,2048]{1,0:T(8,128)(2,1)S(1)} %get-tuple-element.46), channel_id=1, source_target_pairs={{0,1},{1,0},{2,3},{3,2},{4,5},{5,4},{6,7},{7,6},{8,9},{9,8},{10,11... | collective-permute-start | bytes 1572872 | tf_op jit(solution)/shard_map/ppermute | solution.py:290
  60.1 2.3 %collective-permute-start.5 = (bf16[128,2048]{1,0:T(8,128)(2,1)S(1)}, bf16[128,2048]{1,0:T(8,128)(2,1)S(1)}, u32[]{:S(2)}, u32[]{:S(2)}) collective-permute-start(bf16[128,2048]{1,0:T(8,128)(2,1)S(1)} %get-tuple-element.45), channel_id=1, source_target_pairs={{0,1},{1,0},{2,3},{3,2},{4,5},{5,4},{6,7},{7,6},{8,9},{9,8},{10,11... | collective-permute-start | bytes 1572872 | tf_op jit(solution)/shard_map/ppermute | solution.py:290

commit v2 on v1

v2 whole, which is shorter than its diff:
```python
import functools
import math

import jax
import jax.numpy as jnp
from jax import lax
from jax.experimental import pallas as pl
from jax.experimental.pallas import tpu as pltpu
from jax.sharding import PartitionSpec as P

HEAD_SIZE = 128
LAYER = 4
MASKED = -1e30
SCORE_SCALE = math.log2(math.e) * HEAD_SIZE ** (-0.5)
SWAP = [(0, 1), (1, 0)]
VMEM = pl.BlockSpec(memory_space=pltpu.VMEM)
SMEM = pl.BlockSpec(memory_space=pltpu.SMEM)
ANY = pl.BlockSpec(memory_space=pl.ANY)


def inverse_frequency():
    table = []
    for number in range(HEAD_SIZE // 2):
        base_freq = 500000.0 ** (-(2.0 * number) / HEAD_SIZE)
        wavelength = 2.0 * math.pi / base_freq
        smooth = (8192.0 / wavelength - 1.0) / 3.0
        if wavelength < 2048.0:
            table.append(base_freq)
        elif wavelength > 8192.0:
            table.append(base_freq / 8.0)
        else:
            table.append((1.0 - smooth) * base_freq / 8.0 + smooth * base_freq)
    return table


def dot(a, b):
    return jnp.dot(a, b, preferred_element_type=jnp.float32)


def rotated(block, cosine, sine):
    return block * cosine + pltpu.roll(block, HEAD_SIZE // 2, 1) * sine


def first_keys_kernel(chunks, place, own_hbm, key_hbm, key_sum, own, w_key, cosine, sine, starts, sems):
    depth = w_key.shape[0] // chunks
    row_copy = pltpu.make_async_copy(own_hbm, own, sems.at[chunks])
    row_copy.start()
    copies = []
    for number in range(chunks):
        at = pl.ds(number * depth, depth)
        copies.append(pltpu.make_async_copy(key_hbm.at[at], w_key.at[at], sems.at[number]))
        copies[-1].start()
    tokens = cosine.shape[0]
    lane = lax.broadcasted_iota(jnp.int32, (1, HEAD_SIZE), 1)
    pair_of_lane = lane % (HEAD_SIZE // 2)
    freq = jnp.zeros((1, HEAD_SIZE), jnp.float32)
    for number, value in enumerate(inverse_frequency()):
        freq = jnp.where(pair_of_lane == number, jnp.float32(value), freq)
    positions = place[1] * tokens + lax.broadcasted_iota(jnp.int32, (tokens, HEAD_SIZE), 0)
    angles = positions.astype(jnp.float32) * freq
    cosine[...] = jnp.cos(angles)
    turned = jnp.sin(angles)
    sine[...] = jnp.where(lane < HEAD_SIZE // 2, -turned, turned)
    start = jnp.zeros((tokens, HEAD_SIZE), jnp.int32)
    end = jnp.int32(0)
    for number in range(2, place.shape[0]):
        end = end + place[number]
        start = jnp.where(positions >= end, end, start)
    starts[...] = start
    row_copy.wait()
    for number, copy in enumerate(copies):
        at = slice(number * depth, (number + 1) * depth)
        copy.wait()
        product = dot(own[:, at], w_key[at, :])
        key_sum[...] = product if number == 0 else key_sum[...] + product


def keys_kernel(place, other, w_key, key_own, cosine, sine, keys):
    half, width = key_own.shape
    mine = pl.multiple_of(place[0] * half, half)
    theirs = pl.multiple_of((1 - place[0]) * half, half)
    for rows, block in ((mine, key_own[...]), (theirs, dot(other[...], w_key[...]))):
        here = pl.ds(rows, half)
        for head in range(width // HEAD_SIZE):
            at = slice(head * HEAD_SIZE, (head + 1) * HEAD_SIZE)
            keys[here, at] = rotated(block[:, at], cosine[here, :], sine[here, :]).astype(keys.dtype)


def values_kernel(chunks, place, own, other, value_hbm, values, rows, done, w_value, total, sems):
    depth = value_hbm.shape[0] // chunks
    copies = []
    for number in range(chunks):
        at = pl.ds(number * depth, depth)
        copies.append(pltpu.make_async_copy(value_hbm.at[at], w_value.at[at], sems.at[number]))
        copies[-1].start()
    half = own.shape[0]
    rows[pl.ds(pl.multiple_of(place[0] * half, half), half), :] = own[...]
    rows[pl.ds(pl.multiple_of((1 - place[0]) * half, half), half), :] = other[...]
    done[...] = jnp.zeros_like(done)
    for number, copy in enumerate(copies):
        at = slice(number * depth, (number + 1) * depth)
        copy.wait()
        product = dot(rows[:, at], w_value[at, :])
        if number > 0:
            product = product + total[...]
        if number < chunks - 1:
            total[...] = product
        else:
            values[...] = product.astype(values.dtype)


def query_kernel(rows, weight, cosine, sine, after, query, done):
    done[...] = after[...]
    wide = 4 * HEAD_SIZE
    for number in range(weight.shape[1] // wide):
        result = dot(rows[...], weight[:, number * wide : (number + 1) * wide])
        for head in range(wide // HEAD_SIZE):
            at = slice(head * HEAD_SIZE, (head + 1) * HEAD_SIZE)
            out = slice(number * wide + head * HEAD_SIZE, number * wide + (head + 1) * HEAD_SIZE)
            query[:, out] = rotated(result[:, at], cosine[...], sine[...]).astype(query.dtype)


def relay_kernel(place, mine, from_z, after, to_x, to_y, to_d, *done):
    own, earlier = mine[...], from_z[...]
    upper_x, upper_y = place[1] % 2 > 0, place[1] % LAYER >= 2
    to_x[...] = jnp.where(upper_x, earlier, own)
    to_y[...] = jnp.where(upper_y, earlier, own)
    to_d[...] = jnp.where(upper_y, earlier, own)
    for flag in done:
        flag[...] = after[...]


def score_kernel(distances, near, place, starts, query, *refs):
    count = len(distances)
    keys, values = refs[:count], refs[count : count + near]
    weights_out, total, acc, bias = refs[count + near :]
    ones = jnp.ones((near * query.shape[0], HEAD_SIZE), query.dtype)
    tokens = query.shape[0]
    base = place[1] * tokens
    query_pos = base + lax.broadcasted_iota(jnp.int32, (tokens, tokens), 0)
    start = jnp.concatenate([starts[...]] * (tokens // starts.shape[1]), axis=1)
    for number, (even, odd) in enumerate(distances):
        first = base - tokens * jnp.where(place[1] % 2 > 0, odd, even)
        key_pos = first + lax.broadcasted_iota(jnp.int32, (tokens, tokens), 1)
        allowed = (key_pos >= start) & (key_pos <= query_pos)
        bias[:, number * tokens : (number + 1) * tokens] = jnp.where(allowed, 0.0, MASKED)
    group = query.shape[1] // keys[0].shape[1]
    for kv_head in range(keys[0].shape[1] // HEAD_SIZE):
        at = slice(kv_head * HEAD_SIZE, (kv_head + 1) * HEAD_SIZE)
        all_keys = jnp.concatenate([block[:, at] for block in keys], axis=0)
        near_values = jnp.concatenate([block[:, at] for block in values], axis=0)
        near_values = jnp.concatenate([near_values, ones], axis=1)
        for member in range(group):
            head = kv_head * group + member
            scores = lax.dot_general(
                query[:, head * HEAD_SIZE : (head + 1) * HEAD_SIZE], all_keys, (((1,), (1,)), ((), ())),
                preferred_element_type=jnp.float32,
            )
            scores = scores * SCORE_SCALE + bias[...]
            weights = jnp.exp2(scores - jnp.max(scores, axis=1, keepdims=True))
            weights = weights.astype(query.dtype)
            product = dot(weights[:, : near * tokens], near_values)
            acc[head], total[head] = product[:, :HEAD_SIZE], product[:, HEAD_SIZE:]
            weights_out[head] = weights[:, near * tokens :]


def mix_kernel(far, low, high, place, *refs):
    refs = list(refs)
    if far > 0:
        weights, total, acc = (refs.pop(0) for _ in range(3))
        blocks = [refs.pop(0) for _ in range(far)]
        weight, own, send, attended = refs
        group = weights.shape[0] * HEAD_SIZE // blocks[0].shape[1]
        for kv_head in range(blocks[0].shape[1] // HEAD_SIZE):
            values = jnp.concatenate([block[:, kv_head * HEAD_SIZE : (kv_head + 1) * HEAD_SIZE] for block in blocks], axis=0)
            values = jnp.concatenate([values, jnp.ones((values.shape[0], HEAD_SIZE), values.dtype)], axis=1)
            for head in range(kv_head * group, (kv_head + 1) * group):
                product = dot(weights[head], values)
                result = (acc[head] + product[:, :HEAD_SIZE]) / (total[head] + product[:, HEAD_SIZE:])
                attended[:, head * HEAD_SIZE : (head + 1) * HEAD_SIZE] = result.astype(attended.dtype)
    else:
        attended, weight, own, send = refs
    half = own.shape[0]
    on_high = place[0] > 0
    wide = 4 * HEAD_SIZE
    for number in range((high - low) // wide):
        at = slice(number * wide, (number + 1) * wide)
        result = dot(attended[...], weight[:, low + number * wide : low + (number + 1) * wide])
        own[:, at] = jnp.where(on_high, result[half:], result[:half])
        send[:, at] = jnp.where(on_high, result[:half], result[half:]).astype(send.dtype)


def add_kernel(own_low, own_high, got_low, got_high, mixed):
    cut = own_low.shape[1]
    for at, own, got in ((slice(0, cut), own_low, got_low), (slice(cut, mixed.shape[1]), own_high, got_high)):
        mixed[:, at] = (own[...] + got[...].astype(jnp.float32)).astype(mixed.dtype)


def call(kernel, name, outs, in_specs, flops, nbytes, limit, scratch=()):
    return pl.pallas_call(
        kernel,
        out_shape=outs,
        in_specs=in_specs,
        out_specs=[VMEM] * len(outs),
        scratch_shapes=list(scratch),
        name=name,
        cost_estimate=pl.CostEstimate(flops=flops, bytes_accessed=nbytes, transcendentals=0),
        compiler_params=pltpu.CompilerParams(vmem_limit_bytes=limit << 20),
    )


def in_hbm(array):
    return pltpu.with_memory_space_constraint(array, pltpu.HBM)


def body(input_rows, doc_lengths, w_query, key_weight, value_weight, w_out):
    half, model = input_rows.shape
    tokens = 2 * half
    width_q, width_k = w_query.shape[1], key_weight.shape[1]
    heads = width_q // HEAD_SIZE
    shards = lax.axis_size("seq")
    place = jnp.stack([lax.axis_index("head"), lax.axis_index("seq")]).astype(jnp.int32)
    place = jnp.concatenate([place, doc_lengths])
    bf16, f32 = jnp.bfloat16, jnp.float32
    shape = pltpu.VMEM

    other = lax.ppermute(input_rows, "head", SWAP)

    flag = shape((8, HEAD_SIZE), f32)
    table = shape((tokens, HEAD_SIZE), f32)
    kv_shape = shape((tokens, width_k), bf16)
    chunks = 8
    key_own, own, w_key, cosine, sine, starts = call(
        functools.partial(first_keys_kernel, chunks), "keys_own",
        [
            shape((half, width_k), f32), shape((half, model), bf16), shape(key_weight.shape, bf16),
            table, table, shape((tokens, HEAD_SIZE), jnp.int32),
        ],
        [SMEM, ANY, ANY], 2 * half * model * width_k, 2 * model * width_k, 4,
        [pltpu.SemaphoreType.DMA((chunks + 1,))],
    )(place, in_hbm(input_rows), in_hbm(key_weight))
    (keys,) = call(
        keys_kernel, "keys", [kv_shape], [SMEM] + [VMEM] * 5, 2 * half * model * width_k, 2 * model * width_k, 4,
    )(place, other, w_key, key_own, cosine, sine)

    every = range(shards)
    step_z = [(i, i + LAYER) for i in every if i + LAYER < shards]
    keys_z = lax.ppermute(keys, "seq", step_z)

    values, rows, done = call(
        functools.partial(values_kernel, chunks), "values", [kv_shape, shape((tokens, model), bf16), flag],
        [SMEM, VMEM, VMEM, ANY], 9 << 30, 2 * model * width_k, 10,
        [pltpu.VMEM(value_weight.shape, bf16), pltpu.VMEM((tokens, width_k), f32), pltpu.SemaphoreType.DMA((chunks,))],
    )(place, own, other, in_hbm(value_weight))
    values_z = lax.ppermute(values, "seq", step_z)

    def exchange(mine, from_z, after, flags, cost):
        *to, = call(
            relay_kernel, "relay", [kv_shape] * 3 + flags, [SMEM] + [VMEM] * 3, cost, 2 << 20, 4,
        )(place, mine, from_z, after)
        return [lax.ppermute(value, "seq", [(i, i ^ flip) for i in every]) for value, flip in zip(to, (1, 2, 3))], to[3:]

    keys_far, (done,) = exchange(keys, keys_z, done, [flag], 0)
    query, done = call(
        query_kernel, "queries", [shape((tokens, width_q), bf16), flag], [VMEM] * 5,
        2 * tokens * model * width_q, 2 * model * width_q, 8,
    )(rows, w_query, cosine, sine, done)
    values_far, _ = exchange(values, values_z, done, [], 9 << 30)

    far = len(keys_far)
    state = shape((heads, tokens, HEAD_SIZE), f32)
    weights, total, acc = call(
        functools.partial(score_kernel, ((0, 0), (LAYER, LAYER), (3, 1), (2, 2), (1, 3)), 2), "scores",
        [shape((heads, tokens, far * tokens), bf16), state, state], [SMEM] + [VMEM] * (4 + far + 2),
        14 * heads * tokens * tokens * HEAD_SIZE, 8 << 20, 12, [pltpu.VMEM((tokens, (far + 2) * tokens), f32)],
    )(place, starts, query, keys, keys_z, *keys_far, values, values_z)

    columns = w_out.shape[1]
    cut = columns // 2
    out_shape = [shape((half, cut), f32), shape((half, cut), bf16)]
    out_flops = 2 * tokens * width_q * cut
    own_low, send, attended = call(
        functools.partial(mix_kernel, far, 0, cut), "mix_low", out_shape + [shape((tokens, width_q), bf16)],
        [SMEM] + [VMEM] * (4 + far), out_flops + 2 * far * heads * tokens * tokens * HEAD_SIZE, 4 << 20, 6,
    )(place, weights, total, acc, *values_far, w_out)
    parts = [(own_low, lax.ppermute(send, "head", SWAP))]
    own_high, send = call(
        functools.partial(mix_kernel, 0, cut, columns), "mix_high", out_shape, [SMEM] + [VMEM] * 2, out_flops, 4 << 20, 6,
    )(place, attended, w_out)
    parts.append((own_high, lax.ppermute(send, "head", SWAP)))
    (mixed,) = call(
        add_kernel, "add", [jax.ShapeDtypeStruct((half, columns), bf16)], [VMEM] * 4, half * columns, 4 << 20, 16,
    )(parts[0][0], parts[1][0], parts[0][1], parts[1][1])
    return mixed


def solution(mesh):
    in_specs = (
        P(("seq", "head"), None),
        P(),
        P(None, "head"),
        P(None, "head"),
        P(None, "head"),
        P("head", None),
    )
    out_specs = P(("seq", "head"), None)
    return jax.shard_map(body, mesh=mesh, in_specs=in_specs, out_specs=out_specs, check_vma=False)
```

time: 63.7 us -> 56.6 us (0.89)
  the two profiles are of different devices: /device:TPU:25 before, /device:TPU:0 now
where the time goes in v2:
time: 56.6 us; the launch traced here: 56.4 us
  Pallas kernels  32.6 us (58%)
  starting transfers between devices  16.6 us (29%)
  waiting for transfers between devices  6.18 us (11%)
  other arithmetic  0.73 us (1%)
    pallas_call x1, Pallas kernels, body(): call(functools.partial(score_kernel, ((0, 0), (LAYER, LAYER), (3, 1), (2,...  9.63 us
    ppermute x6, starting transfers between devices, exchange(): lax.ppermute(value, 'seq', [(i, i ^ flip) for i in every])  7.11 us
    pallas_call x1, Pallas kernels, body(): call(query_kernel, 'queries', [shape((tokens, width_q), bf16), flag], [VM...  4.8 us
    pallas_call x1, Pallas kernels, body(): call(functools.partial(mix_kernel, far, 0, cut), 'mix_low', out_shape + [...  4.6 us
    ppermute x1, starting transfers between devices, body(): keys_z = lax.ppermute(keys, 'seq', step_z)  4.49 us
    ppermute x6, waiting for transfers between devices, exchange(): lax.ppermute(value, 'seq', [(i, i ^ flip) for i in every])  4.02 us
    ppermute x1, starting transfers between devices, body(): values_z = lax.ppermute(values, 'seq', step_z)  3.94 us
    pallas_call x1, Pallas kernels, body(): call(functools.partial(values_kernel, chunks), 'values', [kv_shape, shape...  3.59 us
  transfers between devices with their start and end apart: 11, of which 5 were waited for; matrix products, arithmetic and copies ran while one was open for 1% of the time, Pallas kernels for 40%

profile of v2, /device:TPU:0, one launch (start us, length us, event | category | flops | bytes accessed | tf_op | source)
XLA Modules:
  0.0 56.4 jit_solution(13526993881970916707)
XLA Ops:
  0.0 0.5 collective-permute-start
  0.5 0.7 %pad_add_fusion.place = s32[10]{0:T(128)S(1)} fusion(s32[8]{0:T(128)} %param.7, s32[1]{0:T(128)} %bitcast.1, s32[1]{0:T(128)} %bitcast), kind=kLoop, calls=%fused_computation | loop fusion | flops 20 | bytes 80 | tf_op jit(solution)/shard_map/concatenate | solution.py:223
  1.2 3.3 %keys_own.1 = (f32[128,512]{1,0:T(8,128)S(1)}, bf16[128,4096]{1,0:T(8,128)(2,1)S(1)}, bf16[4096,512]{1,0:T(8,128)(2,1)S(1)}, f32[256,128]{1,0:T(8,128)S(1)}, f32...) custom-call(s32[10]{0:T(128)S(1)} %pad_add_fusion.place, bf16[128,4096]{1,0:T(8,128)(2,1)} %own_hbm.1, bf16[4096,512]{1,0:T(8,128)(2,1)} %key_hbm.1), custom_call_target="tpu_custom_call" | custom-call | flops 536870912 | bytes 4194304 | tf_op jit(solution)/shard_map/keys_own/pallas_call | solution.py:233
  4.5 0.0 collective-permute-done.other
  4.5 0.0 slice-start.4
  4.5 1.4 %keys.1.mine.refs_0_ = bf16[256,512]{1,0:T(8,128)(2,1)S(1)} custom-call(s32[10]{0:T(128)S(1)} %pad_add_fusion.place, bf16[128,4096]{1,0:T(8,128)(2,1)S(1)} %collective-permute-done.other, bf16[4096,512]{1,0:T(8,128)(2,1)S(1)} %get-tuple-element.36.w_key, f32[128,512]{1,0:T(8,128)S(1)} %get-tuple-element.37.key_own, f32[256,128]{1,0:T(8,128)S(1)} %get-tuple-element.34.cosine, ...), custom_call_target="tpu_custom_call" | custom-call | flops 536870912 | bytes 4194304 | tf_op jit(solution)/shard_map/keys/pallas_call | solution.py:242
  6.0 4.5 %collective-permute-start.1 = (bf16[256,512]{1,0:T(8,128)(2,1)S(1)}, bf16[256,512]{1,0:T(8,128)(2,1)S(1)}, u32[]{:S(2)}, u32[]{:S(2)}) collective-permute-start(bf16[256,512]{1,0:T(8,128)(2,1)S(1)} %keys.1.mine.refs_0_), channel_id=1, source_target_pairs={{0,8},{2,10},{4,12},{6,14},{8,16},{10,18},{12,20},{14,22},{16,24},... | collective-permute-start | bytes 786440 | tf_op jit(solution)/shard_map/ppermute | solution.py:248
  10.5 0.0 slice-start.5
  10.5 0.0 slice-start.7
  10.5 3.6 %values.1 = (bf16[256,512]{1,0:T(8,128)(2,1)S(1)}, bf16[256,4096]{1,0:T(8,128)(2,1)S(1)}, f32[8,128]{1,0:T(8,128)S(1)}) custom-call(s32[10]{0:T(128)S(1)} %pad_add_fusion.place, bf16[128,4096]{1,0:T(8,128)(2,1)S(1)} %get-tuple-element.32.own, bf16[128,4096]{1,0:T(8,128)(2,1)S(1)} %collective-permute-done.other, bf16[4096,512]{1,0:T(8,128)(2,1)} %value_hbm.1), custom_call_target="tpu_custom_call" | custom-call | flops 9663676416 | bytes 4194304 | tf_op jit(solution)/shard_map/values/pallas_call | solution.py:250
  14.1 3.9 %collective-permute-start.5 = (bf16[256,512]{1,0:T(8,128)(2,1)S(1)}, bf16[256,512]{1,0:T(8,128)(2,1)S(1)}, u32[]{:S(2)}, u32[]{:S(2)}) collective-permute-start(bf16[256,512]{1,0:T(8,128)(2,1)S(1)} %get-tuple-element.44.refs_5_.mine), channel_id=1, source_target_pairs={{0,8},{2,10},{4,12},{6,14},{8,16},{10,18},{12,20},{14,22},{16,24},... | collective-permute-start | bytes 786440 | tf_op jit(solution)/shard_map/ppermute | solution.py:255
  18.0 0.6 %relay.2 = (bf16[256,512]{1,0:T(8,128)(2,1)S(1)}, bf16[256,512]{1,0:T(8,128)(2,1)S(1)}, bf16[256,512]{1,0:T(8,128)(2,1)S(1)}, f32[8,128]{1,0:T(8,128)S(1)}) custom-call(s32[10]{0:T(128)S(1)} %pad_add_fusion.place, bf16[256,512]{1,0:T(8,128)(2,1)S(1)} %keys.1.mine.refs_0_, bf16[256,512]{1,0:T(8,128)(2,1)S(1)} %collective-permute-done.1.from_z.refs_1_, ...), custom_call_target="tpu_custom_call" | custom-call | bytes 2097152 | tf_op jit(solution)/shard_map/relay/pallas_call | solution.py:258
  18.7 1.5 %collective-permute-start.2 = (bf16[256,512]{1,0:T(8,128)(2,1)S(1)}, bf16[256,512]{1,0:T(8,128)(2,1)S(1)}, u32[]{:S(2)}, u32[]{:S(2)}) collective-permute-start(bf16[256,512]{1,0:T(8,128)(2,1)S(1)} %get-tuple-element.41), channel_id=1, source_target_pairs={{0,2},{2,0},{4,6},{6,4},{8,10},{10,8},{12,14},{14,12},{16,18},{18,... | collective-permute-start | bytes 786440 | tf_op jit(solution)/shard_map/ppermute | solution.py:261
  20.2 1.5 %collective-permute-start.3 = (bf16[256,512]{1,0:T(8,128)(2,1)S(1)}, bf16[256,512]{1,0:T(8,128)(2,1)S(1)}, u32[]{:S(2)}, u32[]{:S(2)}) collective-permute-start(bf16[256,512]{1,0:T(8,128)(2,1)S(1)} %get-tuple-element.42), channel_id=1, source_target_pairs={{0,4},{2,6},{4,0},{6,2},{8,12},{10,14},{12,8},{14,10},{16,20},{18,... | collective-permute-start | bytes 786440 | tf_op jit(solution)/shard_map/ppermute | solution.py:261
  21.7 0.5 collective-permute-start.4
  22.2 4.8 %queries.1 = (bf16[256,2048]{1,0:T(8,128)(2,1)S(1)}, f32[8,128]{1,0:T(8,128)S(1)}) custom-call(bf16[256,4096]{1,0:T(8,128)(2,1)S(1)} %get-tuple-element.33.rows, bf16[4096,2048]{1,0:T(8,128)(2,1)S(1)} %bitcast.5, f32[256,128]{1,0:T(8,128)S(1)} %get-tuple-element.34.cosine, f32[256,128]{1,0:T(8,128)S(1)} %get-tuple-element.35.sine, ...), custom_call_target="tpu_custom_call" | custom-call | flops 4294967296 | bytes 16777216 | tf_op jit(solution)/shard_map/queries/pallas_call | solution.py:264
  27.1 0.0 slice-start
  27.1 0.6 %relay.3 = (bf16[256,512]{1,0:T(8,128)(2,1)S(1)}, bf16[256,512]{1,0:T(8,128)(2,1)S(1)}, bf16[256,512]{1,0:T(8,128)(2,1)S(1)}) custom-call(s32[10]{0:T(128)S(1)} %pad_add_fusion.place, bf16[256,512]{1,0:T(8,128)(2,1)S(1)} %get-tuple-element.44.refs_5_.mine, bf16[256,512]{1,0:T(8,128)(2,1)S(1)} %collective-permute-done.5.refs_6_.from_z, ...), custom_call_target="tpu_custom_call" | custom-call | flops 9663676416 | bytes 2097152 | tf_op jit(solution)/shard_map/relay/pallas_call | solution.py:258
  27.7 1.6 %collective-permute-start.6 = (bf16[256,512]{1,0:T(8,128)(2,1)S(1)}, bf16[256,512]{1,0:T(8,128)(2,1)S(1)}, u32[]{:S(2)}, u32[]{:S(2)}) collective-permute-start(bf16[256,512]{1,0:T(8,128)(2,1)S(1)} %get-tuple-element.49), channel_id=1, source_target_pairs={{0,2},{2,0},{4,6},{6,4},{8,10},{10,8},{12,14},{14,12},{16,18},{18,... | collective-permute-start | bytes 786440 | tf_op jit(solution)/shard_map/ppermute | solution.py:261
  29.3 1.5 %collective-permute-start.7 = (bf16[256,512]{1,0:T(8,128)(2,1)S(1)}, bf16[256,512]{1,0:T(8,128)(2,1)S(1)}, u32[]{:S(2)}, u32[]{:S(2)}) collective-permute-start(bf16[256,512]{1,0:T(8,128)(2,1)S(1)} %get-tuple-element.50), channel_id=1, source_target_pairs={{0,4},{2,6},{4,0},{6,2},{8,12},{10,14},{12,8},{14,10},{16,20},{18,... | collective-permute-start | bytes 786440 | tf_op jit(solution)/shard_map/ppermute | solution.py:261
  30.8 0.5 collective-permute-start.8
  31.3 2.6 %collective-permute-done.3.refs_3_ = bf16[256,512]{1,0:T(8,128)(2,1)S(1)} collective-permute-done((bf16[256,512]{1,0:T(8,128)(2,1)S(1)}, bf16[256,512]{1,0:T(8,128)(2,1)S(1)}, u32[]{:S(2)}, u32[]{:S(2)}) %collective-permute-start.3) | collective-permute-done | bytes 262176 | tf_op jit(solution)/shard_map/ppermute | solution.py:261
  33.9 0.7 %collective-permute-done.4.refs_4_ = bf16[256,512]{1,0:T(8,128)(2,1)S(1)} collective-permute-done((bf16[256,512]{1,0:T(8,128)(2,1)S(1)}, bf16[256,512]{1,0:T(8,128)(2,1)S(1)}, u32[]{:S(2)}, u32[]{:S(2)}) %collective-permute-start.4) | collective-permute-done | bytes 262176 | tf_op jit(solution)/shard_map/ppermute | solution.py:261
  34.5 9.6 %scores.1 = (bf16[16,256,768]{2,1,0:T(8,128)(2,1)S(1)}, f32[16,256,128]{2,1,0:T(8,128)S(1)}, f32[16,256,128]{2,1,0:T(8,128)S(1)}) custom-call(s32[10]{0:T(128)S(1)} %pad_add_fusion.place, s32[256,128]{1,0:T(8,128)S(1)} %get-tuple-element.31.starts, bf16[256,2048]{1,0:T(8,128)(2,1)S(1)} %get-tuple-element.40.query, bf16[256,512]{1,0:T(8,128)(2,1)S(1)} %keys.1.mine.refs_0_, ...), custom_call_target="tpu_custom_call" | custom-call | flops 1879048192 | bytes 8388608 | tf_op jit(solution)/shard_map/scores/pallas_call | solution.py:272
  44.2 0.8 %collective-permute-done.7.refs_4_ = bf16[256,512]{1,0:T(8,128)(2,1)S(1)} collective-permute-done((bf16[256,512]{1,0:T(8,128)(2,1)S(1)}, bf16[256,512]{1,0:T(8,128)(2,1)S(1)}, u32[]{:S(2)}, u32[]{:S(2)}) %collective-permute-start.7) | collective-permute-done | bytes 262176 | tf_op jit(solution)/shard_map/ppermute | solution.py:261
  45.0 4.6 %mix_low.1 = (f32[128,2048]{1,0:T(8,128)S(1)}, bf16[128,2048]{1,0:T(8,128)(2,1)S(1)}, bf16[256,2048]{1,0:T(8,128)(2,1)S(1)}) custom-call(s32[10]{0:T(128)S(1)} %pad_add_fusion.place, bf16[16,256,768]{2,1,0:T(8,128)(2,1)S(1)} %get-tuple-element.45.refs_0_, f32[16,256,128]{2,1,0:T(8,128)S(1)} %get-tuple-element.46.refs_1_, ...), custom_call_target="tpu_custom_call" | custom-call | flops 2952790016 | bytes 4194304 | tf_op jit(solution)/shard_map/mix_low/pallas_call | solution.py:282
  49.6 2.9 %mix_high.1 = (f32[128,2048]{1,0:T(8,128)S(1)}, bf16[128,2048]{1,0:T(8,128)(2,1)S(1)}) custom-call(s32[10]{0:T(128)S(1)} %pad_add_fusion.place, bf16[256,2048]{1,0:T(8,128)(2,1)S(1)} %get-tuple-element.53.refs_0_, bf16[2048,4096]{1,0:T(8,128)(2,1)S(1)} %bitcast.3), custom_call_target="tpu_custom_call" | custom-call | flops 2147483648 | bytes 4194304 | tf_op jit(solution)/shard_map/mix_high/pallas_call | solution.py:287
  52.5 0.1 collective-permute-start.9
  52.6 0.5 collective-permute-start.10
  53.1 1.4 %collective-permute-done.9.got_low = bf16[128,2048]{1,0:T(8,128)(2,1)S(1)} collective-permute-done((bf16[128,2048]{1,0:T(8,128)(2,1)S(1)}, bf16[128,2048]{1,0:T(8,128)(2,1)S(1)}, u32[]{:S(2)}, u32[]{:S(2)}) %collective-permute-start.9) | collective-permute-done | bytes 524320 | tf_op jit(solution)/shard_map/ppermute | solution.py:286
  54.5 0.7 %collective-permute-done.10.got_high = bf16[128,2048]{1,0:T(8,128)(2,1)S(1)} collective-permute-done((bf16[128,2048]{1,0:T(8,128)(2,1)S(1)}, bf16[128,2048]{1,0:T(8,128)(2,1)S(1)}, u32[]{:S(2)}, u32[]{:S(2)}) %collective-permute-start.10) | collective-permute-done | bytes 524320 | tf_op jit(solution)/shard_map/ppermute | solution.py:290
  55.2 1.2 %add.5 = bf16[128,4096]{1,0:T(8,128)(2,1)} custom-call(f32[128,2048]{1,0:T(8,128)S(1)} %get-tuple-element.52.own_low, f32[128,2048]{1,0:T(8,128)S(1)} %get-tuple-element.54.own_high, bf16[128,2048]{1,0:T(8,128)(2,1)S(1)} %collective-permute-done.9.got_low, bf16[128,2048]{1,0:T(8,128)(2,1)S(1)} %collective-permute-done.10.got_high), custom_call_target="tpu_custom_call" | custom-call | flops 524288 | bytes 4194304 | tf_op jit(solution)/shard_map/add/pallas_call | solution.py:291
  (19 shorter events, 0.0 us)
Async XLA Ops:
  0.0 4.5 %collective-permute-start = (bf16[128,4096]{1,0:T(8,128)(2,1)}, bf16[128,4096]{1,0:T(8,128)(2,1)S(1)}, u32[]{:S(2)}, u32[]{:S(2)}) collective-permute-start(bf16[128,4096]{1,0:T(8,128)(2,1)} %own_hbm.1), channel_id=1, source_target_pairs={{0,1},{1,0},{2,3},{3,2},{4,5},{5,4},{6,7},{7,6},{8,9},{9,8},{10,11... | collective-permute-start | bytes 3145736 | tf_op jit(solution)/shard_map/ppermute | solution.py:227
  4.5 17.7 %slice-start.4 = ((s8[16777216]{0:T(1024)(128)(4,1)}), s8[4194304]{0:T(1024)(128)(4,1)S(1)}, s32[]{:S(2)}) async-start(s8[16777216]{0:T(1024)(128)(4,1)} %bitcast.4), calls=%async_computation.4 | async-start | bytes 8388608
  6.0 12.1 %collective-permute-start.1 = (bf16[256,512]{1,0:T(8,128)(2,1)S(1)}, bf16[256,512]{1,0:T(8,128)(2,1)S(1)}, u32[]{:S(2)}, u32[]{:S(2)}) collective-permute-start(bf16[256,512]{1,0:T(8,128)(2,1)S(1)} %keys.1.mine.refs_0_), channel_id=1, source_target_pairs={{0,8},{2,10},{4,12},{6,14},{8,16},{10,18},{12,20},{14,22},{16,24},... | collective-permute-start | bytes 786440 | tf_op jit(solution)/shard_map/ppermute | solution.py:248
  10.5 11.8 %slice-start.5 = ((s8[16777216]{0:T(1024)(128)(4,1)}), s8[4194304]{0:T(1024)(128)(4,1)S(1)}, s32[]{:S(2)}) async-start(s8[16777216]{0:T(1024)(128)(4,1)} %bitcast.4), calls=%async_computation.5 | async-start | bytes 8388608
  10.5 11.8 %slice-start.6 = ((s8[16777216]{0:T(1024)(128)(4,1)}), s8[4194304]{0:T(1024)(128)(4,1)S(1)}, s32[]{:S(2)}) async-start(s8[16777216]{0:T(1024)(128)(4,1)} %bitcast.4), calls=%async_computation.6 | async-start | bytes 8388608
  10.5 11.7 %slice-start.7 = ((s8[16777216]{0:T(1024)(128)(4,1)}), s8[4194304]{0:T(1024)(128)(4,1)S(1)}, s32[]{:S(2)}) async-start(s8[16777216]{0:T(1024)(128)(4,1)} %bitcast.4), calls=%async_computation.7 | async-start | bytes 8388608
  14.1 13.0 %collective-permute-start.5 = (bf16[256,512]{1,0:T(8,128)(2,1)S(1)}, bf16[256,512]{1,0:T(8,128)(2,1)S(1)}, u32[]{:S(2)}, u32[]{:S(2)}) collective-permute-start(bf16[256,512]{1,0:T(8,128)(2,1)S(1)} %get-tuple-element.44.refs_5_.mine), channel_id=1, source_target_pairs={{0,8},{2,10},{4,12},{6,14},{8,16},{10,18},{12,20},{14,22},{16,24},... | collective-permute-start | bytes 786440 | tf_op jit(solution)/shard_map/ppermute | solution.py:255
  18.7 12.1 %collective-permute-start.2 = (bf16[256,512]{1,0:T(8,128)(2,1)S(1)}, bf16[256,512]{1,0:T(8,128)(2,1)S(1)}, u32[]{:S(2)}, u32[]{:S(2)}) collective-permute-start(bf16[256,512]{1,0:T(8,128)(2,1)S(1)} %get-tuple-element.41), channel_id=1, source_target_pairs={{0,2},{2,0},{4,6},{6,4},{8,10},{10,8},{12,14},{14,12},{16,18},{18,... | collective-permute-start | bytes 786440 | tf_op jit(solution)/shard_map/ppermute | solution.py:261
  20.2 13.6 %collective-permute-start.3 = (bf16[256,512]{1,0:T(8,128)(2,1)S(1)}, bf16[256,512]{1,0:T(8,128)(2,1)S(1)}, u32[]{:S(2)}, u32[]{:S(2)}) collective-permute-start(bf16[256,512]{1,0:T(8,128)(2,1)S(1)} %get-tuple-element.42), channel_id=1, source_target_pairs={{0,4},{2,6},{4,0},{6,2},{8,12},{10,14},{12,8},{14,10},{16,20},{18,... | collective-permute-start | bytes 786440 | tf_op jit(solution)/shard_map/ppermute | solution.py:261
  21.7 12.8 %collective-permute-start.4 = (bf16[256,512]{1,0:T(8,128)(2,1)S(1)}, bf16[256,512]{1,0:T(8,128)(2,1)S(1)}, u32[]{:S(2)}, u32[]{:S(2)}) collective-permute-start(bf16[256,512]{1,0:T(8,128)(2,1)S(1)} %get-tuple-element.43), channel_id=1, source_target_pairs={{0,6},{2,4},{4,2},{6,0},{8,14},{10,12},{12,10},{14,8},{16,22},{18,... | collective-permute-start | bytes 786440 | tf_op jit(solution)/shard_map/ppermute | solution.py:261
  27.1 17.9 %slice-start = ((s8[16777216]{0:T(1024)(128)(4,1)}), s8[4194304]{0:T(1024)(128)(4,1)S(1)}, s32[]{:S(2)}) async-start(s8[16777216]{0:T(1024)(128)(4,1)} %bitcast.2), calls=%async_computation | async-start | bytes 8388608
  27.1 17.9 %slice-start.1 = ((s8[16777216]{0:T(1024)(128)(4,1)}), s8[4194304]{0:T(1024)(128)(4,1)S(1)}, s32[]{:S(2)}) async-start(s8[16777216]{0:T(1024)(128)(4,1)} %bitcast.2), calls=%async_computation.1 | async-start | bytes 8388608
  27.1 17.9 %slice-start.2 = ((s8[16777216]{0:T(1024)(128)(4,1)}), s8[4194304]{0:T(1024)(128)(4,1)S(1)}, s32[]{:S(2)}) async-start(s8[16777216]{0:T(1024)(128)(4,1)} %bitcast.2), calls=%async_computation.2 | async-start | bytes 8388608
  27.1 17.9 %slice-start.3 = ((s8[16777216]{0:T(1024)(128)(4,1)}), s8[4194304]{0:T(1024)(128)(4,1)S(1)}, s32[]{:S(2)}) async-start(s8[16777216]{0:T(1024)(128)(4,1)} %bitcast.2), calls=%async_computation.3 | async-start | bytes 8388608
  27.7 16.4 %collective-permute-start.6 = (bf16[256,512]{1,0:T(8,128)(2,1)S(1)}, bf16[256,512]{1,0:T(8,128)(2,1)S(1)}, u32[]{:S(2)}, u32[]{:S(2)}) collective-permute-start(bf16[256,512]{1,0:T(8,128)(2,1)S(1)} %get-tuple-element.49), channel_id=1, source_target_pairs={{0,2},{2,0},{4,6},{6,4},{8,10},{10,8},{12,14},{14,12},{16,18},{18,... | collective-permute-start | bytes 786440 | tf_op jit(solution)/shard_map/ppermute | solution.py:261
  29.3 15.7 %collective-permute-start.7 = (bf16[256,512]{1,0:T(8,128)(2,1)S(1)}, bf16[256,512]{1,0:T(8,128)(2,1)S(1)}, u32[]{:S(2)}, u32[]{:S(2)}) collective-permute-start(bf16[256,512]{1,0:T(8,128)(2,1)S(1)} %get-tuple-element.50), channel_id=1, source_target_pairs={{0,4},{2,6},{4,0},{6,2},{8,12},{10,14},{12,8},{14,10},{16,20},{18,... | collective-permute-start | bytes 786440 | tf_op jit(solution)/shard_map/ppermute | solution.py:261
  30.8 14.1 %collective-permute-start.8 = (bf16[256,512]{1,0:T(8,128)(2,1)S(1)}, bf16[256,512]{1,0:T(8,128)(2,1)S(1)}, u32[]{:S(2)}, u32[]{:S(2)}) collective-permute-start(bf16[256,512]{1,0:T(8,128)(2,1)S(1)} %get-tuple-element.51), channel_id=1, source_target_pairs={{0,6},{2,4},{4,2},{6,0},{8,14},{10,12},{12,10},{14,8},{16,22},{18,... | collective-permute-start | bytes 786440 | tf_op jit(solution)/shard_map/ppermute | solution.py:261
  52.5 2.0 %collective-permute-start.9 = (bf16[128,2048]{1,0:T(8,128)(2,1)S(1)}, bf16[128,2048]{1,0:T(8,128)(2,1)S(1)}, u32[]{:S(2)}, u32[]{:S(2)}) collective-permute-start(bf16[128,2048]{1,0:T(8,128)(2,1)S(1)} %get-tuple-element.55), channel_id=1, source_target_pairs={{0,1},{1,0},{2,3},{3,2},{4,5},{5,4},{6,7},{7,6},{8,9},{9,8},{10,11... | collective-permute-start | bytes 1572872 | tf_op jit(solution)/shard_map/ppermute | solution.py:286
  52.6 2.6 %collective-permute-start.10 = (bf16[128,2048]{1,0:T(8,128)(2,1)S(1)}, bf16[128,2048]{1,0:T(8,128)(2,1)S(1)}, u32[]{:S(2)}, u32[]{:S(2)}) collective-permute-start(bf16[128,2048]{1,0:T(8,128)(2,1)S(1)} %get-tuple-element.56), channel_id=1, source_target_pairs={{0,1},{1,0},{2,3},{3,2},{4,5},{5,4},{6,7},{7,6},{8,9},{9,8},{10,11... | collective-permute-start | bytes 1572872 | tf_op jit(solution)/shard_map/ppermute | solution.py:290

commit v3 on v2

v3 whole, which is shorter than its diff:
```python
import functools
import math

import jax
import jax.numpy as jnp
from jax import lax
from jax.experimental import pallas as pl
from jax.experimental.pallas import tpu as pltpu
from jax.sharding import PartitionSpec as P

HEAD_SIZE = 128
LAYER = 4
MASKED = -1e30
VALUES_COST = 4 << 30
RELAY_COST = 9 << 30
SCORE_SCALE = math.log2(math.e) * HEAD_SIZE ** (-0.5)
SWAP = [(0, 1), (1, 0)]
VMEM = pl.BlockSpec(memory_space=pltpu.VMEM)
ANY = pl.BlockSpec(memory_space=pl.ANY)


def inverse_frequency():
    table = []
    for number in range(HEAD_SIZE // 2):
        base_freq = 500000.0 ** (-(2.0 * number) / HEAD_SIZE)
        wavelength = 2.0 * math.pi / base_freq
        smooth = (8192.0 / wavelength - 1.0) / 3.0
        if wavelength < 2048.0:
            table.append(base_freq)
        elif wavelength > 8192.0:
            table.append(base_freq / 8.0)
        else:
            table.append((1.0 - smooth) * base_freq / 8.0 + smooth * base_freq)
    return table


def dot(a, b):
    return jnp.dot(a, b, preferred_element_type=jnp.float32)


def rotated(block, cosine, sine):
    return block * cosine + pltpu.roll(block, HEAD_SIZE // 2, 1) * sine


def first_keys_kernel(chunks, lengths_hbm, own_hbm, key_hbm, key_sum, own, w_key, cosine, sine, starts, lengths, sems):
    depth = w_key.shape[0] // chunks
    row_copy = pltpu.make_async_copy(own_hbm, own, sems.at[chunks])
    row_copy.start()
    copies = []
    for number in range(chunks):
        at = pl.ds(number * depth, depth)
        copies.append(pltpu.make_async_copy(key_hbm.at[at], w_key.at[at], sems.at[number]))
        copies[-1].start()
    tokens = cosine.shape[0]
    length_copy = pltpu.make_async_copy(lengths_hbm, lengths, sems.at[chunks + 1])
    length_copy.start()
    lane = lax.broadcasted_iota(jnp.int32, (1, HEAD_SIZE), 1)
    pair_of_lane = lane % (HEAD_SIZE // 2)
    freq = jnp.zeros((1, HEAD_SIZE), jnp.float32)
    for number, value in enumerate(inverse_frequency()):
        freq = jnp.where(pair_of_lane == number, jnp.float32(value), freq)
    positions = lax.axis_index("seq") * tokens + lax.broadcasted_iota(jnp.int32, (tokens, HEAD_SIZE), 0)
    angles = positions.astype(jnp.float32) * freq
    cosine[...] = jnp.cos(angles)
    turned = jnp.sin(angles)
    sine[...] = jnp.where(lane < HEAD_SIZE // 2, -turned, turned)
    length_copy.wait()
    start = jnp.zeros((tokens, HEAD_SIZE), jnp.int32)
    end = jnp.int32(0)
    for number in range(lengths.shape[0]):
        end = end + lengths[number]
        start = jnp.where(positions >= end, end, start)
    starts[...] = start
    row_copy.wait()
    for number, copy in enumerate(copies):
        at = slice(number * depth, (number + 1) * depth)
        copy.wait()
        product = dot(own[:, at], w_key[at, :])
        key_sum[...] = product if number == 0 else key_sum[...] + product


def halves(half):
    core = lax.axis_index("head")
    return pl.ds(pl.multiple_of(core * half, half), half), pl.ds(pl.multiple_of((1 - core) * half, half), half)


def keys_kernel(other, w_key, key_own, cosine, sine, keys):
    half, width = key_own.shape
    mine, theirs = halves(half)
    for here, block in ((mine, key_own[...]), (theirs, dot(other[...], w_key[...]))):
        for head in range(width // HEAD_SIZE):
            at = slice(head * HEAD_SIZE, (head + 1) * HEAD_SIZE)
            keys[here, at] = rotated(block[:, at], cosine[here, :], sine[here, :]).astype(keys.dtype)


def values_kernel(chunks, own, other, value_hbm, values, rows, done, w_value, total, sems):
    depth = w_value.shape[0] // chunks
    copies = []
    for number in range(chunks):
        at = pl.ds(number * depth, depth)
        copies.append(pltpu.make_async_copy(value_hbm.at[at], w_value.at[at], sems.at[number]))
        copies[-1].start()
    mine, theirs = halves(own.shape[0])
    rows[mine, :] = own[...]
    rows[theirs, :] = other[...]
    done[...] = jnp.zeros_like(done)
    for number, copy in enumerate(copies):
        at = slice(number * depth, (number + 1) * depth)
        copy.wait()
        product = dot(rows[:, at], w_value[at, :])
        if number > 0:
            product = product + total[...]
        if number < chunks - 1:
            total[...] = product
        else:
            values[...] = product.astype(values.dtype)


def query_kernel(rows, weight, cosine, sine, after, query, done):
    del after
    done[...] = jnp.zeros_like(done)
    wide = 4 * HEAD_SIZE
    for number in range(weight.shape[1] // wide):
        result = dot(rows[...], weight[:, number * wide : (number + 1) * wide])
        for head in range(wide // HEAD_SIZE):
            at = slice(head * HEAD_SIZE, (head + 1) * HEAD_SIZE)
            out = slice(number * wide + head * HEAD_SIZE, number * wide + (head + 1) * HEAD_SIZE)
            query[:, out] = rotated(result[:, at], cosine[...], sine[...]).astype(query.dtype)


def relay_kernel(plan, own, earlier, *refs):
    index = lax.axis_index("seq")
    outs = refs[len(refs) - len(plan) :]
    for (way, low), out in zip(plan, outs):
        upper = index % 2 > 0 if way == 1 else index % LAYER >= 2
        at = slice(low, low + out.shape[1])
        out[...] = jnp.where(upper, earlier[:, at], own[:, at])


def score_kernel(distances, near, starts, query, *refs):
    count = len(distances)
    keys, refs = refs[:count], refs[count:]
    values, refs = refs[:near], refs[near:]
    weights_a, total_a, acc_a, weights_b, total_b, acc_b, bias = refs
    tokens = query.shape[0]
    index = lax.axis_index("seq")
    base = index * tokens
    query_pos = base + lax.broadcasted_iota(jnp.int32, (tokens, tokens), 0)
    start = jnp.concatenate([starts[...]] * (tokens // starts.shape[1]), axis=1)
    blocks = [slice(number * tokens, (number + 1) * tokens) for number in range(count)]
    for block, (even, odd) in zip(blocks, distances):
        first = base - tokens * jnp.where(index % 2 > 0, odd, even)
        key_pos = first + lax.broadcasted_iota(jnp.int32, (tokens, tokens), 1)
        allowed = (key_pos >= start) & (key_pos <= query_pos)
        bias[:, block] = jnp.where(allowed, 0.0, MASKED)
    heads = query.shape[1] // HEAD_SIZE
    kv_heads = keys[0].shape[1] // HEAD_SIZE
    group = heads // kv_heads
    ones = jnp.ones((tokens, HEAD_SIZE), query.dtype)

    def column(number):
        return slice(number * HEAD_SIZE, (number + 1) * HEAD_SIZE)

    def scores_of(head):
        return [
            lax.dot_general(
                query[:, column(head)], key[:, column(head // group)], (((1,), (1,)), ((), ())),
                preferred_element_type=jnp.float32,
            )
            * SCORE_SCALE
            + bias[:, block]
            for key, block in zip(keys, blocks)
        ]

    scores = scores_of(0)
    for head in range(heads):
        ahead = scores_of(head + 1) if head + 1 < heads else None
        top = jnp.max(functools.reduce(jnp.maximum, scores), axis=1, keepdims=True)
        weights = [jnp.exp2(score - top).astype(query.dtype) for score in scores]
        late = head >= heads // 2
        at = head - heads // 2 if late else head
        product = None
        for number, block in enumerate(values):
            term = dot(weights[number], jnp.concatenate([block[:, column(head // group)], ones], axis=1))
            product = term if product is None else product + term
        weights_out, total, acc = (weights_b, total_b, acc_b) if late else (weights_a, total_a, acc_a)
        acc[at], total[at] = product[:, :HEAD_SIZE], product[:, HEAD_SIZE:]
        for number in range(near, count):
            weights_out[at, :, blocks[number - near]] = weights[number]
        scores = ahead


def attend_far(second, weights, total, acc, blocks, attended):
    heads = weights.shape[0]
    kv_heads = min(block.shape[1] for block in blocks) // HEAD_SIZE
    group = heads // kv_heads
    for kv_head in range(kv_heads):
        pieces = []
        for block in blocks:
            low = (kv_head + (kv_heads if second and block.shape[1] > kv_heads * HEAD_SIZE else 0)) * HEAD_SIZE
            pieces.append(block[:, low : low + HEAD_SIZE])
        values = jnp.concatenate(pieces, axis=0)
        values = jnp.concatenate([values, jnp.ones((values.shape[0], HEAD_SIZE), values.dtype)], axis=1)
        for head in range(kv_head * group, (kv_head + 1) * group):
            product = dot(weights[head], values)
            result = (acc[head] + product[:, :HEAD_SIZE]) / (total[head] + product[:, HEAD_SIZE:])
            attended[:, head * HEAD_SIZE : (head + 1) * HEAD_SIZE] = result.astype(attended.dtype)


WIDE = 4 * HEAD_SIZE


def mix_first_kernel(far, weights, total, acc, *refs):
    blocks, (weight, summed, attended) = refs[:far], refs[far:]
    attend_far(False, weights, total, acc, blocks, attended)
    depth = attended.shape[1]
    for number in range(summed.shape[1] // WIDE):
        at = slice(number * WIDE, (number + 1) * WIDE)
        summed[:, at] = dot(attended[...], weight[:depth, at])


def split_rows(result, own, send, at):
    half = own.shape[0]
    on_high = lax.axis_index("head") > 0
    own[:, at] = jnp.where(on_high, result[half:], result[:half])
    send[:, at] = jnp.where(on_high, result[:half], result[half:]).astype(send.dtype)


def mix_columns(attended, weight, summed, low, own, send):
    depth = attended.shape[1]
    for number in range(own.shape[1] // WIDE):
        here = slice(low + number * WIDE, low + (number + 1) * WIDE)
        result = summed[:, here] + dot(attended[...], weight[depth:, here])
        split_rows(result, own, send, slice(number * WIDE, (number + 1) * WIDE))


def mix_second_kernel(far, weights, total, acc, *refs):
    blocks, (weight, summed, own, send, attended) = refs[:far], refs[far:]
    attend_far(True, weights, total, acc, blocks, attended)
    mix_columns(attended, weight, summed, 0, own, send)


def mix_more_kernel(low, attended, weight, summed, own, send):
    mix_columns(attended, weight, summed, low, own, send)


def mix_last_kernel(low, attended, weight, summed, got_low, own, send):
    del got_low
    mix_columns(attended, weight, summed, low, own, send)


def add_low_kernel(own, got, mixed_hbm, mixed, sem):
    mixed[...] = (own[...] + got[...].astype(jnp.float32)).astype(mixed.dtype)
    copy = pltpu.make_async_copy(mixed, mixed_hbm.at[:, pl.ds(0, mixed.shape[1])], sem)
    copy.start()
    copy.wait()


def add_kernel(own_one, own_two, got_one, got_two, mixed_in, mixed_hbm, mixed, sems):
    del mixed_in
    width = own_one.shape[1]
    low = mixed_hbm.shape[1] - 2 * width
    copies = []
    for number, (own, got) in enumerate(((own_one, got_one), (own_two, got_two))):
        at = pl.ds(number * width, width)
        mixed[:, at] = (own[...] + got[...].astype(jnp.float32)).astype(mixed.dtype)
        copies.append(pltpu.make_async_copy(mixed.at[:, at], mixed_hbm.at[:, pl.ds(low + number * width, width)], sems.at[number]))
        copies[-1].start()
    for copy in copies:
        copy.wait()


def call(kernel, name, outs, in_specs, flops, nbytes, limit, scratch=(), out_specs=None, aliases=None):
    return pl.pallas_call(
        kernel,
        out_shape=outs,
        in_specs=in_specs,
        out_specs=out_specs or [VMEM] * len(outs),
        scratch_shapes=list(scratch),
        input_output_aliases=aliases or {},
        name=name,
        cost_estimate=pl.CostEstimate(flops=flops, bytes_accessed=nbytes, transcendentals=0),
        compiler_params=pltpu.CompilerParams(vmem_limit_bytes=limit << 20),
    )


def in_hbm(array):
    return pltpu.with_memory_space_constraint(array, pltpu.HBM)


def body(input_rows, doc_lengths, w_query, key_weight, value_weight, w_out):
    half, model = input_rows.shape
    tokens = 2 * half
    width_q, width_k = w_query.shape[1], key_weight.shape[1]
    heads = width_q // HEAD_SIZE
    shards = lax.axis_size("seq")
    bf16, f32 = jnp.bfloat16, jnp.float32
    shape = pltpu.VMEM

    other = lax.ppermute(input_rows, "head", SWAP)

    flag = shape((8, HEAD_SIZE), f32)
    table = shape((tokens, HEAD_SIZE), f32)
    kv_shape = shape((tokens, width_k), bf16)
    chunks = 8
    key_own, own, w_key, cosine, sine, starts = call(
        functools.partial(first_keys_kernel, chunks), "keys_own",
        [
            shape((half, width_k), f32), shape((half, model), bf16), shape(key_weight.shape, bf16),
            table, table, shape((tokens, HEAD_SIZE), jnp.int32),
        ],
        [ANY, ANY, ANY], 2 * half * model * width_k, 2 * model * width_k, 4,
        [pltpu.SMEM(doc_lengths.shape, jnp.int32), pltpu.SemaphoreType.DMA((chunks + 2,))],
    )(in_hbm(doc_lengths), in_hbm(input_rows), in_hbm(key_weight))
    (keys,) = call(
        keys_kernel, "keys", [kv_shape], [VMEM] * 5, 2 * half * model * width_k, 2 * model * width_k, 4,
    )(other, w_key, key_own, cosine, sine)

    every = range(shards)
    step_z = [(i, i + LAYER) for i in every if i + LAYER < shards]
    keys_z = lax.ppermute(keys, "seq", step_z)

    values, rows, done = call(
        functools.partial(values_kernel, 4), "values", [kv_shape, shape((tokens, model), bf16), flag], [VMEM, VMEM, ANY],
        VALUES_COST, 2 * model * width_k, 10,
        [pltpu.VMEM(value_weight.shape, bf16), pltpu.VMEM((tokens, width_k), f32), pltpu.SemaphoreType.DMA((4,))],
    )(own, other, in_hbm(value_weight))
    values_z = lax.ppermute(values, "seq", step_z)

    def exchange(mine, earlier, plan, wides, after, cost):
        to = call(
            functools.partial(relay_kernel, plan), "relay", [shape((tokens, wide), bf16) for wide in wides],
            [VMEM] * (2 + len(after)), cost, 2 << 20, 4,
        )(mine, earlier, *after)
        return [lax.ppermute(array, "seq", [(i, i ^ way) for i in every]) for (way, _), array in zip(plan, to)], to[0]

    part = width_k // 2
    keys_far, sent_first = exchange(keys, keys_z, ((1, 0), (2, 0), (3, 0)), [width_k] * 3, [done], RELAY_COST)
    query, done = call(
        query_kernel, "queries", [shape((tokens, width_q), bf16), flag], [VMEM] * 5,
        2 * tokens * model * width_q, 2 * model * width_q, 8,
    )(rows, w_query, cosine, sine, sent_first)
    (values_d, values_x, values_y), _ = exchange(
        values, values_z, ((3, 0), (1, 0), (2, 0)), [width_k, part, part], [done], 9 << 30
    )
    (values_x_more, values_y_more), _ = exchange(values, values_z, ((1, part), (2, part)), [part] * 2, keys_far, 0)
    far_a, far_b = (values_x, values_y, values_d), (values_x_more, values_y_more, values_d)

    far = len(keys_far)
    heads_half = heads // 2
    state = [shape((heads_half, tokens, far * tokens), bf16)] + [shape((heads_half, tokens, HEAD_SIZE), f32)] * 2
    *state_a, weights_b, total_b, acc_b = call(
        functools.partial(score_kernel, ((0, 0), (LAYER, LAYER), (3, 1), (2, 2), (1, 3)), 2), "scores",
        state * 2, [VMEM] * (2 + 2 + far + 2),
        14 * heads * tokens * tokens * HEAD_SIZE, 8 << 20, 16, [pltpu.VMEM((tokens, (far + 2) * tokens), f32)],
    )(starts, query, keys, keys_z, *keys_far, values, values_z)

    columns = w_out.shape[1]
    attended_shape = shape((tokens, width_q // 2), bf16)
    far_flops = far * heads * tokens * tokens * HEAD_SIZE
    out_flops = tokens * width_q * columns
    summed, _ = call(
        functools.partial(mix_first_kernel, far), "mix_first", [shape((tokens, columns), f32), attended_shape],
        [VMEM] * (4 + far), out_flops + far_flops, 4 << 20, 6,
    )(*state_a, *far_a, w_out)

    def out_shapes(wide):
        return [shape((half, wide), f32), shape((half, wide), bf16)]

    cut, wide = columns // 2, columns // 4
    own_low, send, attended = call(
        functools.partial(mix_second_kernel, far), "mix_second", out_shapes(cut) + [attended_shape],
        [VMEM] * (5 + far), out_flops // 2 + far_flops, 4 << 20, 6,
    )(weights_b, total_b, acc_b, *far_b, w_out, summed)
    got_low = lax.ppermute(send, "head", SWAP)
    own_one, send = call(
        functools.partial(mix_more_kernel, cut), "mix_more", out_shapes(wide), [VMEM] * 3, out_flops // 4, 4 << 20, 6,
    )(attended, w_out, summed)
    got_one = lax.ppermute(send, "head", SWAP)
    own_two, send = call(
        functools.partial(mix_last_kernel, cut + wide), "mix_last", out_shapes(wide), [VMEM] * 4, out_flops // 4, 4 << 20, 6,
    )(attended, w_out, summed, got_low)
    got_two = lax.ppermute(send, "head", SWAP)
    (mixed,) = call(
        add_low_kernel, "add_low", [pltpu.HBM((half, columns), bf16)], [VMEM] * 2, half * cut, 2 << 20, 4,
        [pltpu.VMEM((half, cut), bf16), pltpu.SemaphoreType.DMA(())], [ANY],
    )(own_low, got_low)
    (mixed,) = call(
        add_kernel, "add", [pltpu.HBM((half, columns), bf16)], [VMEM] * 4 + [ANY], half * columns, 4 << 20, 4,
        [pltpu.VMEM((half, 2 * wide), bf16), pltpu.SemaphoreType.DMA((2,))], [ANY], {4: 0},
    )(own_one, own_two, got_one, got_two, mixed)
    return mixed


def solution(mesh):
    in_specs = (
        P(("seq", "head"), None),
        P(),
        P(None, "head"),
        P(None, "head"),
        P(None, "head"),
        P("head", None),
    )
    out_specs = P(("seq", "head"), None)
    return jax.shard_map(body, mesh=mesh, in_specs=in_specs, out_specs=out_specs, check_vma=False)
```

time: 56.6 us -> 53.4 us (0.943)
  the two profiles are of different devices: /device:TPU:0 before, /device:TPU:25 now
where the time goes in v3:
time: 53.4 us; the launch traced here: 52.7 us
  Pallas kernels  27.3 us (51%)
  starting transfers between devices  18.5 us (35%)
  waiting for transfers between devices  5.81 us (11%)
  local copies, waits for them, and re-layouts  0.69 us (1%)
    ppermute x8, starting transfers between devices, exchange(): lax.ppermute(array, 'seq', [(i, i ^ way) for i in every])  9.11 us
    pallas_call x1, Pallas kernels, body(): call(functools.partial(score_kernel, ((0, 0), (LAYER, LAYER), (3, 1), (2,...  6.5 us
    ppermute x1, starting transfers between devices, body(): got_low = lax.ppermute(send, 'head', SWAP)  5.19 us
    pallas_call x1, Pallas kernels, body(): call(query_kernel, 'queries', [shape((tokens, width_q), bf16), flag], [VM...  4.77 us
    pallas_call x1, Pallas kernels, body(): call(functools.partial(mix_first_kernel, far), 'mix_first', [shape((token...  3.94 us
    ppermute x1, waiting for transfers between devices, body(): keys_z = lax.ppermute(keys, 'seq', step_z)  3.84 us
    pallas_call x1, Pallas kernels, body(): call(functools.partial(values_kernel, 4), 'values', [kv_shape, shape((tok...  2.84 us
    pallas_call x1, Pallas kernels, body(): call(functools.partial(first_keys_kernel, chunks), 'keys_own', [shape((ha...  2.78 us
  transfers between devices with their start and end apart: 14, of which 4 were waited for; matrix products, arithmetic and copies ran while one was open for 0% of the time, Pallas kernels for 44%

profile of v3, /device:TPU:25, one launch (start us, length us, event | category | flops | bytes accessed | tf_op | source)
XLA Modules:
  0.0 52.7 jit_solution(2657283346316017981)
XLA Ops:
  0.0 0.7 %collective-permute-start = (bf16[128,4096]{1,0:T(8,128)(2,1)}, bf16[128,4096]{1,0:T(8,128)(2,1)S(1)}, u32[]{:S(2)}, u32[]{:S(2)}) collective-permute-start(bf16[128,4096]{1,0:T(8,128)(2,1)} %own_hbm.1), channel_id=1, source_target_pairs={{0,1},{1,0},{2,3},{3,2},{4,5},{5,4},{6,7},{7,6},{8,9},{9,8},{10,11... | collective-permute-start | bytes 3145736 | tf_op jit(solution)/shard_map/ppermute | solution.py:300
  0.7 2.8 %keys_own.1 = (f32[128,512]{1,0:T(8,128)S(1)}, bf16[128,4096]{1,0:T(8,128)(2,1)S(1)}, bf16[4096,512]{1,0:T(8,128)(2,1)S(1)}, f32[256,128]{1,0:T(8,128)S(1)}, f32...) custom-call(s32[8]{0:T(128)} %lengths_hbm.1, bf16[128,4096]{1,0:T(8,128)(2,1)} %own_hbm.1, bf16[4096,512]{1,0:T(8,128)(2,1)} %key_hbm.1), custom_call_target="tpu_custom_call" | custom-call | flops 536870912 | bytes 4194304 | tf_op jit(solution)/shard_map/keys_own/pallas_call | solution.py:306
  3.5 0.8 %keys.1.own.refs_0_ = bf16[256,512]{1,0:T(8,128)(2,1)S(1)} custom-call(bf16[128,4096]{1,0:T(8,128)(2,1)S(1)} %collective-permute-done.other, bf16[4096,512]{1,0:T(8,128)(2,1)S(1)} %get-tuple-element.43.w_key, f32[128,512]{1,0:T(8,128)S(1)} %get-tuple-element.44.key_own, f32[256,128]{1,0:T(8,128)S(1)} %get-tuple-element.41.cosine, ...), custom_call_target="tpu_custom_call" | custom-call | flops 536870912 | bytes 4194304 | tf_op jit(solution)/shard_map/keys/pallas_call | solution.py:315
  4.3 1.3 %collective-permute-start.1 = (bf16[256,512]{1,0:T(8,128)(2,1)S(1)}, bf16[256,512]{1,0:T(8,128)(2,1)S(1)}, u32[]{:S(2)}, u32[]{:S(2)}) collective-permute-start(bf16[256,512]{1,0:T(8,128)(2,1)S(1)} %keys.1.own.refs_0_), channel_id=1, source_target_pairs={{0,8},{2,10},{4,12},{6,14},{8,16},{10,18},{12,20},{14,22},{16,24},... | collective-permute-start | bytes 786440 | tf_op jit(solution)/shard_map/ppermute | solution.py:321
  5.6 2.8 %values.1 = (bf16[256,512]{1,0:T(8,128)(2,1)S(1)}, bf16[256,4096]{1,0:T(8,128)(2,1)S(1)}, f32[8,128]{1,0:T(8,128)S(1)}) custom-call(bf16[128,4096]{1,0:T(8,128)(2,1)S(1)} %get-tuple-element.39.own, bf16[128,4096]{1,0:T(8,128)(2,1)S(1)} %collective-permute-done.other, bf16[4096,512]{1,0:T(8,128)(2,1)} %value_hbm.1), custom_call_target="tpu_custom_call" | custom-call | flops 4294967296 | bytes 4194304 | tf_op jit(solution)/shard_map/values/pallas_call | solution.py:323
  8.5 1.7 %collective-permute-start.5 = (bf16[256,512]{1,0:T(8,128)(2,1)S(1)}, bf16[256,512]{1,0:T(8,128)(2,1)S(1)}, u32[]{:S(2)}, u32[]{:S(2)}) collective-permute-start(bf16[256,512]{1,0:T(8,128)(2,1)S(1)} %get-tuple-element.50.refs_5_.own), channel_id=1, source_target_pairs={{0,8},{2,10},{4,12},{6,14},{8,16},{10,18},{12,20},{14,22},{16,24},... | collective-permute-start | bytes 786440 | tf_op jit(solution)/shard_map/ppermute | solution.py:328
  10.2 3.8 %collective-permute-done.1.earlier.refs_1_ = bf16[256,512]{1,0:T(8,128)(2,1)S(1)} collective-permute-done((bf16[256,512]{1,0:T(8,128)(2,1)S(1)}, bf16[256,512]{1,0:T(8,128)(2,1)S(1)}, u32[]{:S(2)}, u32[]{:S(2)}) %collective-permute-start.1) | collective-permute-done | bytes 262176 | tf_op jit(solution)/shard_map/ppermute | solution.py:321
  14.1 0.1 relay.3
  14.2 1.3 %collective-permute-start.3 = (bf16[256,512]{1,0:T(8,128)(2,1)S(1)}, bf16[256,512]{1,0:T(8,128)(2,1)S(1)}, u32[]{:S(2)}, u32[]{:S(2)}) collective-permute-start(bf16[256,512]{1,0:T(8,128)(2,1)S(1)} %get-tuple-element.48), channel_id=1, source_target_pairs={{0,4},{2,6},{4,0},{6,2},{8,12},{10,14},{12,8},{14,10},{16,20},{18,... | collective-permute-start | bytes 786440 | tf_op jit(solution)/shard_map/ppermute | solution.py:335
  15.5 1.2 %collective-permute-start.4 = (bf16[256,512]{1,0:T(8,128)(2,1)S(1)}, bf16[256,512]{1,0:T(8,128)(2,1)S(1)}, u32[]{:S(2)}, u32[]{:S(2)}) collective-permute-start(bf16[256,512]{1,0:T(8,128)(2,1)S(1)} %get-tuple-element.49), channel_id=1, source_target_pairs={{0,6},{2,4},{4,2},{6,0},{8,14},{10,12},{12,10},{14,8},{16,22},{18,... | collective-permute-start | bytes 786440 | tf_op jit(solution)/shard_map/ppermute | solution.py:335
  16.6 0.3 collective-permute-start.2
  16.9 0.6 %slice-done.7 = s8[4194304]{0:T(1024)(128)(4,1)S(1)} async-done(((s8[16777216]{0:T(1024)(128)(4,1)}), s8[4194304]{0:T(1024)(128)(4,1)S(1)}, s32[]{:S(2)}) %slice-start.7) | async-done | bytes 4194328
  17.5 4.8 %queries.1 = (bf16[256,2048]{1,0:T(8,128)(2,1)S(1)}, f32[8,128]{1,0:T(8,128)S(1)}) custom-call(bf16[256,4096]{1,0:T(8,128)(2,1)S(1)} %get-tuple-element.40.rows, bf16[4096,2048]{1,0:T(8,128)(2,1)S(1)} %bitcast.3, f32[256,128]{1,0:T(8,128)S(1)} %get-tuple-element.41.cosine, f32[256,128]{1,0:T(8,128)S(1)} %get-tuple-element.42.sine, ...), custom_call_target="tpu_custom_call" | custom-call | flops 4294967296 | bytes 16777216 | tf_op jit(solution)/shard_map/queries/pallas_call | solution.py:339
  22.4 0.1 relay.5
  22.4 2.2 %collective-permute-start.8 = (bf16[256,512]{1,0:T(8,128)(2,1)S(1)}, bf16[256,512]{1,0:T(8,128)(2,1)S(1)}, u32[]{:S(2)}, u32[]{:S(2)}) collective-permute-start(bf16[256,512]{1,0:T(8,128)(2,1)S(1)} %get-tuple-element.57), channel_id=1, source_target_pairs={{0,6},{2,4},{4,2},{6,0},{8,14},{10,12},{12,10},{14,8},{16,22},{18,... | collective-permute-start | bytes 786440 | tf_op jit(solution)/shard_map/ppermute | solution.py:335
  24.7 0.3 collective-permute-start.9
  24.9 1.0 %collective-permute-done.3.refs_3_.refs_1_ = bf16[256,512]{1,0:T(8,128)(2,1)S(1)} collective-permute-done((bf16[256,512]{1,0:T(8,128)(2,1)S(1)}, bf16[256,512]{1,0:T(8,128)(2,1)S(1)}, u32[]{:S(2)}, u32[]{:S(2)}) %collective-permute-start.3) | collective-permute-done | bytes 262176 | tf_op jit(solution)/shard_map/ppermute | solution.py:335
  25.9 2.2 %collective-permute-start.10 = (bf16[256,256]{1,0:T(8,128)(2,1)S(1)}, bf16[256,256]{1,0:T(8,128)(2,1)S(1)}, u32[]{:S(2)}, u32[]{:S(2)}) collective-permute-start(bf16[256,256]{1,0:T(8,128)(2,1)S(1)} %get-tuple-element.62), channel_id=1, source_target_pairs={{0,4},{2,6},{4,0},{6,2},{8,12},{10,14},{12,8},{14,10},{16,20},{18,... | collective-permute-start | bytes 393224 | tf_op jit(solution)/shard_map/ppermute | solution.py:335
  28.2 1.3 %collective-permute-start.6 = (bf16[256,256]{1,0:T(8,128)(2,1)S(1)}, bf16[256,256]{1,0:T(8,128)(2,1)S(1)}, u32[]{:S(2)}, u32[]{:S(2)}) collective-permute-start(bf16[256,256]{1,0:T(8,128)(2,1)S(1)} %get-tuple-element.54), channel_id=1, source_target_pairs={{0,2},{2,0},{4,6},{6,4},{8,10},{10,8},{12,14},{14,12},{16,18},{18,... | collective-permute-start | bytes 393224 | tf_op jit(solution)/shard_map/ppermute | solution.py:335
  29.4 0.4 collective-permute-start.7
  29.9 6.5 %scores.1 = (bf16[8,256,768]{2,1,0:T(8,128)(2,1)S(1)}, f32[8,256,128]{2,1,0:T(8,128)S(1)}, f32[8,256,128]{2,1,0:T(8,128)S(1)}, bf16[8,256,768]{2,1,0:T(8,128)(2,...) custom-call(s32[256,128]{1,0:T(8,128)S(1)} %get-tuple-element.38.starts, ...), custom_call_target="tpu_custom_call" | custom-call | flops 1879048192 | bytes 8388608 | tf_op jit(solution)/shard_map/scores/pallas_call | solution.py:352
  36.4 3.9 %mix_first.1 = (f32[256,4096]{1,0:T(8,128)S(1)}, bf16[256,1024]{1,0:T(8,128)(2,1)}) custom-call(bf16[8,256,768]{2,1,0:T(8,128)(2,1)S(1)} %get-tuple-element.58.weights, f32[8,256,128]{2,1,0:T(8,128)S(1)} %get-tuple-element.59.total, f32[8,256,128]{2,1,0:T(8,128)S(1)} %get-tuple-element.60.acc, bf16[256,256]{1,0:T(8,128)(2,1)S(1)} %collective-permute-done.9.refs_0_, ...), custom_call_target="tpu_custom_call" | custom-call | flops 2550136832 | bytes 4194304 | tf_op jit(solution)/shard_map/mix_first/pallas_call | solution.py:362
  40.4 2.2 %mix_second.1 = (f32[128,2048]{1,0:T(8,128)S(1)}, bf16[128,2048]{1,0:T(8,128)(2,1)S(1)}, bf16[256,1024]{1,0:T(8,128)(2,1)S(1)}) custom-call(bf16[8,256,768]{2,1,0:T(8,128)(2,1)S(1)} %get-tuple-element.51.weights, f32[8,256,128]{2,1,0:T(8,128)S(1)} %get-tuple-element.52.total, f32[8,256,128]{2,1,0:T(8,128)S(1)} %get-tuple-element.53.acc, ...), custom_call_target="tpu_custom_call" | custom-call | flops 1476395008 | bytes 4194304 | tf_op jit(solution)/shard_map/mix_second/pallas_call | solution.py:371
  42.6 5.2 %collective-permute-start.11 = (bf16[128,2048]{1,0:T(8,128)(2,1)S(1)}, bf16[128,2048]{1,0:T(8,128)(2,1)S(1)}, u32[]{:S(2)}, u32[]{:S(2)}) collective-permute-start(bf16[128,2048]{1,0:T(8,128)(2,1)S(1)} %get-tuple-element.66), channel_id=1, source_target_pairs={{0,1},{1,0},{2,3},{3,2},{4,5},{5,4},{6,7},{7,6},{8,9},{9,8},{10,11... | collective-permute-start | bytes 1572872 | tf_op jit(solution)/shard_map/ppermute | solution.py:375
  47.8 0.7 %mix_more.1 = (f32[128,1024]{1,0:T(8,128)S(1)}, bf16[128,1024]{1,0:T(8,128)(2,1)S(1)}) custom-call(bf16[256,1024]{1,0:T(8,128)(2,1)S(1)} %get-tuple-element.64.attended, bf16[2048,4096]{1,0:T(8,128)(2,1)S(1)} %bitcast.1, f32[256,4096]{1,0:T(8,128)S(1)} %get-tuple-element.63.refs_4_.summed), custom_call_target="tpu_custom_call" | custom-call | flops 536870912 | bytes 4194304 | tf_op jit(solution)/shard_map/mix_more/pallas_call | solution.py:376
  48.6 0.1 collective-permute-start.12
  48.6 0.7 %collective-permute-done.11.got_low.got = bf16[128,2048]{1,0:T(8,128)(2,1)S(1)} collective-permute-done((bf16[128,2048]{1,0:T(8,128)(2,1)S(1)}, bf16[128,2048]{1,0:T(8,128)(2,1)S(1)}, u32[]{:S(2)}, u32[]{:S(2)}) %collective-permute-start.11) | collective-permute-done | bytes 524320 | tf_op jit(solution)/shard_map/ppermute | solution.py:375
  49.3 0.7 %mix_last.1 = (f32[128,1024]{1,0:T(8,128)S(1)}, bf16[128,1024]{1,0:T(8,128)(2,1)S(1)}) custom-call(bf16[256,1024]{1,0:T(8,128)(2,1)S(1)} %get-tuple-element.64.attended, bf16[2048,4096]{1,0:T(8,128)(2,1)S(1)} %bitcast.1, f32[256,4096]{1,0:T(8,128)S(1)} %get-tuple-element.63.refs_4_.summed, bf16[128,2048]{1,0:T(8,128)(2,1)S(1)} %collective-permute-done.11.got_low.got), custom_call_target="tpu_custom_call" | custom-call | flops 536870912 | bytes 4194304 | tf_op jit(solution)/shard_map/mix_last/pallas_call | solution.py:380
  50.1 0.4 collective-permute-start.13
  50.5 0.9 %add_low.1.mixed_in = bf16[128,4096]{1,0:T(8,128)(2,1)} custom-call(f32[128,2048]{1,0:T(8,128)S(1)} %get-tuple-element.70.own, bf16[128,2048]{1,0:T(8,128)(2,1)S(1)} %collective-permute-done.11.got_low.got), custom_call_target="tpu_custom_call" | custom-call | flops 262144 | bytes 2097152 | tf_op jit(solution)/shard_map/add_low/pallas_call | solution.py:384
  51.4 0.3 collective-permute-done.13.got_two
  51.7 0.8 %add.1 = bf16[128,4096]{1,0:T(8,128)(2,1)} custom-call(f32[128,1024]{1,0:T(8,128)S(1)} %get-tuple-element.65.own_one, f32[128,1024]{1,0:T(8,128)S(1)} %get-tuple-element.67.own_two, bf16[128,1024]{1,0:T(8,128)(2,1)S(1)} %collective-permute-done.12.got_one, bf16[128,1024]{1,0:T(8,128)(2,1)S(1)} %collective-permute-done.13.got_two, ...), custom_call_target="tpu_custom_call", output_to_operand_aliasing={{}: (4, {})} | custom-call | flops 524288 | bytes 4194304 | tf_op jit(solution)/shard_map/add/pallas_call | solution.py:388
  (28 shorter events, 0.1 us)
Async XLA Ops:
  0.0 3.5 %collective-permute-start = (bf16[128,4096]{1,0:T(8,128)(2,1)}, bf16[128,4096]{1,0:T(8,128)(2,1)S(1)}, u32[]{:S(2)}, u32[]{:S(2)}) collective-permute-start(bf16[128,4096]{1,0:T(8,128)(2,1)} %own_hbm.1), channel_id=1, source_target_pairs={{0,1},{1,0},{2,3},{3,2},{4,5},{5,4},{6,7},{7,6},{8,9},{9,8},{10,11... | collective-permute-start | bytes 3145736 | tf_op jit(solution)/shard_map/ppermute | solution.py:300
  4.3 9.8 %collective-permute-start.1 = (bf16[256,512]{1,0:T(8,128)(2,1)S(1)}, bf16[256,512]{1,0:T(8,128)(2,1)S(1)}, u32[]{:S(2)}, u32[]{:S(2)}) collective-permute-start(bf16[256,512]{1,0:T(8,128)(2,1)S(1)} %keys.1.own.refs_0_), channel_id=1, source_target_pairs={{0,8},{2,10},{4,12},{6,14},{8,16},{10,18},{12,20},{14,22},{16,24},... | collective-permute-start | bytes 786440 | tf_op jit(solution)/shard_map/ppermute | solution.py:321
  5.6 11.3 %slice-start.4 = ((s8[16777216]{0:T(1024)(128)(4,1)}), s8[4194304]{0:T(1024)(128)(4,1)S(1)}, s32[]{:S(2)}) async-start(s8[16777216]{0:T(1024)(128)(4,1)} %bitcast.2), calls=%async_computation.4 | async-start | bytes 8388608
  5.6 11.3 %slice-start.5 = ((s8[16777216]{0:T(1024)(128)(4,1)}), s8[4194304]{0:T(1024)(128)(4,1)S(1)}, s32[]{:S(2)}) async-start(s8[16777216]{0:T(1024)(128)(4,1)} %bitcast.2), calls=%async_computation.5 | async-start | bytes 8388608
  8.5 13.8 %collective-permute-start.5 = (bf16[256,512]{1,0:T(8,128)(2,1)S(1)}, bf16[256,512]{1,0:T(8,128)(2,1)S(1)}, u32[]{:S(2)}, u32[]{:S(2)}) collective-permute-start(bf16[256,512]{1,0:T(8,128)(2,1)S(1)} %get-tuple-element.50.refs_5_.own), channel_id=1, source_target_pairs={{0,8},{2,10},{4,12},{6,14},{8,16},{10,18},{12,20},{14,22},{16,24},... | collective-permute-start | bytes 786440 | tf_op jit(solution)/shard_map/ppermute | solution.py:328
  14.1 2.8 %slice-start.6 = ((s8[16777216]{0:T(1024)(128)(4,1)}), s8[4194304]{0:T(1024)(128)(4,1)S(1)}, s32[]{:S(2)}) async-start(s8[16777216]{0:T(1024)(128)(4,1)} %bitcast.2), calls=%async_computation.6 | async-start | bytes 8388608
  14.1 3.5 %slice-start.7 = ((s8[16777216]{0:T(1024)(128)(4,1)}), s8[4194304]{0:T(1024)(128)(4,1)S(1)}, s32[]{:S(2)}) async-start(s8[16777216]{0:T(1024)(128)(4,1)} %bitcast.2), calls=%async_computation.7 | async-start | bytes 8388608
  14.2 11.8 %collective-permute-start.3 = (bf16[256,512]{1,0:T(8,128)(2,1)S(1)}, bf16[256,512]{1,0:T(8,128)(2,1)S(1)}, u32[]{:S(2)}, u32[]{:S(2)}) collective-permute-start(bf16[256,512]{1,0:T(8,128)(2,1)S(1)} %get-tuple-element.48), channel_id=1, source_target_pairs={{0,4},{2,6},{4,0},{6,2},{8,12},{10,14},{12,8},{14,10},{16,20},{18,... | collective-permute-start | bytes 786440 | tf_op jit(solution)/shard_map/ppermute | solution.py:335
  15.5 12.7 %collective-permute-start.4 = (bf16[256,512]{1,0:T(8,128)(2,1)S(1)}, bf16[256,512]{1,0:T(8,128)(2,1)S(1)}, u32[]{:S(2)}, u32[]{:S(2)}) collective-permute-start(bf16[256,512]{1,0:T(8,128)(2,1)S(1)} %get-tuple-element.49), channel_id=1, source_target_pairs={{0,6},{2,4},{4,2},{6,0},{8,14},{10,12},{12,10},{14,8},{16,22},{18,... | collective-permute-start | bytes 786440 | tf_op jit(solution)/shard_map/ppermute | solution.py:335
  16.6 11.5 %collective-permute-start.2 = (bf16[256,512]{1,0:T(8,128)(2,1)S(1)}, bf16[256,512]{1,0:T(8,128)(2,1)S(1)}, u32[]{:S(2)}, u32[]{:S(2)}) collective-permute-start(bf16[256,512]{1,0:T(8,128)(2,1)S(1)} %get-tuple-element.46.after), channel_id=1, source_target_pairs={{0,2},{2,0},{4,6},{6,4},{8,10},{10,8},{12,14},{14,12},{16,18},{18,... | collective-permute-start | bytes 786440 | tf_op jit(solution)/shard_map/ppermute | solution.py:335
  22.3 14.1 %slice-start = ((s8[16777216]{0:T(1024)(128)(4,1)}), s8[4194304]{0:T(1024)(128)(4,1)S(1)}, s32[]{:S(2)}) async-start(s8[16777216]{0:T(1024)(128)(4,1)} %bitcast), calls=%async_computation | async-start | bytes 8388608
  22.3 14.1 %slice-start.1 = ((s8[16777216]{0:T(1024)(128)(4,1)}), s8[4194304]{0:T(1024)(128)(4,1)S(1)}, s32[]{:S(2)}) async-start(s8[16777216]{0:T(1024)(128)(4,1)} %bitcast), calls=%async_computation.1 | async-start | bytes 8388608
  22.3 14.1 %slice-start.2 = ((s8[16777216]{0:T(1024)(128)(4,1)}), s8[4194304]{0:T(1024)(128)(4,1)S(1)}, s32[]{:S(2)}) async-start(s8[16777216]{0:T(1024)(128)(4,1)} %bitcast), calls=%async_computation.2 | async-start | bytes 8388608
  22.4 14.1 %slice-start.3 = ((s8[16777216]{0:T(1024)(128)(4,1)}), s8[4194304]{0:T(1024)(128)(4,1)S(1)}, s32[]{:S(2)}) async-start(s8[16777216]{0:T(1024)(128)(4,1)} %bitcast), calls=%async_computation.3 | async-start | bytes 8388608
  22.4 14.0 %collective-permute-start.8 = (bf16[256,512]{1,0:T(8,128)(2,1)S(1)}, bf16[256,512]{1,0:T(8,128)(2,1)S(1)}, u32[]{:S(2)}, u32[]{:S(2)}) collective-permute-start(bf16[256,512]{1,0:T(8,128)(2,1)S(1)} %get-tuple-element.57), channel_id=1, source_target_pairs={{0,6},{2,4},{4,2},{6,0},{8,14},{10,12},{12,10},{14,8},{16,22},{18,... | collective-permute-start | bytes 786440 | tf_op jit(solution)/shard_map/ppermute | solution.py:335
  24.7 11.7 %collective-permute-start.9 = (bf16[256,256]{1,0:T(8,128)(2,1)S(1)}, bf16[256,256]{1,0:T(8,128)(2,1)S(1)}, u32[]{:S(2)}, u32[]{:S(2)}) collective-permute-start(bf16[256,256]{1,0:T(8,128)(2,1)S(1)} %get-tuple-element.61), channel_id=1, source_target_pairs={{0,2},{2,0},{4,6},{6,4},{8,10},{10,8},{12,14},{14,12},{16,18},{18,... | collective-permute-start | bytes 393224 | tf_op jit(solution)/shard_map/ppermute | solution.py:335
  25.9 10.5 %collective-permute-start.10 = (bf16[256,256]{1,0:T(8,128)(2,1)S(1)}, bf16[256,256]{1,0:T(8,128)(2,1)S(1)}, u32[]{:S(2)}, u32[]{:S(2)}) collective-permute-start(bf16[256,256]{1,0:T(8,128)(2,1)S(1)} %get-tuple-element.62), channel_id=1, source_target_pairs={{0,4},{2,6},{4,0},{6,2},{8,12},{10,14},{12,8},{14,10},{16,20},{18,... | collective-permute-start | bytes 393224 | tf_op jit(solution)/shard_map/ppermute | solution.py:335
  28.2 12.2 %collective-permute-start.6 = (bf16[256,256]{1,0:T(8,128)(2,1)S(1)}, bf16[256,256]{1,0:T(8,128)(2,1)S(1)}, u32[]{:S(2)}, u32[]{:S(2)}) collective-permute-start(bf16[256,256]{1,0:T(8,128)(2,1)S(1)} %get-tuple-element.54), channel_id=1, source_target_pairs={{0,2},{2,0},{4,6},{6,4},{8,10},{10,8},{12,14},{14,12},{16,18},{18,... | collective-permute-start | bytes 393224 | tf_op jit(solution)/shard_map/ppermute | solution.py:335
  29.4 11.0 %collective-permute-start.7 = (bf16[256,256]{1,0:T(8,128)(2,1)S(1)}, bf16[256,256]{1,0:T(8,128)(2,1)S(1)}, u32[]{:S(2)}, u32[]{:S(2)}) collective-permute-start(bf16[256,256]{1,0:T(8,128)(2,1)S(1)} %get-tuple-element.55), channel_id=1, source_target_pairs={{0,4},{2,6},{4,0},{6,2},{8,12},{10,14},{12,8},{14,10},{16,20},{18,... | collective-permute-start | bytes 393224 | tf_op jit(solution)/shard_map/ppermute | solution.py:335
  42.6 6.7 %collective-permute-start.11 = (bf16[128,2048]{1,0:T(8,128)(2,1)S(1)}, bf16[128,2048]{1,0:T(8,128)(2,1)S(1)}, u32[]{:S(2)}, u32[]{:S(2)}) collective-permute-start(bf16[128,2048]{1,0:T(8,128)(2,1)S(1)} %get-tuple-element.66), channel_id=1, source_target_pairs={{0,1},{1,0},{2,3},{3,2},{4,5},{5,4},{6,7},{7,6},{8,9},{9,8},{10,11... | collective-permute-start | bytes 1572872 | tf_op jit(solution)/shard_map/ppermute | solution.py:375
  48.6 2.9 %collective-permute-start.12 = (bf16[128,1024]{1,0:T(8,128)(2,1)S(1)}, bf16[128,1024]{1,0:T(8,128)(2,1)S(1)}, u32[]{:S(2)}, u32[]{:S(2)}) collective-permute-start(bf16[128,1024]{1,0:T(8,128)(2,1)S(1)} %get-tuple-element.68), channel_id=1, source_target_pairs={{0,1},{1,0},{2,3},{3,2},{4,5},{5,4},{6,7},{7,6},{8,9},{9,8},{10,11... | collective-permute-start | bytes 786440 | tf_op jit(solution)/shard_map/ppermute | solution.py:379
  50.1 1.6 %collective-permute-start.13 = (bf16[128,1024]{1,0:T(8,128)(2,1)S(1)}, bf16[128,1024]{1,0:T(8,128)(2,1)S(1)}, u32[]{:S(2)}, u32[]{:S(2)}) collective-permute-start(bf16[128,1024]{1,0:T(8,128)(2,1)S(1)} %get-tuple-element.69), channel_id=1, source_target_pairs={{0,1},{1,0},{2,3},{3,2},{4,5},{5,4},{6,7},{7,6},{8,9},{9,8},{10,11... | collective-permute-start | bytes 786440 | tf_op jit(solution)/shard_map/ppermute | solution.py:383

commit v4 on v3

--- a/solution.py
+++ b/solution.py
@@ -59,11 +59,20 @@
     freq = jnp.zeros((1, HEAD_SIZE), jnp.float32)
     for number, value in enumerate(inverse_frequency()):
         freq = jnp.where(pair_of_lane == number, jnp.float32(value), freq)
-    positions = lax.axis_index("seq") * tokens + lax.broadcasted_iota(jnp.int32, (tokens, HEAD_SIZE), 0)
-    angles = positions.astype(jnp.float32) * freq
-    cosine[...] = jnp.cos(angles)
+    first = lax.axis_index("seq") * tokens
+    half = tokens // 2
+    low_lane = lane < HEAD_SIZE // 2
+    packed = first + lax.broadcasted_iota(jnp.int32, (half, HEAD_SIZE), 0) + jnp.where(low_lane, 0, half)
+    angles = packed.astype(jnp.float32) * freq
+    turned = jnp.cos(angles)
+    other = pltpu.roll(turned, HEAD_SIZE // 2, 1)
+    cosine[:half, :] = jnp.where(low_lane, turned, other)
+    cosine[half:, :] = jnp.where(low_lane, other, turned)
     turned = jnp.sin(angles)
-    sine[...] = jnp.where(lane < HEAD_SIZE // 2, -turned, turned)
+    other = pltpu.roll(turned, HEAD_SIZE // 2, 1)
+    sine[:half, :] = jnp.where(low_lane, -turned, other)
+    sine[half:, :] = jnp.where(low_lane, -other, turned)
+    positions = first + lax.broadcasted_iota(jnp.int32, (tokens, HEAD_SIZE), 0)
     length_copy.wait()
     start = jnp.zeros((tokens, HEAD_SIZE), jnp.int32)
     end = jnp.int32(0)
@@ -137,56 +146,80 @@
         out[...] = jnp.where(upper, earlier[:, at], own[:, at])
 
 
-def score_kernel(distances, near, starts, query, *refs):
-    count = len(distances)
-    keys, refs = refs[:count], refs[count:]
-    values, refs = refs[:near], refs[near:]
-    weights_a, total_a, acc_a, weights_b, total_b, acc_b, bias = refs
-    tokens = query.shape[0]
+def column(number):
+    return slice(number * HEAD_SIZE, (number + 1) * HEAD_SIZE)
+
+
+def fill_bias(bias, distances, starts):
+    tokens = bias.shape[0]
     index = lax.axis_index("seq")
     base = index * tokens
     query_pos = base + lax.broadcasted_iota(jnp.int32, (tokens, tokens), 0)
     start = jnp.concatenate([starts[...]] * (tokens // starts.shape[1]), axis=1)
-    blocks = [slice(number * tokens, (number + 1) * tokens) for number in range(count)]
-    for block, (even, odd) in zip(blocks, distances):
+    for number, (even, odd) in enumerate(distances):
         first = base - tokens * jnp.where(index % 2 > 0, odd, even)
         key_pos = first + lax.broadcasted_iota(jnp.int32, (tokens, tokens), 1)
         allowed = (key_pos >= start) & (key_pos <= query_pos)
-        bias[:, block] = jnp.where(allowed, 0.0, MASKED)
+        bias[:, number * tokens : (number + 1) * tokens] = jnp.where(allowed, 0.0, MASKED)
+
+
+def scores_of(query, keys, bias, head, group):
+    tokens = bias.shape[0]
+    return [
+        lax.dot_general(
+            query[:, column(head)], key[:, column(head // group)], (((1,), (1,)), ((), ())),
+            preferred_element_type=jnp.float32,
+        )
+        * SCORE_SCALE
+        + bias[:, number * tokens : (number + 1) * tokens]
+        for number, key in enumerate(keys)
+    ]
+
+
+def near_kernel(distances, starts, query, *refs):
+    count = len(distances)
+    keys, values, (tops, totals, accs, bias) = refs[:count], refs[count : 2 * count], refs[2 * count :]
+    fill_bias(bias, distances, starts)
+    tokens = query.shape[0]
     heads = query.shape[1] // HEAD_SIZE
-    kv_heads = keys[0].shape[1] // HEAD_SIZE
-    group = heads // kv_heads
+    group = heads * HEAD_SIZE // keys[0].shape[1]
     ones = jnp.ones((tokens, HEAD_SIZE), query.dtype)
-
-    def column(number):
-        return slice(number * HEAD_SIZE, (number + 1) * HEAD_SIZE)
-
-    def scores_of(head):
-        return [
-            lax.dot_general(
-                query[:, column(head)], key[:, column(head // group)], (((1,), (1,)), ((), ())),
-                preferred_element_type=jnp.float32,
-            )
-            * SCORE_SCALE
-            + bias[:, block]
-            for key, block in zip(keys, blocks)
-        ]
-
-    scores = scores_of(0)
+    scores = scores_of(query, keys, bias, 0, group)
     for head in range(heads):
-        ahead = scores_of(head + 1) if head + 1 < heads else None
+        ahead = scores_of(query, keys, bias, head + 1, group) if head + 1 < heads else None
         top = jnp.max(functools.reduce(jnp.maximum, scores), axis=1, keepdims=True)
-        weights = [jnp.exp2(score - top).astype(query.dtype) for score in scores]
-        late = head >= heads // 2
-        at = head - heads // 2 if late else head
         product = None
-        for number, block in enumerate(values):
-            term = dot(weights[number], jnp.concatenate([block[:, column(head // group)], ones], axis=1))
+        for score, block in zip(scores, values):
+            weights = jnp.exp2(score - top).astype(query.dtype)
+            term = dot(weights, jnp.concatenate([block[:, column(head // group)], ones], axis=1))
             product = term if product is None else product + term
-        weights_out, total, acc = (weights_b, total_b, acc_b) if late else (weights_a, total_a, acc_a)
-        acc[at], total[at] = product[:, :HEAD_SIZE], product[:, HEAD_SIZE:]
-        for number in range(near, count):
-            weights_out[at, :, blocks[number - near]] = weights[number]
+        tops[head] = jnp.broadcast_to(top, (tokens, HEAD_SIZE))
+        accs[head], totals[head] = product[:, :HEAD_SIZE], product[:, HEAD_SIZE:]
+        scores = ahead
+
+
+def far_kernel(distances, starts, query, *refs):
+    count = len(distances)
+    keys, (tops, totals, accs) = refs[:count], refs[count : count + 3]
+    outs = (refs[count + 3 : count + 6], refs[count + 6 : count + 9])
+    bias = refs[-1]
+    fill_bias(bias, distances, starts)
+    tokens = query.shape[0]
+    heads = query.shape[1] // HEAD_SIZE
+    group = heads * HEAD_SIZE // keys[0].shape[1]
+    scores = scores_of(query, keys, bias, 0, group)
+    for head in range(heads):
+        ahead = scores_of(query, keys, bias, head + 1, group) if head + 1 < heads else None
+        top = jnp.max(functools.reduce(jnp.maximum, scores), axis=1, keepdims=True)
+        before = tops[head]
+        top = jnp.maximum(jnp.broadcast_to(top, (tokens, HEAD_SIZE)), before)
+        factor = jnp.exp2(before - top)
+        wide_top = jnp.concatenate([top] * (tokens // HEAD_SIZE), axis=1)
+        weights_out, total, acc = outs[2 * head // heads]
+        at = head % (heads // 2)
+        acc[at], total[at] = accs[head] * factor, totals[head] * factor
+        for number, score in enumerate(scores):
+            weights_out[at, :, number * tokens : (number + 1) * tokens] = jnp.exp2(score - wide_top).astype(query.dtype)
         scores = ahead
 
 
@@ -219,52 +252,57 @@
         summed[:, at] = dot(attended[...], weight[:depth, at])
 
 
-def split_rows(result, own, send, at):
-    half = own.shape[0]
-    on_high = lax.axis_index("head") > 0
-    own[:, at] = jnp.where(on_high, result[half:], result[:half])
-    send[:, at] = jnp.where(on_high, result[:half], result[half:]).astype(send.dtype)
-
-
-def mix_columns(attended, weight, summed, low, own, send):
+def rows_product(rows, low, attended, weight, summed, wide):
     depth = attended.shape[1]
+    at = slice(low, low + wide)
+    return summed[rows, at] + dot(attended[rows, :], weight[depth:, at])
+
+
+def send_columns(low, attended, weight, summed, send):
+    theirs = halves(send.shape[0])[1]
+    for number in range(send.shape[1] // WIDE):
+        result = rows_product(theirs, low + number * WIDE, attended, weight, summed, WIDE)
+        send[:, number * WIDE : (number + 1) * WIDE] = result.astype(send.dtype)
+
+
+def mix_second_kernel(far, weights, total, acc, *refs):
+    blocks, (weight, summed, send, attended) = refs[:far], refs[far:]
+    attend_far(True, weights, total, acc, blocks, attended)
+    send_columns(0, attended, weight, summed, send)
+
+
+def own_high_kernel(low, attended, weight, summed, own):
+    mine = halves(own.shape[0])[0]
     for number in range(own.shape[1] // WIDE):
-        here = slice(low + number * WIDE, low + (number + 1) * WIDE)
-        result = summed[:, here] + dot(attended[...], weight[depth:, here])
-        split_rows(result, own, send, slice(number * WIDE, (number + 1) * WIDE))
-
-
-def mix_second_kernel(far, weights, total, acc, *refs):
-    blocks, (weight, summed, own, send, attended) = refs[:far], refs[far:]
-    attend_far(True, weights, total, acc, blocks, attended)
-    mix_columns(attended, weight, summed, 0, own, send)
-
-
-def mix_more_kernel(low, attended, weight, summed, own, send):
-    mix_columns(attended, weight, summed, low, own, send)
-
-
-def mix_last_kernel(low, attended, weight, summed, got_low, own, send):
-    del got_low
-    mix_columns(attended, weight, summed, low, own, send)
-
-
-def add_low_kernel(own, got, mixed_hbm, mixed, sem):
-    mixed[...] = (own[...] + got[...].astype(jnp.float32)).astype(mixed.dtype)
-    copy = pltpu.make_async_copy(mixed, mixed_hbm.at[:, pl.ds(0, mixed.shape[1])], sem)
-    copy.start()
-    copy.wait()
-
-
-def add_kernel(own_one, own_two, got_one, got_two, mixed_in, mixed_hbm, mixed, sems):
+        result = rows_product(mine, low + number * WIDE, attended, weight, summed, WIDE)
+        own[:, number * WIDE : (number + 1) * WIDE] = result
+
+
+def own_low_kernel(attended, weight, summed, got, after, mixed_hbm, mixed, sems):
+    del after
+    mine = halves(got.shape[0])[0]
+    copies = []
+    for number in range(got.shape[1] // WIDE):
+        at = slice(number * WIDE, (number + 1) * WIDE)
+        result = rows_product(mine, number * WIDE, attended, weight, summed, WIDE)
+        mixed[:, at] = (result + got[:, at].astype(jnp.float32)).astype(mixed.dtype)
+        there = mixed_hbm.at[:, pl.ds(number * WIDE, WIDE)]
+        copies.append(pltpu.make_async_copy(mixed.at[:, pl.ds(number * WIDE, WIDE)], there, sems.at[number]))
+        copies[-1].start()
+    for copy in copies:
+        copy.wait()
+
+
+def add_kernel(own, got, mixed_in, mixed_hbm, mixed, sems):
     del mixed_in
-    width = own_one.shape[1]
-    low = mixed_hbm.shape[1] - 2 * width
+    width = own.shape[1]
+    low = mixed_hbm.shape[1] - width
     copies = []
-    for number, (own, got) in enumerate(((own_one, got_one), (own_two, got_two))):
-        at = pl.ds(number * width, width)
-        mixed[:, at] = (own[...] + got[...].astype(jnp.float32)).astype(mixed.dtype)
-        copies.append(pltpu.make_async_copy(mixed.at[:, at], mixed_hbm.at[:, pl.ds(low + number * width, width)], sems.at[number]))
+    for number in range(width // WIDE):
+        at = slice(number * WIDE, (number + 1) * WIDE)
+        mixed[:, at] = (own[:, at] + got[:, at].astype(jnp.float32)).astype(mixed.dtype)
+        there = mixed_hbm.at[:, pl.ds(low + number * WIDE, WIDE)]
+        copies.append(pltpu.make_async_copy(mixed.at[:, pl.ds(number * WIDE, WIDE)], there, sems.at[number]))
         copies[-1].start()
     for copy in copies:
         copy.wait()
@@ -317,8 +355,8 @@
     )(other, w_key, key_own, cosine, sine)
 
     every = range(shards)
-    step_z = [(i, i + LAYER) for i in every if i + LAYER < shards]
-    keys_z = lax.ppermute(keys, "seq", step_z)
+    step_z = [(i, (i + LAYER) % shards) for i in every]
+    keys_z = lax.ppermute(keys, "seq", [(a, b) for a, b in step_z if a < b])
 
     values, rows, done = call(
         functools.partial(values_kernel, 4), "values", [kv_shape, shape((tokens, model), bf16), flag], [VMEM, VMEM, ANY],
@@ -340,20 +378,23 @@
         query_kernel, "queries", [shape((tokens, width_q), bf16), flag], [VMEM] * 5,
         2 * tokens * model * width_q, 2 * model * width_q, 8,
     )(rows, w_query, cosine, sine, sent_first)
+    far = len(keys_far)
+    heads_half = heads // 2
+    state = [shape((heads_half, tokens, far * tokens), bf16)] + [shape((heads_half, tokens, HEAD_SIZE), f32)] * 2
+    near_state = call(
+        functools.partial(near_kernel, ((0, 0), (LAYER, LAYER))), "scores_near", [shape((heads, tokens, HEAD_SIZE), f32)] * 3,
+        [VMEM] * 6, 8 * heads * tokens * tokens * HEAD_SIZE, 8 << 20, 12, [pltpu.VMEM((tokens, 2 * tokens), f32)],
+    )(starts, query, keys, keys_z, values, values_z)
     (values_d, values_x, values_y), _ = exchange(
-        values, values_z, ((3, 0), (1, 0), (2, 0)), [width_k, part, part], [done], 9 << 30
+        values, values_z, ((3, 0), (1, 0), (2, 0)), [width_k, part, part], [near_state[0]], 9 << 30
     )
     (values_x_more, values_y_more), _ = exchange(values, values_z, ((1, part), (2, part)), [part] * 2, keys_far, 0)
     far_a, far_b = (values_x, values_y, values_d), (values_x_more, values_y_more, values_d)
 
-    far = len(keys_far)
-    heads_half = heads // 2
-    state = [shape((heads_half, tokens, far * tokens), bf16)] + [shape((heads_half, tokens, HEAD_SIZE), f32)] * 2
     *state_a, weights_b, total_b, acc_b = call(
-        functools.partial(score_kernel, ((0, 0), (LAYER, LAYER), (3, 1), (2, 2), (1, 3)), 2), "scores",
-        state * 2, [VMEM] * (2 + 2 + far + 2),
-        14 * heads * tokens * tokens * HEAD_SIZE, 8 << 20, 16, [pltpu.VMEM((tokens, (far + 2) * tokens), f32)],
-    )(starts, query, keys, keys_z, *keys_far, values, values_z)
+        functools.partial(far_kernel, ((3, 1), (2, 2), (1, 3))), "scores_far", state * 2, [VMEM] * (2 + far + 3),
+        6 * heads * tokens * tokens * HEAD_SIZE, 8 << 20, 12, [pltpu.VMEM((tokens, far * tokens), f32)],
+    )(starts, query, *keys_far, *near_state)
 
     columns = w_out.shape[1]
     attended_shape = shape((tokens, width_q // 2), bf16)
@@ -364,31 +405,30 @@
         [VMEM] * (4 + far), out_flops + far_flops, 4 << 20, 6,
     )(*state_a, *far_a, w_out)
 
-    def out_shapes(wide):
-        return [shape((half, wide), f32), shape((half, wide), bf16)]
-
-    cut, wide = columns // 2, columns // 4
-    own_low, send, attended = call(
-        functools.partial(mix_second_kernel, far), "mix_second", out_shapes(cut) + [attended_shape],
-        [VMEM] * (5 + far), out_flops // 2 + far_flops, 4 << 20, 6,
+    cut = columns // 2
+    send_shape = shape((half, cut), bf16)
+    quarter = out_flops // 4
+    send, attended = call(
+        functools.partial(mix_second_kernel, far), "mix_second", [send_shape, attended_shape],
+        [VMEM] * (5 + far), quarter + far_flops, 4 << 20, 6,
     )(weights_b, total_b, acc_b, *far_b, w_out, summed)
     got_low = lax.ppermute(send, "head", SWAP)
-    own_one, send = call(
-        functools.partial(mix_more_kernel, cut), "mix_more", out_shapes(wide), [VMEM] * 3, out_flops // 4, 4 << 20, 6,
+    (send,) = call(
+        functools.partial(send_columns, cut), "send_high", [send_shape], [VMEM] * 3, quarter, 4 << 20, 6,
     )(attended, w_out, summed)
-    got_one = lax.ppermute(send, "head", SWAP)
-    own_two, send = call(
-        functools.partial(mix_last_kernel, cut + wide), "mix_last", out_shapes(wide), [VMEM] * 4, out_flops // 4, 4 << 20, 6,
-    )(attended, w_out, summed, got_low)
-    got_two = lax.ppermute(send, "head", SWAP)
+    got_high = lax.ppermute(send, "head", SWAP)
+    (own,) = call(
+        functools.partial(own_high_kernel, cut), "own_high", [shape((half, columns - cut), f32)], [VMEM] * 3,
+        quarter, 4 << 20, 6,
+    )(attended, w_out, summed)
+    mixed_shape = pltpu.HBM((half, columns), bf16)
+    out_scratch = [pltpu.VMEM((half, cut), bf16), pltpu.SemaphoreType.DMA((cut // WIDE,))]
     (mixed,) = call(
-        add_low_kernel, "add_low", [pltpu.HBM((half, columns), bf16)], [VMEM] * 2, half * cut, 2 << 20, 4,
-        [pltpu.VMEM((half, cut), bf16), pltpu.SemaphoreType.DMA(())], [ANY],
-    )(own_low, got_low)
+        own_low_kernel, "own_low", [mixed_shape], [VMEM] * 5, quarter, 4 << 20, 6, out_scratch, [ANY],
+    )(attended, w_out, summed, got_low, own)
     (mixed,) = call(
-        add_kernel, "add", [pltpu.HBM((half, columns), bf16)], [VMEM] * 4 + [ANY], half * columns, 4 << 20, 4,
-        [pltpu.VMEM((half, 2 * wide), bf16), pltpu.SemaphoreType.DMA((2,))], [ANY], {4: 0},
-    )(own_one, own_two, got_one, got_two, mixed)
+        add_kernel, "add", [mixed_shape], [VMEM] * 2 + [ANY], half * cut, 4 << 20, 4, out_scratch, [ANY], {2: 0},
+    )(own, got_high, mixed)
     return mixed
 
 

time: 53.4 us -> 49.9 us (0.934)
  starting transfers between devices: 18.5 us -> 14.2 us
  waiting for transfers between devices: 5.81 us -> 6.67 us
    ppermute x1, starting transfers between devices: 5.19 us -> 2.09 us  [body(): got_low = lax.ppermute(send, 'head', SWAP)]
    ppermute x8, waiting for transfers between devices: 1 us -> 3.15 us  [exchange(): lax.ppermute(array, 'seq', [(i, i ^ way) for i in every])]
    ppermute x8, starting transfers between devices: 9.11 us -> 7.94 us  [exchange(): lax.ppermute(array, 'seq', [(i, i ^ way) for i in every])]
    ppermute x1, waiting for transfers between devices: 0.71 us -> 0.01 us  [body(): got_low = lax.ppermute(send, 'head', SWAP)]
    ppermute x3 -> x2, waiting for transfers between devices: 4.1 us -> 3.51 us  [the longest x1 3.51 us: body(): keys_z = lax.ppermute(keys, 'seq', [(a, b) for a, b in step_z if a < b])]
    ppermute x3 -> x2, starting transfers between devices: 1.81 us -> 1.38 us  [the longest x1 1.29 us: body(): keys_z = lax.ppermute(keys, 'seq', [(a, b) for a, b in step_z if a < b])]
    pallas_call x6 -> x7, Pallas kernels: 11.9 us -> 11.6 us  [the longest x1 3.55 us: body(): call(functools.partial(far_kernel, ((3, 1), (2, 2), (1, 3))), 'scores_far...]
  transfers between devices with their start and end apart: 14 -> 13, of which waited for: 4 -> 3; matrix products, arithmetic and copies ran while one was open for 0% -> 0% of each run, Pallas kernels for 44% -> 49%
where the time goes in v4:
time: 49.9 us; the launch traced here: 49.4 us
  Pallas kernels  27.5 us (55%)
  starting transfers between devices  14.2 us (28%)
  waiting for transfers between devices  6.67 us (13%)
  local copies, waits for them, and re-layouts  0.69 us (1%)
    ppermute x8, starting transfers between devices, exchange(): lax.ppermute(array, 'seq', [(i, i ^ way) for i in every])  7.94 us
    pallas_call x1, Pallas kernels, body(): call(query_kernel, 'queries', [shape((tokens, width_q), bf16), flag], [VM...  5.3 us
    pallas_call x1, Pallas kernels, body(): call(functools.partial(mix_first_kernel, far), 'mix_first', [shape((token...  3.96 us
    pallas_call x1, Pallas kernels, body(): call(functools.partial(far_kernel, ((3, 1), (2, 2), (1, 3))), 'scores_far...  3.55 us
    ppermute x1, waiting for transfers between devices, body(): keys_z = lax.ppermute(keys, 'seq', [(a, b) for a, b in step_z if a < b])  3.51 us
    ppermute x8, waiting for transfers between devices, exchange(): lax.ppermute(array, 'seq', [(i, i ^ way) for i in every])  3.15 us
    pallas_call x1, Pallas kernels, body(): call(functools.partial(values_kernel, 4), 'values', [kv_shape, shape((tok...  2.84 us
    pallas_call x1, Pallas kernels, body(): call(functools.partial(first_keys_kernel, chunks), 'keys_own', [shape((ha...  2.79 us
  transfers between devices with their start and end apart: 13, of which 3 were waited for; matrix products, arithmetic and copies ran while one was open for 0% of the time, Pallas kernels for 49%

profile of v4, /device:TPU:25, one launch (start us, length us, event | category | flops | bytes accessed | tf_op | source)
XLA Modules:
  0.0 49.4 jit_solution(5496148089495038577)
XLA Ops:
  0.0 0.7 %collective-permute-start = (bf16[128,4096]{1,0:T(8,128)(2,1)}, bf16[128,4096]{1,0:T(8,128)(2,1)S(1)}, u32[]{:S(2)}, u32[]{:S(2)}) collective-permute-start(bf16[128,4096]{1,0:T(8,128)(2,1)} %own_hbm.1), channel_id=1, source_target_pairs={{0,1},{1,0},{2,3},{3,2},{4,5},{5,4},{6,7},{7,6},{8,9},{9,8},{10,11... | collective-permute-start | bytes 3145736 | tf_op jit(solution)/shard_map/ppermute | solution.py:338
  0.7 2.8 %keys_own.1 = (f32[128,512]{1,0:T(8,128)S(1)}, bf16[128,4096]{1,0:T(8,128)(2,1)S(1)}, bf16[4096,512]{1,0:T(8,128)(2,1)S(1)}, f32[256,128]{1,0:T(8,128)S(1)}, f32...) custom-call(s32[8]{0:T(128)} %lengths_hbm.1, bf16[128,4096]{1,0:T(8,128)(2,1)} %own_hbm.1, bf16[4096,512]{1,0:T(8,128)(2,1)} %key_hbm.1), custom_call_target="tpu_custom_call" | custom-call | flops 536870912 | bytes 4194304 | tf_op jit(solution)/shard_map/keys_own/pallas_call | solution.py:344
  3.5 0.8 %keys.1.own.refs_0_ = bf16[256,512]{1,0:T(8,128)(2,1)S(1)} custom-call(bf16[128,4096]{1,0:T(8,128)(2,1)S(1)} %collective-permute-done.other, bf16[4096,512]{1,0:T(8,128)(2,1)S(1)} %get-tuple-element.40.w_key, f32[128,512]{1,0:T(8,128)S(1)} %get-tuple-element.41.key_own, f32[256,128]{1,0:T(8,128)S(1)} %get-tuple-element.38.cosine, ...), custom_call_target="tpu_custom_call" | custom-call | flops 536870912 | bytes 4194304 | tf_op jit(solution)/shard_map/keys/pallas_call | solution.py:353
  4.3 1.3 %collective-permute-start.1 = (bf16[256,512]{1,0:T(8,128)(2,1)S(1)}, bf16[256,512]{1,0:T(8,128)(2,1)S(1)}, u32[]{:S(2)}, u32[]{:S(2)}) collective-permute-start(bf16[256,512]{1,0:T(8,128)(2,1)S(1)} %keys.1.own.refs_0_), channel_id=1, source_target_pairs={{0,8},{2,10},{4,12},{6,14},{8,16},{10,18},{12,20},{14,22},{16,24},... | collective-permute-start | bytes 786440 | tf_op jit(solution)/shard_map/ppermute | solution.py:359
  5.6 0.0 slice-start.4
  5.6 2.8 %values.1 = (bf16[256,512]{1,0:T(8,128)(2,1)S(1)}, bf16[256,4096]{1,0:T(8,128)(2,1)S(1)}, f32[8,128]{1,0:T(8,128)S(1)}) custom-call(bf16[128,4096]{1,0:T(8,128)(2,1)S(1)} %get-tuple-element.36.own, bf16[128,4096]{1,0:T(8,128)(2,1)S(1)} %collective-permute-done.other, bf16[4096,512]{1,0:T(8,128)(2,1)} %value_hbm.1), custom_call_target="tpu_custom_call" | custom-call | flops 4294967296 | bytes 4194304 | tf_op jit(solution)/shard_map/values/pallas_call | solution.py:361
  8.5 2.1 %collective-permute-start.5 = (bf16[256,512]{1,0:T(8,128)(2,1)S(1)}, bf16[256,512]{1,0:T(8,128)(2,1)S(1)}, u32[]{:S(2)}, u32[]{:S(2)}) collective-permute-start(bf16[256,512]{1,0:T(8,128)(2,1)S(1)} %get-tuple-element.47.refs_2_.own), channel_id=1, source_target_pairs={{0,8},{2,10},{4,12},{6,14},{8,16},{10,18},{12,20},{14,22},{16,24},... | collective-permute-start | bytes 786440 | tf_op jit(solution)/shard_map/ppermute | solution.py:366
  10.6 3.5 %collective-permute-done.1.earlier.refs_1_ = bf16[256,512]{1,0:T(8,128)(2,1)S(1)} collective-permute-done((bf16[256,512]{1,0:T(8,128)(2,1)S(1)}, bf16[256,512]{1,0:T(8,128)(2,1)S(1)}, u32[]{:S(2)}, u32[]{:S(2)}) %collective-permute-start.1) | collective-permute-done | bytes 262176 | tf_op jit(solution)/shard_map/ppermute | solution.py:359
  14.1 0.1 relay.3
  14.2 1.3 %collective-permute-start.2 = (bf16[256,512]{1,0:T(8,128)(2,1)S(1)}, bf16[256,512]{1,0:T(8,128)(2,1)S(1)}, u32[]{:S(2)}, u32[]{:S(2)}) collective-permute-start(bf16[256,512]{1,0:T(8,128)(2,1)S(1)} %get-tuple-element.43.after), channel_id=1, source_target_pairs={{0,2},{2,0},{4,6},{6,4},{8,10},{10,8},{12,14},{14,12},{16,18},{18,... | collective-permute-start | bytes 786440 | tf_op jit(solution)/shard_map/ppermute | solution.py:373
  15.5 1.2 %collective-permute-start.3 = (bf16[256,512]{1,0:T(8,128)(2,1)S(1)}, bf16[256,512]{1,0:T(8,128)(2,1)S(1)}, u32[]{:S(2)}, u32[]{:S(2)}) collective-permute-start(bf16[256,512]{1,0:T(8,128)(2,1)S(1)} %get-tuple-element.45), channel_id=1, source_target_pairs={{0,4},{2,6},{4,0},{6,2},{8,12},{10,14},{12,8},{14,10},{16,20},{18,... | collective-permute-start | bytes 786440 | tf_op jit(solution)/shard_map/ppermute | solution.py:373
  16.7 0.2 collective-permute-start.4
  16.9 0.7 %slice-done.7 = s8[4194304]{0:T(1024)(128)(4,1)S(1)} async-done(((s8[16777216]{0:T(1024)(128)(4,1)}), s8[4194304]{0:T(1024)(128)(4,1)S(1)}, s32[]{:S(2)}) %slice-start.7) | async-done | bytes 4194328
  17.6 5.3 %queries.1 = (bf16[256,2048]{1,0:T(8,128)(2,1)S(1)}, f32[8,128]{1,0:T(8,128)}) custom-call(bf16[256,4096]{1,0:T(8,128)(2,1)S(1)} %get-tuple-element.37.rows, bf16[4096,2048]{1,0:T(8,128)(2,1)S(1)} %bitcast.3, f32[256,128]{1,0:T(8,128)S(1)} %get-tuple-element.38.cosine, f32[256,128]{1,0:T(8,128)S(1)} %get-tuple-element.39.sine, ...), custom_call_target="tpu_custom_call" | custom-call | flops 4294967296 | bytes 16777216 | tf_op jit(solution)/shard_map/queries/pallas_call | solution.py:377
  22.9 2.7 %scores_near.1 = (f32[16,256,128]{2,1,0:T(8,128)S(1)}, f32[16,256,128]{2,1,0:T(8,128)S(1)}, f32[16,256,128]{2,1,0:T(8,128)S(1)}) custom-call(s32[256,128]{1,0:T(8,128)S(1)} %get-tuple-element.35.starts, bf16[256,2048]{1,0:T(8,128)(2,1)S(1)} %get-tuple-element.44.query, bf16[256,512]{1,0:T(8,128)(2,1)S(1)} %keys.1.own.refs_0_, ...), custom_call_target="tpu_custom_call" | custom-call | flops 1073741824 | bytes 8388608 | tf_op jit(solution)/shard_map/scores_near/pallas_call | solution.py:384
  25.6 0.1 relay.5
  25.7 2.2 %collective-permute-start.8 = (bf16[256,512]{1,0:T(8,128)(2,1)S(1)}, bf16[256,512]{1,0:T(8,128)(2,1)S(1)}, u32[]{:S(2)}, u32[]{:S(2)}) collective-permute-start(bf16[256,512]{1,0:T(8,128)(2,1)S(1)} %get-tuple-element.56), channel_id=1, source_target_pairs={{0,6},{2,4},{4,2},{6,0},{8,14},{10,12},{12,10},{14,8},{16,22},{18,... | collective-permute-start | bytes 786440 | tf_op jit(solution)/shard_map/ppermute | solution.py:373
  27.9 0.3 collective-permute-start.9
  28.2 0.2 collective-permute-start.10
  28.4 1.3 %collective-permute-start.6 = (bf16[256,256]{1,0:T(8,128)(2,1)S(1)}, bf16[256,256]{1,0:T(8,128)(2,1)S(1)}, u32[]{:S(2)}, u32[]{:S(2)}) collective-permute-start(bf16[256,256]{1,0:T(8,128)(2,1)S(1)} %get-tuple-element.54), channel_id=1, source_target_pairs={{0,2},{2,0},{4,6},{6,4},{8,10},{10,8},{12,14},{14,12},{16,18},{18,... | collective-permute-start | bytes 393224 | tf_op jit(solution)/shard_map/ppermute | solution.py:373
  29.7 1.2 %collective-permute-start.7 = (bf16[256,256]{1,0:T(8,128)(2,1)S(1)}, bf16[256,256]{1,0:T(8,128)(2,1)S(1)}, u32[]{:S(2)}, u32[]{:S(2)}) collective-permute-start(bf16[256,256]{1,0:T(8,128)(2,1)S(1)} %get-tuple-element.55), channel_id=1, source_target_pairs={{0,4},{2,6},{4,0},{6,2},{8,12},{10,14},{12,8},{14,10},{16,20},{18,... | collective-permute-start | bytes 393224 | tf_op jit(solution)/shard_map/ppermute | solution.py:373
  31.0 3.6 %scores_far.1 = (bf16[8,256,768]{2,1,0:T(8,128)(2,1)S(1)}, f32[8,256,128]{2,1,0:T(8,128)S(1)}, f32[8,256,128]{2,1,0:T(8,128)S(1)}, bf16[8,256,768]{2,1,0:T(8,128...) custom-call(s32[256,128]{1,0:T(8,128)S(1)} %get-tuple-element.35.starts, ...), custom_call_target="tpu_custom_call" | custom-call | flops 805306368 | bytes 8388608 | tf_op jit(solution)/shard_map/scores_far/pallas_call | solution.py:394
  34.5 1.4 %collective-permute-done.9.refs_0_ = bf16[256,256]{1,0:T(8,128)(2,1)S(1)} collective-permute-done((bf16[256,256]{1,0:T(8,128)(2,1)S(1)}, bf16[256,256]{1,0:T(8,128)(2,1)S(1)}, u32[]{:S(2)}, u32[]{:S(2)}) %collective-permute-start.9) | collective-permute-done | bytes 131104 | tf_op jit(solution)/shard_map/ppermute | solution.py:373
  35.9 1.8 %collective-permute-done.10.refs_1_ = bf16[256,256]{1,0:T(8,128)(2,1)S(1)} collective-permute-done((bf16[256,256]{1,0:T(8,128)(2,1)S(1)}, bf16[256,256]{1,0:T(8,128)(2,1)S(1)}, u32[]{:S(2)}, u32[]{:S(2)}) %collective-permute-start.10) | collective-permute-done | bytes 131104 | tf_op jit(solution)/shard_map/ppermute | solution.py:373
  37.7 4.0 %mix_first.1 = (f32[256,4096]{1,0:T(8,128)S(1)}, bf16[256,1024]{1,0:T(8,128)(2,1)}) custom-call(bf16[8,256,768]{2,1,0:T(8,128)(2,1)S(1)} %get-tuple-element.57.weights, f32[8,256,128]{2,1,0:T(8,128)S(1)} %get-tuple-element.58.total, f32[8,256,128]{2,1,0:T(8,128)S(1)} %get-tuple-element.59.acc, bf16[256,256]{1,0:T(8,128)(2,1)S(1)} %collective-permute-done.9.refs_0_, ...), custom_call_target="tpu_custom_call" | custom-call | flops 2550136832 | bytes 4194304 | tf_op jit(solution)/shard_map/mix_first/pallas_call | solution.py:403
  41.7 1.6 %mix_second.1 = (bf16[128,2048]{1,0:T(8,128)(2,1)S(1)}, bf16[256,1024]{1,0:T(8,128)(2,1)S(1)}) custom-call(bf16[8,256,768]{2,1,0:T(8,128)(2,1)S(1)} %get-tuple-element.51.weights, f32[8,256,128]{2,1,0:T(8,128)S(1)} %get-tuple-element.52.total, f32[8,256,128]{2,1,0:T(8,128)S(1)} %get-tuple-element.53.acc, ...), custom_call_target="tpu_custom_call" | custom-call | flops 939524096 | bytes 4194304 | tf_op jit(solution)/shard_map/mix_second/pallas_call | solution.py:411
  43.3 2.1 %collective-permute-start.12 = (bf16[128,2048]{1,0:T(8,128)(2,1)S(1)}, bf16[128,2048]{1,0:T(8,128)(2,1)S(1)}, u32[]{:S(2)}, u32[]{:S(2)}) collective-permute-start(bf16[128,2048]{1,0:T(8,128)(2,1)S(1)} %get-tuple-element.64), channel_id=1, source_target_pairs={{0,1},{1,0},{2,3},{3,2},{4,5},{5,4},{6,7},{7,6},{8,9},{9,8},{10,11... | collective-permute-start | bytes 1572872 | tf_op jit(solution)/shard_map/ppermute | solution.py:415
  45.3 0.7 %send_high.1 = bf16[128,2048]{1,0:T(8,128)(2,1)S(1)} custom-call(bf16[256,1024]{1,0:T(8,128)(2,1)S(1)} %get-tuple-element.63.attended, bf16[2048,4096]{1,0:T(8,128)(2,1)S(1)} %bitcast.1, f32[256,4096]{1,0:T(8,128)S(1)} %get-tuple-element.62.refs_4_.summed), custom_call_target="tpu_custom_call" | custom-call | flops 536870912 | bytes 4194304 | tf_op jit(solution)/shard_map/send_high/pallas_call | solution.py:416
  46.1 0.1 collective-permute-start.11
  46.2 0.7 %own_high.1.after.own = f32[128,2048]{1,0:T(8,128)S(1)} custom-call(bf16[256,1024]{1,0:T(8,128)(2,1)S(1)} %get-tuple-element.63.attended, bf16[2048,4096]{1,0:T(8,128)(2,1)S(1)} %bitcast.1, f32[256,4096]{1,0:T(8,128)S(1)} %get-tuple-element.62.refs_4_.summed), custom_call_target="tpu_custom_call" | custom-call | flops 536870912 | bytes 4194304 | tf_op jit(solution)/shard_map/own_high/pallas_call | solution.py:420
  46.9 1.4 %own_low.1.mixed_in = bf16[128,4096]{1,0:T(8,128)(2,1)} custom-call(bf16[256,1024]{1,0:T(8,128)(2,1)S(1)} %get-tuple-element.63.attended, bf16[2048,4096]{1,0:T(8,128)(2,1)S(1)} %bitcast.1, f32[256,4096]{1,0:T(8,128)S(1)} %get-tuple-element.62.refs_4_.summed, bf16[128,2048]{1,0:T(8,128)(2,1)S(1)} %collective-permute-done.12.got, ...), custom_call_target="tpu_custom_call" | custom-call | flops 536870912 | bytes 4194304 | tf_op jit(solution)/shard_map/own_low/pallas_call | solution.py:426
  48.4 0.8 %add.1 = bf16[128,4096]{1,0:T(8,128)(2,1)} custom-call(f32[128,2048]{1,0:T(8,128)S(1)} %own_high.1.after.own, bf16[128,2048]{1,0:T(8,128)(2,1)S(1)} %collective-permute-done.11.got, bf16[128,4096]{1,0:T(8,128)(2,1)} %own_low.1.mixed_in), custom_call_target="tpu_custom_call", output_to_operand_aliasing={{}: (2, {})} | custom-call | flops 262144 | bytes 4194304 | tf_op jit(solution)/shard_map/add/pallas_call | solution.py:429
  (27 shorter events, 0.1 us)
Async XLA Ops:
  0.0 3.5 %collective-permute-start = (bf16[128,4096]{1,0:T(8,128)(2,1)}, bf16[128,4096]{1,0:T(8,128)(2,1)S(1)}, u32[]{:S(2)}, u32[]{:S(2)}) collective-permute-start(bf16[128,4096]{1,0:T(8,128)(2,1)} %own_hbm.1), channel_id=1, source_target_pairs={{0,1},{1,0},{2,3},{3,2},{4,5},{5,4},{6,7},{7,6},{8,9},{9,8},{10,11... | collective-permute-start | bytes 3145736 | tf_op jit(solution)/shard_map/ppermute | solution.py:338
  4.3 9.8 %collective-permute-start.1 = (bf16[256,512]{1,0:T(8,128)(2,1)S(1)}, bf16[256,512]{1,0:T(8,128)(2,1)S(1)}, u32[]{:S(2)}, u32[]{:S(2)}) collective-permute-start(bf16[256,512]{1,0:T(8,128)(2,1)S(1)} %keys.1.own.refs_0_), channel_id=1, source_target_pairs={{0,8},{2,10},{4,12},{6,14},{8,16},{10,18},{12,20},{14,22},{16,24},... | collective-permute-start | bytes 786440 | tf_op jit(solution)/shard_map/ppermute | solution.py:359
  5.6 11.3 %slice-start.4 = ((s8[16777216]{0:T(1024)(128)(4,1)}), s8[4194304]{0:T(1024)(128)(4,1)S(1)}, s32[]{:S(2)}) async-start(s8[16777216]{0:T(1024)(128)(4,1)} %bitcast.2), calls=%async_computation.4 | async-start | bytes 8388608
  5.6 11.3 %slice-start.5 = ((s8[16777216]{0:T(1024)(128)(4,1)}), s8[4194304]{0:T(1024)(128)(4,1)S(1)}, s32[]{:S(2)}) async-start(s8[16777216]{0:T(1024)(128)(4,1)} %bitcast.2), calls=%async_computation.5 | async-start | bytes 8388608
  8.5 14.4 %collective-permute-start.5 = (bf16[256,512]{1,0:T(8,128)(2,1)S(1)}, bf16[256,512]{1,0:T(8,128)(2,1)S(1)}, u32[]{:S(2)}, u32[]{:S(2)}) collective-permute-start(bf16[256,512]{1,0:T(8,128)(2,1)S(1)} %get-tuple-element.47.refs_2_.own), channel_id=1, source_target_pairs={{0,8},{2,10},{4,12},{6,14},{8,16},{10,18},{12,20},{14,22},{16,24},... | collective-permute-start | bytes 786440 | tf_op jit(solution)/shard_map/ppermute | solution.py:366
  14.1 2.8 %slice-start.6 = ((s8[16777216]{0:T(1024)(128)(4,1)}), s8[4194304]{0:T(1024)(128)(4,1)S(1)}, s32[]{:S(2)}) async-start(s8[16777216]{0:T(1024)(128)(4,1)} %bitcast.2), calls=%async_computation.6 | async-start | bytes 8388608
  14.1 3.5 %slice-start.7 = ((s8[16777216]{0:T(1024)(128)(4,1)}), s8[4194304]{0:T(1024)(128)(4,1)S(1)}, s32[]{:S(2)}) async-start(s8[16777216]{0:T(1024)(128)(4,1)} %bitcast.2), calls=%async_computation.7 | async-start | bytes 8388608
  14.2 14.0 %collective-permute-start.2 = (bf16[256,512]{1,0:T(8,128)(2,1)S(1)}, bf16[256,512]{1,0:T(8,128)(2,1)S(1)}, u32[]{:S(2)}, u32[]{:S(2)}) collective-permute-start(bf16[256,512]{1,0:T(8,128)(2,1)S(1)} %get-tuple-element.43.after), channel_id=1, source_target_pairs={{0,2},{2,0},{4,6},{6,4},{8,10},{10,8},{12,14},{14,12},{16,18},{18,... | collective-permute-start | bytes 786440 | tf_op jit(solution)/shard_map/ppermute | solution.py:373
  15.5 12.9 %collective-permute-start.3 = (bf16[256,512]{1,0:T(8,128)(2,1)S(1)}, bf16[256,512]{1,0:T(8,128)(2,1)S(1)}, u32[]{:S(2)}, u32[]{:S(2)}) collective-permute-start(bf16[256,512]{1,0:T(8,128)(2,1)S(1)} %get-tuple-element.45), channel_id=1, source_target_pairs={{0,4},{2,6},{4,0},{6,2},{8,12},{10,14},{12,8},{14,10},{16,20},{18,... | collective-permute-start | bytes 786440 | tf_op jit(solution)/shard_map/ppermute | solution.py:373
  16.7 11.7 %collective-permute-start.4 = (bf16[256,512]{1,0:T(8,128)(2,1)S(1)}, bf16[256,512]{1,0:T(8,128)(2,1)S(1)}, u32[]{:S(2)}, u32[]{:S(2)}) collective-permute-start(bf16[256,512]{1,0:T(8,128)(2,1)S(1)} %get-tuple-element.46), channel_id=1, source_target_pairs={{0,6},{2,4},{4,2},{6,0},{8,14},{10,12},{12,10},{14,8},{16,22},{18,... | collective-permute-start | bytes 786440 | tf_op jit(solution)/shard_map/ppermute | solution.py:373
  25.6 12.1 %slice-start = ((s8[16777216]{0:T(1024)(128)(4,1)}), s8[4194304]{0:T(1024)(128)(4,1)S(1)}, s32[]{:S(2)}) async-start(s8[16777216]{0:T(1024)(128)(4,1)} %bitcast), calls=%async_computation | async-start | bytes 8388608
  25.6 12.1 %slice-start.1 = ((s8[16777216]{0:T(1024)(128)(4,1)}), s8[4194304]{0:T(1024)(128)(4,1)S(1)}, s32[]{:S(2)}) async-start(s8[16777216]{0:T(1024)(128)(4,1)} %bitcast), calls=%async_computation.1 | async-start | bytes 8388608
  25.6 12.1 %slice-start.2 = ((s8[16777216]{0:T(1024)(128)(4,1)}), s8[4194304]{0:T(1024)(128)(4,1)S(1)}, s32[]{:S(2)}) async-start(s8[16777216]{0:T(1024)(128)(4,1)} %bitcast), calls=%async_computation.2 | async-start | bytes 8388608
  25.6 12.1 %slice-start.3 = ((s8[16777216]{0:T(1024)(128)(4,1)}), s8[4194304]{0:T(1024)(128)(4,1)S(1)}, s32[]{:S(2)}) async-start(s8[16777216]{0:T(1024)(128)(4,1)} %bitcast), calls=%async_computation.3 | async-start | bytes 8388608
  25.7 12.0 %collective-permute-start.8 = (bf16[256,512]{1,0:T(8,128)(2,1)S(1)}, bf16[256,512]{1,0:T(8,128)(2,1)S(1)}, u32[]{:S(2)}, u32[]{:S(2)}) collective-permute-start(bf16[256,512]{1,0:T(8,128)(2,1)S(1)} %get-tuple-element.56), channel_id=1, source_target_pairs={{0,6},{2,4},{4,2},{6,0},{8,14},{10,12},{12,10},{14,8},{16,22},{18,... | collective-permute-start | bytes 786440 | tf_op jit(solution)/shard_map/ppermute | solution.py:373
  27.9 8.0 %collective-permute-start.9 = (bf16[256,256]{1,0:T(8,128)(2,1)S(1)}, bf16[256,256]{1,0:T(8,128)(2,1)S(1)}, u32[]{:S(2)}, u32[]{:S(2)}) collective-permute-start(bf16[256,256]{1,0:T(8,128)(2,1)S(1)} %get-tuple-element.60), channel_id=1, source_target_pairs={{0,2},{2,0},{4,6},{6,4},{8,10},{10,8},{12,14},{14,12},{16,18},{18,... | collective-permute-start | bytes 393224 | tf_op jit(solution)/shard_map/ppermute | solution.py:373
  28.2 9.5 %collective-permute-start.10 = (bf16[256,256]{1,0:T(8,128)(2,1)S(1)}, bf16[256,256]{1,0:T(8,128)(2,1)S(1)}, u32[]{:S(2)}, u32[]{:S(2)}) collective-permute-start(bf16[256,256]{1,0:T(8,128)(2,1)S(1)} %get-tuple-element.61), channel_id=1, source_target_pairs={{0,4},{2,6},{4,0},{6,2},{8,12},{10,14},{12,8},{14,10},{16,20},{18,... | collective-permute-start | bytes 393224 | tf_op jit(solution)/shard_map/ppermute | solution.py:373
  28.4 13.2 %collective-permute-start.6 = (bf16[256,256]{1,0:T(8,128)(2,1)S(1)}, bf16[256,256]{1,0:T(8,128)(2,1)S(1)}, u32[]{:S(2)}, u32[]{:S(2)}) collective-permute-start(bf16[256,256]{1,0:T(8,128)(2,1)S(1)} %get-tuple-element.54), channel_id=1, source_target_pairs={{0,2},{2,0},{4,6},{6,4},{8,10},{10,8},{12,14},{14,12},{16,18},{18,... | collective-permute-start | bytes 393224 | tf_op jit(solution)/shard_map/ppermute | solution.py:373
  29.7 11.9 %collective-permute-start.7 = (bf16[256,256]{1,0:T(8,128)(2,1)S(1)}, bf16[256,256]{1,0:T(8,128)(2,1)S(1)}, u32[]{:S(2)}, u32[]{:S(2)}) collective-permute-start(bf16[256,256]{1,0:T(8,128)(2,1)S(1)} %get-tuple-element.55), channel_id=1, source_target_pairs={{0,4},{2,6},{4,0},{6,2},{8,12},{10,14},{12,8},{14,10},{16,20},{18,... | collective-permute-start | bytes 393224 | tf_op jit(solution)/shard_map/ppermute | solution.py:373
  43.3 3.6 %collective-permute-start.12 = (bf16[128,2048]{1,0:T(8,128)(2,1)S(1)}, bf16[128,2048]{1,0:T(8,128)(2,1)S(1)}, u32[]{:S(2)}, u32[]{:S(2)}) collective-permute-start(bf16[128,2048]{1,0:T(8,128)(2,1)S(1)} %get-tuple-element.64), channel_id=1, source_target_pairs={{0,1},{1,0},{2,3},{3,2},{4,5},{5,4},{6,7},{7,6},{8,9},{9,8},{10,11... | collective-permute-start | bytes 1572872 | tf_op jit(solution)/shard_map/ppermute | solution.py:415
  46.1 2.3 %collective-permute-start.11 = (bf16[128,2048]{1,0:T(8,128)(2,1)S(1)}, bf16[128,2048]{1,0:T(8,128)(2,1)S(1)}, u32[]{:S(2)}, u32[]{:S(2)}) collective-permute-start(bf16[128,2048]{1,0:T(8,128)(2,1)S(1)} %send_high.1), channel_id=1, source_target_pairs={{0,1},{1,0},{2,3},{3,2},{4,5},{5,4},{6,7},{7,6},{8,9},{9,8},{10,11... | collective-permute-start | bytes 1572872 | tf_op jit(solution)/shard_map/ppermute | solution.py:419

commit v5 on v4

v5 whole, which is shorter than its diff:
```python
import functools
import math

import jax
import jax.numpy as jnp
from jax import lax
from jax.experimental import pallas as pl
from jax.experimental.pallas import tpu as pltpu
from jax.sharding import PartitionSpec as P

HEAD_SIZE = 128
LAYER = 4
MASKED = -1e30
VALUES_COST = 4 << 30
RELAY_COST = 5 << 30
SCORE_SCALE = math.log2(math.e) * HEAD_SIZE ** (-0.5)
SWAP = [(0, 1), (1, 0)]
VMEM = pl.BlockSpec(memory_space=pltpu.VMEM)
ANY = pl.BlockSpec(memory_space=pl.ANY)


def inverse_frequency():
    table = []
    for number in range(HEAD_SIZE // 2):
        base_freq = 500000.0 ** (-(2.0 * number) / HEAD_SIZE)
        wavelength = 2.0 * math.pi / base_freq
        smooth = (8192.0 / wavelength - 1.0) / 3.0
        if wavelength < 2048.0:
            table.append(base_freq)
        elif wavelength > 8192.0:
            table.append(base_freq / 8.0)
        else:
            table.append((1.0 - smooth) * base_freq / 8.0 + smooth * base_freq)
    return table


def dot(a, b):
    return jnp.dot(a, b, preferred_element_type=jnp.float32)


def rotated(block, cosine, sine):
    return block * cosine + pltpu.roll(block, HEAD_SIZE // 2, 1) * sine


def load_columns(low, hbms, buffers, sems, chunks):
    depth, wide = buffers[0].shape[0] // chunks, buffers[0].shape[1]
    copies = []
    for number in range(chunks):
        at = pl.ds(number * depth, depth)
        pair = [
            pltpu.make_async_copy(hbm.at[at, pl.ds(low, wide)], buffer.at[at], sems.at[number * len(hbms) + which])
            for which, (hbm, buffer) in enumerate(zip(hbms, buffers))
        ]
        for copy in pair:
            copy.start()
        copies.append(pair)
    return copies


def piecewise_product(rows, copies, buffers, total, put=None):
    depth, wide = buffers[0].shape[0] // len(copies), buffers[0].shape[1]
    for number, pair in enumerate(copies):
        at = slice(number * depth, (number + 1) * depth)
        for which, (copy, buffer) in enumerate(zip(pair, buffers)):
            copy.wait()
            columns = slice(which * wide, (which + 1) * wide)
            product = dot(rows[:, at], buffer[at, :])
            if number > 0:
                product = product + total[:, columns]
            if put is None or number < len(copies) - 1:
                total[:, columns] = product
            else:
                put(which, product)


def first_kernel(chunks, lengths_hbm, own_hbm, key_hbm, value_hbm, total, own, w_key, w_value, cosine, sine, starts, lengths, sems):
    row_copy = pltpu.make_async_copy(own_hbm, own, sems.at[2 * chunks])
    row_copy.start()
    copies = load_columns(0, (key_hbm, value_hbm), (w_key, w_value), sems, chunks)
    tokens = cosine.shape[0]
    length_copy = pltpu.make_async_copy(lengths_hbm, lengths, sems.at[2 * chunks + 1])
    length_copy.start()
    lane = lax.broadcasted_iota(jnp.int32, (1, HEAD_SIZE), 1)
    pair_of_lane = lane % (HEAD_SIZE // 2)
    freq = jnp.zeros((1, HEAD_SIZE), jnp.float32)
    for number, value in enumerate(inverse_frequency()):
        freq = jnp.where(pair_of_lane == number, jnp.float32(value), freq)
    first = lax.axis_index("seq") * tokens
    half = tokens // 2
    low_lane = lane < HEAD_SIZE // 2
    packed = first + lax.broadcasted_iota(jnp.int32, (half, HEAD_SIZE), 0) + jnp.where(low_lane, 0, half)
    angles = packed.astype(jnp.float32) * freq
    turned = jnp.cos(angles)
    other = pltpu.roll(turned, HEAD_SIZE // 2, 1)
    cosine[:half, :] = jnp.where(low_lane, turned, other)
    cosine[half:, :] = jnp.where(low_lane, other, turned)
    turned = jnp.sin(angles)
    other = pltpu.roll(turned, HEAD_SIZE // 2, 1)
    sine[:half, :] = jnp.where(low_lane, -turned, other)
    sine[half:, :] = jnp.where(low_lane, -other, turned)
    positions = first + lax.broadcasted_iota(jnp.int32, (tokens, HEAD_SIZE), 0)
    length_copy.wait()
    start = jnp.zeros((tokens, HEAD_SIZE), jnp.int32)
    end = jnp.int32(0)
    for number in range(lengths.shape[0]):
        end = end + lengths[number]
        start = jnp.where(positions >= end, end, start)
    starts[...] = start
    row_copy.wait()
    piecewise_product(own, copies, (w_key, w_value), total)


def halves(half):
    core = lax.axis_index("head")
    return pl.ds(pl.multiple_of(core * half, half), half), pl.ds(pl.multiple_of((1 - core) * half, half), half)


def put_block(kv, here, block, cosine, sine, is_key, low):
    for head in range(block.shape[1] // HEAD_SIZE):
        piece = block[:, head * HEAD_SIZE : (head + 1) * HEAD_SIZE]
        if is_key:
            piece = rotated(piece, cosine[here, :], sine[here, :])
        kv[here, low + head * HEAD_SIZE : low + (head + 1) * HEAD_SIZE] = piece.astype(kv.dtype)


def second_kernel(other, w_key, w_value, own_total, cosine, sine, kv):
    half, wide = own_total.shape[0], w_key.shape[1]
    mine, theirs = halves(half)
    for which, weight in enumerate((w_key, w_value)):
        low = which * wide
        put_block(kv, mine, own_total[:, low : low + wide], cosine, sine, which == 0, low)
        put_block(kv, theirs, dot(other[...], weight[...]), cosine, sine, which == 0, low)


def third_kernel(chunks, own, other, key_hbm, value_hbm, cosine, sine, kv, rows, done, w_key, w_value, total, sems):
    wide = w_key.shape[1]
    copies = load_columns(wide, (key_hbm, value_hbm), (w_key, w_value), sems, chunks)
    mine, theirs = halves(own.shape[0])
    rows[mine, :] = own[...]
    rows[theirs, :] = other[...]
    done[...] = jnp.zeros_like(done)
    everything = slice(0, rows.shape[0])

    def put(which, product):
        put_block(kv, everything, product, cosine, sine, which == 0, which * wide)

    piecewise_product(rows, copies, (w_key, w_value), total, put)


def query_kernel(rows, weight, cosine, sine, after, query, done):
    del after
    done[...] = jnp.zeros_like(done)
    wide = 4 * HEAD_SIZE
    for number in range(weight.shape[1] // wide):
        result = dot(rows[...], weight[:, number * wide : (number + 1) * wide])
        for head in range(wide // HEAD_SIZE):
            at = slice(head * HEAD_SIZE, (head + 1) * HEAD_SIZE)
            out = slice(number * wide + head * HEAD_SIZE, number * wide + (head + 1) * HEAD_SIZE)
            query[:, out] = rotated(result[:, at], cosine[...], sine[...]).astype(query.dtype)


def relay_kernel(own, earlier, after, to_x, to_y, to_d):
    del after
    index = lax.axis_index("seq")
    mine, theirs = own[...], earlier[...]
    to_x[...] = jnp.where(index % 2 > 0, theirs, mine)
    by_y = jnp.where(index % LAYER >= 2, theirs, mine)
    to_y[...] = by_y
    to_d[...] = by_y


def column(number):
    return slice(number * HEAD_SIZE, (number + 1) * HEAD_SIZE)


def fill_bias(bias, distances, starts):
    tokens = bias.shape[0]
    index = lax.axis_index("seq")
    base = index * tokens
    query_pos = base + lax.broadcasted_iota(jnp.int32, (tokens, tokens), 0)
    start = jnp.concatenate([starts[...]] * (tokens // starts.shape[1]), axis=1)
    for number, (even, odd) in enumerate(distances):
        first = base - tokens * jnp.where(index % 2 > 0, odd, even)
        key_pos = first + lax.broadcasted_iota(jnp.int32, (tokens, tokens), 1)
        allowed = (key_pos >= start) & (key_pos <= query_pos)
        bias[:, number * tokens : (number + 1) * tokens] = jnp.where(allowed, 0.0, MASKED)


def scores_of(query, keys, bias, head, at):
    tokens = bias.shape[0]
    return [
        lax.dot_general(
            query[:, column(head)], key[:, column(at)], (((1,), (1,)), ((), ())), preferred_element_type=jnp.float32
        )
        * SCORE_SCALE
        + bias[:, number * tokens : (number + 1) * tokens]
        for number, key in enumerate(keys)
    ]


def weighted(weights, blocks, at, ones):
    product = None
    for weight, block in zip(weights, blocks):
        term = dot(weight, jnp.concatenate([block[:, column(at)], ones], axis=1))
        product = term if product is None else product + term
    return product[:, :HEAD_SIZE], product[:, HEAD_SIZE:]


def row_max(scores):
    return jnp.max(functools.reduce(jnp.maximum, scores), axis=1, keepdims=True)


def near_kernel(distances, starts, query, *refs):
    count = len(distances)
    tops, totals, accs, bias = refs[-4:]
    parts = [refs[low : low + count] for low in range(0, len(refs) - 4, count)]
    fill_bias(bias, distances, starts)
    tokens = query.shape[0]
    heads = query.shape[1] // HEAD_SIZE
    kv_part = parts[0][0].shape[1] // (2 * HEAD_SIZE)
    group = heads // (kv_part * len(parts))
    ones = jnp.ones((tokens, HEAD_SIZE), query.dtype)

    def place(head):
        return parts[head // group // kv_part], head // group % kv_part

    def ask(head):
        blocks, at = place(head)
        return scores_of(query, blocks, bias, head, at)

    scores = ask(0)
    for head in range(heads):
        ahead = ask(head + 1) if head + 1 < heads else None
        top = row_max(scores)
        blocks, at = place(head)
        weights = [jnp.exp2(score - top).astype(query.dtype) for score in scores]
        tops[head] = jnp.broadcast_to(top, (tokens, HEAD_SIZE))
        accs[head], totals[head] = weighted(weights, blocks, kv_part + at, ones)
        scores = ahead


def attend_far(low, distances, starts, query, blocks, state, attended, bias):
    tops, totals, accs = state
    fill_bias(bias, distances, starts)
    tokens = query.shape[0]
    heads = attended.shape[1] // HEAD_SIZE
    kv_part = blocks[0].shape[1] // (2 * HEAD_SIZE)
    group = heads // kv_part
    ones = jnp.ones((tokens, HEAD_SIZE), query.dtype)
    scores = scores_of(query, blocks, bias, low, 0)
    for head in range(heads):
        ahead = scores_of(query, blocks, bias, low + head + 1, (head + 1) // group) if head + 1 < heads else None
        before = tops[low + head]
        top = jnp.maximum(jnp.broadcast_to(row_max(scores), (tokens, HEAD_SIZE)), before)
        factor = jnp.exp2(before - top)
        wide_top = jnp.concatenate([top] * (tokens // HEAD_SIZE), axis=1)
        weights = [jnp.exp2(score - wide_top).astype(query.dtype) for score in scores]
        acc, total = weighted(weights, blocks, kv_part + head // group, ones)
        result = (accs[low + head] * factor + acc) / (totals[low + head] * factor + total)
        attended[:, column(head)] = result.astype(attended.dtype)
        scores = ahead


WIDE = 4 * HEAD_SIZE


def mix_first_kernel(distances, starts, query, *refs):
    far = len(distances)
    blocks, state, (weight, summed, attended, bias) = refs[:far], refs[far : far + 3], refs[far + 3 :]
    attend_far(0, distances, starts, query, blocks, state, attended, bias)
    depth = attended.shape[1]
    for number in range(summed.shape[1] // WIDE):
        at = slice(number * WIDE, (number + 1) * WIDE)
        summed[:, at] = dot(attended[...], weight[:depth, at])


def rows_product(rows, low, attended, weight, summed, wide):
    depth = attended.shape[1]
    at = slice(low, low + wide)
    return summed[rows, at] + dot(attended[rows, :], weight[depth:, at])


def send_columns(low, attended, weight, summed, send):
    theirs = halves(send.shape[0])[1]
    for number in range(send.shape[1] // WIDE):
        result = rows_product(theirs, low + number * WIDE, attended, weight, summed, WIDE)
        send[:, number * WIDE : (number + 1) * WIDE] = result.astype(send.dtype)


def mix_second_kernel(low, distances, starts, query, *refs):
    far = len(distances)
    blocks, state, (weight, summed, send, attended, bias) = refs[:far], refs[far : far + 3], refs[far + 3 :]
    attend_far(low, distances, starts, query, blocks, state, attended, bias)
    send_columns(0, attended, weight, summed, send)


def own_high_kernel(low, attended, weight, summed, own):
    mine = halves(own.shape[0])[0]
    for number in range(own.shape[1] // WIDE):
        result = rows_product(mine, low + number * WIDE, attended, weight, summed, WIDE)
        own[:, number * WIDE : (number + 1) * WIDE] = result


def own_low_kernel(attended, weight, summed, got, after, mixed):
    del after
    mine = halves(got.shape[0])[0]
    for number in range(got.shape[1] // WIDE):
        at = slice(number * WIDE, (number + 1) * WIDE)
        result = rows_product(mine, number * WIDE, attended, weight, summed, WIDE)
        mixed[:, at] = (result + got[:, at].astype(jnp.float32)).astype(mixed.dtype)


def add_kernel(mixed_low, own, got, mixed_hbm, mixed, sems):
    low = mixed_low.shape[1]
    copies = [pltpu.make_async_copy(mixed_low, mixed_hbm.at[:, pl.ds(0, low)], sems.at[0])]
    copies[0].start()
    for number in range(own.shape[1] // WIDE):
        at = slice(number * WIDE, (number + 1) * WIDE)
        mixed[:, at] = (own[:, at] + got[:, at].astype(jnp.float32)).astype(mixed.dtype)
        there = mixed_hbm.at[:, pl.ds(low + number * WIDE, WIDE)]
        copies.append(pltpu.make_async_copy(mixed.at[:, pl.ds(number * WIDE, WIDE)], there, sems.at[number + 1]))
        copies[-1].start()
    for copy in copies:
        copy.wait()


def call(kernel, name, outs, in_specs, flops, nbytes, limit, scratch=(), out_specs=None):
    return pl.pallas_call(
        kernel,
        out_shape=outs,
        in_specs=in_specs,
        out_specs=out_specs or [VMEM] * len(outs),
        scratch_shapes=list(scratch),
        name=name,
        cost_estimate=pl.CostEstimate(flops=flops, bytes_accessed=nbytes, transcendentals=0),
        compiler_params=pltpu.CompilerParams(vmem_limit_bytes=limit << 20),
    )


def in_hbm(array):
    return pltpu.with_memory_space_constraint(array, pltpu.HBM)


def body(input_rows, doc_lengths, w_query, key_weight, value_weight, w_out):
    half, model = input_rows.shape
    tokens = 2 * half
    width_q, width_k = w_query.shape[1], key_weight.shape[1]
    heads = width_q // HEAD_SIZE
    shards = lax.axis_size("seq")
    bf16, f32 = jnp.bfloat16, jnp.float32
    shape = pltpu.VMEM

    other = lax.ppermute(input_rows, "head", SWAP)

    flag = shape((8, HEAD_SIZE), f32)
    table = shape((tokens, HEAD_SIZE), f32)
    part = width_k // 2
    kv_shape = shape((tokens, 2 * part), bf16)
    part_shape = shape((model, part), bf16)
    chunks = 4
    kv_flops = 4 * half * model * part
    total, own, w_key, w_value, cosine, sine, starts = call(
        functools.partial(first_kernel, chunks), "keys_values_own",
        [
            shape((half, 2 * part), f32), shape((half, model), bf16), part_shape, part_shape,
            table, table, shape((tokens, HEAD_SIZE), jnp.int32),
        ],
        [ANY] * 4, kv_flops, 2 * model * width_k, 4,
        [pltpu.SMEM(doc_lengths.shape, jnp.int32), pltpu.SemaphoreType.DMA((2 * chunks + 2,))],
    )(in_hbm(doc_lengths), in_hbm(input_rows), in_hbm(key_weight), in_hbm(value_weight))
    (kv_a,) = call(
        second_kernel, "keys_values", [kv_shape], [VMEM] * 6, kv_flops, 2 * model * width_k, 4,
    )(other, w_key, w_value, total, cosine, sine)

    every = range(shards)
    step_z = [(i, (i + LAYER) % shards) for i in every]
    z_a = lax.ppermute(kv_a, "seq", [(a, b) for a, b in step_z if a < b])

    kv_b, rows, done = call(
        functools.partial(third_kernel, chunks), "keys_values_more", [kv_shape, shape((tokens, model), bf16), flag],
        [VMEM, VMEM, ANY, ANY, VMEM, VMEM], VALUES_COST, 2 * model * width_k, 10,
        [part_shape, part_shape, pltpu.VMEM((tokens, 2 * part), f32), pltpu.SemaphoreType.DMA((2 * chunks,))],
    )(own, other, in_hbm(key_weight), in_hbm(value_weight), cosine, sine)
    z_b = lax.ppermute(kv_b, "seq", step_z)

    def exchange(mine, earlier, after, ways, cost):
        to = call(
            relay_kernel, "relay", [kv_shape] * 3, [VMEM] * 3, cost, 2 << 20, 4,
        )(mine, earlier, after)
        got = {way: lax.ppermute(to[way - 1], "seq", [(i, i ^ way) for i in every]) for way in ways}
        return [got[way] for way in (1, 2, 3)], to[0]

    far_a, done = exchange(kv_a, z_a, done, (1, 2, 3), RELAY_COST)
    query, done = call(
        query_kernel, "queries", [shape((tokens, width_q), bf16), flag], [VMEM] * 5,
        2 * tokens * model * width_q, 2 * model * width_q, 8,
    )(rows, w_query, cosine, sine, done)
    far_b, _ = exchange(kv_b, z_b, done, (3, 1, 2), 9 << 30)
    near = call(
        functools.partial(near_kernel, ((0, 0), (LAYER, LAYER))), "scores_near", [shape((heads, tokens, HEAD_SIZE), f32)] * 3,
        [VMEM] * 6, 8 * heads * tokens * tokens * HEAD_SIZE, 8 << 20, 12, [pltpu.VMEM((tokens, 2 * tokens), f32)],
    )(starts, query, kv_a, z_a, kv_b, z_b)

    far = len(far_a)
    distances = ((3, 1), (2, 2), (1, 3))
    bias = pltpu.VMEM((tokens, far * tokens), f32)
    columns = w_out.shape[1]
    attended_shape = shape((tokens, width_q // 2), bf16)
    far_flops = 3 * far * heads * tokens * tokens * HEAD_SIZE
    out_flops = tokens * width_q * columns
    summed, _ = call(
        functools.partial(mix_first_kernel, distances), "mix_first", [shape((tokens, columns), f32), attended_shape],
        [VMEM] * (6 + far), out_flops + far_flops, 4 << 20, 10, [bias],
    )(starts, query, *far_a, *near, w_out)

    cut = columns // 2
    send_shape = shape((half, cut), bf16)
    quarter = out_flops // 4
    send, attended = call(
        functools.partial(mix_second_kernel, heads // 2, distances), "mix_second", [send_shape, attended_shape],
        [VMEM] * (7 + far), quarter + far_flops, 4 << 20, 10, [bias],
    )(starts, query, *far_b, *near, w_out, summed)
    got_low = lax.ppermute(send, "head", SWAP)
    (send,) = call(
        functools.partial(send_columns, cut), "send_high", [send_shape], [VMEM] * 3, quarter, 4 << 20, 6,
    )(attended, w_out, summed)
    got_high = lax.ppermute(send, "head", SWAP)
    (own,) = call(
        functools.partial(own_high_kernel, cut), "own_high", [shape((half, columns - cut), f32)], [VMEM] * 3,
        quarter, 4 << 20, 6,
    )(attended, w_out, summed)
    (mixed,) = call(
        own_low_kernel, "own_low", [send_shape], [VMEM] * 5, quarter, 4 << 20, 6,
    )(attended, w_out, summed, got_low, own)
    (mixed,) = call(
        add_kernel, "add", [pltpu.HBM((half, columns), bf16)], [VMEM] * 3, half * cut, 4 << 20, 4,
        [pltpu.VMEM((half, columns - cut), bf16), pltpu.SemaphoreType.DMA(((columns - cut) // WIDE + 1,))], [ANY],
    )(mixed, own, got_high)
    return mixed


def solution(mesh):
    in_specs = (
        P(("seq", "head"), None),
        P(),
        P(None, "head"),
        P(None, "head"),
        P(None, "head"),
        P("head", None),
    )
    out_specs = P(("seq", "head"), None)
    return jax.shard_map(body, mesh=mesh, in_specs=in_specs, out_specs=out_specs, check_vma=False)
```

time: 49.9 us -> 48.6 us (0.974)
  waiting for transfers between devices: 6.67 us -> 8.95 us
  starting transfers between devices: 14.2 us -> 12 us
  Pallas kernels: 27.5 us -> 26.2 us
    ppermute x10 -> x8, starting transfers between devices: 11.3 us -> 8.88 us  [the longest x6 5.49 us: exchange(): lax.ppermute(to[way - 1], 'seq', [(i, i ^ way) for i in every])]
    ppermute x10 -> x8, waiting for transfers between devices: 6.66 us -> 8.55 us  [the longest x6 6.15 us: exchange(): lax.ppermute(to[way - 1], 'seq', [(i, i ^ way) for i in every])]
    pallas_call x1, Pallas kernels: 5.3 us -> 4.67 us  [body(): call(query_kernel, 'queries', [shape((tokens, width_q), bf16), flag], [VM...]
    pallas_call x11 -> x9, Pallas kernels: 18 us -> 17.4 us  [the longest x1 4.49 us: body(): call(functools.partial(mix_first_kernel, distances), 'mix_first', [shape(...]
  transfers between devices with their start and end apart: 13 -> 11, of which waited for: 3 -> 4; matrix products, arithmetic and copies ran while one was open for 0% -> 0% of each run, Pallas kernels for 49% -> 44%
where the time goes in v5:
time: 48.6 us; the launch traced here: 48.5 us
  Pallas kernels  26.2 us (54%)
  starting transfers between devices  12 us (25%)
  waiting for transfers between devices  8.95 us (18%)
  local copies, waits for them, and re-layouts  0.91 us (2%)
    ppermute x6, waiting for transfers between devices, exchange(): lax.ppermute(to[way - 1], 'seq', [(i, i ^ way) for i in every])  6.15 us
    ppermute x6, starting transfers between devices, exchange(): lax.ppermute(to[way - 1], 'seq', [(i, i ^ way) for i in every])  5.49 us
    pallas_call x1, Pallas kernels, body(): call(query_kernel, 'queries', [shape((tokens, width_q), bf16), flag], [VM...  4.67 us
    pallas_call x1, Pallas kernels, body(): call(functools.partial(mix_first_kernel, distances), 'mix_first', [shape(...  4.49 us
    pallas_call x1, Pallas kernels, body(): call(functools.partial(third_kernel, chunks), 'keys_values_more', [kv_sha...  4 us
    pallas_call x1, Pallas kernels, body(): call(functools.partial(mix_second_kernel, heads // 2, distances), 'mix_se...  3.2 us
    pallas_call x1, Pallas kernels, body(): call(functools.partial(first_kernel, chunks), 'keys_values_own', [shape((...  3.06 us
    pallas_call x1, Pallas kernels, body(): call(functools.partial(near_kernel, ((0, 0), (LAYER, LAYER))), 'scores_ne...  2.69 us
  transfers between devices with their start and end apart: 11, of which 4 were waited for; matrix products, arithmetic and copies ran while one was open for 0% of the time, Pallas kernels for 44%

profile of v5, /device:TPU:25, one launch (start us, length us, event | category | flops | bytes accessed | tf_op | source)
XLA Modules:
  0.0 48.5 jit_solution(936963371991327637)
XLA Ops:
  0.0 0.7 %collective-permute-start = (bf16[128,4096]{1,0:T(8,128)(2,1)}, bf16[128,4096]{1,0:T(8,128)(2,1)S(1)}, u32[]{:S(2)}, u32[]{:S(2)}) collective-permute-start(bf16[128,4096]{1,0:T(8,128)(2,1)} %own_hbm.1), channel_id=1, source_target_pairs={{0,1},{1,0},{2,3},{3,2},{4,5},{5,4},{6,7},{7,6},{8,9},{9,8},{10,11... | collective-permute-start | bytes 3145736 | tf_op jit(solution)/shard_map/ppermute | solution.py:353
  0.7 3.1 %keys_values_own.1 = (f32[128,512]{1,0:T(8,128)S(1)}, bf16[128,4096]{1,0:T(8,128)(2,1)S(1)}, bf16[4096,256]{1,0:T(8,128)(2,1)S(1)}, bf16[4096,256]{1,0:T(8,128)(...) custom-call(s32[8]{0:T(128)} %lengths_hbm.1, bf16[128,4096]{1,0:T(8,128)(2,1)} %own_hbm.1, ...), custom_call_target="tpu_custom_call" | custom-call | flops 536870912 | bytes 4194304 | tf_op jit(solution)/shard_map/keys_values_own/pallas_call | solution.py:362
  3.8 0.8 %keys_values.1.own.refs_0_ = bf16[256,512]{1,0:T(8,128)(2,1)S(1)} custom-call(bf16[128,4096]{1,0:T(8,128)(2,1)S(1)} %collective-permute-done.other, bf16[4096,256]{1,0:T(8,128)(2,1)S(1)} %get-tuple-element.34.w_key, bf16[4096,256]{1,0:T(8,128)(2,1)S(1)} %get-tuple-element.35.w_value, f32[128,512]{1,0:T(8,128)S(1)} %get-tuple-element.36.own_total, ...), custom_call_target="tpu_custom_call" | custom-call | flops 536870912 | bytes 4194304 | tf_op jit(solution)/shard_map/keys_values/pallas_call | solution.py:371
  4.5 1.3 %collective-permute-start.1 = (bf16[256,512]{1,0:T(8,128)(2,1)S(1)}, bf16[256,512]{1,0:T(8,128)(2,1)S(1)}, u32[]{:S(2)}, u32[]{:S(2)}) collective-permute-start(bf16[256,512]{1,0:T(8,128)(2,1)S(1)} %keys_values.1.own.refs_0_), channel_id=1, source_target_pairs={{0,8},{2,10},{4,12},{6,14},{8,16},{10,18},{12,20},{14,22},{16,24},... | collective-permute-start | bytes 786440 | tf_op jit(solution)/shard_map/ppermute | solution.py:377
  5.8 0.0 slice-start.4
  5.9 4.0 %keys_values_more.1 = (bf16[256,512]{1,0:T(8,128)(2,1)S(1)}, bf16[256,4096]{1,0:T(8,128)(2,1)S(1)}, f32[8,128]{1,0:T(8,128)S(1)}) custom-call(bf16[128,4096]{1,0:T(8,128)(2,1)S(1)} %get-tuple-element.30.own, bf16[128,4096]{1,0:T(8,128)(2,1)S(1)} %collective-permute-done.other, bf16[4096,512]{1,0:T(8,128)(2,1)} %key_hbm.3, bf16[4096,512]{1,0:T(8,128)(2,1)} %value_hbm.3, ...), custom_call_target="tpu_custom_call" | custom-call | flops 4294967296 | bytes 4194304 | tf_op jit(solution)/shard_map/keys_values_more/pallas_call | solution.py:379
  9.9 2.1 %collective-permute-start.2 = (bf16[256,512]{1,0:T(8,128)(2,1)S(1)}, bf16[256,512]{1,0:T(8,128)(2,1)S(1)}, u32[]{:S(2)}, u32[]{:S(2)}) collective-permute-start(bf16[256,512]{1,0:T(8,128)(2,1)S(1)} %get-tuple-element.40.own.refs_2_), channel_id=1, source_target_pairs={{0,8},{2,10},{4,12},{6,14},{8,16},{10,18},{12,20},{14,22},{16,24},... | collective-permute-start | bytes 786440 | tf_op jit(solution)/shard_map/ppermute | solution.py:384
  12.0 2.4 %collective-permute-done.1.earlier.refs_1_ = bf16[256,512]{1,0:T(8,128)(2,1)S(1)} collective-permute-done((bf16[256,512]{1,0:T(8,128)(2,1)S(1)}, bf16[256,512]{1,0:T(8,128)(2,1)S(1)}, u32[]{:S(2)}, u32[]{:S(2)}) %collective-permute-start.1) | collective-permute-done | bytes 262176 | tf_op jit(solution)/shard_map/ppermute | solution.py:377
  14.4 0.1 relay.2
  14.5 1.3 %collective-permute-start.6 = (bf16[256,512]{1,0:T(8,128)(2,1)S(1)}, bf16[256,512]{1,0:T(8,128)(2,1)S(1)}, u32[]{:S(2)}, u32[]{:S(2)}) collective-permute-start(bf16[256,512]{1,0:T(8,128)(2,1)S(1)} %get-tuple-element.38.after), channel_id=1, source_target_pairs={{0,2},{2,0},{4,6},{6,4},{8,10},{10,8},{12,14},{14,12},{16,18},{18,... | collective-permute-start | bytes 786440 | tf_op jit(solution)/shard_map/ppermute | solution.py:390
  15.7 1.2 %collective-permute-start.7 = (bf16[256,512]{1,0:T(8,128)(2,1)S(1)}, bf16[256,512]{1,0:T(8,128)(2,1)S(1)}, u32[]{:S(2)}, u32[]{:S(2)}) collective-permute-start(bf16[256,512]{1,0:T(8,128)(2,1)S(1)} %get-tuple-element.48), channel_id=1, source_target_pairs={{0,4},{2,6},{4,0},{6,2},{8,12},{10,14},{12,8},{14,10},{16,20},{18,... | collective-permute-start | bytes 786440 | tf_op jit(solution)/shard_map/ppermute | solution.py:390
  17.0 0.2 collective-permute-start.8
  17.2 0.7 %slice-done.7 = s8[4194304]{0:T(1024)(128)(4,1)S(1)} async-done(((s8[16777216]{0:T(1024)(128)(4,1)}), s8[4194304]{0:T(1024)(128)(4,1)S(1)}, s32[]{:S(2)}) %slice-start.7) | async-done | bytes 4194328
  17.8 4.7 %queries.1 = (bf16[256,2048]{1,0:T(8,128)(2,1)S(1)}, f32[8,128]{1,0:T(8,128)S(1)}) custom-call(bf16[256,4096]{1,0:T(8,128)(2,1)S(1)} %get-tuple-element.33.rows, bf16[4096,2048]{1,0:T(8,128)(2,1)S(1)} %bitcast.3, f32[256,128]{1,0:T(8,128)S(1)} %get-tuple-element.31.cosine, f32[256,128]{1,0:T(8,128)S(1)} %get-tuple-element.32.sine, ...), custom_call_target="tpu_custom_call" | custom-call | flops 4294967296 | bytes 16777216 | tf_op jit(solution)/shard_map/queries/pallas_call | solution.py:394
  22.5 0.0 slice-start
  22.6 0.1 relay.3
  22.7 1.3 %collective-permute-start.3 = (bf16[256,512]{1,0:T(8,128)(2,1)S(1)}, bf16[256,512]{1,0:T(8,128)(2,1)S(1)}, u32[]{:S(2)}, u32[]{:S(2)}) collective-permute-start(bf16[256,512]{1,0:T(8,128)(2,1)S(1)} %get-tuple-element.42), channel_id=1, source_target_pairs={{0,2},{2,0},{4,6},{6,4},{8,10},{10,8},{12,14},{14,12},{16,18},{18,... | collective-permute-start | bytes 786440 | tf_op jit(solution)/shard_map/ppermute | solution.py:390
  23.9 1.2 %collective-permute-start.4 = (bf16[256,512]{1,0:T(8,128)(2,1)S(1)}, bf16[256,512]{1,0:T(8,128)(2,1)S(1)}, u32[]{:S(2)}, u32[]{:S(2)}) collective-permute-start(bf16[256,512]{1,0:T(8,128)(2,1)S(1)} %get-tuple-element.43), channel_id=1, source_target_pairs={{0,4},{2,6},{4,0},{6,2},{8,12},{10,14},{12,8},{14,10},{16,20},{18,... | collective-permute-start | bytes 786440 | tf_op jit(solution)/shard_map/ppermute | solution.py:390
  25.2 2.7 %scores_near.1 = (f32[16,256,128]{2,1,0:T(8,128)S(1)}, f32[16,256,128]{2,1,0:T(8,128)S(1)}, f32[16,256,128]{2,1,0:T(8,128)S(1)}) custom-call(s32[256,128]{1,0:T(8,128)S(1)} %get-tuple-element.29.starts, bf16[256,2048]{1,0:T(8,128)(2,1)S(1)} %get-tuple-element.39.query, bf16[256,512]{1,0:T(8,128)(2,1)S(1)} %keys_values.1.own.refs_0_, ...), custom_call_target="tpu_custom_call" | custom-call | flops 1073741824 | bytes 8388608 | tf_op jit(solution)/shard_map/scores_near/pallas_call | solution.py:399
  27.9 0.3 collective-permute-start.5
  28.2 0.2 slice-done.3
  28.4 4.5 %mix_first.1 = (f32[256,4096]{1,0:T(8,128)S(1)}, bf16[256,1024]{1,0:T(8,128)(2,1)}) custom-call(s32[256,128]{1,0:T(8,128)S(1)} %get-tuple-element.29.starts, bf16[256,2048]{1,0:T(8,128)(2,1)S(1)} %get-tuple-element.39.query, bf16[256,512]{1,0:T(8,128)(2,1)S(1)} %collective-permute-done.6.refs_0_, bf16[256,512]{1,0:T(8,128)(2,1)S(1)} %collective-permute-done.7.refs_1_, ...), custom_call_target="tpu_custom_call" | custom-call | flops 3355443200 | bytes 4194304 | tf_op jit(solution)/shard_map/mix_first/pallas_call | solution.py:411
  32.9 3.7 %collective-permute-done.4.refs_1_ = bf16[256,512]{1,0:T(8,128)(2,1)S(1)} collective-permute-done((bf16[256,512]{1,0:T(8,128)(2,1)S(1)}, bf16[256,512]{1,0:T(8,128)(2,1)S(1)}, u32[]{:S(2)}, u32[]{:S(2)}) %collective-permute-start.4) | collective-permute-done | bytes 262176 | tf_op jit(solution)/shard_map/ppermute | solution.py:390
  36.6 2.4 %collective-permute-done.5.refs_2_ = bf16[256,512]{1,0:T(8,128)(2,1)S(1)} collective-permute-done((bf16[256,512]{1,0:T(8,128)(2,1)S(1)}, bf16[256,512]{1,0:T(8,128)(2,1)S(1)}, u32[]{:S(2)}, u32[]{:S(2)}) %collective-permute-start.5) | collective-permute-done | bytes 262176 | tf_op jit(solution)/shard_map/ppermute | solution.py:390
  39.0 3.2 %mix_second.1 = (bf16[128,2048]{1,0:T(8,128)(2,1)S(1)}, bf16[256,1024]{1,0:T(8,128)(2,1)S(1)}) custom-call(s32[256,128]{1,0:T(8,128)S(1)} %get-tuple-element.29.starts, bf16[256,2048]{1,0:T(8,128)(2,1)S(1)} %get-tuple-element.39.query, bf16[256,512]{1,0:T(8,128)(2,1)S(1)} %collective-permute-done.3.refs_0_, ...), custom_call_target="tpu_custom_call" | custom-call | flops 1744830464 | bytes 4194304 | tf_op jit(solution)/shard_map/mix_second/pallas_call | solution.py:419
  42.2 2.3 %collective-permute-start.9 = (bf16[128,2048]{1,0:T(8,128)(2,1)S(1)}, bf16[128,2048]{1,0:T(8,128)(2,1)S(1)}, u32[]{:S(2)}, u32[]{:S(2)}) collective-permute-start(bf16[128,2048]{1,0:T(8,128)(2,1)S(1)} %get-tuple-element.52), channel_id=1, source_target_pairs={{0,1},{1,0},{2,3},{3,2},{4,5},{5,4},{6,7},{7,6},{8,9},{9,8},{10,11... | collective-permute-start | bytes 1572872 | tf_op jit(solution)/shard_map/ppermute | solution.py:423
  44.6 0.7 %send_high.1 = bf16[128,2048]{1,0:T(8,128)(2,1)S(1)} custom-call(bf16[256,1024]{1,0:T(8,128)(2,1)S(1)} %get-tuple-element.51.attended, bf16[2048,4096]{1,0:T(8,128)(2,1)S(1)} %bitcast.1, f32[256,4096]{1,0:T(8,128)S(1)} %get-tuple-element.50.refs_7_.summed), custom_call_target="tpu_custom_call" | custom-call | flops 536870912 | bytes 4194304 | tf_op jit(solution)/shard_map/send_high/pallas_call | solution.py:424
  45.3 0.1 collective-permute-start.10
  45.4 0.7 %own_high.1.after.own = f32[128,2048]{1,0:T(8,128)S(1)} custom-call(bf16[256,1024]{1,0:T(8,128)(2,1)S(1)} %get-tuple-element.51.attended, bf16[2048,4096]{1,0:T(8,128)(2,1)S(1)} %bitcast.1, f32[256,4096]{1,0:T(8,128)S(1)} %get-tuple-element.50.refs_7_.summed), custom_call_target="tpu_custom_call" | custom-call | flops 536870912 | bytes 4194304 | tf_op jit(solution)/shard_map/own_high/pallas_call | solution.py:428
  46.1 0.7 %own_low.1.mixed_low = bf16[128,2048]{1,0:T(8,128)(2,1)S(1)} custom-call(bf16[256,1024]{1,0:T(8,128)(2,1)S(1)} %get-tuple-element.51.attended, bf16[2048,4096]{1,0:T(8,128)(2,1)S(1)} %bitcast.1, f32[256,4096]{1,0:T(8,128)S(1)} %get-tuple-element.50.refs_7_.summed, bf16[128,2048]{1,0:T(8,128)(2,1)S(1)} %collective-permute-done.9.got, ...), custom_call_target="tpu_custom_call" | custom-call | flops 536870912 | bytes 4194304 | tf_op jit(solution)/shard_map/own_low/pallas_call | solution.py:432
  46.9 0.4 collective-permute-done.10.got
  47.3 1.0 %add.1 = bf16[128,4096]{1,0:T(8,128)(2,1)} custom-call(bf16[128,2048]{1,0:T(8,128)(2,1)S(1)} %own_low.1.mixed_low, f32[128,2048]{1,0:T(8,128)S(1)} %own_high.1.after.own, bf16[128,2048]{1,0:T(8,128)(2,1)S(1)} %collective-permute-done.10.got), custom_call_target="tpu_custom_call" | custom-call | flops 262144 | bytes 4194304 | tf_op jit(solution)/shard_map/add/pallas_call | solution.py:435
  (21 shorter events, 0.0 us)
Async XLA Ops:
  0.0 3.7 %collective-permute-start = (bf16[128,4096]{1,0:T(8,128)(2,1)}, bf16[128,4096]{1,0:T(8,128)(2,1)S(1)}, u32[]{:S(2)}, u32[]{:S(2)}) collective-permute-start(bf16[128,4096]{1,0:T(8,128)(2,1)} %own_hbm.1), channel_id=1, source_target_pairs={{0,1},{1,0},{2,3},{3,2},{4,5},{5,4},{6,7},{7,6},{8,9},{9,8},{10,11... | collective-permute-start | bytes 3145736 | tf_op jit(solution)/shard_map/ppermute | solution.py:353
  4.5 9.8 %collective-permute-start.1 = (bf16[256,512]{1,0:T(8,128)(2,1)S(1)}, bf16[256,512]{1,0:T(8,128)(2,1)S(1)}, u32[]{:S(2)}, u32[]{:S(2)}) collective-permute-start(bf16[256,512]{1,0:T(8,128)(2,1)S(1)} %keys_values.1.own.refs_0_), channel_id=1, source_target_pairs={{0,8},{2,10},{4,12},{6,14},{8,16},{10,18},{12,20},{14,22},{16,24},... | collective-permute-start | bytes 786440 | tf_op jit(solution)/shard_map/ppermute | solution.py:377
  5.8 11.3 %slice-start.4 = ((s8[16777216]{0:T(1024)(128)(4,1)}), s8[4194304]{0:T(1024)(128)(4,1)S(1)}, s32[]{:S(2)}) async-start(s8[16777216]{0:T(1024)(128)(4,1)} %bitcast.2), calls=%async_computation.4 | async-start | bytes 8388608
  5.9 11.3 %slice-start.5 = ((s8[16777216]{0:T(1024)(128)(4,1)}), s8[4194304]{0:T(1024)(128)(4,1)S(1)}, s32[]{:S(2)}) async-start(s8[16777216]{0:T(1024)(128)(4,1)} %bitcast.2), calls=%async_computation.5 | async-start | bytes 8388608
  9.9 12.6 %collective-permute-start.2 = (bf16[256,512]{1,0:T(8,128)(2,1)S(1)}, bf16[256,512]{1,0:T(8,128)(2,1)S(1)}, u32[]{:S(2)}, u32[]{:S(2)}) collective-permute-start(bf16[256,512]{1,0:T(8,128)(2,1)S(1)} %get-tuple-element.40.own.refs_2_), channel_id=1, source_target_pairs={{0,8},{2,10},{4,12},{6,14},{8,16},{10,18},{12,20},{14,22},{16,24},... | collective-permute-start | bytes 786440 | tf_op jit(solution)/shard_map/ppermute | solution.py:384
  14.4 2.8 %slice-start.6 = ((s8[16777216]{0:T(1024)(128)(4,1)}), s8[4194304]{0:T(1024)(128)(4,1)S(1)}, s32[]{:S(2)}) async-start(s8[16777216]{0:T(1024)(128)(4,1)} %bitcast.2), calls=%async_computation.6 | async-start | bytes 8388608
  14.4 3.5 %slice-start.7 = ((s8[16777216]{0:T(1024)(128)(4,1)}), s8[4194304]{0:T(1024)(128)(4,1)S(1)}, s32[]{:S(2)}) async-start(s8[16777216]{0:T(1024)(128)(4,1)} %bitcast.2), calls=%async_computation.7 | async-start | bytes 8388608
  14.5 13.4 %collective-permute-start.6 = (bf16[256,512]{1,0:T(8,128)(2,1)S(1)}, bf16[256,512]{1,0:T(8,128)(2,1)S(1)}, u32[]{:S(2)}, u32[]{:S(2)}) collective-permute-start(bf16[256,512]{1,0:T(8,128)(2,1)S(1)} %get-tuple-element.38.after), channel_id=1, source_target_pairs={{0,2},{2,0},{4,6},{6,4},{8,10},{10,8},{12,14},{14,12},{16,18},{18,... | collective-permute-start | bytes 786440 | tf_op jit(solution)/shard_map/ppermute | solution.py:390
  15.7 12.4 %collective-permute-start.7 = (bf16[256,512]{1,0:T(8,128)(2,1)S(1)}, bf16[256,512]{1,0:T(8,128)(2,1)S(1)}, u32[]{:S(2)}, u32[]{:S(2)}) collective-permute-start(bf16[256,512]{1,0:T(8,128)(2,1)S(1)} %get-tuple-element.48), channel_id=1, source_target_pairs={{0,4},{2,6},{4,0},{6,2},{8,12},{10,14},{12,8},{14,10},{16,20},{18,... | collective-permute-start | bytes 786440 | tf_op jit(solution)/shard_map/ppermute | solution.py:390
  17.0 11.2 %collective-permute-start.8 = (bf16[256,512]{1,0:T(8,128)(2,1)S(1)}, bf16[256,512]{1,0:T(8,128)(2,1)S(1)}, u32[]{:S(2)}, u32[]{:S(2)}) collective-permute-start(bf16[256,512]{1,0:T(8,128)(2,1)S(1)} %get-tuple-element.49), channel_id=1, source_target_pairs={{0,6},{2,4},{4,2},{6,0},{8,14},{10,12},{12,10},{14,8},{16,22},{18,... | collective-permute-start | bytes 786440 | tf_op jit(solution)/shard_map/ppermute | solution.py:390
  22.5 5.6 %slice-start = ((s8[16777216]{0:T(1024)(128)(4,1)}), s8[4194304]{0:T(1024)(128)(4,1)S(1)}, s32[]{:S(2)}) async-start(s8[16777216]{0:T(1024)(128)(4,1)} %bitcast), calls=%async_computation | async-start | bytes 8388608
  22.5 5.6 %slice-start.1 = ((s8[16777216]{0:T(1024)(128)(4,1)}), s8[4194304]{0:T(1024)(128)(4,1)S(1)}, s32[]{:S(2)}) async-start(s8[16777216]{0:T(1024)(128)(4,1)} %bitcast), calls=%async_computation.1 | async-start | bytes 8388608
  22.6 5.6 %slice-start.2 = ((s8[16777216]{0:T(1024)(128)(4,1)}), s8[4194304]{0:T(1024)(128)(4,1)S(1)}, s32[]{:S(2)}) async-start(s8[16777216]{0:T(1024)(128)(4,1)} %bitcast), calls=%async_computation.2 | async-start | bytes 8388608
  22.6 5.8 %slice-start.3 = ((s8[16777216]{0:T(1024)(128)(4,1)}), s8[4194304]{0:T(1024)(128)(4,1)S(1)}, s32[]{:S(2)}) async-start(s8[16777216]{0:T(1024)(128)(4,1)} %bitcast), calls=%async_computation.3 | async-start | bytes 8388608
  22.7 10.2 %collective-permute-start.3 = (bf16[256,512]{1,0:T(8,128)(2,1)S(1)}, bf16[256,512]{1,0:T(8,128)(2,1)S(1)}, u32[]{:S(2)}, u32[]{:S(2)}) collective-permute-start(bf16[256,512]{1,0:T(8,128)(2,1)S(1)} %get-tuple-element.42), channel_id=1, source_target_pairs={{0,2},{2,0},{4,6},{6,4},{8,10},{10,8},{12,14},{14,12},{16,18},{18,... | collective-permute-start | bytes 786440 | tf_op jit(solution)/shard_map/ppermute | solution.py:390
  23.9 12.7 %collective-permute-start.4 = (bf16[256,512]{1,0:T(8,128)(2,1)S(1)}, bf16[256,512]{1,0:T(8,128)(2,1)S(1)}, u32[]{:S(2)}, u32[]{:S(2)}) collective-permute-start(bf16[256,512]{1,0:T(8,128)(2,1)S(1)} %get-tuple-element.43), channel_id=1, source_target_pairs={{0,4},{2,6},{4,0},{6,2},{8,12},{10,14},{12,8},{14,10},{16,20},{18,... | collective-permute-start | bytes 786440 | tf_op jit(solution)/shard_map/ppermute | solution.py:390
  27.9 11.2 %collective-permute-start.5 = (bf16[256,512]{1,0:T(8,128)(2,1)S(1)}, bf16[256,512]{1,0:T(8,128)(2,1)S(1)}, u32[]{:S(2)}, u32[]{:S(2)}) collective-permute-start(bf16[256,512]{1,0:T(8,128)(2,1)S(1)} %get-tuple-element.44), channel_id=1, source_target_pairs={{0,6},{2,4},{4,2},{6,0},{8,14},{10,12},{12,10},{14,8},{16,22},{18,... | collective-permute-start | bytes 786440 | tf_op jit(solution)/shard_map/ppermute | solution.py:390
  42.2 3.9 %collective-permute-start.9 = (bf16[128,2048]{1,0:T(8,128)(2,1)S(1)}, bf16[128,2048]{1,0:T(8,128)(2,1)S(1)}, u32[]{:S(2)}, u32[]{:S(2)}) collective-permute-start(bf16[128,2048]{1,0:T(8,128)(2,1)S(1)} %get-tuple-element.52), channel_id=1, source_target_pairs={{0,1},{1,0},{2,3},{3,2},{4,5},{5,4},{6,7},{7,6},{8,9},{9,8},{10,11... | collective-permute-start | bytes 1572872 | tf_op jit(solution)/shard_map/ppermute | solution.py:423
  45.3 2.0 %collective-permute-start.10 = (bf16[128,2048]{1,0:T(8,128)(2,1)S(1)}, bf16[128,2048]{1,0:T(8,128)(2,1)S(1)}, u32[]{:S(2)}, u32[]{:S(2)}) collective-permute-start(bf16[128,2048]{1,0:T(8,128)(2,1)S(1)} %send_high.1), channel_id=1, source_target_pairs={{0,1},{1,0},{2,3},{3,2},{4,5},{5,4},{6,7},{7,6},{8,9},{9,8},{10,11... | collective-permute-start | bytes 1572872 | tf_op jit(solution)/shard_map/ppermute | solution.py:427

commit v6 on v5

--- a/solution.py
+++ b/solution.py
@@ -159,14 +159,13 @@
             query[:, out] = rotated(result[:, at], cosine[...], sine[...]).astype(query.dtype)
 
 
-def relay_kernel(own, earlier, after, to_x, to_y, to_d):
-    del after
+def relay_kernel(plan, own, earlier, *refs):
+    outs = refs[len(refs) - len(plan) :]
     index = lax.axis_index("seq")
-    mine, theirs = own[...], earlier[...]
-    to_x[...] = jnp.where(index % 2 > 0, theirs, mine)
-    by_y = jnp.where(index % LAYER >= 2, theirs, mine)
-    to_y[...] = by_y
-    to_d[...] = by_y
+    for (way, heads), out in zip(plan, outs):
+        upper = index % 2 > 0 if way == 1 else index % LAYER >= 2
+        for number, head in enumerate(heads):
+            out[:, column(number)] = jnp.where(upper, earlier[:, column(head)], own[:, column(head)])
 
 
 def column(number):
@@ -186,7 +185,7 @@
         bias[:, number * tokens : (number + 1) * tokens] = jnp.where(allowed, 0.0, MASKED)
 
 
-def scores_of(query, keys, bias, head, at):
+def scores_of(query, keys, bias, head):
     tokens = bias.shape[0]
     return [
         lax.dot_general(
@@ -194,13 +193,13 @@
         )
         * SCORE_SCALE
         + bias[:, number * tokens : (number + 1) * tokens]
-        for number, key in enumerate(keys)
+        for number, (key, at) in enumerate(keys)
     ]
 
 
-def weighted(weights, blocks, at, ones):
+def weighted(weights, blocks, ones):
     product = None
-    for weight, block in zip(weights, blocks):
+    for weight, (block, at) in zip(weights, blocks):
         term = dot(weight, jnp.concatenate([block[:, column(at)], ones], axis=1))
         product = term if product is None else product + term
     return product[:, :HEAD_SIZE], product[:, HEAD_SIZE:]
@@ -226,7 +225,7 @@
 
     def ask(head):
         blocks, at = place(head)
-        return scores_of(query, blocks, bias, head, at)
+        return scores_of(query, [(block, at) for block in blocks], bias, head)
 
     scores = ask(0)
     for head in range(heads):
@@ -235,27 +234,30 @@
         blocks, at = place(head)
         weights = [jnp.exp2(score - top).astype(query.dtype) for score in scores]
         tops[head] = jnp.broadcast_to(top, (tokens, HEAD_SIZE))
-        accs[head], totals[head] = weighted(weights, blocks, kv_part + at, ones)
+        accs[head], totals[head] = weighted(weights, [(block, kv_part + at) for block in blocks], ones)
         scores = ahead
 
 
-def attend_far(low, distances, starts, query, blocks, state, attended, bias):
+def attend_far(low, places, distances, starts, query, blocks, state, attended, bias):
     tops, totals, accs = state
     fill_bias(bias, distances, starts)
     tokens = query.shape[0]
     heads = attended.shape[1] // HEAD_SIZE
-    kv_part = blocks[0].shape[1] // (2 * HEAD_SIZE)
-    group = heads // kv_part
+    group = heads // len(places)
     ones = jnp.ones((tokens, HEAD_SIZE), query.dtype)
-    scores = scores_of(query, blocks, bias, low, 0)
+
+    def ask(head):
+        return scores_of(query, list(zip(blocks, places[head // group][0])), bias, low + head)
+
+    scores = ask(0)
     for head in range(heads):
-        ahead = scores_of(query, blocks, bias, low + head + 1, (head + 1) // group) if head + 1 < heads else None
+        ahead = ask(head + 1) if head + 1 < heads else None
         before = tops[low + head]
         top = jnp.maximum(jnp.broadcast_to(row_max(scores), (tokens, HEAD_SIZE)), before)
         factor = jnp.exp2(before - top)
         wide_top = jnp.concatenate([top] * (tokens // HEAD_SIZE), axis=1)
         weights = [jnp.exp2(score - wide_top).astype(query.dtype) for score in scores]
-        acc, total = weighted(weights, blocks, kv_part + head // group, ones)
+        acc, total = weighted(weights, list(zip(blocks, places[head // group][1])), ones)
         result = (accs[low + head] * factor + acc) / (totals[low + head] * factor + total)
         attended[:, column(head)] = result.astype(attended.dtype)
         scores = ahead
@@ -264,18 +266,23 @@
 WIDE = 4 * HEAD_SIZE
 
 
-def mix_first_kernel(distances, starts, query, *refs):
+def mix_first_kernel(places, distances, starts, query, *refs):
     far = len(distances)
     blocks, state, (weight, summed, attended, bias) = refs[:far], refs[far : far + 3], refs[far + 3 :]
-    attend_far(0, distances, starts, query, blocks, state, attended, bias)
-    depth = attended.shape[1]
+    attend_far(0, places, distances, starts, query, blocks, state, attended, bias)
     for number in range(summed.shape[1] // WIDE):
         at = slice(number * WIDE, (number + 1) * WIDE)
-        summed[:, at] = dot(attended[...], weight[:depth, at])
+        summed[:, at] = dot(attended[...], weight[: attended.shape[1], at])
+
+
+def attend_kernel(low, places, distances, starts, query, *refs):
+    far = len(distances)
+    blocks, state, (attended, bias) = refs[:far], refs[far : far + 3], refs[far + 3 :]
+    attend_far(low, places, distances, starts, query, blocks, state, attended, bias)
 
 
 def rows_product(rows, low, attended, weight, summed, wide):
-    depth = attended.shape[1]
+    depth = weight.shape[0] - attended.shape[1]
     at = slice(low, low + wide)
     return summed[rows, at] + dot(attended[rows, :], weight[depth:, at])
 
@@ -287,10 +294,14 @@
         send[:, number * WIDE : (number + 1) * WIDE] = result.astype(send.dtype)
 
 
-def mix_second_kernel(low, distances, starts, query, *refs):
+def mix_last_kernel(low, places, distances, starts, query, *refs):
     far = len(distances)
-    blocks, state, (weight, summed, send, attended, bias) = refs[:far], refs[far : far + 3], refs[far + 3 :]
-    attend_far(low, distances, starts, query, blocks, state, attended, bias)
+    blocks, state, refs = refs[:far], refs[far : far + 3], refs[far + 3 :]
+    before, weight, summed, send, attended, bias = refs
+    done = before.shape[1]
+    attended[:, :done] = before[...]
+    late = attended.at[:, pl.ds(done, attended.shape[1] - done)]
+    attend_far(low, places, distances, starts, query, blocks, state, late, bias)
     send_columns(0, attended, weight, summed, send)
 
 
@@ -383,43 +394,65 @@
     )(own, other, in_hbm(key_weight), in_hbm(value_weight), cosine, sine)
     z_b = lax.ppermute(kv_b, "seq", step_z)
 
-    def exchange(mine, earlier, after, ways, cost):
+    def exchange(mine, earlier, after, plan, cost):
         to = call(
-            relay_kernel, "relay", [kv_shape] * 3, [VMEM] * 3, cost, 2 << 20, 4,
-        )(mine, earlier, after)
-        got = {way: lax.ppermute(to[way - 1], "seq", [(i, i ^ way) for i in every]) for way in ways}
-        return [got[way] for way in (1, 2, 3)], to[0]
-
-    far_a, done = exchange(kv_a, z_a, done, (1, 2, 3), RELAY_COST)
+            functools.partial(relay_kernel, plan), "relay",
+            [shape((tokens, len(taken) * HEAD_SIZE), bf16) for _, taken in plan], [VMEM] * (2 + len(after)), cost, 2 << 20, 4,
+        )(mine, earlier, *after)
+        return [lax.ppermute(array, "seq", [(i, i ^ way) for i in every]) for (way, _), array in zip(plan, to)], to[0]
+
+    kv_part = part // HEAD_SIZE
+    kv_cut = kv_part // 2
+    everything = tuple(range(2 * kv_part))
+    early = tuple(range(kv_cut)) + tuple(range(kv_part, kv_part + kv_cut))
+    late = tuple(range(kv_cut, kv_part)) + tuple(range(kv_part + kv_cut, 2 * kv_part))
+    (x_a, y_a, d_a), done = exchange(kv_a, z_a, [kv_b], ((1, everything), (2, everything), (3, everything)), RELAY_COST)
+    far_a = d_a, x_a, y_a
     query, done = call(
         query_kernel, "queries", [shape((tokens, width_q), bf16), flag], [VMEM] * 5,
         2 * tokens * model * width_q, 2 * model * width_q, 8,
     )(rows, w_query, cosine, sine, done)
-    far_b, _ = exchange(kv_b, z_b, done, (3, 1, 2), 9 << 30)
+    (d_b,), _ = exchange(kv_b, z_b, [done], ((3, everything),), 9 << 30)
     near = call(
         functools.partial(near_kernel, ((0, 0), (LAYER, LAYER))), "scores_near", [shape((heads, tokens, HEAD_SIZE), f32)] * 3,
         [VMEM] * 6, 8 * heads * tokens * tokens * HEAD_SIZE, 8 << 20, 12, [pltpu.VMEM((tokens, 2 * tokens), f32)],
     )(starts, query, kv_a, z_a, kv_b, z_b)
+    (x_early, y_early), done = exchange(kv_b, z_b, [near[0]], ((1, early), (2, early)), 0)
+    (x_late, y_late), _ = exchange(kv_b, z_b, [done, *far_a], ((1, late), (2, late)), 0)
 
     far = len(far_a)
-    distances = ((3, 1), (2, 2), (1, 3))
+    distances = ((1, 3), (3, 1), (2, 2))
     bias = pltpu.VMEM((tokens, far * tokens), f32)
     columns = w_out.shape[1]
-    attended_shape = shape((tokens, width_q // 2), bf16)
-    far_flops = 3 * far * heads * tokens * tokens * HEAD_SIZE
-    out_flops = tokens * width_q * columns
+    far_flops = 6 * far * heads * tokens * tokens * HEAD_SIZE
+    out_flops = 2 * tokens * width_q * columns
+    heads_part, heads_cut = heads // 2, heads // 2 // kv_part * kv_cut
+    whole = [((head,) * far, (kv_part + head,) * far) for head in range(kv_part)]
+    places_early = [((n, n, n), (kv_part + n, kv_cut + n, kv_cut + n)) for n in range(kv_cut)]
+    rest = kv_part - kv_cut
+    places_late = [((kv_cut + n, n, n), (kv_part + kv_cut + n, rest + n, rest + n)) for n in range(rest)]
+
+    def attended_shape(count):
+        return shape((tokens, count * HEAD_SIZE), bf16)
+
     summed, _ = call(
-        functools.partial(mix_first_kernel, distances), "mix_first", [shape((tokens, columns), f32), attended_shape],
-        [VMEM] * (6 + far), out_flops + far_flops, 4 << 20, 10, [bias],
+        functools.partial(mix_first_kernel, whole, distances), "mix_first",
+        [shape((tokens, columns), f32), attended_shape(heads_part)], [VMEM] * (6 + far),
+        (out_flops + far_flops) // 2, 4 << 20, 10, [bias],
     )(starts, query, *far_a, *near, w_out)
+    (early_heads,) = call(
+        functools.partial(attend_kernel, heads_part, places_early, distances), "attend_early",
+        [attended_shape(heads_cut)], [VMEM] * (5 + far), far_flops // 4, 4 << 20, 10, [bias],
+    )(starts, query, d_b, x_early, y_early, *near)
 
     cut = columns // 2
     send_shape = shape((half, cut), bf16)
-    quarter = out_flops // 4
+    quarter = out_flops // 8
+    low = heads_part + heads_cut
     send, attended = call(
-        functools.partial(mix_second_kernel, heads // 2, distances), "mix_second", [send_shape, attended_shape],
-        [VMEM] * (7 + far), quarter + far_flops, 4 << 20, 10, [bias],
-    )(starts, query, *far_b, *near, w_out, summed)
+        functools.partial(mix_last_kernel, low, places_late, distances), "mix_last",
+        [send_shape, attended_shape(heads_part)], [VMEM] * (8 + far), quarter + far_flops // 4, 4 << 20, 10, [bias],
+    )(starts, query, d_b, x_late, y_late, *near, early_heads, w_out, summed)
     got_low = lax.ppermute(send, "head", SWAP)
     (send,) = call(
         functools.partial(send_columns, cut), "send_high", [send_shape], [VMEM] * 3, quarter, 4 << 20, 6,

time: 48.6 us -> 49.6 us (1.021)
  starting transfers between devices: 12 us -> 14.4 us
  waiting for transfers between devices: 8.95 us -> 7.47 us
  Pallas kernels: 26.2 us -> 27.1 us
  local copies, waits for them, and re-layouts: 0.91 us -> 0.05 us
    ppermute x6 -> x8, starting transfers between devices: 5.49 us -> 6.88 us  [exchange(): lax.ppermute(array, 'seq', [(i, i ^ way) for i in every])]
    ppermute x6 -> x8, waiting for transfers between devices: 6.15 us -> 4.88 us  [exchange(): lax.ppermute(array, 'seq', [(i, i ^ way) for i in every])]
    ppermute x1, starting transfers between devices: 2.33 us -> 3.32 us  [body(): got_low = lax.ppermute(send, 'head', SWAP)]
    unnamed x16, local copies, waits for them, and re-layouts: 0.91 us -> 0.05 us
    pallas_call x4 -> x7, Pallas kernels: 7.84 us -> 8.56 us  [the longest x1 4.49 us: body(): call(functools.partial(mix_first_kernel, whole, distances), 'mix_first',...]
  transfers between devices with their start and end apart: 11 -> 13, of which waited for: 4 -> 5; matrix products, arithmetic and copies ran while one was open for 0% -> 0% of each run, Pallas kernels for 44% -> 47%
where the time goes in v6:
time: 49.6 us; the launch traced here: 49.4 us
  Pallas kernels  27.1 us (55%)
  starting transfers between devices  14.4 us (29%)
  waiting for transfers between devices  7.47 us (15%)
    ppermute x8, starting transfers between devices, exchange(): lax.ppermute(array, 'seq', [(i, i ^ way) for i in every])  6.88 us
    ppermute x8, waiting for transfers between devices, exchange(): lax.ppermute(array, 'seq', [(i, i ^ way) for i in every])  4.88 us
    pallas_call x1, Pallas kernels, body(): call(query_kernel, 'queries', [shape((tokens, width_q), bf16), flag], [VM...  4.67 us
    pallas_call x1, Pallas kernels, body(): call(functools.partial(mix_first_kernel, whole, distances), 'mix_first',...  4.49 us
    pallas_call x1, Pallas kernels, body(): call(functools.partial(third_kernel, chunks), 'keys_values_more', [kv_sha...  4.19 us
    ppermute x1, starting transfers between devices, body(): got_low = lax.ppermute(send, 'head', SWAP)  3.32 us
    pallas_call x1, Pallas kernels, body(): call(functools.partial(first_kernel, chunks), 'keys_values_own', [shape((...  3.06 us
    pallas_call x1, Pallas kernels, body(): call(functools.partial(near_kernel, ((0, 0), (LAYER, LAYER))), 'scores_ne...  2.69 us
  transfers between devices with their start and end apart: 13, of which 5 were waited for; matrix products, arithmetic and copies ran while one was open for 0% of the time, Pallas kernels for 47%

profile of v6, /device:TPU:25, one launch (start us, length us, event | category | flops | bytes accessed | tf_op | source)
XLA Modules:
  0.0 49.4 jit_solution(7409080564984162289)
XLA Ops:
  0.0 0.7 %collective-permute-start = (bf16[128,4096]{1,0:T(8,128)(2,1)}, bf16[128,4096]{1,0:T(8,128)(2,1)S(1)}, u32[]{:S(2)}, u32[]{:S(2)}) collective-permute-start(bf16[128,4096]{1,0:T(8,128)(2,1)} %own_hbm.1), channel_id=1, source_target_pairs={{0,1},{1,0},{2,3},{3,2},{4,5},{5,4},{6,7},{7,6},{8,9},{9,8},{10,11... | collective-permute-start | bytes 3145736 | tf_op jit(solution)/shard_map/ppermute | solution.py:364
  0.7 3.1 %keys_values_own.1 = (f32[128,512]{1,0:T(8,128)S(1)}, bf16[128,4096]{1,0:T(8,128)(2,1)S(1)}, bf16[4096,256]{1,0:T(8,128)(2,1)S(1)}, bf16[4096,256]{1,0:T(8,128)(...) custom-call(s32[8]{0:T(128)} %lengths_hbm.1, bf16[128,4096]{1,0:T(8,128)(2,1)} %own_hbm.1, ...), custom_call_target="tpu_custom_call" | custom-call | flops 536870912 | bytes 4194304 | tf_op jit(solution)/shard_map/keys_values_own/pallas_call | solution.py:373
  3.8 0.8 %keys_values.1.own.refs_0_ = bf16[256,512]{1,0:T(8,128)(2,1)S(1)} custom-call(bf16[128,4096]{1,0:T(8,128)(2,1)S(1)} %collective-permute-done.other, bf16[4096,256]{1,0:T(8,128)(2,1)S(1)} %get-tuple-element.34.w_key, bf16[4096,256]{1,0:T(8,128)(2,1)S(1)} %get-tuple-element.35.w_value, f32[128,512]{1,0:T(8,128)S(1)} %get-tuple-element.36.own_total, ...), custom_call_target="tpu_custom_call" | custom-call | flops 536870912 | bytes 4194304 | tf_op jit(solution)/shard_map/keys_values/pallas_call | solution.py:382
  4.5 1.3 %collective-permute-start.1 = (bf16[256,512]{1,0:T(8,128)(2,1)S(1)}, bf16[256,512]{1,0:T(8,128)(2,1)S(1)}, u32[]{:S(2)}, u32[]{:S(2)}) collective-permute-start(bf16[256,512]{1,0:T(8,128)(2,1)S(1)} %keys_values.1.own.refs_0_), channel_id=1, source_target_pairs={{0,8},{2,10},{4,12},{6,14},{8,16},{10,18},{12,20},{14,22},{16,24},... | collective-permute-start | bytes 786440 | tf_op jit(solution)/shard_map/ppermute | solution.py:388
  5.9 4.2 %keys_values_more.1 = (bf16[256,512]{1,0:T(8,128)(2,1)S(1)}, bf16[256,4096]{1,0:T(8,128)(2,1)S(1)}, f32[8,128]{1,0:T(8,128)}) custom-call(bf16[128,4096]{1,0:T(8,128)(2,1)S(1)} %get-tuple-element.30.own, bf16[128,4096]{1,0:T(8,128)(2,1)S(1)} %collective-permute-done.other, bf16[4096,512]{1,0:T(8,128)(2,1)} %key_hbm.3, bf16[4096,512]{1,0:T(8,128)(2,1)} %value_hbm.3, ...), custom_call_target="tpu_custom_call" | custom-call | flops 4294967296 | bytes 4194304 | tf_op jit(solution)/shard_map/keys_values_more/pallas_call | solution.py:390
  10.1 2.1 %collective-permute-start.2 = (bf16[256,512]{1,0:T(8,128)(2,1)S(1)}, bf16[256,512]{1,0:T(8,128)(2,1)S(1)}, u32[]{:S(2)}, u32[]{:S(2)}) collective-permute-start(bf16[256,512]{1,0:T(8,128)(2,1)S(1)} %get-tuple-element.37.refs_0_.own.refs_2_), channel_id=1, source_target_pairs={{0,8},{2,10},{4,12},{6,14},{8,16},{10,18},{12,20},{14,22},{16,24},... | collective-permute-start | bytes 786440 | tf_op jit(solution)/shard_map/ppermute | solution.py:395
  12.2 2.2 %collective-permute-done.1.earlier.refs_1_ = bf16[256,512]{1,0:T(8,128)(2,1)S(1)} collective-permute-done((bf16[256,512]{1,0:T(8,128)(2,1)S(1)}, bf16[256,512]{1,0:T(8,128)(2,1)S(1)}, u32[]{:S(2)}, u32[]{:S(2)}) %collective-permute-start.1) | collective-permute-done | bytes 262176 | tf_op jit(solution)/shard_map/ppermute | solution.py:388
  14.4 0.2 relay.4
  14.6 2.2 %collective-permute-start.4 = (bf16[256,512]{1,0:T(8,128)(2,1)S(1)}, bf16[256,512]{1,0:T(8,128)(2,1)S(1)}, u32[]{:S(2)}, u32[]{:S(2)}) collective-permute-start(bf16[256,512]{1,0:T(8,128)(2,1)S(1)} %get-tuple-element.43), channel_id=1, source_target_pairs={{0,6},{2,4},{4,2},{6,0},{8,14},{10,12},{12,10},{14,8},{16,22},{18,... | collective-permute-start | bytes 786440 | tf_op jit(solution)/shard_map/ppermute | solution.py:402
  16.8 0.2 collective-permute-start.6
  17.0 0.3 collective-permute-start.5
  17.3 4.7 %queries.1 = (bf16[256,2048]{1,0:T(8,128)(2,1)S(1)}, f32[8,128]{1,0:T(8,128)S(1)}) custom-call(bf16[256,4096]{1,0:T(8,128)(2,1)S(1)} %get-tuple-element.33.rows, bf16[4096,2048]{1,0:T(8,128)(2,1)S(1)} %bitcast.3, f32[256,128]{1,0:T(8,128)S(1)} %get-tuple-element.31.cosine, f32[256,128]{1,0:T(8,128)S(1)} %get-tuple-element.32.sine, ...), custom_call_target="tpu_custom_call" | custom-call | flops 4294967296 | bytes 16777216 | tf_op jit(solution)/shard_map/queries/pallas_call | solution.py:411
  22.1 0.1 relay.5
  22.1 2.2 %collective-permute-start.3 = (bf16[256,512]{1,0:T(8,128)(2,1)S(1)}, bf16[256,512]{1,0:T(8,128)(2,1)S(1)}, u32[]{:S(2)}, u32[]{:S(2)}) collective-permute-start(bf16[256,512]{1,0:T(8,128)(2,1)S(1)} %relay.5), channel_id=1, source_target_pairs={{0,6},{2,4},{4,2},{6,0},{8,14},{10,12},{12,10},{14,8},{16,22},{18,... | collective-permute-start | bytes 786440 | tf_op jit(solution)/shard_map/ppermute | solution.py:402
  24.4 2.7 %scores_near.1 = (f32[16,256,128]{2,1,0:T(8,128)S(1)}, f32[16,256,128]{2,1,0:T(8,128)S(1)}, f32[16,256,128]{2,1,0:T(8,128)S(1)}) custom-call(s32[256,128]{1,0:T(8,128)S(1)} %get-tuple-element.29.starts, bf16[256,2048]{1,0:T(8,128)(2,1)S(1)} %get-tuple-element.39.query, bf16[256,512]{1,0:T(8,128)(2,1)S(1)} %keys_values.1.own.refs_0_, ...), custom_call_target="tpu_custom_call" | custom-call | flops 1073741824 | bytes 8388608 | tf_op jit(solution)/shard_map/scores_near/pallas_call | solution.py:416
  27.2 0.3 collective-permute-start.10
  27.4 0.3 collective-permute-start.9
  27.7 3.2 %collective-permute-done.6.refs_3_.refs_2_ = bf16[256,512]{1,0:T(8,128)(2,1)S(1)} collective-permute-done((bf16[256,512]{1,0:T(8,128)(2,1)S(1)}, bf16[256,512]{1,0:T(8,128)(2,1)S(1)}, u32[]{:S(2)}, u32[]{:S(2)}) %collective-permute-start.6) | collective-permute-done | bytes 262176 | tf_op jit(solution)/shard_map/ppermute | solution.py:402
  31.0 1.3 %collective-permute-start.7 = (bf16[256,256]{1,0:T(8,128)(2,1)S(1)}, bf16[256,256]{1,0:T(8,128)(2,1)S(1)}, u32[]{:S(2)}, u32[]{:S(2)}) collective-permute-start(bf16[256,256]{1,0:T(8,128)(2,1)S(1)} %get-tuple-element.45), channel_id=1, source_target_pairs={{0,2},{2,0},{4,6},{6,4},{8,10},{10,8},{12,14},{14,12},{16,18},{18,... | collective-permute-start | bytes 393224 | tf_op jit(solution)/shard_map/ppermute | solution.py:402
  32.3 0.1 collective-permute-start.8
  32.4 4.5 %mix_first.1 = (f32[256,4096]{1,0:T(8,128)S(1)}, bf16[256,1024]{1,0:T(8,128)(2,1)}) custom-call(s32[256,128]{1,0:T(8,128)S(1)} %get-tuple-element.29.starts, bf16[256,2048]{1,0:T(8,128)(2,1)S(1)} %get-tuple-element.39.query, bf16[256,512]{1,0:T(8,128)(2,1)S(1)} %collective-permute-done.4.refs_1_.refs_0_, ...), custom_call_target="tpu_custom_call" | custom-call | flops 3355443200 | bytes 4194304 | tf_op jit(solution)/shard_map/mix_first/pallas_call | solution.py:438
  36.9 0.8 %collective-permute-done.10.refs_2_ = bf16[256,256]{1,0:T(8,128)(2,1)S(1)} collective-permute-done((bf16[256,256]{1,0:T(8,128)(2,1)S(1)}, bf16[256,256]{1,0:T(8,128)(2,1)S(1)}, u32[]{:S(2)}, u32[]{:S(2)}) %collective-permute-start.10) | collective-permute-done | bytes 131104 | tf_op jit(solution)/shard_map/ppermute | solution.py:402
  37.7 1.6 %attend_early.1.refs_6_ = bf16[256,512]{1,0:T(8,128)(2,1)S(1)} custom-call(s32[256,128]{1,0:T(8,128)S(1)} %get-tuple-element.29.starts, bf16[256,2048]{1,0:T(8,128)(2,1)S(1)} %get-tuple-element.39.query, bf16[256,512]{1,0:T(8,128)(2,1)S(1)} %collective-permute-done.3.refs_0_, bf16[256,256]{1,0:T(8,128)(2,1)S(1)} %collective-permute-done.9.refs_1_, ...), custom_call_target="tpu_custom_call" | custom-call | flops 603979776 | bytes 4194304 | tf_op jit(solution)/shard_map/attend_early/pallas_call | solution.py:443
  39.4 0.8 %collective-permute-done.8.refs_2_ = bf16[256,256]{1,0:T(8,128)(2,1)S(1)} collective-permute-done((bf16[256,256]{1,0:T(8,128)(2,1)S(1)}, bf16[256,256]{1,0:T(8,128)(2,1)S(1)}, u32[]{:S(2)}, u32[]{:S(2)}) %collective-permute-start.8) | collective-permute-done | bytes 131104 | tf_op jit(solution)/shard_map/ppermute | solution.py:402
  40.2 2.0 %mix_last.1 = (bf16[128,2048]{1,0:T(8,128)(2,1)S(1)}, bf16[256,1024]{1,0:T(8,128)(2,1)S(1)}) custom-call(s32[256,128]{1,0:T(8,128)S(1)} %get-tuple-element.29.starts, bf16[256,2048]{1,0:T(8,128)(2,1)S(1)} %get-tuple-element.39.query, bf16[256,512]{1,0:T(8,128)(2,1)S(1)} %collective-permute-done.3.refs_0_, ...), custom_call_target="tpu_custom_call" | custom-call | flops 1140850688 | bytes 4194304 | tf_op jit(solution)/shard_map/mix_last/pallas_call | solution.py:452
  42.2 3.3 %collective-permute-start.11 = (bf16[128,2048]{1,0:T(8,128)(2,1)S(1)}, bf16[128,2048]{1,0:T(8,128)(2,1)S(1)}, u32[]{:S(2)}, u32[]{:S(2)}) collective-permute-start(bf16[128,2048]{1,0:T(8,128)(2,1)S(1)} %get-tuple-element.52), channel_id=1, source_target_pairs={{0,1},{1,0},{2,3},{3,2},{4,5},{5,4},{6,7},{7,6},{8,9},{9,8},{10,11... | collective-permute-start | bytes 1572872 | tf_op jit(solution)/shard_map/ppermute | solution.py:456
  45.6 0.7 %send_high.1 = bf16[128,2048]{1,0:T(8,128)(2,1)S(1)} custom-call(bf16[256,1024]{1,0:T(8,128)(2,1)S(1)} %get-tuple-element.51.attended, bf16[2048,4096]{1,0:T(8,128)(2,1)S(1)} %bitcast.1, f32[256,4096]{1,0:T(8,128)S(1)} %get-tuple-element.50.refs_8_.summed), custom_call_target="tpu_custom_call" | custom-call | flops 536870912 | bytes 4194304 | tf_op jit(solution)/shard_map/send_high/pallas_call | solution.py:457
  46.3 0.1 collective-permute-start.12
  46.4 0.7 %own_high.1.after.own = f32[128,2048]{1,0:T(8,128)S(1)} custom-call(bf16[256,1024]{1,0:T(8,128)(2,1)S(1)} %get-tuple-element.51.attended, bf16[2048,4096]{1,0:T(8,128)(2,1)S(1)} %bitcast.1, f32[256,4096]{1,0:T(8,128)S(1)} %get-tuple-element.50.refs_8_.summed), custom_call_target="tpu_custom_call" | custom-call | flops 536870912 | bytes 4194304 | tf_op jit(solution)/shard_map/own_high/pallas_call | solution.py:461
  47.1 0.8 %own_low.1.mixed_low = bf16[128,2048]{1,0:T(8,128)(2,1)S(1)} custom-call(bf16[256,1024]{1,0:T(8,128)(2,1)S(1)} %get-tuple-element.51.attended, bf16[2048,4096]{1,0:T(8,128)(2,1)S(1)} %bitcast.1, f32[256,4096]{1,0:T(8,128)S(1)} %get-tuple-element.50.refs_8_.summed, bf16[128,2048]{1,0:T(8,128)(2,1)S(1)} %collective-permute-done.11.got, ...), custom_call_target="tpu_custom_call" | custom-call | flops 536870912 | bytes 4194304 | tf_op jit(solution)/shard_map/own_low/pallas_call | solution.py:465
  47.9 0.4 collective-permute-done.12.got
  48.3 1.0 %add.1 = bf16[128,4096]{1,0:T(8,128)(2,1)} custom-call(bf16[128,2048]{1,0:T(8,128)(2,1)S(1)} %own_low.1.mixed_low, f32[128,2048]{1,0:T(8,128)S(1)} %own_high.1.after.own, bf16[128,2048]{1,0:T(8,128)(2,1)S(1)} %collective-permute-done.12.got), custom_call_target="tpu_custom_call" | custom-call | flops 262144 | bytes 4194304 | tf_op jit(solution)/shard_map/add/pallas_call | solution.py:468
  (28 shorter events, 0.2 us)
Async XLA Ops:
  0.0 3.7 %collective-permute-start = (bf16[128,4096]{1,0:T(8,128)(2,1)}, bf16[128,4096]{1,0:T(8,128)(2,1)S(1)}, u32[]{:S(2)}, u32[]{:S(2)}) collective-permute-start(bf16[128,4096]{1,0:T(8,128)(2,1)} %own_hbm.1), channel_id=1, source_target_pairs={{0,1},{1,0},{2,3},{3,2},{4,5},{5,4},{6,7},{7,6},{8,9},{9,8},{10,11... | collective-permute-start | bytes 3145736 | tf_op jit(solution)/shard_map/ppermute | solution.py:364
  4.5 9.8 %collective-permute-start.1 = (bf16[256,512]{1,0:T(8,128)(2,1)S(1)}, bf16[256,512]{1,0:T(8,128)(2,1)S(1)}, u32[]{:S(2)}, u32[]{:S(2)}) collective-permute-start(bf16[256,512]{1,0:T(8,128)(2,1)S(1)} %keys_values.1.own.refs_0_), channel_id=1, source_target_pairs={{0,8},{2,10},{4,12},{6,14},{8,16},{10,18},{12,20},{14,22},{16,24},... | collective-permute-start | bytes 786440 | tf_op jit(solution)/shard_map/ppermute | solution.py:388
  5.8 11.5 %slice-start.4 = ((s8[16777216]{0:T(1024)(128)(4,1)}), s8[4194304]{0:T(1024)(128)(4,1)S(1)}, s32[]{:S(2)}) async-start(s8[16777216]{0:T(1024)(128)(4,1)} %bitcast.2), calls=%async_computation.4 | async-start | bytes 8388608
  5.9 11.5 %slice-start.5 = ((s8[16777216]{0:T(1024)(128)(4,1)}), s8[4194304]{0:T(1024)(128)(4,1)S(1)}, s32[]{:S(2)}) async-start(s8[16777216]{0:T(1024)(128)(4,1)} %bitcast.2), calls=%async_computation.5 | async-start | bytes 8388608
  10.1 7.2 %slice-start.6 = ((s8[16777216]{0:T(1024)(128)(4,1)}), s8[4194304]{0:T(1024)(128)(4,1)S(1)}, s32[]{:S(2)}) async-start(s8[16777216]{0:T(1024)(128)(4,1)} %bitcast.2), calls=%async_computation.6 | async-start | bytes 8388608
  10.1 7.2 %slice-start.7 = ((s8[16777216]{0:T(1024)(128)(4,1)}), s8[4194304]{0:T(1024)(128)(4,1)S(1)}, s32[]{:S(2)}) async-start(s8[16777216]{0:T(1024)(128)(4,1)} %bitcast.2), calls=%async_computation.7 | async-start | bytes 8388608
  10.1 11.9 %collective-permute-start.2 = (bf16[256,512]{1,0:T(8,128)(2,1)S(1)}, bf16[256,512]{1,0:T(8,128)(2,1)S(1)}, u32[]{:S(2)}, u32[]{:S(2)}) collective-permute-start(bf16[256,512]{1,0:T(8,128)(2,1)S(1)} %get-tuple-element.37.refs_0_.own.refs_2_), channel_id=1, source_target_pairs={{0,8},{2,10},{4,12},{6,14},{8,16},{10,18},{12,20},{14,22},{16,24},... | collective-permute-start | bytes 786440 | tf_op jit(solution)/shard_map/ppermute | solution.py:395
  14.6 12.9 %collective-permute-start.4 = (bf16[256,512]{1,0:T(8,128)(2,1)S(1)}, bf16[256,512]{1,0:T(8,128)(2,1)S(1)}, u32[]{:S(2)}, u32[]{:S(2)}) collective-permute-start(bf16[256,512]{1,0:T(8,128)(2,1)S(1)} %get-tuple-element.43), channel_id=1, source_target_pairs={{0,6},{2,4},{4,2},{6,0},{8,14},{10,12},{12,10},{14,8},{16,22},{18,... | collective-permute-start | bytes 786440 | tf_op jit(solution)/shard_map/ppermute | solution.py:402
  16.8 14.1 %collective-permute-start.6 = (bf16[256,512]{1,0:T(8,128)(2,1)S(1)}, bf16[256,512]{1,0:T(8,128)(2,1)S(1)}, u32[]{:S(2)}, u32[]{:S(2)}) collective-permute-start(bf16[256,512]{1,0:T(8,128)(2,1)S(1)} %get-tuple-element.44), channel_id=1, source_target_pairs={{0,4},{2,6},{4,0},{6,2},{8,12},{10,14},{12,8},{14,10},{16,20},{18,... | collective-permute-start | bytes 786440 | tf_op jit(solution)/shard_map/ppermute | solution.py:402
  17.0 13.9 %collective-permute-start.5 = (bf16[256,512]{1,0:T(8,128)(2,1)S(1)}, bf16[256,512]{1,0:T(8,128)(2,1)S(1)}, u32[]{:S(2)}, u32[]{:S(2)}) collective-permute-start(bf16[256,512]{1,0:T(8,128)(2,1)S(1)} %get-tuple-element.38.after), channel_id=1, source_target_pairs={{0,2},{2,0},{4,6},{6,4},{8,10},{10,8},{12,14},{14,12},{16,18},{18,... | collective-permute-start | bytes 786440 | tf_op jit(solution)/shard_map/ppermute | solution.py:402
  22.0 10.4 %slice-start = ((s8[16777216]{0:T(1024)(128)(4,1)}), s8[4194304]{0:T(1024)(128)(4,1)S(1)}, s32[]{:S(2)}) async-start(s8[16777216]{0:T(1024)(128)(4,1)} %bitcast), calls=%async_computation | async-start | bytes 8388608
  22.0 10.4 %slice-start.1 = ((s8[16777216]{0:T(1024)(128)(4,1)}), s8[4194304]{0:T(1024)(128)(4,1)S(1)}, s32[]{:S(2)}) async-start(s8[16777216]{0:T(1024)(128)(4,1)} %bitcast), calls=%async_computation.1 | async-start | bytes 8388608
  22.0 10.4 %slice-start.2 = ((s8[16777216]{0:T(1024)(128)(4,1)}), s8[4194304]{0:T(1024)(128)(4,1)S(1)}, s32[]{:S(2)}) async-start(s8[16777216]{0:T(1024)(128)(4,1)} %bitcast), calls=%async_computation.2 | async-start | bytes 8388608
  22.0 10.4 %slice-start.3 = ((s8[16777216]{0:T(1024)(128)(4,1)}), s8[4194304]{0:T(1024)(128)(4,1)S(1)}, s32[]{:S(2)}) async-start(s8[16777216]{0:T(1024)(128)(4,1)} %bitcast), calls=%async_computation.3 | async-start | bytes 8388608
  22.1 15.6 %collective-permute-start.3 = (bf16[256,512]{1,0:T(8,128)(2,1)S(1)}, bf16[256,512]{1,0:T(8,128)(2,1)S(1)}, u32[]{:S(2)}, u32[]{:S(2)}) collective-permute-start(bf16[256,512]{1,0:T(8,128)(2,1)S(1)} %relay.5), channel_id=1, source_target_pairs={{0,6},{2,4},{4,2},{6,0},{8,14},{10,12},{12,10},{14,8},{16,22},{18,... | collective-permute-start | bytes 786440 | tf_op jit(solution)/shard_map/ppermute | solution.py:402
  27.2 10.6 %collective-permute-start.10 = (bf16[256,256]{1,0:T(8,128)(2,1)S(1)}, bf16[256,256]{1,0:T(8,128)(2,1)S(1)}, u32[]{:S(2)}, u32[]{:S(2)}) collective-permute-start(bf16[256,256]{1,0:T(8,128)(2,1)S(1)} %get-tuple-element.49), channel_id=1, source_target_pairs={{0,4},{2,6},{4,0},{6,2},{8,12},{10,14},{12,8},{14,10},{16,20},{18,... | collective-permute-start | bytes 393224 | tf_op jit(solution)/shard_map/ppermute | solution.py:402
  27.4 10.3 %collective-permute-start.9 = (bf16[256,256]{1,0:T(8,128)(2,1)S(1)}, bf16[256,256]{1,0:T(8,128)(2,1)S(1)}, u32[]{:S(2)}, u32[]{:S(2)}) collective-permute-start(bf16[256,256]{1,0:T(8,128)(2,1)S(1)} %get-tuple-element.42.refs_0_), channel_id=1, source_target_pairs={{0,2},{2,0},{4,6},{6,4},{8,10},{10,8},{12,14},{14,12},{16,18},{18,... | collective-permute-start | bytes 393224 | tf_op jit(solution)/shard_map/ppermute | solution.py:402
  31.0 8.3 %collective-permute-start.7 = (bf16[256,256]{1,0:T(8,128)(2,1)S(1)}, bf16[256,256]{1,0:T(8,128)(2,1)S(1)}, u32[]{:S(2)}, u32[]{:S(2)}) collective-permute-start(bf16[256,256]{1,0:T(8,128)(2,1)S(1)} %get-tuple-element.45), channel_id=1, source_target_pairs={{0,2},{2,0},{4,6},{6,4},{8,10},{10,8},{12,14},{14,12},{16,18},{18,... | collective-permute-start | bytes 393224 | tf_op jit(solution)/shard_map/ppermute | solution.py:402
  32.3 7.9 %collective-permute-start.8 = (bf16[256,256]{1,0:T(8,128)(2,1)S(1)}, bf16[256,256]{1,0:T(8,128)(2,1)S(1)}, u32[]{:S(2)}, u32[]{:S(2)}) collective-permute-start(bf16[256,256]{1,0:T(8,128)(2,1)S(1)} %get-tuple-element.46), channel_id=1, source_target_pairs={{0,4},{2,6},{4,0},{6,2},{8,12},{10,14},{12,8},{14,10},{16,20},{18,... | collective-permute-start | bytes 393224 | tf_op jit(solution)/shard_map/ppermute | solution.py:402
  42.2 4.9 %collective-permute-start.11 = (bf16[128,2048]{1,0:T(8,128)(2,1)S(1)}, bf16[128,2048]{1,0:T(8,128)(2,1)S(1)}, u32[]{:S(2)}, u32[]{:S(2)}) collective-permute-start(bf16[128,2048]{1,0:T(8,128)(2,1)S(1)} %get-tuple-element.52), channel_id=1, source_target_pairs={{0,1},{1,0},{2,3},{3,2},{4,5},{5,4},{6,7},{7,6},{8,9},{9,8},{10,11... | collective-permute-start | bytes 1572872 | tf_op jit(solution)/shard_map/ppermute | solution.py:456
  46.3 2.0 %collective-permute-start.12 = (bf16[128,2048]{1,0:T(8,128)(2,1)S(1)}, bf16[128,2048]{1,0:T(8,128)(2,1)S(1)}, u32[]{:S(2)}, u32[]{:S(2)}) collective-permute-start(bf16[128,2048]{1,0:T(8,128)(2,1)S(1)} %send_high.1), channel_id=1, source_target_pairs={{0,1},{1,0},{2,3},{3,2},{4,5},{5,4},{6,7},{7,6},{8,9},{9,8},{10,11... | collective-permute-start | bytes 1572872 | tf_op jit(solution)/shard_map/ppermute | solution.py:460

commit v7 on v5

--- a/solution.py
+++ b/solution.py
@@ -159,14 +159,13 @@
             query[:, out] = rotated(result[:, at], cosine[...], sine[...]).astype(query.dtype)
 
 
-def relay_kernel(own, earlier, after, to_x, to_y, to_d):
+def relay_kernel(ways, own, earlier, after, *outs):
     del after
     index = lax.axis_index("seq")
     mine, theirs = own[...], earlier[...]
-    to_x[...] = jnp.where(index % 2 > 0, theirs, mine)
-    by_y = jnp.where(index % LAYER >= 2, theirs, mine)
-    to_y[...] = by_y
-    to_d[...] = by_y
+    for way, out in zip(ways, outs):
+        upper = index % 2 > 0 if way == 1 else index % LAYER >= 2
+        out[...] = jnp.where(upper, theirs, mine)
 
 
 def column(number):
@@ -239,26 +238,37 @@
         scores = ahead
 
 
-def attend_far(low, distances, starts, query, blocks, state, attended, bias):
+def join(scores, blocks, at, state, head, ones, dtype):
     tops, totals, accs = state
-    fill_bias(bias, distances, starts)
+    before = tops[head]
+    tokens = before.shape[0]
+    top = jnp.maximum(jnp.broadcast_to(row_max(scores), before.shape), before)
+    factor = jnp.exp2(before - top)
+    wide_top = jnp.concatenate([top] * (tokens // HEAD_SIZE), axis=1)
+    weights = [jnp.exp2(score - wide_top).astype(dtype) for score in scores]
+    acc, total = weighted(weights, blocks, at, ones)
+    return top, totals[head] * factor + total, accs[head] * factor + acc
+
+
+def attend_far(low, skip, query, blocks, state, bias, put):
     tokens = query.shape[0]
-    heads = attended.shape[1] // HEAD_SIZE
     kv_part = blocks[0].shape[1] // (2 * HEAD_SIZE)
+    heads = query.shape[1] // HEAD_SIZE // 2
     group = heads // kv_part
     ones = jnp.ones((tokens, HEAD_SIZE), query.dtype)
     scores = scores_of(query, blocks, bias, low, 0)
     for head in range(heads):
         ahead = scores_of(query, blocks, bias, low + head + 1, (head + 1) // group) if head + 1 < heads else None
-        before = tops[low + head]
-        top = jnp.maximum(jnp.broadcast_to(row_max(scores), (tokens, HEAD_SIZE)), before)
-        factor = jnp.exp2(before - top)
-        wide_top = jnp.concatenate([top] * (tokens // HEAD_SIZE), axis=1)
-        weights = [jnp.exp2(score - wide_top).astype(query.dtype) for score in scores]
-        acc, total = weighted(weights, blocks, kv_part + head // group, ones)
-        result = (accs[low + head] * factor + acc) / (totals[low + head] * factor + total)
-        attended[:, column(head)] = result.astype(attended.dtype)
+        put(head, *join(scores, blocks, kv_part + head // group, state, skip + head, ones, query.dtype))
         scores = ahead
+
+
+def into(attended):
+    def put(head, top, total, acc):
+        del top
+        attended[:, column(head)] = (acc / total).astype(attended.dtype)
+
+    return put
 
 
 WIDE = 4 * HEAD_SIZE
@@ -267,11 +277,19 @@
 def mix_first_kernel(distances, starts, query, *refs):
     far = len(distances)
     blocks, state, (weight, summed, attended, bias) = refs[:far], refs[far : far + 3], refs[far + 3 :]
-    attend_far(0, distances, starts, query, blocks, state, attended, bias)
+    fill_bias(bias, distances, starts)
+    attend_far(0, 0, query, blocks, state, bias, into(attended))
     depth = attended.shape[1]
     for number in range(summed.shape[1] // WIDE):
         at = slice(number * WIDE, (number + 1) * WIDE)
         summed[:, at] = dot(attended[...], weight[:depth, at])
+
+
+def middle_kernel(low, query, block, tops, totals, accs, bias, new_tops, new_totals, new_accs):
+    def put(head, top, total, acc):
+        new_tops[head], new_totals[head], new_accs[head] = top, total, acc
+
+    attend_far(low, low, query, [block], (tops, totals, accs), bias, put)
 
 
 def rows_product(rows, low, attended, weight, summed, wide):
@@ -287,10 +305,10 @@
         send[:, number * WIDE : (number + 1) * WIDE] = result.astype(send.dtype)
 
 
-def mix_second_kernel(low, distances, starts, query, *refs):
-    far = len(distances)
-    blocks, state, (weight, summed, send, attended, bias) = refs[:far], refs[far : far + 3], refs[far + 3 :]
-    attend_far(low, distances, starts, query, blocks, state, attended, bias)
+def mix_second_kernel(low, query, *refs):
+    blocks, state, (bias, weight, summed, send, attended) = refs[:-8], refs[-8:-5], refs[-5:]
+    skipped = bias.shape[1] - len(blocks) * bias.shape[0]
+    attend_far(low, 0, query, blocks, state, bias.at[:, pl.ds(skipped, len(blocks) * bias.shape[0])], into(attended))
     send_columns(0, attended, weight, summed, send)
 
 
@@ -385,41 +403,48 @@
 
     def exchange(mine, earlier, after, ways, cost):
         to = call(
-            relay_kernel, "relay", [kv_shape] * 3, [VMEM] * 3, cost, 2 << 20, 4,
+            functools.partial(relay_kernel, ways), "relay", [kv_shape] * len(ways), [VMEM] * 3, cost, 2 << 20, 4,
         )(mine, earlier, after)
-        got = {way: lax.ppermute(to[way - 1], "seq", [(i, i ^ way) for i in every]) for way in ways}
-        return [got[way] for way in (1, 2, 3)], to[0]
-
-    far_a, done = exchange(kv_a, z_a, done, (1, 2, 3), RELAY_COST)
+        return [lax.ppermute(array, "seq", [(i, i ^ way) for i in every]) for way, array in zip(ways, to)], to[0]
+
+    (x_a, y_a, d_a), done = exchange(kv_a, z_a, kv_b, (1, 2, 3), RELAY_COST)
+    far_a = d_a, x_a, y_a
     query, done = call(
         query_kernel, "queries", [shape((tokens, width_q), bf16), flag], [VMEM] * 5,
         2 * tokens * model * width_q, 2 * model * width_q, 8,
     )(rows, w_query, cosine, sine, done)
-    far_b, _ = exchange(kv_b, z_b, done, (3, 1, 2), 9 << 30)
+    (d_b,), _ = exchange(kv_b, z_b, done, (3,), 9 << 30)
     near = call(
         functools.partial(near_kernel, ((0, 0), (LAYER, LAYER))), "scores_near", [shape((heads, tokens, HEAD_SIZE), f32)] * 3,
         [VMEM] * 6, 8 * heads * tokens * tokens * HEAD_SIZE, 8 << 20, 12, [pltpu.VMEM((tokens, 2 * tokens), f32)],
     )(starts, query, kv_a, z_a, kv_b, z_b)
+    (x_b, y_b), _ = exchange(kv_b, z_b, near[0], (1, 2), 0)
+    far_b = d_b, x_b, y_b
 
     far = len(far_a)
-    distances = ((3, 1), (2, 2), (1, 3))
-    bias = pltpu.VMEM((tokens, far * tokens), f32)
+    distances = ((1, 3), (3, 1), (2, 2))
+    bias_shape = shape((tokens, far * tokens), f32)
     columns = w_out.shape[1]
     attended_shape = shape((tokens, width_q // 2), bf16)
     far_flops = 3 * far * heads * tokens * tokens * HEAD_SIZE
     out_flops = tokens * width_q * columns
-    summed, _ = call(
-        functools.partial(mix_first_kernel, distances), "mix_first", [shape((tokens, columns), f32), attended_shape],
-        [VMEM] * (6 + far), out_flops + far_flops, 4 << 20, 10, [bias],
+    summed, _, bias = call(
+        functools.partial(mix_first_kernel, distances), "mix_first",
+        [shape((tokens, columns), f32), attended_shape, bias_shape],
+        [VMEM] * (6 + far), out_flops + far_flops, 4 << 20, 10,
     )(starts, query, *far_a, *near, w_out)
+    middle = call(
+        functools.partial(middle_kernel, heads // 2), "attend_middle", [shape((heads // 2, tokens, HEAD_SIZE), f32)] * 3,
+        [VMEM] * 6, far_flops // far, 4 << 20, 10,
+    )(query, far_b[0], *near, bias)
 
     cut = columns // 2
     send_shape = shape((half, cut), bf16)
     quarter = out_flops // 4
     send, attended = call(
-        functools.partial(mix_second_kernel, heads // 2, distances), "mix_second", [send_shape, attended_shape],
-        [VMEM] * (7 + far), quarter + far_flops, 4 << 20, 10, [bias],
-    )(starts, query, *far_b, *near, w_out, summed)
+        functools.partial(mix_second_kernel, heads // 2), "mix_second", [send_shape, attended_shape],
+        [VMEM] * (6 + far), quarter + far_flops, 4 << 20, 10,
+    )(query, *far_b[1:], *middle, bias, w_out, summed)
     got_low = lax.ppermute(send, "head", SWAP)
     (send,) = call(
         functools.partial(send_columns, cut), "send_high", [send_shape], [VMEM] * 3, quarter, 4 << 20, 6,

time: 48.6 us -> 47.7 us (0.981)
  starting transfers between devices: 12 us -> 10.5 us
  Pallas kernels: 26.2 us -> 27.5 us
  local copies, waits for them, and re-layouts: 0.91 us -> 0.05 us
    ppermute x1, starting transfers between devices: 2.33 us -> 0.83 us  [body(): got_low = lax.ppermute(send, 'head', SWAP)]
    unnamed x16, local copies, waits for them, and re-layouts: 0.91 us -> 0.05 us
    pallas_call x3 -> x5, Pallas kernels: 3.35 us -> 3.78 us  [the longest x1 2.33 us: body(): call(functools.partial(mix_second_kernel, heads // 2), 'mix_second', [sen...]
  transfers between devices with their start and end apart: 11 -> 11, of which waited for: 4 -> 5; matrix products, arithmetic and copies ran while one was open for 0% -> 0% of each run, Pallas kernels for 44% -> 49%
where the time goes in v7:
time: 47.7 us; the launch traced here: 47.5 us
  Pallas kernels  27.5 us (58%)
  starting transfers between devices  10.5 us (22%)
  waiting for transfers between devices  9.02 us (19%)
    ppermute x6, waiting for transfers between devices, exchange(): lax.ppermute(array, 'seq', [(i, i ^ way) for i in every])  6.42 us
    ppermute x6, starting transfers between devices, exchange(): lax.ppermute(array, 'seq', [(i, i ^ way) for i in every])  5.49 us
    pallas_call x1, Pallas kernels, body(): call(query_kernel, 'queries', [shape((tokens, width_q), bf16), flag], [VM...  4.78 us
    pallas_call x1, Pallas kernels, body(): call(functools.partial(mix_first_kernel, distances), 'mix_first', [shape(...  4.71 us
    pallas_call x1, Pallas kernels, body(): call(functools.partial(third_kernel, chunks), 'keys_values_more', [kv_sha...  4.19 us
    pallas_call x1, Pallas kernels, body(): call(functools.partial(first_kernel, chunks), 'keys_values_own', [shape((...  3.06 us
    pallas_call x1, Pallas kernels, body(): call(functools.partial(near_kernel, ((0, 0), (LAYER, LAYER))), 'scores_ne...  2.99 us
    pallas_call x1, Pallas kernels, body(): call(functools.partial(mix_second_kernel, heads // 2), 'mix_second', [sen...  2.33 us
  transfers between devices with their start and end apart: 11, of which 5 were waited for; matrix products, arithmetic and copies ran while one was open for 0% of the time, Pallas kernels for 49%

profile of v7, /device:TPU:25, one launch (start us, length us, event | category | flops | bytes accessed | tf_op | source)
XLA Modules:
  0.0 47.5 jit_solution(14456268071042161517)
XLA Ops:
  0.0 0.7 %collective-permute-start = (bf16[128,4096]{1,0:T(8,128)(2,1)}, bf16[128,4096]{1,0:T(8,128)(2,1)S(1)}, u32[]{:S(2)}, u32[]{:S(2)}) collective-permute-start(bf16[128,4096]{1,0:T(8,128)(2,1)} %own_hbm.1), channel_id=1, source_target_pairs={{0,1},{1,0},{2,3},{3,2},{4,5},{5,4},{6,7},{7,6},{8,9},{9,8},{10,11... | collective-permute-start | bytes 3145736 | tf_op jit(solution)/shard_map/ppermute | solution.py:371
  0.7 3.1 %keys_values_own.1 = (f32[128,512]{1,0:T(8,128)S(1)}, bf16[128,4096]{1,0:T(8,128)(2,1)S(1)}, bf16[4096,256]{1,0:T(8,128)(2,1)S(1)}, bf16[4096,256]{1,0:T(8,128)(...) custom-call(s32[8]{0:T(128)} %lengths_hbm.1, bf16[128,4096]{1,0:T(8,128)(2,1)} %own_hbm.1, ...), custom_call_target="tpu_custom_call" | custom-call | flops 536870912 | bytes 4194304 | tf_op jit(solution)/shard_map/keys_values_own/pallas_call | solution.py:380
  3.8 0.8 %keys_values.1.own.refs_0_ = bf16[256,512]{1,0:T(8,128)(2,1)S(1)} custom-call(bf16[128,4096]{1,0:T(8,128)(2,1)S(1)} %collective-permute-done.other, bf16[4096,256]{1,0:T(8,128)(2,1)S(1)} %get-tuple-element.35.w_key, bf16[4096,256]{1,0:T(8,128)(2,1)S(1)} %get-tuple-element.36.w_value, f32[128,512]{1,0:T(8,128)S(1)} %get-tuple-element.37.own_total, ...), custom_call_target="tpu_custom_call" | custom-call | flops 536870912 | bytes 4194304 | tf_op jit(solution)/shard_map/keys_values/pallas_call | solution.py:389
  4.5 1.3 %collective-permute-start.1 = (bf16[256,512]{1,0:T(8,128)(2,1)S(1)}, bf16[256,512]{1,0:T(8,128)(2,1)S(1)}, u32[]{:S(2)}, u32[]{:S(2)}) collective-permute-start(bf16[256,512]{1,0:T(8,128)(2,1)S(1)} %keys_values.1.own.refs_0_), channel_id=1, source_target_pairs={{0,8},{2,10},{4,12},{6,14},{8,16},{10,18},{12,20},{14,22},{16,24},... | collective-permute-start | bytes 786440 | tf_op jit(solution)/shard_map/ppermute | solution.py:395
  5.8 0.0 slice-start.4
  5.9 4.2 %keys_values_more.1 = (bf16[256,512]{1,0:T(8,128)(2,1)S(1)}, bf16[256,4096]{1,0:T(8,128)(2,1)S(1)}, f32[8,128]{1,0:T(8,128)}) custom-call(bf16[128,4096]{1,0:T(8,128)(2,1)S(1)} %get-tuple-element.31.own, bf16[128,4096]{1,0:T(8,128)(2,1)S(1)} %collective-permute-done.other, bf16[4096,512]{1,0:T(8,128)(2,1)} %key_hbm.3, bf16[4096,512]{1,0:T(8,128)(2,1)} %value_hbm.3, ...), custom_call_target="tpu_custom_call" | custom-call | flops 4294967296 | bytes 4194304 | tf_op jit(solution)/shard_map/keys_values_more/pallas_call | solution.py:397
  10.1 0.0 slice-start.6
  10.1 2.1 %collective-permute-start.2 = (bf16[256,512]{1,0:T(8,128)(2,1)S(1)}, bf16[256,512]{1,0:T(8,128)(2,1)S(1)}, u32[]{:S(2)}, u32[]{:S(2)}) collective-permute-start(bf16[256,512]{1,0:T(8,128)(2,1)S(1)} %get-tuple-element.38.after.refs_2_.own), channel_id=1, source_target_pairs={{0,8},{2,10},{4,12},{6,14},{8,16},{10,18},{12,20},{14,22},{16,24},... | collective-permute-start | bytes 786440 | tf_op jit(solution)/shard_map/ppermute | solution.py:402
  12.2 2.2 %collective-permute-done.1.earlier.refs_1_ = bf16[256,512]{1,0:T(8,128)(2,1)S(1)} collective-permute-done((bf16[256,512]{1,0:T(8,128)(2,1)S(1)}, bf16[256,512]{1,0:T(8,128)(2,1)S(1)}, u32[]{:S(2)}, u32[]{:S(2)}) %collective-permute-start.1) | collective-permute-done | bytes 262176 | tf_op jit(solution)/shard_map/ppermute | solution.py:395
  14.4 0.1 relay.3
  14.5 2.2 %collective-permute-start.6 = (bf16[256,512]{1,0:T(8,128)(2,1)S(1)}, bf16[256,512]{1,0:T(8,128)(2,1)S(1)}, u32[]{:S(2)}, u32[]{:S(2)}) collective-permute-start(bf16[256,512]{1,0:T(8,128)(2,1)S(1)} %get-tuple-element.48), channel_id=1, source_target_pairs={{0,6},{2,4},{4,2},{6,0},{8,14},{10,12},{12,10},{14,8},{16,22},{18,... | collective-permute-start | bytes 786440 | tf_op jit(solution)/shard_map/ppermute | solution.py:408
  16.7 0.2 collective-permute-start.8
  16.9 0.2 collective-permute-start.7
  17.2 4.8 %queries.1 = (bf16[256,2048]{1,0:T(8,128)(2,1)S(1)}, f32[8,128]{1,0:T(8,128)S(1)}) custom-call(bf16[256,4096]{1,0:T(8,128)(2,1)S(1)} %get-tuple-element.34.rows, bf16[4096,2048]{1,0:T(8,128)(2,1)S(1)} %bitcast.3, f32[256,128]{1,0:T(8,128)S(1)} %get-tuple-element.32.cosine, f32[256,128]{1,0:T(8,128)S(1)} %get-tuple-element.33.sine, ...), custom_call_target="tpu_custom_call" | custom-call | flops 4294967296 | bytes 16777216 | tf_op jit(solution)/shard_map/queries/pallas_call | solution.py:412
  22.1 2.2 %collective-permute-start.5 = (bf16[256,512]{1,0:T(8,128)(2,1)S(1)}, bf16[256,512]{1,0:T(8,128)(2,1)S(1)}, u32[]{:S(2)}, u32[]{:S(2)}) collective-permute-start(bf16[256,512]{1,0:T(8,128)(2,1)S(1)} %relay.5), channel_id=1, source_target_pairs={{0,6},{2,4},{4,2},{6,0},{8,14},{10,12},{12,10},{14,8},{16,22},{18,... | collective-permute-start | bytes 786440 | tf_op jit(solution)/shard_map/ppermute | solution.py:408
  24.3 3.0 %scores_near.1 = (f32[16,256,128]{2,1,0:T(8,128)S(1)}, f32[16,256,128]{2,1,0:T(8,128)S(1)}, f32[16,256,128]{2,1,0:T(8,128)S(1)}) custom-call(s32[256,128]{1,0:T(8,128)S(1)} %get-tuple-element.41.starts, bf16[256,2048]{1,0:T(8,128)(2,1)S(1)} %get-tuple-element.40.query, bf16[256,512]{1,0:T(8,128)(2,1)S(1)} %keys_values.1.own.refs_0_, ...), custom_call_target="tpu_custom_call" | custom-call | flops 1073741824 | bytes 8388608 | tf_op jit(solution)/shard_map/scores_near/pallas_call | solution.py:417
  27.3 0.1 relay.4
  27.4 0.3 collective-permute-start.3
  27.7 0.2 collective-permute-start.4
  27.9 2.9 %collective-permute-done.8.refs_2_ = bf16[256,512]{1,0:T(8,128)(2,1)S(1)} collective-permute-done((bf16[256,512]{1,0:T(8,128)(2,1)S(1)}, bf16[256,512]{1,0:T(8,128)(2,1)S(1)}, u32[]{:S(2)}, u32[]{:S(2)}) %collective-permute-start.8) | collective-permute-done | bytes 262176 | tf_op jit(solution)/shard_map/ppermute | solution.py:408
  30.9 4.7 %mix_first.1 = (f32[256,4096]{1,0:T(8,128)S(1)}, bf16[256,1024]{1,0:T(8,128)(2,1)}, f32[256,768]{1,0:T(8,128)S(1)}) custom-call(s32[256,128]{1,0:T(8,128)S(1)} %get-tuple-element.41.starts, bf16[256,2048]{1,0:T(8,128)(2,1)S(1)} %get-tuple-element.40.query, bf16[256,512]{1,0:T(8,128)(2,1)S(1)} %collective-permute-done.6.refs_0_, ...), custom_call_target="tpu_custom_call" | custom-call | flops 3355443200 | bytes 4194304 | tf_op jit(solution)/shard_map/mix_first/pallas_call | solution.py:431
  35.6 1.3 %attend_middle.1 = (f32[8,256,128]{2,1,0:T(8,128)S(1)}, f32[8,256,128]{2,1,0:T(8,128)S(1)}, f32[8,256,128]{2,1,0:T(8,128)S(1)}) custom-call(bf16[256,2048]{1,0:T(8,128)(2,1)S(1)} %get-tuple-element.40.query, bf16[256,512]{1,0:T(8,128)(2,1)S(1)} %collective-permute-done.5.block, f32[16,256,128]{2,1,0:T(8,128)S(1)} %get-tuple-element.42.after.refs_3_.tops, ...), custom_call_target="tpu_custom_call" | custom-call | flops 402653184 | bytes 4194304 | tf_op jit(solution)/shard_map/attend_middle/pallas_call | solution.py:436
  36.9 2.2 %collective-permute-done.3.refs_0_ = bf16[256,512]{1,0:T(8,128)(2,1)S(1)} collective-permute-done((bf16[256,512]{1,0:T(8,128)(2,1)S(1)}, bf16[256,512]{1,0:T(8,128)(2,1)S(1)}, u32[]{:S(2)}, u32[]{:S(2)}) %collective-permute-start.3) | collective-permute-done | bytes 262176 | tf_op jit(solution)/shard_map/ppermute | solution.py:408
  39.1 1.3 %collective-permute-done.4.refs_1_ = bf16[256,512]{1,0:T(8,128)(2,1)S(1)} collective-permute-done((bf16[256,512]{1,0:T(8,128)(2,1)S(1)}, bf16[256,512]{1,0:T(8,128)(2,1)S(1)}, u32[]{:S(2)}, u32[]{:S(2)}) %collective-permute-start.4) | collective-permute-done | bytes 262176 | tf_op jit(solution)/shard_map/ppermute | solution.py:408
  40.4 2.3 %mix_second.1 = (bf16[128,2048]{1,0:T(8,128)(2,1)S(1)}, bf16[256,1024]{1,0:T(8,128)(2,1)S(1)}) custom-call(bf16[256,2048]{1,0:T(8,128)(2,1)S(1)} %get-tuple-element.40.query, bf16[256,512]{1,0:T(8,128)(2,1)S(1)} %collective-permute-done.3.refs_0_, bf16[256,512]{1,0:T(8,128)(2,1)S(1)} %collective-permute-done.4.refs_1_, ...), custom_call_target="tpu_custom_call" | custom-call | flops 1744830464 | bytes 4194304 | tf_op jit(solution)/shard_map/mix_second/pallas_call | solution.py:444
  42.7 0.8 %collective-permute-start.9 = (bf16[128,2048]{1,0:T(8,128)(2,1)S(1)}, bf16[128,2048]{1,0:T(8,128)(2,1)S(1)}, u32[]{:S(2)}, u32[]{:S(2)}) collective-permute-start(bf16[128,2048]{1,0:T(8,128)(2,1)S(1)} %get-tuple-element.56), channel_id=1, source_target_pairs={{0,1},{1,0},{2,3},{3,2},{4,5},{5,4},{6,7},{7,6},{8,9},{9,8},{10,11... | collective-permute-start | bytes 1572872 | tf_op jit(solution)/shard_map/ppermute | solution.py:448
  43.6 0.7 %send_high.1 = bf16[128,2048]{1,0:T(8,128)(2,1)S(1)} custom-call(bf16[256,1024]{1,0:T(8,128)(2,1)S(1)} %get-tuple-element.55.attended, bf16[2048,4096]{1,0:T(8,128)(2,1)S(1)} %bitcast.1, f32[256,4096]{1,0:T(8,128)S(1)} %get-tuple-element.54.refs_7_.summed), custom_call_target="tpu_custom_call" | custom-call | flops 536870912 | bytes 4194304 | tf_op jit(solution)/shard_map/send_high/pallas_call | solution.py:449
  44.3 0.1 collective-permute-start.10
  44.4 0.7 %own_high.1.after.own = f32[128,2048]{1,0:T(8,128)S(1)} custom-call(bf16[256,1024]{1,0:T(8,128)(2,1)S(1)} %get-tuple-element.55.attended, bf16[2048,4096]{1,0:T(8,128)(2,1)S(1)} %bitcast.1, f32[256,4096]{1,0:T(8,128)S(1)} %get-tuple-element.54.refs_7_.summed), custom_call_target="tpu_custom_call" | custom-call | flops 536870912 | bytes 4194304 | tf_op jit(solution)/shard_map/own_high/pallas_call | solution.py:453
  45.1 0.7 %own_low.1.mixed_low = bf16[128,2048]{1,0:T(8,128)(2,1)S(1)} custom-call(bf16[256,1024]{1,0:T(8,128)(2,1)S(1)} %get-tuple-element.55.attended, bf16[2048,4096]{1,0:T(8,128)(2,1)S(1)} %bitcast.1, f32[256,4096]{1,0:T(8,128)S(1)} %get-tuple-element.54.refs_7_.summed, bf16[128,2048]{1,0:T(8,128)(2,1)S(1)} %collective-permute-done.9.got, ...), custom_call_target="tpu_custom_call" | custom-call | flops 536870912 | bytes 4194304 | tf_op jit(solution)/shard_map/own_low/pallas_call | solution.py:457
  45.9 0.4 collective-permute-done.10.got
  46.3 1.0 %add.1 = bf16[128,4096]{1,0:T(8,128)(2,1)} custom-call(bf16[128,2048]{1,0:T(8,128)(2,1)S(1)} %own_low.1.mixed_low, f32[128,2048]{1,0:T(8,128)S(1)} %own_high.1.after.own, bf16[128,2048]{1,0:T(8,128)(2,1)S(1)} %collective-permute-done.10.got), custom_call_target="tpu_custom_call" | custom-call | flops 262144 | bytes 4194304 | tf_op jit(solution)/shard_map/add/pallas_call | solution.py:460
  (23 shorter events, 0.1 us)
Async XLA Ops:
  0.0 3.7 %collective-permute-start = (bf16[128,4096]{1,0:T(8,128)(2,1)}, bf16[128,4096]{1,0:T(8,128)(2,1)S(1)}, u32[]{:S(2)}, u32[]{:S(2)}) collective-permute-start(bf16[128,4096]{1,0:T(8,128)(2,1)} %own_hbm.1), channel_id=1, source_target_pairs={{0,1},{1,0},{2,3},{3,2},{4,5},{5,4},{6,7},{7,6},{8,9},{9,8},{10,11... | collective-permute-start | bytes 3145736 | tf_op jit(solution)/shard_map/ppermute | solution.py:371
  4.5 9.8 %collective-permute-start.1 = (bf16[256,512]{1,0:T(8,128)(2,1)S(1)}, bf16[256,512]{1,0:T(8,128)(2,1)S(1)}, u32[]{:S(2)}, u32[]{:S(2)}) collective-permute-start(bf16[256,512]{1,0:T(8,128)(2,1)S(1)} %keys_values.1.own.refs_0_), channel_id=1, source_target_pairs={{0,8},{2,10},{4,12},{6,14},{8,16},{10,18},{12,20},{14,22},{16,24},... | collective-permute-start | bytes 786440 | tf_op jit(solution)/shard_map/ppermute | solution.py:395
  5.8 11.3 %slice-start.4 = ((s8[16777216]{0:T(1024)(128)(4,1)}), s8[4194304]{0:T(1024)(128)(4,1)S(1)}, s32[]{:S(2)}) async-start(s8[16777216]{0:T(1024)(128)(4,1)} %bitcast.2), calls=%async_computation.4 | async-start | bytes 8388608
  5.9 11.3 %slice-start.5 = ((s8[16777216]{0:T(1024)(128)(4,1)}), s8[4194304]{0:T(1024)(128)(4,1)S(1)}, s32[]{:S(2)}) async-start(s8[16777216]{0:T(1024)(128)(4,1)} %bitcast.2), calls=%async_computation.5 | async-start | bytes 8388608
  10.1 7.1 %slice-start.6 = ((s8[16777216]{0:T(1024)(128)(4,1)}), s8[4194304]{0:T(1024)(128)(4,1)S(1)}, s32[]{:S(2)}) async-start(s8[16777216]{0:T(1024)(128)(4,1)} %bitcast.2), calls=%async_computation.6 | async-start | bytes 8388608
  10.1 7.1 %slice-start.7 = ((s8[16777216]{0:T(1024)(128)(4,1)}), s8[4194304]{0:T(1024)(128)(4,1)S(1)}, s32[]{:S(2)}) async-start(s8[16777216]{0:T(1024)(128)(4,1)} %bitcast.2), calls=%async_computation.7 | async-start | bytes 8388608
  10.1 11.9 %collective-permute-start.2 = (bf16[256,512]{1,0:T(8,128)(2,1)S(1)}, bf16[256,512]{1,0:T(8,128)(2,1)S(1)}, u32[]{:S(2)}, u32[]{:S(2)}) collective-permute-start(bf16[256,512]{1,0:T(8,128)(2,1)S(1)} %get-tuple-element.38.after.refs_2_.own), channel_id=1, source_target_pairs={{0,8},{2,10},{4,12},{6,14},{8,16},{10,18},{12,20},{14,22},{16,24},... | collective-permute-start | bytes 786440 | tf_op jit(solution)/shard_map/ppermute | solution.py:402
  14.5 13.3 %collective-permute-start.6 = (bf16[256,512]{1,0:T(8,128)(2,1)S(1)}, bf16[256,512]{1,0:T(8,128)(2,1)S(1)}, u32[]{:S(2)}, u32[]{:S(2)}) collective-permute-start(bf16[256,512]{1,0:T(8,128)(2,1)S(1)} %get-tuple-element.48), channel_id=1, source_target_pairs={{0,6},{2,4},{4,2},{6,0},{8,14},{10,12},{12,10},{14,8},{16,22},{18,... | collective-permute-start | bytes 786440 | tf_op jit(solution)/shard_map/ppermute | solution.py:408
  16.7 14.1 %collective-permute-start.8 = (bf16[256,512]{1,0:T(8,128)(2,1)S(1)}, bf16[256,512]{1,0:T(8,128)(2,1)S(1)}, u32[]{:S(2)}, u32[]{:S(2)}) collective-permute-start(bf16[256,512]{1,0:T(8,128)(2,1)S(1)} %get-tuple-element.49), channel_id=1, source_target_pairs={{0,4},{2,6},{4,0},{6,2},{8,12},{10,14},{12,8},{14,10},{16,20},{18,... | collective-permute-start | bytes 786440 | tf_op jit(solution)/shard_map/ppermute | solution.py:408
  16.9 13.9 %collective-permute-start.7 = (bf16[256,512]{1,0:T(8,128)(2,1)S(1)}, bf16[256,512]{1,0:T(8,128)(2,1)S(1)}, u32[]{:S(2)}, u32[]{:S(2)}) collective-permute-start(bf16[256,512]{1,0:T(8,128)(2,1)S(1)} %get-tuple-element.39.after), channel_id=1, source_target_pairs={{0,2},{2,0},{4,6},{6,4},{8,10},{10,8},{12,14},{14,12},{16,18},{18,... | collective-permute-start | bytes 786440 | tf_op jit(solution)/shard_map/ppermute | solution.py:408
  22.0 8.8 %slice-start = ((s8[16777216]{0:T(1024)(128)(4,1)}), s8[4194304]{0:T(1024)(128)(4,1)S(1)}, s32[]{:S(2)}) async-start(s8[16777216]{0:T(1024)(128)(4,1)} %bitcast), calls=%async_computation | async-start | bytes 8388608
  22.0 8.8 %slice-start.1 = ((s8[16777216]{0:T(1024)(128)(4,1)}), s8[4194304]{0:T(1024)(128)(4,1)S(1)}, s32[]{:S(2)}) async-start(s8[16777216]{0:T(1024)(128)(4,1)} %bitcast), calls=%async_computation.1 | async-start | bytes 8388608
  22.0 8.8 %slice-start.2 = ((s8[16777216]{0:T(1024)(128)(4,1)}), s8[4194304]{0:T(1024)(128)(4,1)S(1)}, s32[]{:S(2)}) async-start(s8[16777216]{0:T(1024)(128)(4,1)} %bitcast), calls=%async_computation.2 | async-start | bytes 8388608
  22.0 8.8 %slice-start.3 = ((s8[16777216]{0:T(1024)(128)(4,1)}), s8[4194304]{0:T(1024)(128)(4,1)S(1)}, s32[]{:S(2)}) async-start(s8[16777216]{0:T(1024)(128)(4,1)} %bitcast), calls=%async_computation.3 | async-start | bytes 8388608
  22.1 13.5 %collective-permute-start.5 = (bf16[256,512]{1,0:T(8,128)(2,1)S(1)}, bf16[256,512]{1,0:T(8,128)(2,1)S(1)}, u32[]{:S(2)}, u32[]{:S(2)}) collective-permute-start(bf16[256,512]{1,0:T(8,128)(2,1)S(1)} %relay.5), channel_id=1, source_target_pairs={{0,6},{2,4},{4,2},{6,0},{8,14},{10,12},{12,10},{14,8},{16,22},{18,... | collective-permute-start | bytes 786440 | tf_op jit(solution)/shard_map/ppermute | solution.py:408
  27.4 11.7 %collective-permute-start.3 = (bf16[256,512]{1,0:T(8,128)(2,1)S(1)}, bf16[256,512]{1,0:T(8,128)(2,1)S(1)}, u32[]{:S(2)}, u32[]{:S(2)}) collective-permute-start(bf16[256,512]{1,0:T(8,128)(2,1)S(1)} %get-tuple-element.43), channel_id=1, source_target_pairs={{0,2},{2,0},{4,6},{6,4},{8,10},{10,8},{12,14},{14,12},{16,18},{18,... | collective-permute-start | bytes 786440 | tf_op jit(solution)/shard_map/ppermute | solution.py:408
  27.7 12.7 %collective-permute-start.4 = (bf16[256,512]{1,0:T(8,128)(2,1)S(1)}, bf16[256,512]{1,0:T(8,128)(2,1)S(1)}, u32[]{:S(2)}, u32[]{:S(2)}) collective-permute-start(bf16[256,512]{1,0:T(8,128)(2,1)S(1)} %get-tuple-element.44), channel_id=1, source_target_pairs={{0,4},{2,6},{4,0},{6,2},{8,12},{10,14},{12,8},{14,10},{16,20},{18,... | collective-permute-start | bytes 786440 | tf_op jit(solution)/shard_map/ppermute | solution.py:408
  42.7 2.4 %collective-permute-start.9 = (bf16[128,2048]{1,0:T(8,128)(2,1)S(1)}, bf16[128,2048]{1,0:T(8,128)(2,1)S(1)}, u32[]{:S(2)}, u32[]{:S(2)}) collective-permute-start(bf16[128,2048]{1,0:T(8,128)(2,1)S(1)} %get-tuple-element.56), channel_id=1, source_target_pairs={{0,1},{1,0},{2,3},{3,2},{4,5},{5,4},{6,7},{7,6},{8,9},{9,8},{10,11... | collective-permute-start | bytes 1572872 | tf_op jit(solution)/shard_map/ppermute | solution.py:448
  44.3 2.0 %collective-permute-start.10 = (bf16[128,2048]{1,0:T(8,128)(2,1)S(1)}, bf16[128,2048]{1,0:T(8,128)(2,1)S(1)}, u32[]{:S(2)}, u32[]{:S(2)}) collective-permute-start(bf16[128,2048]{1,0:T(8,128)(2,1)S(1)} %send_high.1), channel_id=1, source_target_pairs={{0,1},{1,0},{2,3},{3,2},{4,5},{5,4},{6,7},{7,6},{8,9},{9,8},{10,11... | collective-permute-start | bytes 1572872 | tf_op jit(solution)/shard_map/ppermute | solution.py:452

commit v8 on v7

--- a/solution.py
+++ b/solution.py
@@ -285,11 +285,14 @@
         summed[:, at] = dot(attended[...], weight[:depth, at])
 
 
-def middle_kernel(low, query, block, tops, totals, accs, bias, new_tops, new_totals, new_accs):
+def middle_kernel(low, query, first, second, tops, totals, accs, bias, new_tops, new_totals, new_accs):
+    tokens = bias.shape[0]
+    late = bias.at[:, pl.ds(bias.shape[1] - 2 * tokens, 2 * tokens)]
+
     def put(head, top, total, acc):
         new_tops[head], new_totals[head], new_accs[head] = top, total, acc
 
-    attend_far(low, low, query, [block], (tops, totals, accs), bias, put)
+    attend_far(low, low, query, [first, second], (tops, totals, accs), late, put)
 
 
 def rows_product(rows, low, attended, weight, summed, wide):
@@ -305,10 +308,9 @@
         send[:, number * WIDE : (number + 1) * WIDE] = result.astype(send.dtype)
 
 
-def mix_second_kernel(low, query, *refs):
-    blocks, state, (bias, weight, summed, send, attended) = refs[:-8], refs[-8:-5], refs[-5:]
-    skipped = bias.shape[1] - len(blocks) * bias.shape[0]
-    attend_far(low, 0, query, blocks, state, bias.at[:, pl.ds(skipped, len(blocks) * bias.shape[0])], into(attended))
+def mix_second_kernel(low, query, block, tops, totals, accs, bias, weight, summed, send, attended):
+    first = bias.at[:, pl.ds(0, bias.shape[0])]
+    attend_far(low, 0, query, [block], (tops, totals, accs), first, into(attended))
     send_columns(0, attended, weight, summed, send)
 
 
@@ -375,7 +377,7 @@
     part = width_k // 2
     kv_shape = shape((tokens, 2 * part), bf16)
     part_shape = shape((model, part), bf16)
-    chunks = 4
+    chunks = 2
     kv_flops = 4 * half * model * part
     total, own, w_key, w_value, cosine, sine, starts = call(
         functools.partial(first_kernel, chunks), "keys_values_own",
@@ -413,13 +415,12 @@
         query_kernel, "queries", [shape((tokens, width_q), bf16), flag], [VMEM] * 5,
         2 * tokens * model * width_q, 2 * model * width_q, 8,
     )(rows, w_query, cosine, sine, done)
-    (d_b,), _ = exchange(kv_b, z_b, done, (3,), 9 << 30)
+    (x_b, y_b), _ = exchange(kv_b, z_b, done, (1, 2), 9 << 30)
     near = call(
         functools.partial(near_kernel, ((0, 0), (LAYER, LAYER))), "scores_near", [shape((heads, tokens, HEAD_SIZE), f32)] * 3,
         [VMEM] * 6, 8 * heads * tokens * tokens * HEAD_SIZE, 8 << 20, 12, [pltpu.VMEM((tokens, 2 * tokens), f32)],
     )(starts, query, kv_a, z_a, kv_b, z_b)
-    (x_b, y_b), _ = exchange(kv_b, z_b, near[0], (1, 2), 0)
-    far_b = d_b, x_b, y_b
+    (d_b,), _ = exchange(kv_b, z_b, near[0], (3,), 0)
 
     far = len(far_a)
     distances = ((1, 3), (3, 1), (2, 2))
@@ -435,16 +436,16 @@
     )(starts, query, *far_a, *near, w_out)
     middle = call(
         functools.partial(middle_kernel, heads // 2), "attend_middle", [shape((heads // 2, tokens, HEAD_SIZE), f32)] * 3,
-        [VMEM] * 6, far_flops // far, 4 << 20, 10,
-    )(query, far_b[0], *near, bias)
+        [VMEM] * 7, far_flops // far * 2, 4 << 20, 10,
+    )(query, x_b, y_b, *near, bias)
 
     cut = columns // 2
     send_shape = shape((half, cut), bf16)
     quarter = out_flops // 4
     send, attended = call(
         functools.partial(mix_second_kernel, heads // 2), "mix_second", [send_shape, attended_shape],
-        [VMEM] * (6 + far), quarter + far_flops, 4 << 20, 10,
-    )(query, *far_b[1:], *middle, bias, w_out, summed)
+        [VMEM] * 8, quarter + far_flops // far, 4 << 20, 10,
+    )(query, d_b, *middle, bias, w_out, summed)
     got_low = lax.ppermute(send, "head", SWAP)
     (send,) = call(
         functools.partial(send_columns, cut), "send_high", [send_shape], [VMEM] * 3, quarter, 4 << 20, 6,

time: 47.7 us -> 46.9 us (0.983)
  waiting for transfers between devices: 9.02 us -> 7.2 us
  starting transfers between devices: 10.5 us -> 11.8 us
    ppermute x6, waiting for transfers between devices: 6.42 us -> 4.44 us  [exchange(): lax.ppermute(array, 'seq', [(i, i ^ way) for i in every])]
    ppermute x1, starting transfers between devices: 0.83 us -> 2.15 us  [body(): got_low = lax.ppermute(send, 'head', SWAP)]
    pallas_call x1, Pallas kernels: 2.33 us -> 1.71 us  [body(): call(functools.partial(mix_second_kernel, heads // 2), 'mix_second', [sen...]
    pallas_call x1, Pallas kernels: 1.28 us -> 1.79 us  [body(): call(functools.partial(middle_kernel, heads // 2), 'attend_middle', [shap...]
  transfers between devices with their start and end apart: 11 -> 11, of which waited for: 5 -> 5; matrix products, arithmetic and copies ran while one was open for 0% -> 0% of each run, Pallas kernels for 49% -> 51%
where the time goes in v8:
time: 46.9 us; the launch traced here: 46.7 us
  Pallas kernels  27.2 us (58%)
  starting transfers between devices  11.8 us (25%)
  waiting for transfers between devices  7.2 us (15%)
    ppermute x6, starting transfers between devices, exchange(): lax.ppermute(array, 'seq', [(i, i ^ way) for i in every])  5.49 us
    pallas_call x1, Pallas kernels, body(): call(query_kernel, 'queries', [shape((tokens, width_q), bf16), flag], [VM...  4.78 us
    pallas_call x1, Pallas kernels, body(): call(functools.partial(mix_first_kernel, distances), 'mix_first', [shape(...  4.72 us
    ppermute x6, waiting for transfers between devices, exchange(): lax.ppermute(array, 'seq', [(i, i ^ way) for i in every])  4.44 us
    pallas_call x1, Pallas kernels, body(): call(functools.partial(third_kernel, chunks), 'keys_values_more', [kv_sha...  4.02 us
    pallas_call x1, Pallas kernels, body(): call(functools.partial(first_kernel, chunks), 'keys_values_own', [shape((...  3.07 us
    pallas_call x1, Pallas kernels, body(): call(functools.partial(near_kernel, ((0, 0), (LAYER, LAYER))), 'scores_ne...  2.98 us
    ppermute x1, waiting for transfers between devices, body(): z_a = lax.ppermute(kv_a, 'seq', [(a, b) for a, b in step_z if a < b])  2.36 us
  transfers between devices with their start and end apart: 11, of which 5 were waited for; matrix products, arithmetic and copies ran while one was open for 0% of the time, Pallas kernels for 51%

profile of v8, /device:TPU:25, one launch (start us, length us, event | category | flops | bytes accessed | tf_op | source)
XLA Modules:
  0.0 46.7 jit_solution(3937692467026629762)
XLA Ops:
  0.0 0.7 %collective-permute-start = (bf16[128,4096]{1,0:T(8,128)(2,1)}, bf16[128,4096]{1,0:T(8,128)(2,1)S(1)}, u32[]{:S(2)}, u32[]{:S(2)}) collective-permute-start(bf16[128,4096]{1,0:T(8,128)(2,1)} %own_hbm.1), channel_id=1, source_target_pairs={{0,1},{1,0},{2,3},{3,2},{4,5},{5,4},{6,7},{7,6},{8,9},{9,8},{10,11... | collective-permute-start | bytes 3145736 | tf_op jit(solution)/shard_map/ppermute | solution.py:373
  0.7 3.1 %keys_values_own.1 = (f32[128,512]{1,0:T(8,128)S(1)}, bf16[128,4096]{1,0:T(8,128)(2,1)S(1)}, bf16[4096,256]{1,0:T(8,128)(2,1)S(1)}, bf16[4096,256]{1,0:T(8,128)(...) custom-call(s32[8]{0:T(128)} %lengths_hbm.1, bf16[128,4096]{1,0:T(8,128)(2,1)} %own_hbm.1, ...), custom_call_target="tpu_custom_call" | custom-call | flops 536870912 | bytes 4194304 | tf_op jit(solution)/shard_map/keys_values_own/pallas_call | solution.py:382
  3.8 0.8 %keys_values.1.own.refs_0_ = bf16[256,512]{1,0:T(8,128)(2,1)S(1)} custom-call(bf16[128,4096]{1,0:T(8,128)(2,1)S(1)} %collective-permute-done.other, bf16[4096,256]{1,0:T(8,128)(2,1)S(1)} %get-tuple-element.35.w_key, bf16[4096,256]{1,0:T(8,128)(2,1)S(1)} %get-tuple-element.36.w_value, f32[128,512]{1,0:T(8,128)S(1)} %get-tuple-element.37.own_total, ...), custom_call_target="tpu_custom_call" | custom-call | flops 536870912 | bytes 4194304 | tf_op jit(solution)/shard_map/keys_values/pallas_call | solution.py:391
  4.6 1.3 %collective-permute-start.1 = (bf16[256,512]{1,0:T(8,128)(2,1)S(1)}, bf16[256,512]{1,0:T(8,128)(2,1)S(1)}, u32[]{:S(2)}, u32[]{:S(2)}) collective-permute-start(bf16[256,512]{1,0:T(8,128)(2,1)S(1)} %keys_values.1.own.refs_0_), channel_id=1, source_target_pairs={{0,8},{2,10},{4,12},{6,14},{8,16},{10,18},{12,20},{14,22},{16,24},... | collective-permute-start | bytes 786440 | tf_op jit(solution)/shard_map/ppermute | solution.py:397
  5.9 0.0 slice-start.4
  5.9 4.0 %keys_values_more.1 = (bf16[256,512]{1,0:T(8,128)(2,1)S(1)}, bf16[256,4096]{1,0:T(8,128)(2,1)S(1)}, f32[8,128]{1,0:T(8,128)}) custom-call(bf16[128,4096]{1,0:T(8,128)(2,1)S(1)} %get-tuple-element.31.own, bf16[128,4096]{1,0:T(8,128)(2,1)S(1)} %collective-permute-done.other, bf16[4096,512]{1,0:T(8,128)(2,1)} %key_hbm.3, bf16[4096,512]{1,0:T(8,128)(2,1)} %value_hbm.3, ...), custom_call_target="tpu_custom_call" | custom-call | flops 4294967296 | bytes 4194304 | tf_op jit(solution)/shard_map/keys_values_more/pallas_call | solution.py:399
  9.9 0.0 slice-start.6
  9.9 2.1 %collective-permute-start.2 = (bf16[256,512]{1,0:T(8,128)(2,1)S(1)}, bf16[256,512]{1,0:T(8,128)(2,1)S(1)}, u32[]{:S(2)}, u32[]{:S(2)}) collective-permute-start(bf16[256,512]{1,0:T(8,128)(2,1)S(1)} %get-tuple-element.38.after.refs_2_.own), channel_id=1, source_target_pairs={{0,8},{2,10},{4,12},{6,14},{8,16},{10,18},{12,20},{14,22},{16,24},... | collective-permute-start | bytes 786440 | tf_op jit(solution)/shard_map/ppermute | solution.py:404
  12.0 2.4 %collective-permute-done.1.earlier.refs_1_ = bf16[256,512]{1,0:T(8,128)(2,1)S(1)} collective-permute-done((bf16[256,512]{1,0:T(8,128)(2,1)S(1)}, bf16[256,512]{1,0:T(8,128)(2,1)S(1)}, u32[]{:S(2)}, u32[]{:S(2)}) %collective-permute-start.1) | collective-permute-done | bytes 262176 | tf_op jit(solution)/shard_map/ppermute | solution.py:397
  14.4 0.1 relay.3
  14.5 2.2 %collective-permute-start.6 = (bf16[256,512]{1,0:T(8,128)(2,1)S(1)}, bf16[256,512]{1,0:T(8,128)(2,1)S(1)}, u32[]{:S(2)}, u32[]{:S(2)}) collective-permute-start(bf16[256,512]{1,0:T(8,128)(2,1)S(1)} %get-tuple-element.48), channel_id=1, source_target_pairs={{0,6},{2,4},{4,2},{6,0},{8,14},{10,12},{12,10},{14,8},{16,22},{18,... | collective-permute-start | bytes 786440 | tf_op jit(solution)/shard_map/ppermute | solution.py:410
  16.7 0.2 collective-permute-start.8
  16.9 0.3 collective-permute-start.7
  17.2 4.8 %queries.1 = (bf16[256,2048]{1,0:T(8,128)(2,1)S(1)}, f32[8,128]{1,0:T(8,128)S(1)}) custom-call(bf16[256,4096]{1,0:T(8,128)(2,1)S(1)} %get-tuple-element.34.rows, bf16[4096,2048]{1,0:T(8,128)(2,1)S(1)} %bitcast.3, f32[256,128]{1,0:T(8,128)S(1)} %get-tuple-element.32.cosine, f32[256,128]{1,0:T(8,128)S(1)} %get-tuple-element.33.sine, ...), custom_call_target="tpu_custom_call" | custom-call | flops 4294967296 | bytes 16777216 | tf_op jit(solution)/shard_map/queries/pallas_call | solution.py:414
  22.1 0.1 relay.5
  22.1 1.3 %collective-permute-start.4 = (bf16[256,512]{1,0:T(8,128)(2,1)S(1)}, bf16[256,512]{1,0:T(8,128)(2,1)S(1)}, u32[]{:S(2)}, u32[]{:S(2)}) collective-permute-start(bf16[256,512]{1,0:T(8,128)(2,1)S(1)} %get-tuple-element.44), channel_id=1, source_target_pairs={{0,2},{2,0},{4,6},{6,4},{8,10},{10,8},{12,14},{14,12},{16,18},{18,... | collective-permute-start | bytes 786440 | tf_op jit(solution)/shard_map/ppermute | solution.py:410
  23.4 1.2 %collective-permute-start.5 = (bf16[256,512]{1,0:T(8,128)(2,1)S(1)}, bf16[256,512]{1,0:T(8,128)(2,1)S(1)}, u32[]{:S(2)}, u32[]{:S(2)}) collective-permute-start(bf16[256,512]{1,0:T(8,128)(2,1)S(1)} %get-tuple-element.45), channel_id=1, source_target_pairs={{0,4},{2,6},{4,0},{6,2},{8,12},{10,14},{12,8},{14,10},{16,20},{18,... | collective-permute-start | bytes 786440 | tf_op jit(solution)/shard_map/ppermute | solution.py:410
  24.7 3.0 %scores_near.1 = (f32[16,256,128]{2,1,0:T(8,128)S(1)}, f32[16,256,128]{2,1,0:T(8,128)S(1)}, f32[16,256,128]{2,1,0:T(8,128)S(1)}) custom-call(s32[256,128]{1,0:T(8,128)S(1)} %get-tuple-element.41.starts, bf16[256,2048]{1,0:T(8,128)(2,1)S(1)} %get-tuple-element.40.query, bf16[256,512]{1,0:T(8,128)(2,1)S(1)} %keys_values.1.own.refs_0_, ...), custom_call_target="tpu_custom_call" | custom-call | flops 1073741824 | bytes 8388608 | tf_op jit(solution)/shard_map/scores_near/pallas_call | solution.py:419
  27.7 0.3 collective-permute-start.3
  28.0 1.3 %collective-permute-done.8.refs_2_ = bf16[256,512]{1,0:T(8,128)(2,1)S(1)} collective-permute-done((bf16[256,512]{1,0:T(8,128)(2,1)S(1)}, bf16[256,512]{1,0:T(8,128)(2,1)S(1)}, u32[]{:S(2)}, u32[]{:S(2)}) %collective-permute-start.8) | collective-permute-done | bytes 262176 | tf_op jit(solution)/shard_map/ppermute | solution.py:410
  29.3 4.7 %mix_first.1 = (f32[256,4096]{1,0:T(8,128)S(1)}, bf16[256,1024]{1,0:T(8,128)(2,1)}, f32[256,768]{1,0:T(8,128)S(1)}) custom-call(s32[256,128]{1,0:T(8,128)S(1)} %get-tuple-element.41.starts, bf16[256,2048]{1,0:T(8,128)(2,1)S(1)} %get-tuple-element.40.query, bf16[256,512]{1,0:T(8,128)(2,1)S(1)} %collective-permute-done.6.refs_0_, ...), custom_call_target="tpu_custom_call" | custom-call | flops 3355443200 | bytes 4194304 | tf_op jit(solution)/shard_map/mix_first/pallas_call | solution.py:432
  34.1 2.4 %collective-permute-done.5.second = bf16[256,512]{1,0:T(8,128)(2,1)S(1)} collective-permute-done((bf16[256,512]{1,0:T(8,128)(2,1)S(1)}, bf16[256,512]{1,0:T(8,128)(2,1)S(1)}, u32[]{:S(2)}, u32[]{:S(2)}) %collective-permute-start.5) | collective-permute-done | bytes 262176 | tf_op jit(solution)/shard_map/ppermute | solution.py:410
  36.4 1.8 %attend_middle.1 = (f32[8,256,128]{2,1,0:T(8,128)S(1)}, f32[8,256,128]{2,1,0:T(8,128)S(1)}, f32[8,256,128]{2,1,0:T(8,128)S(1)}) custom-call(bf16[256,2048]{1,0:T(8,128)(2,1)S(1)} %get-tuple-element.40.query, bf16[256,512]{1,0:T(8,128)(2,1)S(1)} %collective-permute-done.4.first, bf16[256,512]{1,0:T(8,128)(2,1)S(1)} %collective-permute-done.5.second, ...), custom_call_target="tpu_custom_call" | custom-call | flops 805306368 | bytes 4194304 | tf_op jit(solution)/shard_map/attend_middle/pallas_call | solution.py:437
  38.2 0.7 %collective-permute-done.3.block = bf16[256,512]{1,0:T(8,128)(2,1)S(1)} collective-permute-done((bf16[256,512]{1,0:T(8,128)(2,1)S(1)}, bf16[256,512]{1,0:T(8,128)(2,1)S(1)}, u32[]{:S(2)}, u32[]{:S(2)}) %collective-permute-start.3) | collective-permute-done | bytes 262176 | tf_op jit(solution)/shard_map/ppermute | solution.py:410
  39.0 1.7 %mix_second.1 = (bf16[128,2048]{1,0:T(8,128)(2,1)S(1)}, bf16[256,1024]{1,0:T(8,128)(2,1)S(1)}) custom-call(bf16[256,2048]{1,0:T(8,128)(2,1)S(1)} %get-tuple-element.40.query, bf16[256,512]{1,0:T(8,128)(2,1)S(1)} %collective-permute-done.3.block, f32[8,256,128]{2,1,0:T(8,128)S(1)} %get-tuple-element.51.tops, f32[8,256,128]{2,1,0:T(8,128)S(1)} %get-tuple-element.52.totals, ...), custom_call_target="tpu_custom_call" | custom-call | flops 939524096 | bytes 4194304 | tf_op jit(solution)/shard_map/mix_second/pallas_call | solution.py:445
  40.7 2.1 %collective-permute-start.9 = (bf16[128,2048]{1,0:T(8,128)(2,1)S(1)}, bf16[128,2048]{1,0:T(8,128)(2,1)S(1)}, u32[]{:S(2)}, u32[]{:S(2)}) collective-permute-start(bf16[128,2048]{1,0:T(8,128)(2,1)S(1)} %get-tuple-element.56), channel_id=1, source_target_pairs={{0,1},{1,0},{2,3},{3,2},{4,5},{5,4},{6,7},{7,6},{8,9},{9,8},{10,11... | collective-permute-start | bytes 1572872 | tf_op jit(solution)/shard_map/ppermute | solution.py:449
  42.8 0.7 %send_high.1 = bf16[128,2048]{1,0:T(8,128)(2,1)S(1)} custom-call(bf16[256,1024]{1,0:T(8,128)(2,1)S(1)} %get-tuple-element.55.attended, bf16[2048,4096]{1,0:T(8,128)(2,1)S(1)} %bitcast.1, f32[256,4096]{1,0:T(8,128)S(1)} %get-tuple-element.54.summed), custom_call_target="tpu_custom_call" | custom-call | flops 536870912 | bytes 4194304 | tf_op jit(solution)/shard_map/send_high/pallas_call | solution.py:450
  43.6 0.1 collective-permute-start.10
  43.6 0.7 %own_high.1.after.own = f32[128,2048]{1,0:T(8,128)S(1)} custom-call(bf16[256,1024]{1,0:T(8,128)(2,1)S(1)} %get-tuple-element.55.attended, bf16[2048,4096]{1,0:T(8,128)(2,1)S(1)} %bitcast.1, f32[256,4096]{1,0:T(8,128)S(1)} %get-tuple-element.54.summed), custom_call_target="tpu_custom_call" | custom-call | flops 536870912 | bytes 4194304 | tf_op jit(solution)/shard_map/own_high/pallas_call | solution.py:454
  44.4 0.7 %own_low.1.mixed_low = bf16[128,2048]{1,0:T(8,128)(2,1)S(1)} custom-call(bf16[256,1024]{1,0:T(8,128)(2,1)S(1)} %get-tuple-element.55.attended, bf16[2048,4096]{1,0:T(8,128)(2,1)S(1)} %bitcast.1, f32[256,4096]{1,0:T(8,128)S(1)} %get-tuple-element.54.summed, bf16[128,2048]{1,0:T(8,128)(2,1)S(1)} %collective-permute-done.9.got, f32[128,2048]{1,0:T(8,128)S(1)} %own_high.1.after.own), custom_call_target="tpu_custom_call" | custom-call | flops 536870912 | bytes 4194304 | tf_op jit(solution)/shard_map/own_low/pallas_call | solution.py:458
  45.1 0.4 collective-permute-done.10.got
  45.5 1.0 %add.1 = bf16[128,4096]{1,0:T(8,128)(2,1)} custom-call(bf16[128,2048]{1,0:T(8,128)(2,1)S(1)} %own_low.1.mixed_low, f32[128,2048]{1,0:T(8,128)S(1)} %own_high.1.after.own, bf16[128,2048]{1,0:T(8,128)(2,1)S(1)} %collective-permute-done.10.got), custom_call_target="tpu_custom_call" | custom-call | flops 262144 | bytes 4194304 | tf_op jit(solution)/shard_map/add/pallas_call | solution.py:461
  (23 shorter events, 0.1 us)
Async XLA Ops:
  0.0 3.8 %collective-permute-start = (bf16[128,4096]{1,0:T(8,128)(2,1)}, bf16[128,4096]{1,0:T(8,128)(2,1)S(1)}, u32[]{:S(2)}, u32[]{:S(2)}) collective-permute-start(bf16[128,4096]{1,0:T(8,128)(2,1)} %own_hbm.1), channel_id=1, source_target_pairs={{0,1},{1,0},{2,3},{3,2},{4,5},{5,4},{6,7},{7,6},{8,9},{9,8},{10,11... | collective-permute-start | bytes 3145736 | tf_op jit(solution)/shard_map/ppermute | solution.py:373
  4.6 9.8 %collective-permute-start.1 = (bf16[256,512]{1,0:T(8,128)(2,1)S(1)}, bf16[256,512]{1,0:T(8,128)(2,1)S(1)}, u32[]{:S(2)}, u32[]{:S(2)}) collective-permute-start(bf16[256,512]{1,0:T(8,128)(2,1)S(1)} %keys_values.1.own.refs_0_), channel_id=1, source_target_pairs={{0,8},{2,10},{4,12},{6,14},{8,16},{10,18},{12,20},{14,22},{16,24},... | collective-permute-start | bytes 786440 | tf_op jit(solution)/shard_map/ppermute | solution.py:397
  5.9 11.3 %slice-start.4 = ((s8[16777216]{0:T(1024)(128)(4,1)}), s8[4194304]{0:T(1024)(128)(4,1)S(1)}, s32[]{:S(2)}) async-start(s8[16777216]{0:T(1024)(128)(4,1)} %bitcast.2), calls=%async_computation.4 | async-start | bytes 8388608
  5.9 11.3 %slice-start.5 = ((s8[16777216]{0:T(1024)(128)(4,1)}), s8[4194304]{0:T(1024)(128)(4,1)S(1)}, s32[]{:S(2)}) async-start(s8[16777216]{0:T(1024)(128)(4,1)} %bitcast.2), calls=%async_computation.5 | async-start | bytes 8388608
  9.9 7.3 %slice-start.6 = ((s8[16777216]{0:T(1024)(128)(4,1)}), s8[4194304]{0:T(1024)(128)(4,1)S(1)}, s32[]{:S(2)}) async-start(s8[16777216]{0:T(1024)(128)(4,1)} %bitcast.2), calls=%async_computation.6 | async-start | bytes 8388608
  9.9 7.3 %slice-start.7 = ((s8[16777216]{0:T(1024)(128)(4,1)}), s8[4194304]{0:T(1024)(128)(4,1)S(1)}, s32[]{:S(2)}) async-start(s8[16777216]{0:T(1024)(128)(4,1)} %bitcast.2), calls=%async_computation.7 | async-start | bytes 8388608
  9.9 12.1 %collective-permute-start.2 = (bf16[256,512]{1,0:T(8,128)(2,1)S(1)}, bf16[256,512]{1,0:T(8,128)(2,1)S(1)}, u32[]{:S(2)}, u32[]{:S(2)}) collective-permute-start(bf16[256,512]{1,0:T(8,128)(2,1)S(1)} %get-tuple-element.38.after.refs_2_.own), channel_id=1, source_target_pairs={{0,8},{2,10},{4,12},{6,14},{8,16},{10,18},{12,20},{14,22},{16,24},... | collective-permute-start | bytes 786440 | tf_op jit(solution)/shard_map/ppermute | solution.py:404
  14.5 13.2 %collective-permute-start.6 = (bf16[256,512]{1,0:T(8,128)(2,1)S(1)}, bf16[256,512]{1,0:T(8,128)(2,1)S(1)}, u32[]{:S(2)}, u32[]{:S(2)}) collective-permute-start(bf16[256,512]{1,0:T(8,128)(2,1)S(1)} %get-tuple-element.48), channel_id=1, source_target_pairs={{0,6},{2,4},{4,2},{6,0},{8,14},{10,12},{12,10},{14,8},{16,22},{18,... | collective-permute-start | bytes 786440 | tf_op jit(solution)/shard_map/ppermute | solution.py:410
  16.7 12.6 %collective-permute-start.8 = (bf16[256,512]{1,0:T(8,128)(2,1)S(1)}, bf16[256,512]{1,0:T(8,128)(2,1)S(1)}, u32[]{:S(2)}, u32[]{:S(2)}) collective-permute-start(bf16[256,512]{1,0:T(8,128)(2,1)S(1)} %get-tuple-element.49), channel_id=1, source_target_pairs={{0,4},{2,6},{4,0},{6,2},{8,12},{10,14},{12,8},{14,10},{16,20},{18,... | collective-permute-start | bytes 786440 | tf_op jit(solution)/shard_map/ppermute | solution.py:410
  16.9 12.4 %collective-permute-start.7 = (bf16[256,512]{1,0:T(8,128)(2,1)S(1)}, bf16[256,512]{1,0:T(8,128)(2,1)S(1)}, u32[]{:S(2)}, u32[]{:S(2)}) collective-permute-start(bf16[256,512]{1,0:T(8,128)(2,1)S(1)} %get-tuple-element.39.after), channel_id=1, source_target_pairs={{0,2},{2,0},{4,6},{6,4},{8,10},{10,8},{12,14},{14,12},{16,18},{18,... | collective-permute-start | bytes 786440 | tf_op jit(solution)/shard_map/ppermute | solution.py:410
  17.2 12.1 %slice-start = ((s8[16777216]{0:T(1024)(128)(4,1)}), s8[4194304]{0:T(1024)(128)(4,1)S(1)}, s32[]{:S(2)}) async-start(s8[16777216]{0:T(1024)(128)(4,1)} %bitcast), calls=%async_computation | async-start | bytes 8388608
  17.2 12.1 %slice-start.1 = ((s8[16777216]{0:T(1024)(128)(4,1)}), s8[4194304]{0:T(1024)(128)(4,1)S(1)}, s32[]{:S(2)}) async-start(s8[16777216]{0:T(1024)(128)(4,1)} %bitcast), calls=%async_computation.1 | async-start | bytes 8388608
  22.0 7.3 %slice-start.2 = ((s8[16777216]{0:T(1024)(128)(4,1)}), s8[4194304]{0:T(1024)(128)(4,1)S(1)}, s32[]{:S(2)}) async-start(s8[16777216]{0:T(1024)(128)(4,1)} %bitcast), calls=%async_computation.2 | async-start | bytes 8388608
  22.0 7.3 %slice-start.3 = ((s8[16777216]{0:T(1024)(128)(4,1)}), s8[4194304]{0:T(1024)(128)(4,1)S(1)}, s32[]{:S(2)}) async-start(s8[16777216]{0:T(1024)(128)(4,1)} %bitcast), calls=%async_computation.3 | async-start | bytes 8388608
  22.1 11.9 %collective-permute-start.4 = (bf16[256,512]{1,0:T(8,128)(2,1)S(1)}, bf16[256,512]{1,0:T(8,128)(2,1)S(1)}, u32[]{:S(2)}, u32[]{:S(2)}) collective-permute-start(bf16[256,512]{1,0:T(8,128)(2,1)S(1)} %get-tuple-element.44), channel_id=1, source_target_pairs={{0,2},{2,0},{4,6},{6,4},{8,10},{10,8},{12,14},{14,12},{16,18},{18,... | collective-permute-start | bytes 786440 | tf_op jit(solution)/shard_map/ppermute | solution.py:410
  23.4 13.0 %collective-permute-start.5 = (bf16[256,512]{1,0:T(8,128)(2,1)S(1)}, bf16[256,512]{1,0:T(8,128)(2,1)S(1)}, u32[]{:S(2)}, u32[]{:S(2)}) collective-permute-start(bf16[256,512]{1,0:T(8,128)(2,1)S(1)} %get-tuple-element.45), channel_id=1, source_target_pairs={{0,4},{2,6},{4,0},{6,2},{8,12},{10,14},{12,8},{14,10},{16,20},{18,... | collective-permute-start | bytes 786440 | tf_op jit(solution)/shard_map/ppermute | solution.py:410
  27.7 11.3 %collective-permute-start.3 = (bf16[256,512]{1,0:T(8,128)(2,1)S(1)}, bf16[256,512]{1,0:T(8,128)(2,1)S(1)}, u32[]{:S(2)}, u32[]{:S(2)}) collective-permute-start(bf16[256,512]{1,0:T(8,128)(2,1)S(1)} %relay.4), channel_id=1, source_target_pairs={{0,6},{2,4},{4,2},{6,0},{8,14},{10,12},{12,10},{14,8},{16,22},{18,... | collective-permute-start | bytes 786440 | tf_op jit(solution)/shard_map/ppermute | solution.py:410
  40.7 3.7 %collective-permute-start.9 = (bf16[128,2048]{1,0:T(8,128)(2,1)S(1)}, bf16[128,2048]{1,0:T(8,128)(2,1)S(1)}, u32[]{:S(2)}, u32[]{:S(2)}) collective-permute-start(bf16[128,2048]{1,0:T(8,128)(2,1)S(1)} %get-tuple-element.56), channel_id=1, source_target_pairs={{0,1},{1,0},{2,3},{3,2},{4,5},{5,4},{6,7},{7,6},{8,9},{9,8},{10,11... | collective-permute-start | bytes 1572872 | tf_op jit(solution)/shard_map/ppermute | solution.py:449
  43.6 2.0 %collective-permute-start.10 = (bf16[128,2048]{1,0:T(8,128)(2,1)S(1)}, bf16[128,2048]{1,0:T(8,128)(2,1)S(1)}, u32[]{:S(2)}, u32[]{:S(2)}) collective-permute-start(bf16[128,2048]{1,0:T(8,128)(2,1)S(1)} %send_high.1), channel_id=1, source_target_pairs={{0,1},{1,0},{2,3},{3,2},{4,5},{5,4},{6,7},{7,6},{8,9},{9,8},{10,11... | collective-permute-start | bytes 1572872 | tf_op jit(solution)/shard_map/ppermute | solution.py:453

commit v9 on v8

--- a/solution.py
+++ b/solution.py
@@ -285,7 +285,7 @@
         summed[:, at] = dot(attended[...], weight[:depth, at])
 
 
-def middle_kernel(low, query, first, second, tops, totals, accs, bias, new_tops, new_totals, new_accs):
+def middle_kernel(low, query, second, first, tops, totals, accs, bias, new_tops, new_totals, new_accs):
     tokens = bias.shape[0]
     late = bias.at[:, pl.ds(bias.shape[1] - 2 * tokens, 2 * tokens)]
 
@@ -334,11 +334,11 @@
     low = mixed_low.shape[1]
     copies = [pltpu.make_async_copy(mixed_low, mixed_hbm.at[:, pl.ds(0, low)], sems.at[0])]
     copies[0].start()
-    for number in range(own.shape[1] // WIDE):
-        at = slice(number * WIDE, (number + 1) * WIDE)
+    for number in range(own.shape[1] // (2 * WIDE)):
+        at = slice(number * 2 * WIDE, (number + 1) * (2 * WIDE))
         mixed[:, at] = (own[:, at] + got[:, at].astype(jnp.float32)).astype(mixed.dtype)
-        there = mixed_hbm.at[:, pl.ds(low + number * WIDE, WIDE)]
-        copies.append(pltpu.make_async_copy(mixed.at[:, pl.ds(number * WIDE, WIDE)], there, sems.at[number + 1]))
+        there = mixed_hbm.at[:, pl.ds(low + number * 2 * WIDE, 2 * WIDE)]
+        copies.append(pltpu.make_async_copy(mixed.at[:, pl.ds(number * 2 * WIDE, 2 * WIDE)], there, sems.at[number + 1]))
         copies[-1].start()
     for copy in copies:
         copy.wait()
@@ -409,7 +409,8 @@
         )(mine, earlier, after)
         return [lax.ppermute(array, "seq", [(i, i ^ way) for i in every]) for way, array in zip(ways, to)], to[0]
 
-    (x_a, y_a, d_a), done = exchange(kv_a, z_a, kv_b, (1, 2, 3), RELAY_COST)
+    (d_a,), done = exchange(kv_a, z_a, kv_b, (3,), RELAY_COST)
+    (x_a, y_a), done = exchange(kv_a, z_a, done, (1, 2), 0)
     far_a = d_a, x_a, y_a
     query, done = call(
         query_kernel, "queries", [shape((tokens, width_q), bf16), flag], [VMEM] * 5,
@@ -437,7 +438,7 @@
     middle = call(
         functools.partial(middle_kernel, heads // 2), "attend_middle", [shape((heads // 2, tokens, HEAD_SIZE), f32)] * 3,
         [VMEM] * 7, far_flops // far * 2, 4 << 20, 10,
-    )(query, x_b, y_b, *near, bias)
+    )(query, y_b, x_b, *near, bias)
 
     cut = columns // 2
     send_shape = shape((half, cut), bf16)
@@ -460,7 +461,7 @@
     )(attended, w_out, summed, got_low, own)
     (mixed,) = call(
         add_kernel, "add", [pltpu.HBM((half, columns), bf16)], [VMEM] * 3, half * cut, 4 << 20, 4,
-        [pltpu.VMEM((half, columns - cut), bf16), pltpu.SemaphoreType.DMA(((columns - cut) // WIDE + 1,))], [ANY],
+        [pltpu.VMEM((half, columns - cut), bf16), pltpu.SemaphoreType.DMA(((columns - cut) // (2 * WIDE) + 1,))], [ANY],
     )(mixed, own, got_high)
     return mixed
 

time: 46.9 us -> 46.9 us (level)
  no operation moved by 1% of the time
where the time goes in v9:
time: 46.9 us; the launch traced here: 46.7 us
  Pallas kernels  27.3 us (58%)
  starting transfers between devices  11.9 us (25%)
  waiting for transfers between devices  7.01 us (15%)
    ppermute x6, starting transfers between devices, exchange(): lax.ppermute(array, 'seq', [(i, i ^ way) for i in every])  5.56 us
    pallas_call x1, Pallas kernels, body(): call(query_kernel, 'queries', [shape((tokens, width_q), bf16), flag], [VM...  4.78 us
    pallas_call x1, Pallas kernels, body(): call(functools.partial(mix_first_kernel, distances), 'mix_first', [shape(...  4.71 us
    ppermute x6, waiting for transfers between devices, exchange(): lax.ppermute(array, 'seq', [(i, i ^ way) for i in every])  4.26 us
    pallas_call x1, Pallas kernels, body(): call(functools.partial(third_kernel, chunks), 'keys_values_more', [kv_sha...  4.02 us
    pallas_call x1, Pallas kernels, body(): call(functools.partial(first_kernel, chunks), 'keys_values_own', [shape((...  3.07 us
    pallas_call x1, Pallas kernels, body(): call(functools.partial(near_kernel, ((0, 0), (LAYER, LAYER))), 'scores_ne...  2.98 us
    ppermute x1, waiting for transfers between devices, body(): z_a = lax.ppermute(kv_a, 'seq', [(a, b) for a, b in step_z if a < b])  2.36 us
  transfers between devices with their start and end apart: 11, of which 5 were waited for; matrix products, arithmetic and copies ran while one was open for 0% of the time, Pallas kernels for 51%

profile of v9, /device:TPU:25, one launch (start us, length us, event | category | flops | bytes accessed | tf_op | source)
XLA Modules:
  0.0 46.7 jit_solution(9624276866111248989)
XLA Ops:
  0.0 0.7 %collective-permute-start = (bf16[128,4096]{1,0:T(8,128)(2,1)}, bf16[128,4096]{1,0:T(8,128)(2,1)S(1)}, u32[]{:S(2)}, u32[]{:S(2)}) collective-permute-start(bf16[128,4096]{1,0:T(8,128)(2,1)} %own_hbm.1), channel_id=1, source_target_pairs={{0,1},{1,0},{2,3},{3,2},{4,5},{5,4},{6,7},{7,6},{8,9},{9,8},{10,11... | collective-permute-start | bytes 3145736 | tf_op jit(solution)/shard_map/ppermute | solution.py:373
  0.7 3.1 %keys_values_own.1 = (f32[128,512]{1,0:T(8,128)S(1)}, bf16[128,4096]{1,0:T(8,128)(2,1)S(1)}, bf16[4096,256]{1,0:T(8,128)(2,1)S(1)}, bf16[4096,256]{1,0:T(8,128)(...) custom-call(s32[8]{0:T(128)} %lengths_hbm.1, bf16[128,4096]{1,0:T(8,128)(2,1)} %own_hbm.1, ...), custom_call_target="tpu_custom_call" | custom-call | flops 536870912 | bytes 4194304 | tf_op jit(solution)/shard_map/keys_values_own/pallas_call | solution.py:382
  3.8 0.8 %keys_values.1.own.refs_0_ = bf16[256,512]{1,0:T(8,128)(2,1)S(1)} custom-call(bf16[128,4096]{1,0:T(8,128)(2,1)S(1)} %collective-permute-done.other, bf16[4096,256]{1,0:T(8,128)(2,1)S(1)} %get-tuple-element.34.w_key, bf16[4096,256]{1,0:T(8,128)(2,1)S(1)} %get-tuple-element.35.w_value, f32[128,512]{1,0:T(8,128)S(1)} %get-tuple-element.36.own_total, ...), custom_call_target="tpu_custom_call" | custom-call | flops 536870912 | bytes 4194304 | tf_op jit(solution)/shard_map/keys_values/pallas_call | solution.py:391
  4.6 1.3 %collective-permute-start.1 = (bf16[256,512]{1,0:T(8,128)(2,1)S(1)}, bf16[256,512]{1,0:T(8,128)(2,1)S(1)}, u32[]{:S(2)}, u32[]{:S(2)}) collective-permute-start(bf16[256,512]{1,0:T(8,128)(2,1)S(1)} %keys_values.1.own.refs_0_), channel_id=1, source_target_pairs={{0,8},{2,10},{4,12},{6,14},{8,16},{10,18},{12,20},{14,22},{16,24},... | collective-permute-start | bytes 786440 | tf_op jit(solution)/shard_map/ppermute | solution.py:397
  5.9 0.0 slice-start.4
  5.9 4.0 %keys_values_more.1 = (bf16[256,512]{1,0:T(8,128)(2,1)S(1)}, bf16[256,4096]{1,0:T(8,128)(2,1)S(1)}, f32[8,128]{1,0:T(8,128)}) custom-call(bf16[128,4096]{1,0:T(8,128)(2,1)S(1)} %get-tuple-element.30.own, bf16[128,4096]{1,0:T(8,128)(2,1)S(1)} %collective-permute-done.other, bf16[4096,512]{1,0:T(8,128)(2,1)} %key_hbm.3, bf16[4096,512]{1,0:T(8,128)(2,1)} %value_hbm.3, ...), custom_call_target="tpu_custom_call" | custom-call | flops 4294967296 | bytes 4194304 | tf_op jit(solution)/shard_map/keys_values_more/pallas_call | solution.py:399
  9.9 0.0 slice-start.6
  9.9 2.1 %collective-permute-start.2 = (bf16[256,512]{1,0:T(8,128)(2,1)S(1)}, bf16[256,512]{1,0:T(8,128)(2,1)S(1)}, u32[]{:S(2)}, u32[]{:S(2)}) collective-permute-start(bf16[256,512]{1,0:T(8,128)(2,1)S(1)} %get-tuple-element.37.after.refs_2_.own), channel_id=1, source_target_pairs={{0,8},{2,10},{4,12},{6,14},{8,16},{10,18},{12,20},{14,22},{16,24},... | collective-permute-start | bytes 786440 | tf_op jit(solution)/shard_map/ppermute | solution.py:404
  12.0 2.4 %collective-permute-done.1.earlier.refs_1_ = bf16[256,512]{1,0:T(8,128)(2,1)S(1)} collective-permute-done((bf16[256,512]{1,0:T(8,128)(2,1)S(1)}, bf16[256,512]{1,0:T(8,128)(2,1)S(1)}, u32[]{:S(2)}, u32[]{:S(2)}) %collective-permute-start.1) | collective-permute-done | bytes 262176 | tf_op jit(solution)/shard_map/ppermute | solution.py:397
  14.4 2.2 %collective-permute-start.6 = (bf16[256,512]{1,0:T(8,128)(2,1)S(1)}, bf16[256,512]{1,0:T(8,128)(2,1)S(1)}, u32[]{:S(2)}, u32[]{:S(2)}) collective-permute-start(bf16[256,512]{1,0:T(8,128)(2,1)S(1)} %relay.4.after), channel_id=1, source_target_pairs={{0,6},{2,4},{4,2},{6,0},{8,14},{10,12},{12,10},{14,8},{16,22},{18,... | collective-permute-start | bytes 786440 | tf_op jit(solution)/shard_map/ppermute | solution.py:410
  16.7 0.1 relay.5
  16.7 0.3 collective-permute-start.8
  17.0 0.3 collective-permute-start.7
  17.3 4.8 %queries.1 = (bf16[256,2048]{1,0:T(8,128)(2,1)S(1)}, f32[8,128]{1,0:T(8,128)S(1)}) custom-call(bf16[256,4096]{1,0:T(8,128)(2,1)S(1)} %get-tuple-element.33.rows, bf16[4096,2048]{1,0:T(8,128)(2,1)S(1)} %bitcast.3, f32[256,128]{1,0:T(8,128)S(1)} %get-tuple-element.31.cosine, f32[256,128]{1,0:T(8,128)S(1)} %get-tuple-element.32.sine, ...), custom_call_target="tpu_custom_call" | custom-call | flops 4294967296 | bytes 16777216 | tf_op jit(solution)/shard_map/queries/pallas_call | solution.py:415
  22.1 0.1 relay.7
  22.2 1.3 %collective-permute-start.4 = (bf16[256,512]{1,0:T(8,128)(2,1)S(1)}, bf16[256,512]{1,0:T(8,128)(2,1)S(1)}, u32[]{:S(2)}, u32[]{:S(2)}) collective-permute-start(bf16[256,512]{1,0:T(8,128)(2,1)S(1)} %get-tuple-element.43), channel_id=1, source_target_pairs={{0,4},{2,6},{4,0},{6,2},{8,12},{10,14},{12,8},{14,10},{16,20},{18,... | collective-permute-start | bytes 786440 | tf_op jit(solution)/shard_map/ppermute | solution.py:410
  23.5 1.2 %collective-permute-start.5 = (bf16[256,512]{1,0:T(8,128)(2,1)S(1)}, bf16[256,512]{1,0:T(8,128)(2,1)S(1)}, u32[]{:S(2)}, u32[]{:S(2)}) collective-permute-start(bf16[256,512]{1,0:T(8,128)(2,1)S(1)} %get-tuple-element.44), channel_id=1, source_target_pairs={{0,2},{2,0},{4,6},{6,4},{8,10},{10,8},{12,14},{14,12},{16,18},{18,... | collective-permute-start | bytes 786440 | tf_op jit(solution)/shard_map/ppermute | solution.py:410
  24.7 3.0 %scores_near.1 = (f32[16,256,128]{2,1,0:T(8,128)S(1)}, f32[16,256,128]{2,1,0:T(8,128)S(1)}, f32[16,256,128]{2,1,0:T(8,128)S(1)}) custom-call(s32[256,128]{1,0:T(8,128)S(1)} %get-tuple-element.40.starts, bf16[256,2048]{1,0:T(8,128)(2,1)S(1)} %get-tuple-element.39.query, bf16[256,512]{1,0:T(8,128)(2,1)S(1)} %keys_values.1.own.refs_0_, ...), custom_call_target="tpu_custom_call" | custom-call | flops 1073741824 | bytes 8388608 | tf_op jit(solution)/shard_map/scores_near/pallas_call | solution.py:420
  27.8 0.3 collective-permute-start.3
  28.0 1.2 %collective-permute-done.8.refs_2_ = bf16[256,512]{1,0:T(8,128)(2,1)S(1)} collective-permute-done((bf16[256,512]{1,0:T(8,128)(2,1)S(1)}, bf16[256,512]{1,0:T(8,128)(2,1)S(1)}, u32[]{:S(2)}, u32[]{:S(2)}) %collective-permute-start.8) | collective-permute-done | bytes 262176 | tf_op jit(solution)/shard_map/ppermute | solution.py:410
  29.3 4.7 %mix_first.1 = (f32[256,4096]{1,0:T(8,128)S(1)}, bf16[256,1024]{1,0:T(8,128)(2,1)}, f32[256,768]{1,0:T(8,128)S(1)}) custom-call(s32[256,128]{1,0:T(8,128)S(1)} %get-tuple-element.40.starts, bf16[256,2048]{1,0:T(8,128)(2,1)S(1)} %get-tuple-element.39.query, bf16[256,512]{1,0:T(8,128)(2,1)S(1)} %collective-permute-done.6.refs_0_, ...), custom_call_target="tpu_custom_call" | custom-call | flops 3355443200 | bytes 4194304 | tf_op jit(solution)/shard_map/mix_first/pallas_call | solution.py:433
  34.0 2.4 %collective-permute-done.4.second = bf16[256,512]{1,0:T(8,128)(2,1)S(1)} collective-permute-done((bf16[256,512]{1,0:T(8,128)(2,1)S(1)}, bf16[256,512]{1,0:T(8,128)(2,1)S(1)}, u32[]{:S(2)}, u32[]{:S(2)}) %collective-permute-start.4) | collective-permute-done | bytes 262176 | tf_op jit(solution)/shard_map/ppermute | solution.py:410
  36.4 1.9 %attend_middle.1 = (f32[8,256,128]{2,1,0:T(8,128)S(1)}, f32[8,256,128]{2,1,0:T(8,128)S(1)}, f32[8,256,128]{2,1,0:T(8,128)S(1)}) custom-call(bf16[256,2048]{1,0:T(8,128)(2,1)S(1)} %get-tuple-element.39.query, bf16[256,512]{1,0:T(8,128)(2,1)S(1)} %collective-permute-done.4.second, bf16[256,512]{1,0:T(8,128)(2,1)S(1)} %collective-permute-done.5.first, ...), custom_call_target="tpu_custom_call" | custom-call | flops 805306368 | bytes 4194304 | tf_op jit(solution)/shard_map/attend_middle/pallas_call | solution.py:438
  38.3 0.7 %collective-permute-done.3.block = bf16[256,512]{1,0:T(8,128)(2,1)S(1)} collective-permute-done((bf16[256,512]{1,0:T(8,128)(2,1)S(1)}, bf16[256,512]{1,0:T(8,128)(2,1)S(1)}, u32[]{:S(2)}, u32[]{:S(2)}) %collective-permute-start.3) | collective-permute-done | bytes 262176 | tf_op jit(solution)/shard_map/ppermute | solution.py:410
  38.9 1.7 %mix_second.1 = (bf16[128,2048]{1,0:T(8,128)(2,1)S(1)}, bf16[256,1024]{1,0:T(8,128)(2,1)S(1)}) custom-call(bf16[256,2048]{1,0:T(8,128)(2,1)S(1)} %get-tuple-element.39.query, bf16[256,512]{1,0:T(8,128)(2,1)S(1)} %collective-permute-done.3.block, f32[8,256,128]{2,1,0:T(8,128)S(1)} %get-tuple-element.49.tops, f32[8,256,128]{2,1,0:T(8,128)S(1)} %get-tuple-element.50.totals, ...), custom_call_target="tpu_custom_call" | custom-call | flops 939524096 | bytes 4194304 | tf_op jit(solution)/shard_map/mix_second/pallas_call | solution.py:446
  40.6 2.2 %collective-permute-start.9 = (bf16[128,2048]{1,0:T(8,128)(2,1)S(1)}, bf16[128,2048]{1,0:T(8,128)(2,1)S(1)}, u32[]{:S(2)}, u32[]{:S(2)}) collective-permute-start(bf16[128,2048]{1,0:T(8,128)(2,1)S(1)} %get-tuple-element.54), channel_id=1, source_target_pairs={{0,1},{1,0},{2,3},{3,2},{4,5},{5,4},{6,7},{7,6},{8,9},{9,8},{10,11... | collective-permute-start | bytes 1572872 | tf_op jit(solution)/shard_map/ppermute | solution.py:450
  42.8 0.7 %send_high.1 = bf16[128,2048]{1,0:T(8,128)(2,1)S(1)} custom-call(bf16[256,1024]{1,0:T(8,128)(2,1)S(1)} %get-tuple-element.53.attended, bf16[2048,4096]{1,0:T(8,128)(2,1)S(1)} %bitcast.1, f32[256,4096]{1,0:T(8,128)S(1)} %get-tuple-element.52.summed), custom_call_target="tpu_custom_call" | custom-call | flops 536870912 | bytes 4194304 | tf_op jit(solution)/shard_map/send_high/pallas_call | solution.py:451
  43.5 0.1 collective-permute-start.10
  43.6 0.7 %own_high.1.after.own = f32[128,2048]{1,0:T(8,128)S(1)} custom-call(bf16[256,1024]{1,0:T(8,128)(2,1)S(1)} %get-tuple-element.53.attended, bf16[2048,4096]{1,0:T(8,128)(2,1)S(1)} %bitcast.1, f32[256,4096]{1,0:T(8,128)S(1)} %get-tuple-element.52.summed), custom_call_target="tpu_custom_call" | custom-call | flops 536870912 | bytes 4194304 | tf_op jit(solution)/shard_map/own_high/pallas_call | solution.py:455
  44.3 0.8 %own_low.1.mixed_low = bf16[128,2048]{1,0:T(8,128)(2,1)S(1)} custom-call(bf16[256,1024]{1,0:T(8,128)(2,1)S(1)} %get-tuple-element.53.attended, bf16[2048,4096]{1,0:T(8,128)(2,1)S(1)} %bitcast.1, f32[256,4096]{1,0:T(8,128)S(1)} %get-tuple-element.52.summed, bf16[128,2048]{1,0:T(8,128)(2,1)S(1)} %collective-permute-done.9.got, f32[128,2048]{1,0:T(8,128)S(1)} %own_high.1.after.own), custom_call_target="tpu_custom_call" | custom-call | flops 536870912 | bytes 4194304 | tf_op jit(solution)/shard_map/own_low/pallas_call | solution.py:459
  45.1 0.4 collective-permute-done.10.got
  45.5 1.0 %add.1 = bf16[128,4096]{1,0:T(8,128)(2,1)} custom-call(bf16[128,2048]{1,0:T(8,128)(2,1)S(1)} %own_low.1.mixed_low, f32[128,2048]{1,0:T(8,128)S(1)} %own_high.1.after.own, bf16[128,2048]{1,0:T(8,128)(2,1)S(1)} %collective-permute-done.10.got), custom_call_target="tpu_custom_call" | custom-call | flops 262144 | bytes 4194304 | tf_op jit(solution)/shard_map/add/pallas_call | solution.py:462
  (24 shorter events, 0.1 us)
Async XLA Ops:
  0.0 3.8 %collective-permute-start = (bf16[128,4096]{1,0:T(8,128)(2,1)}, bf16[128,4096]{1,0:T(8,128)(2,1)S(1)}, u32[]{:S(2)}, u32[]{:S(2)}) collective-permute-start(bf16[128,4096]{1,0:T(8,128)(2,1)} %own_hbm.1), channel_id=1, source_target_pairs={{0,1},{1,0},{2,3},{3,2},{4,5},{5,4},{6,7},{7,6},{8,9},{9,8},{10,11... | collective-permute-start | bytes 3145736 | tf_op jit(solution)/shard_map/ppermute | solution.py:373
  4.6 9.8 %collective-permute-start.1 = (bf16[256,512]{1,0:T(8,128)(2,1)S(1)}, bf16[256,512]{1,0:T(8,128)(2,1)S(1)}, u32[]{:S(2)}, u32[]{:S(2)}) collective-permute-start(bf16[256,512]{1,0:T(8,128)(2,1)S(1)} %keys_values.1.own.refs_0_), channel_id=1, source_target_pairs={{0,8},{2,10},{4,12},{6,14},{8,16},{10,18},{12,20},{14,22},{16,24},... | collective-permute-start | bytes 786440 | tf_op jit(solution)/shard_map/ppermute | solution.py:397
  5.9 11.4 %slice-start.4 = ((s8[16777216]{0:T(1024)(128)(4,1)}), s8[4194304]{0:T(1024)(128)(4,1)S(1)}, s32[]{:S(2)}) async-start(s8[16777216]{0:T(1024)(128)(4,1)} %bitcast.2), calls=%async_computation.4 | async-start | bytes 8388608
  5.9 11.4 %slice-start.5 = ((s8[16777216]{0:T(1024)(128)(4,1)}), s8[4194304]{0:T(1024)(128)(4,1)S(1)}, s32[]{:S(2)}) async-start(s8[16777216]{0:T(1024)(128)(4,1)} %bitcast.2), calls=%async_computation.5 | async-start | bytes 8388608
  9.9 7.4 %slice-start.6 = ((s8[16777216]{0:T(1024)(128)(4,1)}), s8[4194304]{0:T(1024)(128)(4,1)S(1)}, s32[]{:S(2)}) async-start(s8[16777216]{0:T(1024)(128)(4,1)} %bitcast.2), calls=%async_computation.6 | async-start | bytes 8388608
  9.9 7.4 %slice-start.7 = ((s8[16777216]{0:T(1024)(128)(4,1)}), s8[4194304]{0:T(1024)(128)(4,1)S(1)}, s32[]{:S(2)}) async-start(s8[16777216]{0:T(1024)(128)(4,1)} %bitcast.2), calls=%async_computation.7 | async-start | bytes 8388608
  9.9 12.2 %collective-permute-start.2 = (bf16[256,512]{1,0:T(8,128)(2,1)S(1)}, bf16[256,512]{1,0:T(8,128)(2,1)S(1)}, u32[]{:S(2)}, u32[]{:S(2)}) collective-permute-start(bf16[256,512]{1,0:T(8,128)(2,1)S(1)} %get-tuple-element.37.after.refs_2_.own), channel_id=1, source_target_pairs={{0,8},{2,10},{4,12},{6,14},{8,16},{10,18},{12,20},{14,22},{16,24},... | collective-permute-start | bytes 786440 | tf_op jit(solution)/shard_map/ppermute | solution.py:404
  14.4 13.4 %collective-permute-start.6 = (bf16[256,512]{1,0:T(8,128)(2,1)S(1)}, bf16[256,512]{1,0:T(8,128)(2,1)S(1)}, u32[]{:S(2)}, u32[]{:S(2)}) collective-permute-start(bf16[256,512]{1,0:T(8,128)(2,1)S(1)} %relay.4.after), channel_id=1, source_target_pairs={{0,6},{2,4},{4,2},{6,0},{8,14},{10,12},{12,10},{14,8},{16,22},{18,... | collective-permute-start | bytes 786440 | tf_op jit(solution)/shard_map/ppermute | solution.py:410
  16.7 12.5 %collective-permute-start.8 = (bf16[256,512]{1,0:T(8,128)(2,1)S(1)}, bf16[256,512]{1,0:T(8,128)(2,1)S(1)}, u32[]{:S(2)}, u32[]{:S(2)}) collective-permute-start(bf16[256,512]{1,0:T(8,128)(2,1)S(1)} %get-tuple-element.47), channel_id=1, source_target_pairs={{0,4},{2,6},{4,0},{6,2},{8,12},{10,14},{12,8},{14,10},{16,20},{18,... | collective-permute-start | bytes 786440 | tf_op jit(solution)/shard_map/ppermute | solution.py:410
  17.0 12.2 %collective-permute-start.7 = (bf16[256,512]{1,0:T(8,128)(2,1)S(1)}, bf16[256,512]{1,0:T(8,128)(2,1)S(1)}, u32[]{:S(2)}, u32[]{:S(2)}) collective-permute-start(bf16[256,512]{1,0:T(8,128)(2,1)S(1)} %get-tuple-element.38.after), channel_id=1, source_target_pairs={{0,2},{2,0},{4,6},{6,4},{8,10},{10,8},{12,14},{14,12},{16,18},{18,... | collective-permute-start | bytes 786440 | tf_op jit(solution)/shard_map/ppermute | solution.py:410
  17.3 11.9 %slice-start = ((s8[16777216]{0:T(1024)(128)(4,1)}), s8[4194304]{0:T(1024)(128)(4,1)S(1)}, s32[]{:S(2)}) async-start(s8[16777216]{0:T(1024)(128)(4,1)} %bitcast), calls=%async_computation | async-start | bytes 8388608
  17.3 11.9 %slice-start.1 = ((s8[16777216]{0:T(1024)(128)(4,1)}), s8[4194304]{0:T(1024)(128)(4,1)S(1)}, s32[]{:S(2)}) async-start(s8[16777216]{0:T(1024)(128)(4,1)} %bitcast), calls=%async_computation.1 | async-start | bytes 8388608
  22.1 7.1 %slice-start.2 = ((s8[16777216]{0:T(1024)(128)(4,1)}), s8[4194304]{0:T(1024)(128)(4,1)S(1)}, s32[]{:S(2)}) async-start(s8[16777216]{0:T(1024)(128)(4,1)} %bitcast), calls=%async_computation.2 | async-start | bytes 8388608
  22.1 7.1 %slice-start.3 = ((s8[16777216]{0:T(1024)(128)(4,1)}), s8[4194304]{0:T(1024)(128)(4,1)S(1)}, s32[]{:S(2)}) async-start(s8[16777216]{0:T(1024)(128)(4,1)} %bitcast), calls=%async_computation.3 | async-start | bytes 8388608
  22.2 14.2 %collective-permute-start.4 = (bf16[256,512]{1,0:T(8,128)(2,1)S(1)}, bf16[256,512]{1,0:T(8,128)(2,1)S(1)}, u32[]{:S(2)}, u32[]{:S(2)}) collective-permute-start(bf16[256,512]{1,0:T(8,128)(2,1)S(1)} %get-tuple-element.43), channel_id=1, source_target_pairs={{0,4},{2,6},{4,0},{6,2},{8,12},{10,14},{12,8},{14,10},{16,20},{18,... | collective-permute-start | bytes 786440 | tf_op jit(solution)/shard_map/ppermute | solution.py:410
  23.5 12.9 %collective-permute-start.5 = (bf16[256,512]{1,0:T(8,128)(2,1)S(1)}, bf16[256,512]{1,0:T(8,128)(2,1)S(1)}, u32[]{:S(2)}, u32[]{:S(2)}) collective-permute-start(bf16[256,512]{1,0:T(8,128)(2,1)S(1)} %get-tuple-element.44), channel_id=1, source_target_pairs={{0,2},{2,0},{4,6},{6,4},{8,10},{10,8},{12,14},{14,12},{16,18},{18,... | collective-permute-start | bytes 786440 | tf_op jit(solution)/shard_map/ppermute | solution.py:410
  27.8 11.1 %collective-permute-start.3 = (bf16[256,512]{1,0:T(8,128)(2,1)S(1)}, bf16[256,512]{1,0:T(8,128)(2,1)S(1)}, u32[]{:S(2)}, u32[]{:S(2)}) collective-permute-start(bf16[256,512]{1,0:T(8,128)(2,1)S(1)} %relay.6), channel_id=1, source_target_pairs={{0,6},{2,4},{4,2},{6,0},{8,14},{10,12},{12,10},{14,8},{16,22},{18,... | collective-permute-start | bytes 786440 | tf_op jit(solution)/shard_map/ppermute | solution.py:410
  40.6 3.7 %collective-permute-start.9 = (bf16[128,2048]{1,0:T(8,128)(2,1)S(1)}, bf16[128,2048]{1,0:T(8,128)(2,1)S(1)}, u32[]{:S(2)}, u32[]{:S(2)}) collective-permute-start(bf16[128,2048]{1,0:T(8,128)(2,1)S(1)} %get-tuple-element.54), channel_id=1, source_target_pairs={{0,1},{1,0},{2,3},{3,2},{4,5},{5,4},{6,7},{7,6},{8,9},{9,8},{10,11... | collective-permute-start | bytes 1572872 | tf_op jit(solution)/shard_map/ppermute | solution.py:450
  43.5 2.0 %collective-permute-start.10 = (bf16[128,2048]{1,0:T(8,128)(2,1)S(1)}, bf16[128,2048]{1,0:T(8,128)(2,1)S(1)}, u32[]{:S(2)}, u32[]{:S(2)}) collective-permute-start(bf16[128,2048]{1,0:T(8,128)(2,1)S(1)} %send_high.1), channel_id=1, source_target_pairs={{0,1},{1,0},{2,3},{3,2},{4,5},{5,4},{6,7},{7,6},{8,9},{9,8},{10,11... | collective-permute-start | bytes 1572872 | tf_op jit(solution)/shard_map/ppermute | solution.py:454

commit v10 on v9

--- a/solution.py
+++ b/solution.py
@@ -42,11 +42,16 @@
     return block * cosine + pltpu.roll(block, HEAD_SIZE // 2, 1) * sine
 
 
+def piece_bounds(depth, chunks):
+    cuts = [0, depth * 3 // 4, depth] if chunks == 2 else [depth * number // chunks for number in range(chunks + 1)]
+    return list(zip(cuts[:-1], cuts[1:]))
+
+
 def load_columns(low, hbms, buffers, sems, chunks):
-    depth, wide = buffers[0].shape[0] // chunks, buffers[0].shape[1]
+    depth, wide = buffers[0].shape
     copies = []
-    for number in range(chunks):
-        at = pl.ds(number * depth, depth)
+    for number, (first, last) in enumerate(piece_bounds(depth, chunks)):
+        at = pl.ds(first, last - first)
         pair = [
             pltpu.make_async_copy(hbm.at[at, pl.ds(low, wide)], buffer.at[at], sems.at[number * len(hbms) + which])
             for which, (hbm, buffer) in enumerate(zip(hbms, buffers))
@@ -58,9 +63,9 @@
 
 
 def piecewise_product(rows, copies, buffers, total, put=None):
-    depth, wide = buffers[0].shape[0] // len(copies), buffers[0].shape[1]
-    for number, pair in enumerate(copies):
-        at = slice(number * depth, (number + 1) * depth)
+    depth, wide = buffers[0].shape
+    for number, (pair, (first, last)) in enumerate(zip(copies, piece_bounds(depth, len(copies)))):
+        at = slice(first, last)
         for which, (copy, buffer) in enumerate(zip(pair, buffers)):
             copy.wait()
             columns = slice(which * wide, (which + 1) * wide)

time: 46.9 us -> 47.3 us (level)
  Pallas kernels: 27.3 us -> 27.9 us
  transfers between devices with their start and end apart: 11 -> 11, of which waited for: 5 -> 5; matrix products, arithmetic and copies ran while one was open for 0% -> 0% of each run, Pallas kernels for 51% -> 52%
where the time goes in v10:
time: 47.3 us; the launch traced here: 46.9 us
  Pallas kernels  27.9 us (59%)
  starting transfers between devices  11.9 us (25%)
  waiting for transfers between devices  6.65 us (14%)
    ppermute x6, starting transfers between devices, exchange(): lax.ppermute(array, 'seq', [(i, i ^ way) for i in every])  5.56 us
    pallas_call x1, Pallas kernels, body(): call(query_kernel, 'queries', [shape((tokens, width_q), bf16), flag], [VM...  4.78 us
    pallas_call x1, Pallas kernels, body(): call(functools.partial(mix_first_kernel, distances), 'mix_first', [shape(...  4.71 us
    pallas_call x1, Pallas kernels, body(): call(functools.partial(third_kernel, chunks), 'keys_values_more', [kv_sha...  4.38 us
    ppermute x6, waiting for transfers between devices, exchange(): lax.ppermute(array, 'seq', [(i, i ^ way) for i in every])  4.26 us
    pallas_call x1, Pallas kernels, body(): call(functools.partial(first_kernel, chunks), 'keys_values_own', [shape((...  3.27 us
    pallas_call x1, Pallas kernels, body(): call(functools.partial(near_kernel, ((0, 0), (LAYER, LAYER))), 'scores_ne...  2.98 us
    ppermute x1, starting transfers between devices, body(): got_low = lax.ppermute(send, 'head', SWAP)  2.16 us
  transfers between devices with their start and end apart: 11, of which 5 were waited for; matrix products, arithmetic and copies ran while one was open for 0% of the time, Pallas kernels for 52%

profile of v10, /device:TPU:25, one launch (start us, length us, event | category | flops | bytes accessed | tf_op | source)
XLA Modules:
  0.0 46.9 jit_solution(3162772823502072814)
XLA Ops:
  0.0 0.7 %collective-permute-start = (bf16[128,4096]{1,0:T(8,128)(2,1)}, bf16[128,4096]{1,0:T(8,128)(2,1)S(1)}, u32[]{:S(2)}, u32[]{:S(2)}) collective-permute-start(bf16[128,4096]{1,0:T(8,128)(2,1)} %own_hbm.1), channel_id=1, source_target_pairs={{0,1},{1,0},{2,3},{3,2},{4,5},{5,4},{6,7},{7,6},{8,9},{9,8},{10,11... | collective-permute-start | bytes 3145736 | tf_op jit(solution)/shard_map/ppermute | solution.py:378
  0.7 3.3 %keys_values_own.1 = (f32[128,512]{1,0:T(8,128)S(1)}, bf16[128,4096]{1,0:T(8,128)(2,1)S(1)}, bf16[4096,256]{1,0:T(8,128)(2,1)S(1)}, bf16[4096,256]{1,0:T(8,128)(...) custom-call(s32[8]{0:T(128)} %lengths_hbm.1, bf16[128,4096]{1,0:T(8,128)(2,1)} %own_hbm.1, ...), custom_call_target="tpu_custom_call" | custom-call | flops 536870912 | bytes 4194304 | tf_op jit(solution)/shard_map/keys_values_own/pallas_call | solution.py:387
  4.0 0.8 %keys_values.1.own.refs_0_ = bf16[256,512]{1,0:T(8,128)(2,1)S(1)} custom-call(bf16[128,4096]{1,0:T(8,128)(2,1)S(1)} %collective-permute-done.other, bf16[4096,256]{1,0:T(8,128)(2,1)S(1)} %get-tuple-element.34.w_key, bf16[4096,256]{1,0:T(8,128)(2,1)S(1)} %get-tuple-element.35.w_value, f32[128,512]{1,0:T(8,128)S(1)} %get-tuple-element.36.own_total, ...), custom_call_target="tpu_custom_call" | custom-call | flops 536870912 | bytes 4194304 | tf_op jit(solution)/shard_map/keys_values/pallas_call | solution.py:396
  4.8 1.3 %collective-permute-start.1 = (bf16[256,512]{1,0:T(8,128)(2,1)S(1)}, bf16[256,512]{1,0:T(8,128)(2,1)S(1)}, u32[]{:S(2)}, u32[]{:S(2)}) collective-permute-start(bf16[256,512]{1,0:T(8,128)(2,1)S(1)} %keys_values.1.own.refs_0_), channel_id=1, source_target_pairs={{0,8},{2,10},{4,12},{6,14},{8,16},{10,18},{12,20},{14,22},{16,24},... | collective-permute-start | bytes 786440 | tf_op jit(solution)/shard_map/ppermute | solution.py:402
  6.1 0.0 slice-start.4
  6.1 4.4 %keys_values_more.1 = (bf16[256,512]{1,0:T(8,128)(2,1)S(1)}, bf16[256,4096]{1,0:T(8,128)(2,1)S(1)}, f32[8,128]{1,0:T(8,128)}) custom-call(bf16[128,4096]{1,0:T(8,128)(2,1)S(1)} %get-tuple-element.30.own, bf16[128,4096]{1,0:T(8,128)(2,1)S(1)} %collective-permute-done.other, bf16[4096,512]{1,0:T(8,128)(2,1)} %key_hbm.3, bf16[4096,512]{1,0:T(8,128)(2,1)} %value_hbm.3, ...), custom_call_target="tpu_custom_call" | custom-call | flops 4294967296 | bytes 4194304 | tf_op jit(solution)/shard_map/keys_values_more/pallas_call | solution.py:404
  10.5 2.1 %collective-permute-start.2 = (bf16[256,512]{1,0:T(8,128)(2,1)S(1)}, bf16[256,512]{1,0:T(8,128)(2,1)S(1)}, u32[]{:S(2)}, u32[]{:S(2)}) collective-permute-start(bf16[256,512]{1,0:T(8,128)(2,1)S(1)} %get-tuple-element.37.after.refs_2_.own), channel_id=1, source_target_pairs={{0,8},{2,10},{4,12},{6,14},{8,16},{10,18},{12,20},{14,22},{16,24},... | collective-permute-start | bytes 786440 | tf_op jit(solution)/shard_map/ppermute | solution.py:409
  12.6 2.0 %collective-permute-done.1.earlier.refs_1_ = bf16[256,512]{1,0:T(8,128)(2,1)S(1)} collective-permute-done((bf16[256,512]{1,0:T(8,128)(2,1)S(1)}, bf16[256,512]{1,0:T(8,128)(2,1)S(1)}, u32[]{:S(2)}, u32[]{:S(2)}) %collective-permute-start.1) | collective-permute-done | bytes 262176 | tf_op jit(solution)/shard_map/ppermute | solution.py:402
  14.6 2.2 %collective-permute-start.6 = (bf16[256,512]{1,0:T(8,128)(2,1)S(1)}, bf16[256,512]{1,0:T(8,128)(2,1)S(1)}, u32[]{:S(2)}, u32[]{:S(2)}) collective-permute-start(bf16[256,512]{1,0:T(8,128)(2,1)S(1)} %relay.4.after), channel_id=1, source_target_pairs={{0,6},{2,4},{4,2},{6,0},{8,14},{10,12},{12,10},{14,8},{16,22},{18,... | collective-permute-start | bytes 786440 | tf_op jit(solution)/shard_map/ppermute | solution.py:415
  16.9 0.1 relay.5
  16.9 0.3 collective-permute-start.8
  17.2 0.3 collective-permute-start.7
  17.5 4.8 %queries.1 = (bf16[256,2048]{1,0:T(8,128)(2,1)S(1)}, f32[8,128]{1,0:T(8,128)S(1)}) custom-call(bf16[256,4096]{1,0:T(8,128)(2,1)S(1)} %get-tuple-element.33.rows, bf16[4096,2048]{1,0:T(8,128)(2,1)S(1)} %bitcast.3, f32[256,128]{1,0:T(8,128)S(1)} %get-tuple-element.31.cosine, f32[256,128]{1,0:T(8,128)S(1)} %get-tuple-element.32.sine, ...), custom_call_target="tpu_custom_call" | custom-call | flops 4294967296 | bytes 16777216 | tf_op jit(solution)/shard_map/queries/pallas_call | solution.py:420
  22.3 0.0 slice-start.2
  22.3 0.1 relay.7
  22.4 1.3 %collective-permute-start.4 = (bf16[256,512]{1,0:T(8,128)(2,1)S(1)}, bf16[256,512]{1,0:T(8,128)(2,1)S(1)}, u32[]{:S(2)}, u32[]{:S(2)}) collective-permute-start(bf16[256,512]{1,0:T(8,128)(2,1)S(1)} %get-tuple-element.43), channel_id=1, source_target_pairs={{0,4},{2,6},{4,0},{6,2},{8,12},{10,14},{12,8},{14,10},{16,20},{18,... | collective-permute-start | bytes 786440 | tf_op jit(solution)/shard_map/ppermute | solution.py:415
  23.7 1.2 %collective-permute-start.5 = (bf16[256,512]{1,0:T(8,128)(2,1)S(1)}, bf16[256,512]{1,0:T(8,128)(2,1)S(1)}, u32[]{:S(2)}, u32[]{:S(2)}) collective-permute-start(bf16[256,512]{1,0:T(8,128)(2,1)S(1)} %get-tuple-element.44), channel_id=1, source_target_pairs={{0,2},{2,0},{4,6},{6,4},{8,10},{10,8},{12,14},{14,12},{16,18},{18,... | collective-permute-start | bytes 786440 | tf_op jit(solution)/shard_map/ppermute | solution.py:415
  24.9 3.0 %scores_near.1 = (f32[16,256,128]{2,1,0:T(8,128)S(1)}, f32[16,256,128]{2,1,0:T(8,128)S(1)}, f32[16,256,128]{2,1,0:T(8,128)S(1)}) custom-call(s32[256,128]{1,0:T(8,128)S(1)} %get-tuple-element.40.starts, bf16[256,2048]{1,0:T(8,128)(2,1)S(1)} %get-tuple-element.39.query, bf16[256,512]{1,0:T(8,128)(2,1)S(1)} %keys_values.1.own.refs_0_, ...), custom_call_target="tpu_custom_call" | custom-call | flops 1073741824 | bytes 8388608 | tf_op jit(solution)/shard_map/scores_near/pallas_call | solution.py:425
  28.0 0.3 collective-permute-start.3
  28.2 1.2 %collective-permute-done.8.refs_2_ = bf16[256,512]{1,0:T(8,128)(2,1)S(1)} collective-permute-done((bf16[256,512]{1,0:T(8,128)(2,1)S(1)}, bf16[256,512]{1,0:T(8,128)(2,1)S(1)}, u32[]{:S(2)}, u32[]{:S(2)}) %collective-permute-start.8) | collective-permute-done | bytes 262176 | tf_op jit(solution)/shard_map/ppermute | solution.py:415
  29.5 4.7 %mix_first.1 = (f32[256,4096]{1,0:T(8,128)S(1)}, bf16[256,1024]{1,0:T(8,128)(2,1)}, f32[256,768]{1,0:T(8,128)S(1)}) custom-call(s32[256,128]{1,0:T(8,128)S(1)} %get-tuple-element.40.starts, bf16[256,2048]{1,0:T(8,128)(2,1)S(1)} %get-tuple-element.39.query, bf16[256,512]{1,0:T(8,128)(2,1)S(1)} %collective-permute-done.6.refs_0_, ...), custom_call_target="tpu_custom_call" | custom-call | flops 3355443200 | bytes 4194304 | tf_op jit(solution)/shard_map/mix_first/pallas_call | solution.py:438
  34.2 2.4 %collective-permute-done.4.second = bf16[256,512]{1,0:T(8,128)(2,1)S(1)} collective-permute-done((bf16[256,512]{1,0:T(8,128)(2,1)S(1)}, bf16[256,512]{1,0:T(8,128)(2,1)S(1)}, u32[]{:S(2)}, u32[]{:S(2)}) %collective-permute-start.4) | collective-permute-done | bytes 262176 | tf_op jit(solution)/shard_map/ppermute | solution.py:415
  36.6 1.9 %attend_middle.1 = (f32[8,256,128]{2,1,0:T(8,128)S(1)}, f32[8,256,128]{2,1,0:T(8,128)S(1)}, f32[8,256,128]{2,1,0:T(8,128)S(1)}) custom-call(bf16[256,2048]{1,0:T(8,128)(2,1)S(1)} %get-tuple-element.39.query, bf16[256,512]{1,0:T(8,128)(2,1)S(1)} %collective-permute-done.4.second, bf16[256,512]{1,0:T(8,128)(2,1)S(1)} %collective-permute-done.5.first, ...), custom_call_target="tpu_custom_call" | custom-call | flops 805306368 | bytes 4194304 | tf_op jit(solution)/shard_map/attend_middle/pallas_call | solution.py:443
  38.5 0.7 %collective-permute-done.3.block = bf16[256,512]{1,0:T(8,128)(2,1)S(1)} collective-permute-done((bf16[256,512]{1,0:T(8,128)(2,1)S(1)}, bf16[256,512]{1,0:T(8,128)(2,1)S(1)}, u32[]{:S(2)}, u32[]{:S(2)}) %collective-permute-start.3) | collective-permute-done | bytes 262176 | tf_op jit(solution)/shard_map/ppermute | solution.py:415
  39.1 1.7 %mix_second.1 = (bf16[128,2048]{1,0:T(8,128)(2,1)S(1)}, bf16[256,1024]{1,0:T(8,128)(2,1)S(1)}) custom-call(bf16[256,2048]{1,0:T(8,128)(2,1)S(1)} %get-tuple-element.39.query, bf16[256,512]{1,0:T(8,128)(2,1)S(1)} %collective-permute-done.3.block, f32[8,256,128]{2,1,0:T(8,128)S(1)} %get-tuple-element.49.tops, f32[8,256,128]{2,1,0:T(8,128)S(1)} %get-tuple-element.50.totals, ...), custom_call_target="tpu_custom_call" | custom-call | flops 939524096 | bytes 4194304 | tf_op jit(solution)/shard_map/mix_second/pallas_call | solution.py:451
  40.8 2.2 %collective-permute-start.9 = (bf16[128,2048]{1,0:T(8,128)(2,1)S(1)}, bf16[128,2048]{1,0:T(8,128)(2,1)S(1)}, u32[]{:S(2)}, u32[]{:S(2)}) collective-permute-start(bf16[128,2048]{1,0:T(8,128)(2,1)S(1)} %get-tuple-element.54), channel_id=1, source_target_pairs={{0,1},{1,0},{2,3},{3,2},{4,5},{5,4},{6,7},{7,6},{8,9},{9,8},{10,11... | collective-permute-start | bytes 1572872 | tf_op jit(solution)/shard_map/ppermute | solution.py:455
  43.0 0.7 %send_high.1 = bf16[128,2048]{1,0:T(8,128)(2,1)S(1)} custom-call(bf16[256,1024]{1,0:T(8,128)(2,1)S(1)} %get-tuple-element.53.attended, bf16[2048,4096]{1,0:T(8,128)(2,1)S(1)} %bitcast.1, f32[256,4096]{1,0:T(8,128)S(1)} %get-tuple-element.52.summed), custom_call_target="tpu_custom_call" | custom-call | flops 536870912 | bytes 4194304 | tf_op jit(solution)/shard_map/send_high/pallas_call | solution.py:456
  43.7 0.1 collective-permute-start.10
  43.8 0.7 %own_high.1.after.own = f32[128,2048]{1,0:T(8,128)S(1)} custom-call(bf16[256,1024]{1,0:T(8,128)(2,1)S(1)} %get-tuple-element.53.attended, bf16[2048,4096]{1,0:T(8,128)(2,1)S(1)} %bitcast.1, f32[256,4096]{1,0:T(8,128)S(1)} %get-tuple-element.52.summed), custom_call_target="tpu_custom_call" | custom-call | flops 536870912 | bytes 4194304 | tf_op jit(solution)/shard_map/own_high/pallas_call | solution.py:460
  44.6 0.8 %own_low.1.mixed_low = bf16[128,2048]{1,0:T(8,128)(2,1)S(1)} custom-call(bf16[256,1024]{1,0:T(8,128)(2,1)S(1)} %get-tuple-element.53.attended, bf16[2048,4096]{1,0:T(8,128)(2,1)S(1)} %bitcast.1, f32[256,4096]{1,0:T(8,128)S(1)} %get-tuple-element.52.summed, bf16[128,2048]{1,0:T(8,128)(2,1)S(1)} %collective-permute-done.9.got, f32[128,2048]{1,0:T(8,128)S(1)} %own_high.1.after.own), custom_call_target="tpu_custom_call" | custom-call | flops 536870912 | bytes 4194304 | tf_op jit(solution)/shard_map/own_low/pallas_call | solution.py:464
  45.3 0.4 collective-permute-done.10.got
  45.7 1.0 %add.1 = bf16[128,4096]{1,0:T(8,128)(2,1)} custom-call(bf16[128,2048]{1,0:T(8,128)(2,1)S(1)} %own_low.1.mixed_low, f32[128,2048]{1,0:T(8,128)S(1)} %own_high.1.after.own, bf16[128,2048]{1,0:T(8,128)(2,1)S(1)} %collective-permute-done.10.got), custom_call_target="tpu_custom_call" | custom-call | flops 262144 | bytes 4194304 | tf_op jit(solution)/shard_map/add/pallas_call | solution.py:467
  (24 shorter events, 0.1 us)
Async XLA Ops:
  0.0 4.0 %collective-permute-start = (bf16[128,4096]{1,0:T(8,128)(2,1)}, bf16[128,4096]{1,0:T(8,128)(2,1)S(1)}, u32[]{:S(2)}, u32[]{:S(2)}) collective-permute-start(bf16[128,4096]{1,0:T(8,128)(2,1)} %own_hbm.1), channel_id=1, source_target_pairs={{0,1},{1,0},{2,3},{3,2},{4,5},{5,4},{6,7},{7,6},{8,9},{9,8},{10,11... | collective-permute-start | bytes 3145736 | tf_op jit(solution)/shard_map/ppermute | solution.py:378
  4.8 9.8 %collective-permute-start.1 = (bf16[256,512]{1,0:T(8,128)(2,1)S(1)}, bf16[256,512]{1,0:T(8,128)(2,1)S(1)}, u32[]{:S(2)}, u32[]{:S(2)}) collective-permute-start(bf16[256,512]{1,0:T(8,128)(2,1)S(1)} %keys_values.1.own.refs_0_), channel_id=1, source_target_pairs={{0,8},{2,10},{4,12},{6,14},{8,16},{10,18},{12,20},{14,22},{16,24},... | collective-permute-start | bytes 786440 | tf_op jit(solution)/shard_map/ppermute | solution.py:402
  6.1 11.4 %slice-start.4 = ((s8[16777216]{0:T(1024)(128)(4,1)}), s8[4194304]{0:T(1024)(128)(4,1)S(1)}, s32[]{:S(2)}) async-start(s8[16777216]{0:T(1024)(128)(4,1)} %bitcast.2), calls=%async_computation.4 | async-start | bytes 8388608
  6.1 11.4 %slice-start.5 = ((s8[16777216]{0:T(1024)(128)(4,1)}), s8[4194304]{0:T(1024)(128)(4,1)S(1)}, s32[]{:S(2)}) async-start(s8[16777216]{0:T(1024)(128)(4,1)} %bitcast.2), calls=%async_computation.5 | async-start | bytes 8388608
  10.5 7.0 %slice-start.6 = ((s8[16777216]{0:T(1024)(128)(4,1)}), s8[4194304]{0:T(1024)(128)(4,1)S(1)}, s32[]{:S(2)}) async-start(s8[16777216]{0:T(1024)(128)(4,1)} %bitcast.2), calls=%async_computation.6 | async-start | bytes 8388608
  10.5 7.0 %slice-start.7 = ((s8[16777216]{0:T(1024)(128)(4,1)}), s8[4194304]{0:T(1024)(128)(4,1)S(1)}, s32[]{:S(2)}) async-start(s8[16777216]{0:T(1024)(128)(4,1)} %bitcast.2), calls=%async_computation.7 | async-start | bytes 8388608
  10.5 11.8 %collective-permute-start.2 = (bf16[256,512]{1,0:T(8,128)(2,1)S(1)}, bf16[256,512]{1,0:T(8,128)(2,1)S(1)}, u32[]{:S(2)}, u32[]{:S(2)}) collective-permute-start(bf16[256,512]{1,0:T(8,128)(2,1)S(1)} %get-tuple-element.37.after.refs_2_.own), channel_id=1, source_target_pairs={{0,8},{2,10},{4,12},{6,14},{8,16},{10,18},{12,20},{14,22},{16,24},... | collective-permute-start | bytes 786440 | tf_op jit(solution)/shard_map/ppermute | solution.py:409
  14.6 13.4 %collective-permute-start.6 = (bf16[256,512]{1,0:T(8,128)(2,1)S(1)}, bf16[256,512]{1,0:T(8,128)(2,1)S(1)}, u32[]{:S(2)}, u32[]{:S(2)}) collective-permute-start(bf16[256,512]{1,0:T(8,128)(2,1)S(1)} %relay.4.after), channel_id=1, source_target_pairs={{0,6},{2,4},{4,2},{6,0},{8,14},{10,12},{12,10},{14,8},{16,22},{18,... | collective-permute-start | bytes 786440 | tf_op jit(solution)/shard_map/ppermute | solution.py:415
  16.9 12.5 %collective-permute-start.8 = (bf16[256,512]{1,0:T(8,128)(2,1)S(1)}, bf16[256,512]{1,0:T(8,128)(2,1)S(1)}, u32[]{:S(2)}, u32[]{:S(2)}) collective-permute-start(bf16[256,512]{1,0:T(8,128)(2,1)S(1)} %get-tuple-element.47), channel_id=1, source_target_pairs={{0,4},{2,6},{4,0},{6,2},{8,12},{10,14},{12,8},{14,10},{16,20},{18,... | collective-permute-start | bytes 786440 | tf_op jit(solution)/shard_map/ppermute | solution.py:415
  17.2 12.2 %collective-permute-start.7 = (bf16[256,512]{1,0:T(8,128)(2,1)S(1)}, bf16[256,512]{1,0:T(8,128)(2,1)S(1)}, u32[]{:S(2)}, u32[]{:S(2)}) collective-permute-start(bf16[256,512]{1,0:T(8,128)(2,1)S(1)} %get-tuple-element.38.after), channel_id=1, source_target_pairs={{0,2},{2,0},{4,6},{6,4},{8,10},{10,8},{12,14},{14,12},{16,18},{18,... | collective-permute-start | bytes 786440 | tf_op jit(solution)/shard_map/ppermute | solution.py:415
  17.5 11.9 %slice-start = ((s8[16777216]{0:T(1024)(128)(4,1)}), s8[4194304]{0:T(1024)(128)(4,1)S(1)}, s32[]{:S(2)}) async-start(s8[16777216]{0:T(1024)(128)(4,1)} %bitcast), calls=%async_computation | async-start | bytes 8388608
  17.5 11.9 %slice-start.1 = ((s8[16777216]{0:T(1024)(128)(4,1)}), s8[4194304]{0:T(1024)(128)(4,1)S(1)}, s32[]{:S(2)}) async-start(s8[16777216]{0:T(1024)(128)(4,1)} %bitcast), calls=%async_computation.1 | async-start | bytes 8388608
  22.3 7.1 %slice-start.2 = ((s8[16777216]{0:T(1024)(128)(4,1)}), s8[4194304]{0:T(1024)(128)(4,1)S(1)}, s32[]{:S(2)}) async-start(s8[16777216]{0:T(1024)(128)(4,1)} %bitcast), calls=%async_computation.2 | async-start | bytes 8388608
  22.3 7.1 %slice-start.3 = ((s8[16777216]{0:T(1024)(128)(4,1)}), s8[4194304]{0:T(1024)(128)(4,1)S(1)}, s32[]{:S(2)}) async-start(s8[16777216]{0:T(1024)(128)(4,1)} %bitcast), calls=%async_computation.3 | async-start | bytes 8388608
  22.4 14.2 %collective-permute-start.4 = (bf16[256,512]{1,0:T(8,128)(2,1)S(1)}, bf16[256,512]{1,0:T(8,128)(2,1)S(1)}, u32[]{:S(2)}, u32[]{:S(2)}) collective-permute-start(bf16[256,512]{1,0:T(8,128)(2,1)S(1)} %get-tuple-element.43), channel_id=1, source_target_pairs={{0,4},{2,6},{4,0},{6,2},{8,12},{10,14},{12,8},{14,10},{16,20},{18,... | collective-permute-start | bytes 786440 | tf_op jit(solution)/shard_map/ppermute | solution.py:415
  23.7 12.9 %collective-permute-start.5 = (bf16[256,512]{1,0:T(8,128)(2,1)S(1)}, bf16[256,512]{1,0:T(8,128)(2,1)S(1)}, u32[]{:S(2)}, u32[]{:S(2)}) collective-permute-start(bf16[256,512]{1,0:T(8,128)(2,1)S(1)} %get-tuple-element.44), channel_id=1, source_target_pairs={{0,2},{2,0},{4,6},{6,4},{8,10},{10,8},{12,14},{14,12},{16,18},{18,... | collective-permute-start | bytes 786440 | tf_op jit(solution)/shard_map/ppermute | solution.py:415
  28.0 11.1 %collective-permute-start.3 = (bf16[256,512]{1,0:T(8,128)(2,1)S(1)}, bf16[256,512]{1,0:T(8,128)(2,1)S(1)}, u32[]{:S(2)}, u32[]{:S(2)}) collective-permute-start(bf16[256,512]{1,0:T(8,128)(2,1)S(1)} %relay.6), channel_id=1, source_target_pairs={{0,6},{2,4},{4,2},{6,0},{8,14},{10,12},{12,10},{14,8},{16,22},{18,... | collective-permute-start | bytes 786440 | tf_op jit(solution)/shard_map/ppermute | solution.py:415
  40.8 3.7 %collective-permute-start.9 = (bf16[128,2048]{1,0:T(8,128)(2,1)S(1)}, bf16[128,2048]{1,0:T(8,128)(2,1)S(1)}, u32[]{:S(2)}, u32[]{:S(2)}) collective-permute-start(bf16[128,2048]{1,0:T(8,128)(2,1)S(1)} %get-tuple-element.54), channel_id=1, source_target_pairs={{0,1},{1,0},{2,3},{3,2},{4,5},{5,4},{6,7},{7,6},{8,9},{9,8},{10,11... | collective-permute-start | bytes 1572872 | tf_op jit(solution)/shard_map/ppermute | solution.py:455
  43.7 2.0 %collective-permute-start.10 = (bf16[128,2048]{1,0:T(8,128)(2,1)S(1)}, bf16[128,2048]{1,0:T(8,128)(2,1)S(1)}, u32[]{:S(2)}, u32[]{:S(2)}) collective-permute-start(bf16[128,2048]{1,0:T(8,128)(2,1)S(1)} %send_high.1), channel_id=1, source_target_pairs={{0,1},{1,0},{2,3},{3,2},{4,5},{5,4},{6,7},{7,6},{8,9},{9,8},{10,11... | collective-permute-start | bytes 1572872 | tf_op jit(solution)/shard_map/ppermute | solution.py:459
